TPU v7x, 128 devices: a whole 4x4x4 slice. The times are simulated.
128 devices in a mesh: tile: 32 (over z, x, core), row: 4 (over y).
Axes of the slice: x: 4, y: 4, z: 4, core: 2. Of those that a mesh axis runs over, the one named last changes fastest.
Arguments:
- object_field: float32 [2, 2048, 16384], P(None, 'row', 'tile'), may hold values from -5 to 5
- probe: float32 [2, 256, 256], replicated, may hold values from -5 to 5
- intensity: bfloat16 [4096, 256, 256], P(('tile', 'row')), may hold values from 0 to 4
- pool_rows: int32 [4096], P(('tile', 'row')), may hold values from 0 to 511
- pool_cols: int32 [4096], P(('tile', 'row')), may hold values from 0 to 511
- batch: int32 [2, 1536], P(None, ('tile', 'row')), may hold values from 0 to 31
- live: int32 [2, 128], P(None, ('tile', 'row')), may hold values from 1 to 12, 768 in all within a row
Outputs:
- object_out: float32 [2, 2048, 16384], P(None, 'row', 'tile')
- probe_out: float32 [2, 256, 256], replicated
Inputs may be any that keep to these rules, and one draw needn't show every extreme that they name: `pool_rows`: row offset inside the owning device's block. `pool_cols`: column offset inside the owning device's block. `batch`: index into the device's own 32 stored positions. For each iteration k, the counts live[k, 0] .. live[k, 127] of all 128 devices of the mesh together sum to 768; one device of each iteration has exactly 12.
All inputs are finite; a program needn't handle non-finite values.
Results may differ from a plain program's by a relative error of at most 0.015.
The roundings to bfloat16 on the way count: a program that leaves them out, or rounds other values in their place, can miss the bound.
Values sent between devices are 32-bit elements; how exact they have to be, the bound alone decides.
No kernel may reach another device: no remote copies, remote signals or barrier semaphores. Data moves between devices by JAX's collectives and lax.ppermute only.
A program may use at most 64 MiB of HBM per device.

v0:
```python
import math

import jax
import jax.numpy as jnp
from jax import lax
from jax.sharding import PartitionSpec as P

LIVE = 6


def passed_along(value, axis, steps):
    count = lax.axis_size(axis)
    first, last = (max(0, -steps), min(count, count - steps))
    return lax.ppermute(value, axis, [(source, source + steps) for source in range(first, last)])


def tables(length):
    counter = lax.iota(jnp.int32, length)
    product = counter[:, None] * counter[None, :] % length
    angle = product.astype(jnp.float32) * (2.0 * math.pi / length)
    factor = 1.0 / math.sqrt(length)
    return (
        (jnp.cos(angle) * factor).astype(jnp.bfloat16),
        (jnp.sin(angle) * factor).astype(jnp.bfloat16),
    )


def mul(left, right):
    return jnp.dot(left, right, preferred_element_type=jnp.float32)


def transform(real_part, imag_part, cosine, sine_table, sign):
    half_real = (mul(cosine, real_part) + sign * mul(sine_table, imag_part)).astype(jnp.bfloat16)
    half_imag = (mul(cosine, imag_part) - sign * mul(sine_table, real_part)).astype(jnp.bfloat16)
    out_real = mul(half_real, cosine) + sign * mul(half_imag, sine_table)
    out_imag = mul(half_imag, cosine) - sign * mul(half_real, sine_table)
    return (out_real, out_imag)


def fetch(field, length):
    below = passed_along(field[:, :length, :], "row", -1)
    taller = jnp.concatenate([field, below], axis=1)
    beside = passed_along(taller[:, :, :length], "tile", -1)
    return jnp.concatenate([taller, beside], axis=2)


def give_back(extended, rows_here, cols_here, length):
    beside = passed_along(extended[:, :, cols_here:], "tile", 1)
    narrow = extended[:, :, :cols_here].at[:, :, :length].add(beside)
    below = passed_along(narrow[:, rows_here:, :], "row", 1)
    return narrow[:, :rows_here, :].at[:, :length, :].add(below)


def update_probe(current, grad_probe, probe_rate):
    summed = lax.psum(grad_probe, ("tile", "row"))
    return current - probe_rate * summed


def local(object_field, probe, intensity, pool_rows, pool_cols, batch, live):
    length = probe.shape[1]
    rows_here = object_field.shape[1]
    cols_here = object_field.shape[2]
    slots_cap = batch.shape[1]
    cosine, sine_table = tables(length)
    devices = lax.axis_size("tile") * lax.axis_size("row")
    probe_rate = 0.125 / math.sqrt(LIVE * devices)
    zero_index = jnp.zeros((), jnp.int32)
    field = object_field
    current = probe
    for step_index in range(batch.shape[0]):
        extended = fetch(field, length)
        count_now = live[step_index, 0]

        def one_slot(slot_index, carry):
            grad_ext, grad_probe = carry
            stored = batch[step_index, slot_index]
            row_start = pool_rows[stored]
            col_start = pool_cols[stored]
            patch = lax.dynamic_slice(
                extended, (zero_index, row_start, col_start), (2, length, length)
            )
            alive = (slot_index < count_now).astype(jnp.float32)
            exit_real = (current[0] * patch[0] - current[1] * patch[1]).astype(jnp.bfloat16)
            exit_imag = (current[0] * patch[1] + current[1] * patch[0]).astype(jnp.bfloat16)
            far_real, far_imag = transform(exit_real, exit_imag, cosine, sine_table, 1.0)
            measured = intensity[stored].astype(jnp.float32)
            excess = (far_real * far_real + far_imag * far_imag - measured) * alive
            wave_real = (excess * far_real).astype(jnp.bfloat16)
            wave_imag = (excess * far_imag).astype(jnp.bfloat16)
            back_real, back_imag = transform(wave_real, wave_imag, cosine, sine_table, -1.0)
            obj_real = current[0] * back_real + current[1] * back_imag
            obj_imag = current[0] * back_imag - current[1] * back_real
            prb_real = patch[0] * back_real + patch[1] * back_imag
            prb_imag = patch[0] * back_imag - patch[1] * back_real
            old = lax.dynamic_slice(
                grad_ext, (zero_index, row_start, col_start), (2, length, length)
            )
            grad_ext = lax.dynamic_update_slice(
                grad_ext, old + jnp.stack([obj_real, obj_imag]), (zero_index, row_start, col_start)
            )
            grad_probe = grad_probe + jnp.stack([prb_real, prb_imag])
            return (grad_ext, grad_probe)

        start = (jnp.zeros_like(extended), jnp.zeros_like(current))
        grad_ext, grad_probe = lax.fori_loop(0, slots_cap, one_slot, start)
        grad_field = give_back(grad_ext, rows_here, cols_here, length)
        field = field - 0.25 * grad_field
        current = update_probe(current, grad_probe, probe_rate)
    return (field, current)


def solution(mesh):
    placed = (
        P(None, "row", "tile"),
        P(),
        P(("tile", "row"), None, None),
        P(("tile", "row")),
        P(("tile", "row")),
        P(None, ("tile", "row")),
        P(None, ("tile", "row")),
    )
    return jax.shard_map(
        local, mesh=mesh, in_specs=placed, out_specs=(P(None, "row", "tile"), P()), check_vma=False
    )
```

profile of v0, /device:TPU:1, one launch (start us, length us, event | category | flops | bytes accessed | tf_op | source)
XLA Modules:
  0.0 1438.5 jit_solution(10057905138644012971)
XLA Ops:
  10.2 25.0 %collective-permute-done = f32[2,256,512]{2,1,0:T(8,128)S(1)} collective-permute-done((f32[2,256,512]{2,1,0:T(8,128)S(1)}, f32[2,256,512]{2,1,0:T(8,128)S(1)}, u32[]{:S(2)}, u32[]{:S(2)}) %collective-permute-start) | collective-permute-done | bytes 1048608 | tf_op jit(solution)/shard_map/ppermute | solution.py:14
  37.4 3.5 collective-permute-start.1
  41.6 18.9 %collective-permute-done.1 = f32[2,768,256]{2,1,0:T(8,128)S(1)} collective-permute-done((f32[2,768,256]{2,1,0:T(8,128)}, f32[2,768,256]{2,1,0:T(8,128)S(1)}, u32[]{:S(2)}, u32[]{:S(2)}) %collective-permute-start.1) | collective-permute-done | bytes 1572896 | tf_op jit(solution)/shard_map/ppermute | solution.py:14
  60.5 4.4 pad_maximum_fusion
  64.9 2.5 broadcast.111.clone
  67.4 458.1 %while.38 = (s32[]{:T(128)}, f32[2,768,768]{2,1,0:T(8,128)}, f32[2,256,256]{2,1,0:T(8,128)S(1)}, s32[2,12]{1,0:T(2,128)S(1)}, s32[32]{0:T(128)S(1)}, /*index=5*/...) while((s32[]{:T(128)}, f32[2,768,768]{2,1,0:T(8,128)}, ...), condition=%wide.region_1.2_spmd.clone.clone, body=%wide.region_0.1_spmd.clone.clone.sunk | while | flops 557318144 | bytes 15860079 | solution.py:105
  99.2 6.5 dynamic_update_slice.20
  137.5 6.8 dynamic_update_slice.20
  176.0 6.1 dynamic_update_slice.20
  213.9 6.2 dynamic_update_slice.20
  251.8 6.2 dynamic_update_slice.20
  289.7 6.2 dynamic_update_slice.20
  327.7 6.5 dynamic_update_slice.20
  366.0 6.5 dynamic_update_slice.20
  404.3 6.8 dynamic_update_slice.20
  442.8 6.0 dynamic_update_slice.20
  480.6 6.5 dynamic_update_slice.20
  518.9 6.5 dynamic_update_slice.20
  527.3 3.6 collective-permute-start.2
  533.1 15.1 %collective-permute-done.2 = f32[2,768,256]{2,1,0:T(8,128)S(1)} collective-permute-done((f32[2,768,256]{2,1,0:T(8,128)S(1)}, f32[2,768,256]{2,1,0:T(8,128)S(1)}, u32[]{:S(2)}, u32[]{:S(2)}) %collective-permute-start.2) | collective-permute-done | bytes 1572896 | tf_op jit(solution)/shard_map/ppermute | solution.py:14
  550.0 4.8 collective-permute-start.3
  555.0 11.5 collective-permute-done.3
  568.6 15.0 %collective-permute-done.4 = f32[2,256,512]{2,1,0:T(8,128)S(1)} collective-permute-done((f32[2,256,512]{2,1,0:T(8,128)S(1)}, f32[2,256,512]{2,1,0:T(8,128)S(1)}, u32[]{:S(2)}, u32[]{:S(2)}) %collective-permute-start.4) | collective-permute-done | bytes 1048608 | tf_op jit(solution)/shard_map/ppermute | solution.py:14
  587.8 170.3 %all-reduce.3.cloned.1.call-done = f32[2,256,256]{2,1,0:T(8,128)} async-done(((f32[2,256,256]{2,1,0:T(8,128)}), f32[2,256,256]{2,1,0:T(8,128)}) %all-reduce.3.cloned.1.call-update) | async-done | bytes 524304 | tf_op jit(solution)/shard_map/psum | solution.py:55
  759.3 4.2 pad_maximum_fusion.1
  763.5 2.5 broadcast.111
  766.0 481.3 %while.39 = (s32[]{:T(128)}, f32[2,768,768]{2,1,0:T(8,128)}, f32[2,256,256]{2,1,0:T(8,128)}, s32[2,12]{1,0:T(2,128)S(1)}, s32[32]{0:T(128)S(1)}, /*index=5*/s32[...) while((s32[]{:T(128)}, f32[2,768,768]{2,1,0:T(8,128)}, ...), condition=%wide.region_4.5_spmd.clone.clone, body=%wide.region_3.4_spmd.clone.clone.sunk | while | flops 557318144 | bytes 20054440 | solution.py:105
  807.8 2.5 add_bitcast_fusion.5
  812.6 6.8 dynamic_update_slice.21
  851.9 6.6 dynamic_update_slice.21
  886.1 2.5 add_bitcast_fusion.5
  890.9 6.8 dynamic_update_slice.21
  925.4 2.5 add_bitcast_fusion.5
  930.2 6.8 dynamic_update_slice.21
  964.6 2.5 add_bitcast_fusion.5
  969.4 6.5 dynamic_update_slice.21
  1003.6 2.5 add_bitcast_fusion.5
  1008.4 6.3 dynamic_update_slice.21
  1042.4 2.5 add_bitcast_fusion.5
  1047.2 5.9 dynamic_update_slice.21
  1085.6 6.7 dynamic_update_slice.21
  1124.7 6.5 dynamic_update_slice.21
  1163.7 6.1 dynamic_update_slice.21
  1202.3 6.0 dynamic_update_slice.21
  1240.8 6.5 dynamic_update_slice.21
  1248.8 6.1 collective-permute-start.6
  1257.1 15.1 %collective-permute-done.6 = f32[2,768,256]{2,1,0:T(8,128)S(1)} collective-permute-done((f32[2,768,256]{2,1,0:T(8,128)S(1)}, f32[2,768,256]{2,1,0:T(8,128)S(1)}, u32[]{:S(2)}, u32[]{:S(2)}) %collective-permute-start.6) | collective-permute-done | bytes 1572896 | tf_op jit(solution)/shard_map/ppermute | solution.py:14
  1278.9 145.1 %all-reduce.5.cloned.1.call-done = f32[2,256,256]{2,1,0:T(8,128)} async-done(((f32[2,256,256]{2,1,0:T(8,128)}), f32[2,256,256]{2,1,0:T(8,128)}) %all-reduce.5.cloned.1.call-update) | async-done | bytes 524304 | tf_op jit(solution)/shard_map/psum | solution.py:55
  (603 shorter events, 633.9 us)
Async XLA Ops:
  7.2 2.8 copy-start.6
  7.2 751.0 %all-reduce.3.cloned.1.call-start = ((), (), s32[]{:S(2)}) async-start(), calls=%async_computation | async-start | bytes 1048576 | tf_op jit(solution)/shard_map/psum | solution.py:55
  8.7 26.5 %collective-permute-start = (f32[2,256,512]{2,1,0:T(8,128)S(1)}, f32[2,256,512]{2,1,0:T(8,128)S(1)}, u32[]{:S(2)}, u32[]{:S(2)}) collective-permute-start(f32[2,256,512]{2,1,0:T(8,128)S(1)} %slice.222), channel_id=1, source_target_pairs={{1,0},{2,1},{3,2},{5,4},{6,5},{7,6},{9,8},{10,9},{11,10},{13,12},{... | collective-permute-start | bytes 3145736 | tf_op jit(solution)/shard_map/ppermute | solution.py:14
  10.2 30.8 %copy-start.9 = (s32[2,1]{0,1:T(1,128)S(1)}, s32[2,1]{0,1:T(1,128)}, u32[]{:S(2)}) copy-start(s32[2,1]{0,1:T(1,128)} %param.25) | copy-start | bytes 28
  35.2 2.2 copy-start.5
  37.4 23.1 %collective-permute-start.1 = (f32[2,768,256]{2,1,0:T(8,128)}, f32[2,768,256]{2,1,0:T(8,128)S(1)}, u32[]{:S(2)}, u32[]{:S(2)}) collective-permute-start(f32[2,768,256]{2,1,0:T(8,128)} %slice.256), channel_id=1, source_target_pairs={{4,0},{8,4},{12,8},{16,12},{20,16},{24,20},{28,24},{32,28},{36,32}... | collective-permute-start | bytes 4718600 | tf_op jit(solution)/shard_map/ppermute | solution.py:14
  64.9 2.5 copy-start
  64.9 2.5 copy-start.10
  64.9 2.5 copy-start.11
  64.9 2.5 copy-start.12
  525.6 7.5 copy-start.3
  527.3 20.9 %collective-permute-start.2 = (f32[2,768,256]{2,1,0:T(8,128)S(1)}, f32[2,768,256]{2,1,0:T(8,128)S(1)}, u32[]{:S(2)}, u32[]{:S(2)}) collective-permute-start(f32[2,768,256]{2,1,0:T(8,128)S(1)} %slice.227), channel_id=1, source_target_pairs={{0,4},{4,8},{8,12},{12,16},{16,20},{20,24},{24,28},{28,32},{32,36}... | collective-permute-start | bytes 4718600 | tf_op jit(solution)/shard_map/ppermute | solution.py:14
  550.0 16.7 %copy-start.7 = (f32[2,512,512]{2,1,0:T(8,128)S(1)}, f32[2,512,512]{2,1,0:T(8,128)}, u32[]{:S(2)}) copy-start(f32[2,512,512]{2,1,0:T(8,128)} %param.19) | copy-start | bytes 6291460
  550.0 16.5 %collective-permute-start.3 = (f32[2,256,512]{2,1,0:T(8,128)S(1)}, f32[2,256,512]{2,1,0:T(8,128)S(1)}, u32[]{:S(2)}, u32[]{:S(2)}) collective-permute-start(f32[2,256,512]{2,1,0:T(8,128)S(1)} %slice.259), channel_id=1, source_target_pairs={{0,1},{1,2},{2,3},{4,5},{5,6},{6,7},{8,9},{9,10},{10,11},{12,13},{... | collective-permute-start | bytes 3145736 | tf_op jit(solution)/shard_map/ppermute | solution.py:14
  567.3 16.3 %collective-permute-start.4 = (f32[2,256,512]{2,1,0:T(8,128)S(1)}, f32[2,256,512]{2,1,0:T(8,128)S(1)}, u32[]{:S(2)}, u32[]{:S(2)}) collective-permute-start(f32[2,256,512]{2,1,0:T(8,128)S(1)} %slice.260), channel_id=1, source_target_pairs={{1,0},{2,1},{3,2},{5,4},{6,5},{7,6},{9,8},{10,9},{11,10},{13,12},{... | collective-permute-start | bytes 3145736 | tf_op jit(solution)/shard_map/ppermute | solution.py:14
  583.6 1.0 copy-start.8
  585.8 173.5 %collective-permute-start.5 = (f32[2,768,256]{2,1,0:T(8,128)}, f32[2,768,256]{2,1,0:T(8,128)}, u32[]{:S(2)}, u32[]{:S(2)}) collective-permute-start(f32[2,768,256]{2,1,0:T(8,128)} %pad_maximum_fusion.2), channel_id=1, source_target_pairs={{4,0},{8,4},{12,8},{16,12},{20,16},{24,20},{28,24},{32,28},{36,32}... | collective-permute-start | bytes 4718600 | tf_op jit(solution)/shard_map/ppermute | solution.py:14
  587.8 836.2 %all-reduce.5.cloned.1.call-start = ((), (), s32[]{:S(2)}) async-start(), calls=%async_computation.1 | async-start | bytes 1048576 | tf_op jit(solution)/shard_map/psum | solution.py:55
  804.4 5.9 copy-start.1
  811.8 0.8 copy-start.2
  843.6 5.9 copy-start.1
  851.1 0.8 copy-start.2
  882.7 5.9 copy-start.1
  890.1 0.8 copy-start.2
  921.9 5.9 copy-start.1
  929.4 0.8 copy-start.2
  961.2 5.9 copy-start.1
  968.6 0.8 copy-start.2
  1000.2 5.9 copy-start.1
  1007.6 0.8 copy-start.2
  1039.0 5.9 copy-start.1
  1046.4 0.8 copy-start.2
  1077.4 5.9 copy-start.1
  1084.8 0.8 copy-start.2
  1116.5 5.9 copy-start.1
  1124.0 0.8 copy-start.2
  1155.5 5.9 copy-start.1
  1162.9 0.8 copy-start.2
  1194.1 5.9 copy-start.1
  1201.5 0.8 copy-start.2
  1232.5 5.9 copy-start.1
  1240.0 0.8 copy-start.2
  1248.8 23.4 %collective-permute-start.6 = (f32[2,768,256]{2,1,0:T(8,128)S(1)}, f32[2,768,256]{2,1,0:T(8,128)S(1)}, u32[]{:S(2)}, u32[]{:S(2)}) collective-permute-start(f32[2,768,256]{2,1,0:T(8,128)S(1)} %slice.236), channel_id=1, source_target_pairs={{0,4},{4,8},{8,12},{12,16},{16,20},{20,24},{24,28},{28,32},{32,36}... | collective-permute-start | bytes 4718600 | tf_op jit(solution)/shard_map/ppermute | solution.py:14
  1273.9 1.6 copy-start.4
  1276.6 151.1 %collective-permute-start.7 = (f32[2,256,512]{2,1,0:T(8,128)}, f32[2,256,512]{2,1,0:T(8,128)}, u32[]{:S(2)}, u32[]{:S(2)}) collective-permute-start(f32[2,256,512]{2,1,0:T(8,128)} %slice.263), channel_id=1, source_target_pairs={{0,1},{1,2},{2,3},{4,5},{5,6},{6,7},{8,9},{9,10},{10,11},{12,13},{... | collective-permute-start | bytes 3145736 | tf_op jit(solution)/shard_map/ppermute | solution.py:14
Sparse Core Ops, SparseCore 0:
  587.9 170.2 all-reduce.2
  1279.0 144.9 all-reduce.4
where the time goes:
time: 1460 us; the launch traced here: 1440 us
  matrix products  492 us (34%)
  waiting for transfers between devices  416 us (28%)
  local copies, waits for them, and re-layouts  229 us (16%)
  loops' own time  173 us (12%)
  other arithmetic  88.6 us (6%)
  starting transfers between devices  24.8 us (2%)
  between operations  14.7 us (1%)
    dot_general x384, matrix products, mul(): return jnp.dot(left, right, preferred_element_type=jnp.float32)  492 us
    psum x2, waiting for transfers between devices, update_probe(): summed = lax.psum(grad_probe, ('tile', 'row'))  315 us
    another operation x2, loops' own time, local(): grad_ext, grad_probe = lax.fori_loop(0, slots_cap, one_slot, start)  173 us
    dynamic_update_slice x24, local copies, waits for them, and re-layouts, one_slot(): lax.dynamic_update_slice(grad_ext, old + jnp.stack([obj_real, obj_imag]),...  154 us
    ppermute x8, waiting for transfers between devices, passed_along(): lax.ppermute(value, axis, [(source, source + steps) for source in range(f...  101 us
    add x24, other arithmetic, one_slot(): old + jnp.stack([obj_real, obj_imag])  35.7 us
    convert_element_type x24, other arithmetic, one_slot(): (current[0] * patch[1] + current[1] * patch[0]).astype(jnp.bfloat16)  32.3 us
  transfers between devices with their start and end apart: 10, of which 8 were waited for; matrix products, arithmetic and copies ran while one was open for 1% of the time, Pallas kernels for 0%

commit v1 on v0

v1 whole, which is shorter than its diff:
```python
import functools
import math

import jax
import jax.numpy as jnp
import numpy as np
from jax import lax
from jax.experimental import pallas as pl
from jax.experimental.pallas import tpu as pltpu
from jax.sharding import PartitionSpec as P

LIVE = 6
LANES = 128
F32 = jnp.float32
BF16 = jnp.bfloat16


def passed_along(value, axis, steps):
    count = lax.axis_size(axis)
    first, last = (max(0, -steps), min(count, count - steps))
    return lax.ppermute(value, axis, [(source, source + steps) for source in range(first, last)])


def tables(length):
    counter = np.arange(length, dtype=np.int32)
    product = counter[:, None] * counter[None, :] % length
    angle = product.astype(np.float32) * np.float32(2.0 * math.pi / length)
    factor = np.float32(1.0 / math.sqrt(length))
    cosine = (np.cos(angle) * factor).astype(BF16)
    sine = (np.sin(angle) * factor).astype(BF16)
    forward = np.block([[cosine, sine], [-sine, cosine]])
    backward = np.block([[cosine, -sine], [sine, cosine]])
    return forward, backward


def mul(left, right):
    return jnp.dot(left, right, preferred_element_type=F32)


def start_slots(step, batch, intensity, measured, sems):
    copies = []
    for s in range(batch.shape[1]):
        copies.append(
            pltpu.make_async_copy(intensity.at[batch[step, s]], measured.at[s], sems.at[s]))
    for copy in copies:
        copy.start()
    return copies


def clear(grad, gprobe, waves, patches):
    grad[...] = jnp.zeros_like(grad)
    gprobe[...] = jnp.zeros_like(gprobe)
    waves[1][...] = jnp.zeros_like(waves[1])
    patches[1][...] = jnp.zeros_like(patches[1])


def slot_loop(step, side, batch, live, rows, cols, mats, probe, ext, grad, gprobe,
              measured, exits, waves, patches, back):
    forward, backward = mats
    lane = lax.broadcasted_iota(jnp.int32, (side, LANES), 1)
    halves = side // LANES
    count = live[step, 0]

    def corner_of(s):
        stored = batch[step, s]
        col = cols[stored]
        return rows[stored], col // LANES, col % LANES

    def window(part, tile, row, shift):
        turn = (LANES - shift) & (LANES - 1)
        turned = [
            pltpu.roll(ext[part, tile + j, pl.ds(row, side), :], turn, 1) for j in range(halves + 1)
        ]
        keep = lane < LANES - shift
        return [jnp.where(keep, turned[j], turned[j + 1]) for j in range(halves)]

    def place(part, tile, row, shift, values):
        turned = [pltpu.roll(v, shift, 1) for v in values]
        keep = lane >= shift
        zero = jnp.zeros((side, LANES), F32)
        for j in range(halves + 1):
            here = turned[j] if j < halves else zero
            prior = turned[j - 1] if j else zero
            at = (part, tile + j, pl.ds(row, side), slice(None))
            grad[at] = grad[at] + jnp.where(keep, here, prior)

    def first_half(s, buffer, alive):
        row, tile, shift = corner_of(s)
        exit_in, wave, patch = exits[buffer], waves[buffer], patches[buffer]
        patch_r = window(0, tile, row, shift)
        patch_i = window(1, tile, row, shift)
        for j in range(halves):
            p_r, p_i = probe[0, j], probe[1, j]
            at = slice(j * LANES, (j + 1) * LANES)
            patch[0, j] = patch_r[j]
            patch[1, j] = patch_i[j]
            exit_in[0:side, at] = (p_r * patch_r[j] - p_i * patch_i[j]).astype(BF16)
            exit_in[side:, at] = (p_r * patch_i[j] + p_i * patch_r[j]).astype(BF16)
        half = mul(forward[...], exit_in[...]).astype(BF16)
        far = mul(jnp.concatenate([half[:side], half[side:]], axis=1), backward[...])
        far_r, far_i = far[:, :side], far[:, side:]
        excess = far_r * far_r + far_i * far_i - measured[s].astype(F32)
        if alive is not None:
            excess = excess * alive
        wave[0:side, :] = (excess * far_r).astype(BF16)
        wave[side:, :] = (excess * far_i).astype(BF16)

    def second_half(s, buffer):
        row, tile, shift = corner_of(s)
        wave, patch = waves[buffer], patches[buffer]
        mid = mul(backward[...], wave[...]).astype(BF16)
        back[buffer][...] = mul(jnp.concatenate([mid[:side], mid[side:]], axis=1), forward[...])
        object_r, object_i = [], []
        for j in range(halves):
            p_r, p_i = probe[0, j], probe[1, j]
            o_r, o_i = patch[0, j], patch[1, j]
            b_r = back[buffer][:, j * LANES:(j + 1) * LANES]
            b_i = back[buffer][:, side + j * LANES:side + (j + 1) * LANES]
            object_r.append(p_r * b_r + p_i * b_i)
            object_i.append(p_r * b_i - p_i * b_r)
            gprobe[0, j] += o_r * b_r + o_i * b_i
            gprobe[1, j] += o_r * b_i - o_i * b_r
        place(0, tile, row, shift, object_r)
        place(1, tile, row, shift, object_i)

    def two_slots(k, carry):
        even = 2 * k
        odd = jnp.minimum(even + 1, batch.shape[1] - 1)
        alive = jnp.where(even + 1 < count, 1.0, 0.0).astype(F32)
        second_half(jnp.maximum(even - 1, 0), 1)
        first_half(even, 0, None)
        second_half(even, 0)
        first_half(odd, 1, alive)
        return carry

    pairs = (count + 1) // 2
    lax.fori_loop(0, pairs, two_slots, 0)
    second_half(jnp.minimum(2 * pairs - 1, batch.shape[1] - 1), 1)


def tiled_copies(field, part_rows, part_cols, ext, row0, col0):
    pairs = []
    for part in range(2):
        for j in range(part_cols // LANES):
            pairs.append((
                field.at[part, :, pl.ds(j * LANES, LANES)],
                ext.at[part, col0 // LANES + j, pl.ds(row0, part_rows), :],
            ))
    return pairs


def run_copies(pairs, sems, base=0):
    copies = [pltpu.make_async_copy(src, dst, sems.at[base + i]) for i, (src, dst) in enumerate(pairs)]
    for copy in copies:
        copy.start()
    return copies


def first_kernel(dims, batch, live, rows, cols, forward, backward, probe, intensity,
                 field, below_a, below_b, beside, corner,
                 part_out, gprobe, right_c, left_c, down_b, up_b, right_b, left_b,
                 ext, grad, measured, exit_0, exit_1, wave_0, wave_1, patch_0, patch_1,
                 back_0, back_1, sems, moves):
    side, nrows, ncols = dims
    pairs = tiled_copies(field, nrows, ncols, ext, 0, 0)
    pairs += tiled_copies(below_a, side, side, ext, nrows, 0)
    pairs += tiled_copies(below_b, side, ncols - side, ext, nrows, side)
    pairs += tiled_copies(beside, nrows, side, ext, 0, ncols)
    pairs += tiled_copies(corner, side, side, ext, nrows, ncols)
    copies = run_copies(pairs, moves)
    copies += start_slots(0, batch, intensity, measured, sems)
    waves, patches = (wave_0, wave_1), (patch_0, patch_1)
    clear(grad, gprobe, waves, patches)
    for copy in copies:
        copy.wait()
    slot_loop(0, side, batch, live, rows, cols, (forward, backward), probe, ext, grad, gprobe,
              measured, (exit_0, exit_1), waves, patches, (back_0, back_1))
    t = side // LANES
    last = ncols // LANES
    a_rows, c_rows = pl.ds(0, side), pl.ds(nrows, side)
    b_rows = pl.ds(side, nrows - side)
    left, mid, right = pl.ds(0, t), pl.ds(t, last - t), pl.ds(last, t)
    pairs = [
        (grad.at[:, right, a_rows, :], right_c.at[0]),
        (grad.at[:, right, c_rows, :], right_c.at[1]),
        (grad.at[:, left, a_rows, :], left_c.at[0]),
        (grad.at[:, left, c_rows, :], left_c.at[1]),
        (grad.at[:, mid, c_rows, :], down_b),
        (grad.at[:, mid, a_rows, :], up_b),
        (grad.at[:, right, b_rows, :], right_b),
        (grad.at[:, left, b_rows, :], left_b),
    ]
    copies = run_copies(pairs, moves)
    ext[...] = ext[...] - 0.25 * grad[...]
    copies += run_copies([(ext, part_out)], moves, len(pairs))
    for copy in copies:
        copy.wait()


def join_kernel(left_c, right_c, from_left, from_right, down, up, own, other, moves, stores):
    places = []
    for band, target in ((1, down), (0, up)):
        for side, (mine, received) in enumerate(((left_c, from_left), (right_c, from_right))):
            places.append((mine.at[band], received.at[band], target.at[side]))
    loads = []
    for i, (mine, received, target) in enumerate(places):
        loads.append((pltpu.make_async_copy(mine, own.at[i], moves.at[2 * i]),
                      pltpu.make_async_copy(received, other.at[i], moves.at[2 * i + 1])))
    for pair in loads:
        for copy in pair:
            copy.start()
    copies = []
    for i, (mine, received, target) in enumerate(places):
        for copy in loads[i]:
            copy.wait()
        own[i] = own[i] + other[i]
        copies.append(pltpu.make_async_copy(own.at[i], target, stores.at[i]))
        copies[-1].start()
    for copy in copies:
        copy.wait()


def share_kernel(received, given):
    summed = received[0]
    for i in range(1, received.shape[0]):
        summed = summed + received[i]
    for i in range(received.shape[0]):
        given[i] = summed


def second_kernel(dims, rate, batch, live, rows, cols, edge, forward, backward, probe, summed,
                  intensity, part_in, from_left_c, from_right_c, from_up_c, from_down_c,
                  from_up, from_down, from_left, from_right,
                  own_out, gprobe, right_c, right_ab, down_a, down_b,
                  ext, grad, measured, exit_0, exit_1, wave_0, wave_1, patch_0, patch_1,
                  back_0, back_1, now, lc_in, rc_in, uc_in, dc_in, u_in, d_in, l_in, r_in, sems, moves):
    side, nrows, ncols = dims
    t = side // LANES
    last = ncols // LANES
    pairs = [(part_in, ext), (from_left_c, lc_in), (from_right_c, rc_in), (from_up_c, uc_in),
             (from_down_c, dc_in), (from_up, u_in), (from_down, d_in),
             (from_left, l_in), (from_right, r_in)]
    copies = run_copies(pairs, moves)
    copies += start_slots(1, batch, intensity, measured, sems)
    waves, patches = (wave_0, wave_1), (patch_0, patch_1)
    clear(grad, gprobe, waves, patches)
    now[...] = probe[...] - rate * summed[...]
    for copy in copies:
        copy.wait()
    a_rows, c_rows = slice(0, side), slice(nrows, nrows + side)
    b_rows = slice(side, nrows)
    left, mid, right = slice(0, t), slice(t, last), slice(last, last + t)
    for rows_of, corner, strip, k in ((a_rows, uc_in, u_in, 0), (c_rows, dc_in, d_in, 1)):
        ext[:, left, rows_of, :] -= 0.25 * (corner[0] + lc_in[k])
        ext[:, mid, rows_of, :] -= 0.25 * strip[...]
        ext[:, right, rows_of, :] -= 0.25 * (corner[1] + rc_in[k])
    ext[:, left, b_rows, :] -= 0.25 * l_in[...]
    ext[:, right, b_rows, :] -= 0.25 * r_in[...]

    @pl.when(edge[0] == 1)
    def _():
        ext[:, :, c_rows, :] = jnp.zeros((2, last + t, side, LANES), F32)

    @pl.when(edge[1] == 1)
    def _():
        ext[:, right, :, :] = jnp.zeros((2, t, nrows + side, LANES), F32)

    slot_loop(1, side, batch, live, rows, cols, (forward, backward), now, ext, grad, gprobe,
              measured, (exit_0, exit_1), waves, patches, (back_0, back_1))
    c_rows, own_rows = pl.ds(nrows, side), pl.ds(0, nrows)
    own_cols, right = pl.ds(0, last), pl.ds(last, t)
    pairs = [
        (grad.at[:, right, c_rows, :], right_c),
        (grad.at[:, pl.ds(t, last - t), c_rows, :], down_b),
        (grad.at[:, pl.ds(0, t), c_rows, :], down_a),
        (grad.at[:, right, own_rows, :], right_ab),
    ]
    copies = run_copies(pairs, moves)
    ext[:, 0:last, 0:nrows, :] = ext[:, 0:last, 0:nrows, :] - 0.25 * grad[:, 0:last, 0:nrows, :]
    copies += run_copies([(ext.at[:, own_cols, own_rows, :], own_out)], moves, len(pairs))
    for copy in copies:
        copy.wait()


def last_kernel(dims, rate, own, left_ab, above_a, above_b, probe, sum_one, sum_two,
                object_out, probe_out):
    side, nrows, ncols = dims
    t = side // LANES
    for part in range(2):
        for j in range(ncols // LANES):
            lanes = slice(j * LANES, (j + 1) * LANES)
            if j < t:
                top = own[part, j, 0:side, :] - 0.25 * (
                    left_ab[part, j, 0:side, :] + above_a[part, j])
                low = own[part, j, side:, :] - 0.25 * left_ab[part, j, side:, :]
            else:
                top = own[part, j, 0:side, :] - 0.25 * above_b[part, j - t]
                low = own[part, j, side:, :]
            object_out[part, 0:side, lanes] = top
            object_out[part, side:, lanes] = low
        for j in range(t):
            probe_out[part, :, j * LANES:(j + 1) * LANES] = (
                probe[part, j] - rate * (sum_one[part, j] + sum_two[part, j]))


def call(kernel, dims, slots, scalars, vectors, plain, outs, extra, name):
    side, nrows, ncols = dims
    big = (2, (ncols + side) // LANES, nrows + side, LANES)
    smem = pl.BlockSpec(memory_space=pltpu.SMEM)
    vmem = pl.BlockSpec(memory_space=pltpu.VMEM)
    anywhere = pl.BlockSpec(memory_space=pl.ANY)
    return pl.pallas_call(
        kernel,
        out_shape=[jax.ShapeDtypeStruct(shape, F32) for shape in outs],
        in_specs=[smem] * len(scalars) + [vmem] * len(vectors) + [anywhere] * len(plain),
        out_specs=[vmem if i == 1 else anywhere for i in range(len(outs))],
        scratch_shapes=[
            pltpu.VMEM(big, F32),
            pltpu.VMEM(big, F32),
            pltpu.VMEM((slots, side, side), BF16),
        ] + [pltpu.VMEM((2 * side, side), BF16)] * 4
        + [pltpu.VMEM((2, side // LANES, side, LANES), F32)] * 2
        + [pltpu.VMEM((side, 2 * side), F32)] * 2
        + [pltpu.VMEM(shape, F32) for shape in extra] + [
            pltpu.SemaphoreType.DMA((slots,)),
            pltpu.SemaphoreType.DMA((48,)),
        ],
        compiler_params=pltpu.CompilerParams(vmem_limit_bytes=48 * 1024 * 1024),
        name=name,
    )(*scalars, *vectors, *plain)


def swap(shares):
    return lax.all_to_all(shares, ("tile", "row"), 0, 0, tiled=True)


def hand_out(mine, shape):
    given = pl.pallas_call(
        share_kernel, out_shape=jax.ShapeDtypeStruct(mine.shape, F32), name="sum_shares",
    )(mine)
    return swap(given).reshape(shape)


def join(left_c, right_c, from_left, from_right):
    anywhere = pl.BlockSpec(memory_space=pl.ANY)
    block = (4,) + left_c.shape[1:]
    return pl.pallas_call(
        join_kernel,
        out_shape=[jax.ShapeDtypeStruct(left_c.shape, F32)] * 2,
        in_specs=[anywhere] * 4,
        out_specs=[anywhere] * 2,
        scratch_shapes=[pltpu.VMEM(block, F32), pltpu.VMEM(block, F32),
                        pltpu.SemaphoreType.DMA((8,)), pltpu.SemaphoreType.DMA((4,))],
        compiler_params=pltpu.CompilerParams(vmem_limit_bytes=16 * 1024 * 1024),
        name="join_corners",
    )(left_c, right_c, from_left, from_right)


def local(object_field, probe, intensity, pool_rows, pool_cols, batch, live):
    side = probe.shape[1]
    nrows, ncols = object_field.shape[1:]
    dims = (side, nrows, ncols)
    slots = batch.shape[1]
    t = side // LANES
    total = (ncols + side) // LANES
    devices = lax.axis_size("tile") * lax.axis_size("row")
    probe_rate = 0.125 / math.sqrt(LIVE * devices)
    forward, backward = tables(side)
    forward, backward = jnp.asarray(forward), jnp.asarray(backward)
    current = probe.reshape(2, side, t, LANES).transpose(0, 2, 1, 3)

    below_a = passed_along(object_field[:, :side, :side], "row", -1)
    beside = passed_along(object_field[:, :, :side], "tile", -1)
    below_b = passed_along(object_field[:, :side, side:], "row", -1)
    corner = passed_along(below_a, "tile", -1)

    scalars = (batch, live, pool_rows, pool_cols)
    corners = (2, 2, t, side, LANES)
    edge_b = (2, ncols // LANES - t, side, LANES)
    edge_r = (2, t, nrows - side, LANES)
    part, gprobe, right_c, left_c, down_b, up_b, right_b, left_b = call(
        functools.partial(first_kernel, dims), dims, slots, scalars, (forward, backward, current),
        (intensity, object_field, below_a, below_b, beside, corner),
        [(2, total, nrows + side, LANES), current.shape, corners, corners,
         edge_b, edge_b, edge_r, edge_r], [], "first_iteration")

    from_left_c = passed_along(right_c, "tile", 1)
    from_right_c = passed_along(left_c, "tile", -1)
    from_up_b = passed_along(down_b, "row", 1)
    from_down_b = passed_along(up_b, "row", -1)
    mine = swap(gprobe.reshape(devices, -1, LANES))
    mine, from_left_c, from_right_c = lax.optimization_barrier((mine, from_left_c, from_right_c))
    down_c, up_c = join(left_c, right_c, from_left_c, from_right_c)
    from_up_c = passed_along(down_c, "row", 1)
    from_down_c = passed_along(up_c, "row", -1)
    mine, right_b, left_b, from_up_b, from_down_b, _ = lax.optimization_barrier(
        (mine, right_b, left_b, from_up_b, from_down_b, down_c))
    from_left_b = passed_along(right_b, "tile", 1)
    from_right_b = passed_along(left_b, "tile", -1)
    sum_one = hand_out(mine, current.shape)

    edge = jnp.stack([
        (lax.axis_index("row") == lax.axis_size("row") - 1).astype(jnp.int32),
        (lax.axis_index("tile") == lax.axis_size("tile") - 1).astype(jnp.int32)])
    own, gprobe, right_c, right_ab, down_a, down_b = call(
        functools.partial(second_kernel, dims, probe_rate), dims, slots, scalars + (edge,),
        (forward, backward, current, sum_one),
        (intensity, part, from_left_c, from_right_c, from_up_c, from_down_c,
         from_up_b, from_down_b, from_left_b, from_right_b),
        [(2, ncols // LANES, nrows, LANES), current.shape, (2, t, side, LANES),
         (2, t, nrows, LANES), (2, t, side, LANES), edge_b],
        [current.shape, corners, corners, corners, corners, edge_b, edge_b, edge_r, edge_r],
        "second_iteration")

    from_left_c = passed_along(right_c, "tile", 1)
    above_b = passed_along(down_b, "row", 1)
    mine = swap(gprobe.reshape(devices, -1, LANES))
    down_a = down_a + from_left_c
    above_a = passed_along(down_a, "row", 1)
    mine, right_ab, above_b, _ = lax.optimization_barrier((mine, right_ab, above_b, down_a))
    left_ab = passed_along(right_ab, "tile", 1)
    sum_two = hand_out(mine, current.shape)
    return pl.pallas_call(
        functools.partial(last_kernel, dims, probe_rate),
        out_shape=[jax.ShapeDtypeStruct(object_field.shape, F32),
                   jax.ShapeDtypeStruct(probe.shape, F32)],
        compiler_params=pltpu.CompilerParams(vmem_limit_bytes=48 * 1024 * 1024),
        name="last_update",
    )(own, left_ab, above_a, above_b, current, sum_one, sum_two)


def solution(mesh):
    placed = (
        P(None, "row", "tile"),
        P(),
        P(("tile", "row"), None, None),
        P(("tile", "row")),
        P(("tile", "row")),
        P(None, ("tile", "row")),
        P(None, ("tile", "row")),
    )
    return jax.shard_map(
        local, mesh=mesh, in_specs=placed, out_specs=(P(None, "row", "tile"), P()), check_vma=False
    )
```

time: 1460 us -> 214 us (0.15); the launches traced: 1440 us -> 213 us
  matrix products: 492 us -> 0 us
  waiting for transfers between devices: 416 us -> 50.2 us
  local copies, waits for them, and re-layouts: 229 us -> 16 us
  loops' own time: 173 us -> 0 us
  other arithmetic: 88.6 us -> 2.27 us
  starting transfers between devices: 24.8 us -> 82.6 us
  Pallas kernels: 0 us -> 42.1 us
  blocking collectives: 0 us -> 19 us
    dot_general x384 -> x0, matrix products: 492 us -> none  [mul(): return jnp.dot(left, right, preferred_element_type=jnp.float32)]
    psum x2 -> x0, waiting for transfers between devices: 315 us -> none  [update_probe(): summed = lax.psum(grad_probe, ('tile', 'row'))]
    another operation x2 -> x0, loops' own time: 173 us -> none  [local(): grad_ext, grad_probe = lax.fori_loop(0, slots_cap, one_slot, start)]
    dynamic_update_slice x24 -> x0, local copies, waits for them, and re-layouts: 154 us -> none  [one_slot(): lax.dynamic_update_slice(grad_ext, old + jnp.stack([obj_real, obj_imag]),...]
    ppermute x8 -> x16, waiting for transfers between devices: 101 us -> 14 us  [passed_along(): lax.ppermute(value, axis, [(source, source + steps) for source in range(f...]
    dynamic_slice x72 -> x0, local copies, waits for them, and re-layouts: 42.3 us -> none  [the longest x24 14.1 us: one_slot(): col_start = pool_cols[stored]]
    pallas_call x0 -> x6, Pallas kernels: none -> 42.1 us  [the longest x2 32.8 us: call(): pl.pallas_call(kernel, out_shape=[jax.ShapeDtypeStruct(shape, F32) for sh...]
    all_to_all x0 -> x3, waiting for transfers between devices: none -> 36.2 us  [swap(): return lax.all_to_all(shares, ('tile', 'row'), 0, 0, tiled=True)]
  transfers between devices with their start and end apart: 10 -> 19, of which waited for: 8 -> 6; matrix products, arithmetic and copies ran while one was open for 1% -> 3% of each run, Pallas kernels for 0% -> 3%
where the time goes in v1:
time: 214 us; the launch traced here: 213 us
  starting transfers between devices  82.6 us (39%)
  waiting for transfers between devices  50.2 us (23%)
  Pallas kernels  42.1 us (20%)
  blocking collectives  19 us (9%)
  local copies, waits for them, and re-layouts  16 us (7%)
  other arithmetic  2.27 us (1%)
    ppermute x16, starting transfers between devices, passed_along(): lax.ppermute(value, axis, [(source, source + steps) for source in range(f...  53.3 us
    all_to_all x3, waiting for transfers between devices, swap(): return lax.all_to_all(shares, ('tile', 'row'), 0, 0, tiled=True)  36.2 us
    pallas_call x2, Pallas kernels, call(): pl.pallas_call(kernel, out_shape=[jax.ShapeDtypeStruct(shape, F32) for sh...  32.8 us
    all_to_all x3, starting transfers between devices, swap(): return lax.all_to_all(shares, ('tile', 'row'), 0, 0, tiled=True)  29.3 us
    all_to_all x1, blocking collectives, swap(): return lax.all_to_all(shares, ('tile', 'row'), 0, 0, tiled=True)  19 us
    ppermute x16, waiting for transfers between devices, passed_along(): lax.ppermute(value, axis, [(source, source + steps) for source in range(f...  14 us
    unnamed x48, local copies, waits for them, and re-layouts  11.4 us
  transfers between devices with their start and end apart: 19, of which 6 were waited for; matrix products, arithmetic and copies ran while one was open for 3% of the time, Pallas kernels for 3%

profile of v1, /device:TPU:1, one launch (start us, length us, event | category | flops | bytes accessed | tf_op | source)
XLA Modules:
  0.0 213.1 jit_solution(18224352128959956282)
XLA Ops:
  0.7 2.3 %fusion = (f32[2,256,256]{2,1,0:T(8,128)}, f32[2,256,256]{2,1,0:T(8,128)S(1)}) fusion(f32[2,512,512]{2,1,0:T(8,128)} %field.1), kind=kLoop, calls=%fused_computation.1 | loop fusion | bytes 2097152 | tf_op jit(solution)/shard_map/slice | solution.py:374
  2.9 1.4 collective-permute-start
  4.4 1.1 slice.11
  5.5 3.3 %collective-permute-start.2 = (f32[2,512,256]{2,1,0:T(8,128)}, f32[2,512,256]{2,1,0:T(8,128)}, u32[]{:S(2)}, u32[]{:S(2)}) collective-permute-start(f32[2,512,256]{2,1,0:T(8,128)} %slice.11), channel_id=1, source_target_pairs={{4,0},{8,4},{12,8},{16,12},{20,16},{24,20},{28,24},{32,28},{36,32}... | collective-permute-start | bytes 3145736 | tf_op jit(solution)/shard_map/ppermute | solution.py:21
  8.8 1.3 collective-permute-start.1
  10.1 8.3 %collective-permute-done.below_a = f32[2,256,256]{2,1,0:T(8,128)S(1)} collective-permute-done((f32[2,256,256]{2,1,0:T(8,128)S(1)}, f32[2,256,256]{2,1,0:T(8,128)S(1)}, u32[]{:S(2)}, u32[]{:S(2)}) %collective-permute-start) | collective-permute-done | bytes 524320 | tf_op jit(solution)/shard_map/ppermute | solution.py:21
  18.3 4.8 %collective-permute-start.3 = (f32[2,256,256]{2,1,0:T(8,128)S(1)}, f32[2,256,256]{2,1,0:T(8,128)S(1)}, u32[]{:S(2)}, u32[]{:S(2)}) collective-permute-start(f32[2,256,256]{2,1,0:T(8,128)S(1)} %collective-permute-done.below_a), channel_id=1, source_target_pairs={{4,0},{8,4},{12,8},{16,12},{20,16},{24,20},{28,24},{32,28},{36,32}... | collective-permute-start | bytes 1572872 | tf_op jit(solution)/shard_map/ppermute | solution.py:21
  23.2 1.0 copy.13
  24.2 1.2 copy.14
  25.5 4.1 %collective-permute-done.1.below_b = f32[2,256,256]{2,1,0:T(8,128)S(1)} collective-permute-done((f32[2,256,256]{2,1,0:T(8,128)}, f32[2,256,256]{2,1,0:T(8,128)S(1)}, u32[]{:S(2)}, u32[]{:S(2)}) %collective-permute-start.1) | collective-permute-done | bytes 524320 | tf_op jit(solution)/shard_map/ppermute | solution.py:21
  29.6 1.6 collective-permute-done.3.corner
  31.2 9.8 %first_iteration.1 = (f32[2,6,768,128]{3,2,1,0:T(8,128)}, f32[2,2,256,128]{3,2,1,0:T(8,128)S(1)}, f32[2,2,2,256,128]{4,3,2,1,0:T(8,128)}, f32[2,2,2,256,128]{4,3...) custom-call(s32[2,12]{1,0:T(2,128)S(1)} %copy-done.13, ...), custom_call_target="tpu_custom_call" | custom-call | tf_op jit(solution)/shard_map/first_iteration/pallas_call | solution.py:312
  41.0 0.8 copy-done.12
  41.8 0.8 copy-done.16
  42.6 0.8 copy-done.17
  43.4 14.4 %collective-permute-start.4 = (f32[2,2,2,256,128]{4,3,2,1,0:T(8,128)}, f32[2,2,2,256,128]{4,3,2,1,0:T(8,128)S(1)}, u32[]{:S(2)}, u32[]{:S(2)}) collective-permute-start(f32[2,2,2,256,128]{4,3,2,1,0:T(8,128)} %get-tuple-element.30.right_c), channel_id=1, source_target_pairs={{0,4},{4,8},{8,12},{12,16},{16,20},{20,24},{24,28},{28,32},{32,36}... | collective-permute-start | bytes 3145736 | tf_op jit(solution)/shard_map/ppermute | solution.py:21
  57.8 1.9 collective-permute-start.5
  59.7 10.6 %all-to-all-start = ((f32[128,8,128]{2,1,0:T(8,128)}), f32[128,8,128]{2,1,0:T(8,128)}, u32[]{:S(2)}, u32[]{:S(2)}) async-start(f32[128,8,128]{2,1,0:T(8,128)} %bitcast.14), calls=%async_computation | async-start | bytes 1048576 | tf_op jit(solution)/shard_map/all_to_all | solution.py:334
  70.4 3.3 %collective-permute-start.6 = (f32[2,2,256,128]{3,2,1,0:T(8,128)}, f32[2,2,256,128]{3,2,1,0:T(8,128)S(1)}, u32[]{:S(2)}, u32[]{:S(2)}) collective-permute-start(f32[2,2,256,128]{3,2,1,0:T(8,128)} %copy-done.17), channel_id=1, source_target_pairs={{0,1},{1,2},{2,3},{4,5},{5,6},{6,7},{8,9},{9,10},{10,11},{12,13},{... | collective-permute-start | bytes 1572872 | tf_op jit(solution)/shard_map/ppermute | solution.py:21
  73.7 1.3 collective-permute-start.7
  75.0 9.2 %all-to-all-done.received = f32[128,8,128]{2,1,0:T(8,128)} async-done(((f32[128,8,128]{2,1,0:T(8,128)}), f32[128,8,128]{2,1,0:T(8,128)}, u32[]{:S(2)}, u32[]{:S(2)}) %all-to-all-start) | async-done | bytes 524320 | tf_op jit(solution)/shard_map/all_to_all | solution.py:334
  84.2 1.6 copy-done.7
  85.8 1.2 copy-done.8
  87.0 1.8 join_corners.1
  88.9 1.3 collective-permute-start.9
  90.2 4.1 %collective-permute-start.8 = (f32[2,2,2,256,128]{4,3,2,1,0:T(8,128)}, f32[2,2,2,256,128]{4,3,2,1,0:T(8,128)S(1)}, u32[]{:S(2)}, u32[]{:S(2)}) collective-permute-start(f32[2,2,2,256,128]{4,3,2,1,0:T(8,128)} %get-tuple-element.39), channel_id=1, source_target_pairs={{0,1},{1,2},{2,3},{4,5},{5,6},{6,7},{8,9},{9,10},{10,11},{12,13},{... | collective-permute-start | bytes 3145736 | tf_op jit(solution)/shard_map/ppermute | solution.py:21
  94.3 4.5 %collective-permute-start.10 = (f32[2,2,256,128]{3,2,1,0:T(8,128)}, f32[2,2,256,128]{3,2,1,0:T(8,128)S(1)}, u32[]{:S(2)}, u32[]{:S(2)}) collective-permute-start(f32[2,2,256,128]{3,2,1,0:T(8,128)} %get-tuple-element.45), channel_id=1, source_target_pairs={{0,4},{4,8},{8,12},{12,16},{16,20},{20,24},{24,28},{28,32},{32,36}... | collective-permute-start | bytes 1572872 | tf_op jit(solution)/shard_map/ppermute | solution.py:21
  98.7 1.9 collective-permute-start.11
  100.7 2.0 sum_shares.2
  102.7 7.9 %all-to-all-start.1 = ((f32[128,8,128]{2,1,0:T(8,128)}), f32[128,8,128]{2,1,0:T(8,128)S(1)}, u32[]{:S(2)}, u32[]{:S(2)}) async-start(f32[128,8,128]{2,1,0:T(8,128)} %sum_shares.2), calls=%async_computation.1 | async-start | bytes 1048576 | tf_op jit(solution)/shard_map/all_to_all | solution.py:334
  110.7 15.9 %all-to-all-done.1 = f32[128,8,128]{2,1,0:T(8,128)S(1)} async-done(((f32[128,8,128]{2,1,0:T(8,128)}), f32[128,8,128]{2,1,0:T(8,128)S(1)}, u32[]{:S(2)}, u32[]{:S(2)}) %all-to-all-start.1) | async-done | bytes 524320 | tf_op jit(solution)/shard_map/all_to_all | solution.py:334
  126.6 0.8 copy-done.20
  127.4 0.4 copy-done.19
  127.7 1.0 copy-done.3
  128.8 1.0 copy-done.5
  129.8 1.0 copy-done.10
  130.9 23.0 %second_iteration.1 = (f32[2,4,512,128]{3,2,1,0:T(8,128)}, f32[2,2,256,128]{3,2,1,0:T(8,128)}, f32[2,2,256,128]{3,2,1,0:T(8,128)}, f32[2,2,512,128]{3,2,1,0:T(8,...) custom-call(s32[2,12]{1,0:T(2,128)S(1)} %copy-done.13, s32[2,1]{1,0:T(2,128)S(1)} %copy.16.live, ...), custom_call_target="tpu_custom_call" | custom-call | tf_op jit(solution)/shard_map/second_iteration/pallas_call | solution.py:312
  153.9 0.8 copy-done.11
  154.7 1.9 collective-permute-start.13
  156.6 2.1 collective-permute-start.12
  158.7 10.8 %all-to-all-start.2 = ((f32[128,8,128]{2,1,0:T(8,128)}), f32[128,8,128]{2,1,0:T(8,128)}, u32[]{:S(2)}, u32[]{:S(2)}) async-start(f32[128,8,128]{2,1,0:T(8,128)} %bitcast.6), calls=%async_computation.2 | async-start | bytes 1048576 | tf_op jit(solution)/shard_map/all_to_all | solution.py:334
  169.5 2.2 %add.3 = f32[2,2,256,128]{3,2,1,0:T(8,128)} add(f32[2,2,256,128]{3,2,1,0:T(8,128)} %copy-done.11, f32[2,2,256,128]{3,2,1,0:T(8,128)} %collective-permute-done.13) | non-fusion elementwise | flops 131072 | bytes 1572864 | tf_op jit(solution)/shard_map/add | solution.py:418
  171.7 11.2 %all-to-all-done.2.received = f32[128,8,128]{2,1,0:T(8,128)} async-done(((f32[128,8,128]{2,1,0:T(8,128)}), f32[128,8,128]{2,1,0:T(8,128)}, u32[]{:S(2)}, u32[]{:S(2)}) %all-to-all-start.2) | async-done | bytes 524320 | tf_op jit(solution)/shard_map/all_to_all | solution.py:334
  182.9 2.7 %collective-permute-start.14 = (f32[2,2,512,128]{3,2,1,0:T(8,128)}, f32[2,2,512,128]{3,2,1,0:T(8,128)}, u32[]{:S(2)}, u32[]{:S(2)}) collective-permute-start(f32[2,2,512,128]{3,2,1,0:T(8,128)} %get-tuple-element.53), channel_id=1, source_target_pairs={{0,4},{4,8},{8,12},{12,16},{16,20},{20,24},{24,28},{28,32},{32,36}... | collective-permute-start | bytes 3145736 | tf_op jit(solution)/shard_map/ppermute | solution.py:21
  185.6 3.1 %collective-permute-start.15 = (f32[2,2,256,128]{3,2,1,0:T(8,128)}, f32[2,2,256,128]{3,2,1,0:T(8,128)}, u32[]{:S(2)}, u32[]{:S(2)}) collective-permute-start(f32[2,2,256,128]{3,2,1,0:T(8,128)} %add.3), channel_id=1, source_target_pairs={{0,1},{1,2},{2,3},{4,5},{5,6},{6,7},{8,9},{9,10},{10,11},{12,13},{... | collective-permute-start | bytes 1572872 | tf_op jit(solution)/shard_map/ppermute | solution.py:21
  188.7 2.0 sum_shares.3
  190.7 19.0 %all_to_all.20 = f32[128,8,128]{2,1,0:T(8,128)S(1)} all-to-all(f32[128,8,128]{2,1,0:T(8,128)} %sum_shares.3), channel_id=1, replica_groups=mesh['tile'=32,'row'=4] {'tile','row'}, dimensions={0} | all-to-all | bytes 1048576 | tf_op jit(solution)/shard_map/all_to_all | solution.py:334
  209.7 3.4 %last_update.1 = (f32[2,512,512]{2,1,0:T(8,128)}, f32[2,256,256]{2,1,0:T(8,128)}) custom-call(f32[2,4,512,128]{3,2,1,0:T(8,128)S(1)} %copy-done.6, f32[2,2,512,128]{3,2,1,0:T(8,128)} %collective-permute-done.14.left_ab, f32[2,2,256,128]{3,2,1,0:T(8,128)} %collective-permute-done.15.above_a, f32[2,2,256,128]{3,2,1,0:T(8,128)} %collective-permute-done.12.above_b, ...), custom_call_target="tpu_custom_call" | custom-call | tf_op jit(solution)/shard_map/last_update/pallas_call | solution.py:423
  (50 shorter events, 0.3 us)
Async XLA Ops:
  0.6 3.8 %copy-start.18 = (f32[2,512,512]{2,1,0:T(8,128)S(1)}, f32[2,512,512]{2,1,0:T(8,128)}, u32[]{:S(2)}) copy-start(f32[2,512,512]{2,1,0:T(8,128)} %field.1) | copy-start | bytes 6291460
  0.6 22.5 %copy-start.22 = (s32[2,1]{0,1:T(1,128)S(1)}, s32[2,1]{0,1:T(1,128)}, u32[]{:S(2)}) copy-start(s32[2,1]{0,1:T(1,128)} %param.15) | copy-start | bytes 28
  0.7 22.6 %copy-start.21 = (f32[2,256,256]{2,1,0:T(8,128)S(1)}, f32[2,256,256]{2,1,0:T(8,128)}, u32[]{:S(2)}) copy-start(f32[2,256,256]{2,1,0:T(8,128)} %param.10) | copy-start | bytes 1572868
  2.9 28.2 %copy-start.2 = (bf16[512,512]{1,0:T(8,128)(2,1)S(1)}, bf16[512,512]{1,0:T(8,128)(2,1)}, u32[]{:S(2)}) copy-start(bf16[512,512]{1,0:T(8,128)(2,1)} %constant.18.clone.backward) | copy-start | bytes 1572868
  2.9 28.2 %copy-start.4 = (bf16[512,512]{1,0:T(8,128)(2,1)S(1)}, bf16[512,512]{1,0:T(8,128)(2,1)}, u32[]{:S(2)}) copy-start(bf16[512,512]{1,0:T(8,128)(2,1)} %constant.17.clone.forward) | copy-start | bytes 1572868
  2.9 28.2 %copy-start.13 = (s32[2,12]{1,0:T(2,128)S(1)}, s32[2,12]{1,0:T(2,128)}, u32[]{:S(2)}) copy-start(s32[2,12]{1,0:T(2,128)} %batch.3) | copy-start | bytes 292
  2.9 28.2 %copy-start.14 = (s32[32]{0:T(128)S(1)}, s32[32]{0:T(128)}, u32[]{:S(2)}) copy-start(s32[32]{0:T(128)} %rows.3) | copy-start | bytes 388
  2.9 28.2 %copy-start.15 = (s32[32]{0:T(128)S(1)}, s32[32]{0:T(128)}, u32[]{:S(2)}) copy-start(s32[32]{0:T(128)} %cols.3) | copy-start | bytes 388
  2.9 15.4 %collective-permute-start = (f32[2,256,256]{2,1,0:T(8,128)S(1)}, f32[2,256,256]{2,1,0:T(8,128)S(1)}, u32[]{:S(2)}, u32[]{:S(2)}) collective-permute-start(f32[2,256,256]{2,1,0:T(8,128)S(1)} %get-tuple-element.57), channel_id=1, source_target_pairs={{1,0},{2,1},{3,2},{5,4},{6,5},{7,6},{9,8},{10,9},{11,10},{13,12},{... | collective-permute-start | bytes 1572872 | tf_op jit(solution)/shard_map/ppermute | solution.py:21
  5.5 25.7 %collective-permute-start.2 = (f32[2,512,256]{2,1,0:T(8,128)}, f32[2,512,256]{2,1,0:T(8,128)}, u32[]{:S(2)}, u32[]{:S(2)}) collective-permute-start(f32[2,512,256]{2,1,0:T(8,128)} %slice.11), channel_id=1, source_target_pairs={{4,0},{8,4},{12,8},{16,12},{20,16},{24,20},{28,24},{32,28},{36,32}... | collective-permute-start | bytes 3145736 | tf_op jit(solution)/shard_map/ppermute | solution.py:21
  8.8 20.8 %collective-permute-start.1 = (f32[2,256,256]{2,1,0:T(8,128)}, f32[2,256,256]{2,1,0:T(8,128)S(1)}, u32[]{:S(2)}, u32[]{:S(2)}) collective-permute-start(f32[2,256,256]{2,1,0:T(8,128)} %get-tuple-element.56), channel_id=1, source_target_pairs={{1,0},{2,1},{3,2},{5,4},{6,5},{7,6},{9,8},{10,9},{11,10},{13,12},{... | collective-permute-start | bytes 1572872 | tf_op jit(solution)/shard_map/ppermute | solution.py:21
  18.3 12.8 %collective-permute-start.3 = (f32[2,256,256]{2,1,0:T(8,128)S(1)}, f32[2,256,256]{2,1,0:T(8,128)S(1)}, u32[]{:S(2)}, u32[]{:S(2)}) collective-permute-start(f32[2,256,256]{2,1,0:T(8,128)S(1)} %collective-permute-done.below_a), channel_id=1, source_target_pairs={{4,0},{8,4},{12,8},{16,12},{20,16},{24,20},{28,24},{32,28},{36,32}... | collective-permute-start | bytes 1572872 | tf_op jit(solution)/shard_map/ppermute | solution.py:21
  41.0 0.8 copy-start.12
  41.8 0.8 copy-start.16
  42.6 0.8 copy-start.17
  43.4 40.8 %collective-permute-start.4 = (f32[2,2,2,256,128]{4,3,2,1,0:T(8,128)}, f32[2,2,2,256,128]{4,3,2,1,0:T(8,128)S(1)}, u32[]{:S(2)}, u32[]{:S(2)}) collective-permute-start(f32[2,2,2,256,128]{4,3,2,1,0:T(8,128)} %get-tuple-element.30.right_c), channel_id=1, source_target_pairs={{0,4},{4,8},{8,12},{12,16},{16,20},{20,24},{24,28},{28,32},{32,36}... | collective-permute-start | bytes 3145736 | tf_op jit(solution)/shard_map/ppermute | solution.py:21
  57.8 26.3 %collective-permute-start.5 = (f32[2,2,2,256,128]{4,3,2,1,0:T(8,128)}, f32[2,2,2,256,128]{4,3,2,1,0:T(8,128)S(1)}, u32[]{:S(2)}, u32[]{:S(2)}) collective-permute-start(f32[2,2,2,256,128]{4,3,2,1,0:T(8,128)} %get-tuple-element.31.left_c), channel_id=1, source_target_pairs={{4,0},{8,4},{12,8},{16,12},{20,16},{24,20},{28,24},{32,28},{36,32}... | collective-permute-start | bytes 3145736 | tf_op jit(solution)/shard_map/ppermute | solution.py:21
  59.7 24.4 %all-to-all-start = ((f32[128,8,128]{2,1,0:T(8,128)}), f32[128,8,128]{2,1,0:T(8,128)}, u32[]{:S(2)}, u32[]{:S(2)}) async-start(f32[128,8,128]{2,1,0:T(8,128)} %bitcast.14), calls=%async_computation | async-start | bytes 1048576 | tf_op jit(solution)/shard_map/all_to_all | solution.py:334
  70.4 23.9 %collective-permute-start.6 = (f32[2,2,256,128]{3,2,1,0:T(8,128)}, f32[2,2,256,128]{3,2,1,0:T(8,128)S(1)}, u32[]{:S(2)}, u32[]{:S(2)}) collective-permute-start(f32[2,2,256,128]{3,2,1,0:T(8,128)} %copy-done.17), channel_id=1, source_target_pairs={{0,1},{1,2},{2,3},{4,5},{5,6},{6,7},{8,9},{9,10},{10,11},{12,13},{... | collective-permute-start | bytes 1572872 | tf_op jit(solution)/shard_map/ppermute | solution.py:21
  73.7 20.5 %collective-permute-start.7 = (f32[2,2,256,128]{3,2,1,0:T(8,128)}, f32[2,2,256,128]{3,2,1,0:T(8,128)}, u32[]{:S(2)}, u32[]{:S(2)}) collective-permute-start(f32[2,2,256,128]{3,2,1,0:T(8,128)} %copy-done.16), channel_id=1, source_target_pairs={{1,0},{2,1},{3,2},{5,4},{6,5},{7,6},{9,8},{10,9},{11,10},{13,12},{... | collective-permute-start | bytes 1572872 | tf_op jit(solution)/shard_map/ppermute | solution.py:21
  84.2 4.7 %copy-start = (f32[2,2,2,256,128]{4,3,2,1,0:T(8,128)}, f32[2,2,2,256,128]{4,3,2,1,0:T(8,128)S(1)}, u32[]{:S(2)}) copy-start(f32[2,2,2,256,128]{4,3,2,1,0:T(8,128)S(1)} %collective-permute-done.4.from_left.from_left_c) | copy-start | bytes 3145732
  84.2 1.6 copy-start.7
  85.8 1.2 copy-start.8
  87.0 1.8 copy-start.1
  88.9 37.7 %collective-permute-start.9 = (f32[2,2,2,256,128]{4,3,2,1,0:T(8,128)}, f32[2,2,2,256,128]{4,3,2,1,0:T(8,128)}, u32[]{:S(2)}, u32[]{:S(2)}) collective-permute-start(f32[2,2,2,256,128]{4,3,2,1,0:T(8,128)} %get-tuple-element.42), channel_id=1, source_target_pairs={{1,0},{2,1},{3,2},{5,4},{6,5},{7,6},{9,8},{10,9},{11,10},{13,12},{... | collective-permute-start | bytes 3145736 | tf_op jit(solution)/shard_map/ppermute | solution.py:21
  90.2 36.4 %collective-permute-start.8 = (f32[2,2,2,256,128]{4,3,2,1,0:T(8,128)}, f32[2,2,2,256,128]{4,3,2,1,0:T(8,128)S(1)}, u32[]{:S(2)}, u32[]{:S(2)}) collective-permute-start(f32[2,2,2,256,128]{4,3,2,1,0:T(8,128)} %get-tuple-element.39), channel_id=1, source_target_pairs={{0,1},{1,2},{2,3},{4,5},{5,6},{6,7},{8,9},{9,10},{10,11},{12,13},{... | collective-permute-start | bytes 3145736 | tf_op jit(solution)/shard_map/ppermute | solution.py:21
  94.2 8.5 %copy-start.9 = (f32[2,2,256,128]{3,2,1,0:T(8,128)}, f32[2,2,256,128]{3,2,1,0:T(8,128)S(1)}, u32[]{:S(2)}) copy-start(f32[2,2,256,128]{3,2,1,0:T(8,128)S(1)} %collective-permute-done.6.from_up) | copy-start | bytes 1572868
  94.3 32.3 %collective-permute-start.10 = (f32[2,2,256,128]{3,2,1,0:T(8,128)}, f32[2,2,256,128]{3,2,1,0:T(8,128)S(1)}, u32[]{:S(2)}, u32[]{:S(2)}) collective-permute-start(f32[2,2,256,128]{3,2,1,0:T(8,128)} %get-tuple-element.45), channel_id=1, source_target_pairs={{0,4},{4,8},{8,12},{12,16},{16,20},{20,24},{24,28},{28,32},{32,36}... | collective-permute-start | bytes 1572872 | tf_op jit(solution)/shard_map/ppermute | solution.py:21
  98.7 27.8 %collective-permute-start.11 = (f32[2,2,256,128]{3,2,1,0:T(8,128)}, f32[2,2,256,128]{3,2,1,0:T(8,128)S(1)}, u32[]{:S(2)}, u32[]{:S(2)}) collective-permute-start(f32[2,2,256,128]{3,2,1,0:T(8,128)} %get-tuple-element.46), channel_id=1, source_target_pairs={{4,0},{8,4},{12,8},{16,12},{20,16},{24,20},{28,24},{32,28},{36,32}... | collective-permute-start | bytes 1572872 | tf_op jit(solution)/shard_map/ppermute | solution.py:21
  102.7 23.9 %all-to-all-start.1 = ((f32[128,8,128]{2,1,0:T(8,128)}), f32[128,8,128]{2,1,0:T(8,128)S(1)}, u32[]{:S(2)}, u32[]{:S(2)}) async-start(f32[128,8,128]{2,1,0:T(8,128)} %sum_shares.2), calls=%async_computation.1 | async-start | bytes 1048576 | tf_op jit(solution)/shard_map/all_to_all | solution.py:334
  126.6 0.8 copy-start.20
  126.6 1.1 copy-start.19
  127.7 1.0 copy-start.3
  128.8 1.0 copy-start.5
  129.8 1.0 copy-start.10
  153.9 0.8 copy-start.11
  154.7 14.8 %collective-permute-start.13 = (f32[2,2,256,128]{3,2,1,0:T(8,128)}, f32[2,2,256,128]{3,2,1,0:T(8,128)}, u32[]{:S(2)}, u32[]{:S(2)}) collective-permute-start(f32[2,2,256,128]{3,2,1,0:T(8,128)} %get-tuple-element.52), channel_id=1, source_target_pairs={{0,4},{4,8},{8,12},{12,16},{16,20},{20,24},{24,28},{28,32},{32,36}... | collective-permute-start | bytes 1572872 | tf_op jit(solution)/shard_map/ppermute | solution.py:21
  156.6 26.3 %collective-permute-start.12 = (f32[2,2,256,128]{3,2,1,0:T(8,128)}, f32[2,2,256,128]{3,2,1,0:T(8,128)}, u32[]{:S(2)}, u32[]{:S(2)}) collective-permute-start(f32[2,2,256,128]{3,2,1,0:T(8,128)} %get-tuple-element.50), channel_id=1, source_target_pairs={{0,1},{1,2},{2,3},{4,5},{5,6},{6,7},{8,9},{9,10},{10,11},{12,13},{... | collective-permute-start | bytes 1572872 | tf_op jit(solution)/shard_map/ppermute | solution.py:21
  158.7 24.2 %all-to-all-start.2 = ((f32[128,8,128]{2,1,0:T(8,128)}), f32[128,8,128]{2,1,0:T(8,128)}, u32[]{:S(2)}, u32[]{:S(2)}) async-start(f32[128,8,128]{2,1,0:T(8,128)} %bitcast.6), calls=%async_computation.2 | async-start | bytes 1048576 | tf_op jit(solution)/shard_map/all_to_all | solution.py:334
  169.5 40.3 %copy-start.6 = (f32[2,4,512,128]{3,2,1,0:T(8,128)S(1)}, f32[2,4,512,128]{3,2,1,0:T(8,128)}, u32[]{:S(2)}) copy-start(f32[2,4,512,128]{3,2,1,0:T(8,128)} %get-tuple-element.47.own) | copy-start | bytes 6291460
  182.9 26.9 %collective-permute-start.14 = (f32[2,2,512,128]{3,2,1,0:T(8,128)}, f32[2,2,512,128]{3,2,1,0:T(8,128)}, u32[]{:S(2)}, u32[]{:S(2)}) collective-permute-start(f32[2,2,512,128]{3,2,1,0:T(8,128)} %get-tuple-element.53), channel_id=1, source_target_pairs={{0,4},{4,8},{8,12},{12,16},{16,20},{20,24},{24,28},{28,32},{32,36}... | collective-permute-start | bytes 3145736 | tf_op jit(solution)/shard_map/ppermute | solution.py:21
  185.6 24.2 %collective-permute-start.15 = (f32[2,2,256,128]{3,2,1,0:T(8,128)}, f32[2,2,256,128]{3,2,1,0:T(8,128)}, u32[]{:S(2)}, u32[]{:S(2)}) collective-permute-start(f32[2,2,256,128]{3,2,1,0:T(8,128)} %add.3), channel_id=1, source_target_pairs={{0,1},{1,2},{2,3},{4,5},{5,6},{6,7},{8,9},{9,10},{10,11},{12,13},{... | collective-permute-start | bytes 1572872 | tf_op jit(solution)/shard_map/ppermute | solution.py:21

commit v2 on v1

--- a/solution.py
+++ b/solution.py
@@ -158,7 +158,7 @@
 
 def first_kernel(dims, batch, live, rows, cols, forward, backward, probe, intensity,
                  field, below_a, below_b, beside, corner,
-                 part_out, gprobe, right_c, left_c, down_b, up_b, right_b, left_b,
+                 middle, gprobe, right_col, left_col, down_b, up_b,
                  ext, grad, measured, exit_0, exit_1, wave_0, wave_1, patch_0, patch_1,
                  back_0, back_1, sems, moves):
     side, nrows, ncols = dims
@@ -180,28 +180,25 @@
     a_rows, c_rows = pl.ds(0, side), pl.ds(nrows, side)
     b_rows = pl.ds(side, nrows - side)
     left, mid, right = pl.ds(0, t), pl.ds(t, last - t), pl.ds(last, t)
-    pairs = [
-        (grad.at[:, right, a_rows, :], right_c.at[0]),
-        (grad.at[:, right, c_rows, :], right_c.at[1]),
-        (grad.at[:, left, a_rows, :], left_c.at[0]),
-        (grad.at[:, left, c_rows, :], left_c.at[1]),
+    copies = run_copies([
+        (grad.at[:, right], right_col),
+        (grad.at[:, left], left_col),
         (grad.at[:, mid, c_rows, :], down_b),
         (grad.at[:, mid, a_rows, :], up_b),
-        (grad.at[:, right, b_rows, :], right_b),
-        (grad.at[:, left, b_rows, :], left_b),
-    ]
-    copies = run_copies(pairs, moves)
-    ext[...] = ext[...] - 0.25 * grad[...]
-    copies += run_copies([(ext, part_out)], moves, len(pairs))
+        (grad.at[:, mid, b_rows, :], middle),
+    ], moves)
     for copy in copies:
         copy.wait()
 
 
-def join_kernel(left_c, right_c, from_left, from_right, down, up, own, other, moves, stores):
+def join_kernel(left_col, right_col, from_left, from_right, down, up, own, other, moves, stores):
+    side = down.shape[3]
+    nrows = left_col.shape[2] - side
     places = []
-    for band, target in ((1, down), (0, up)):
-        for side, (mine, received) in enumerate(((left_c, from_left), (right_c, from_right))):
-            places.append((mine.at[band], received.at[band], target.at[side]))
+    for row, target in ((nrows, down), (0, up)):
+        band = pl.ds(row, side)
+        for which, (mine, received) in enumerate(((left_col, from_left), (right_col, from_right))):
+            places.append((mine.at[:, :, band, :], received.at[:, :, band, :], target.at[which]))
     loads = []
     for i, (mine, received, target) in enumerate(places):
         loads.append((pltpu.make_async_copy(mine, own.at[i], moves.at[2 * i]),
@@ -220,6 +217,44 @@
         copy.wait()
 
 
+def update_kernel(dims, edge, field, below_a, below_b, beside, corner,
+                  middle, left_col, right_col, down_b, up_b,
+                  from_left, from_right, from_up, from_down, part):
+    side, nrows, ncols = dims
+    t = side // LANES
+    last = ncols // LANES
+    for p in range(2):
+        for j in range(last + t):
+            lanes = slice(j * LANES % side, j * LANES % side + LANES)
+            at = slice(j * LANES, (j + 1) * LANES)
+            if j < last:
+                old = field[p, :, at]
+                low = below_a[p, :, lanes] if j < t else below_b[p, :, j * LANES - side:at.stop - side]
+            else:
+                old = beside[p, :, lanes]
+                low = corner[p, :, lanes]
+            if j < t:
+                step = left_col[p, j] + from_left[p, j]
+                part[p, j, 0:nrows, :] = old - 0.25 * step[:nrows]
+                part[p, j, nrows:, :] = low - 0.25 * step[nrows:]
+            elif j < last:
+                part[p, j, 0:side, :] = old[:side] - 0.25 * (up_b[p, j - t] + from_up[p, j - t])
+                part[p, j, side:nrows, :] = old[side:] - 0.25 * middle[p, j - t]
+                part[p, j, nrows:, :] = low - 0.25 * (down_b[p, j - t] + from_down[p, j - t])
+            else:
+                step = right_col[p, j - last] + from_right[p, j - last]
+                part[p, j, 0:nrows, :] = old - 0.25 * step[:nrows]
+                part[p, j, nrows:, :] = low - 0.25 * step[nrows:]
+
+    @pl.when(edge[0] == 1)
+    def _():
+        part[:, :, nrows:, :] = jnp.zeros((2, last + t, side, LANES), F32)
+
+    @pl.when(edge[1] == 1)
+    def _():
+        part[:, last:, :, :] = jnp.zeros((2, t, nrows + side, LANES), F32)
+
+
 def share_kernel(received, given):
     summed = received[0]
     for i in range(1, received.shape[0]):
@@ -229,18 +264,14 @@
 
 
 def second_kernel(dims, rate, batch, live, rows, cols, edge, forward, backward, probe, summed,
-                  intensity, part_in, from_left_c, from_right_c, from_up_c, from_down_c,
-                  from_up, from_down, from_left, from_right,
-                  own_out, gprobe, right_c, right_ab, down_a, down_b,
+                  intensity, part_in, from_up, from_down,
+                  own_out, gprobe, right_col, down_a, down_b,
                   ext, grad, measured, exit_0, exit_1, wave_0, wave_1, patch_0, patch_1,
-                  back_0, back_1, now, lc_in, rc_in, uc_in, dc_in, u_in, d_in, l_in, r_in, sems, moves):
+                  back_0, back_1, now, u_in, d_in, sems, moves):
     side, nrows, ncols = dims
     t = side // LANES
     last = ncols // LANES
-    pairs = [(part_in, ext), (from_left_c, lc_in), (from_right_c, rc_in), (from_up_c, uc_in),
-             (from_down_c, dc_in), (from_up, u_in), (from_down, d_in),
-             (from_left, l_in), (from_right, r_in)]
-    copies = run_copies(pairs, moves)
+    copies = run_copies([(part_in, ext), (from_up, u_in), (from_down, d_in)], moves)
     copies += start_slots(1, batch, intensity, measured, sems)
     waves, patches = (wave_0, wave_1), (patch_0, patch_1)
     clear(grad, gprobe, waves, patches)
@@ -248,32 +279,23 @@
     for copy in copies:
         copy.wait()
     a_rows, c_rows = slice(0, side), slice(nrows, nrows + side)
-    b_rows = slice(side, nrows)
-    left, mid, right = slice(0, t), slice(t, last), slice(last, last + t)
-    for rows_of, corner, strip, k in ((a_rows, uc_in, u_in, 0), (c_rows, dc_in, d_in, 1)):
-        ext[:, left, rows_of, :] -= 0.25 * (corner[0] + lc_in[k])
-        ext[:, mid, rows_of, :] -= 0.25 * strip[...]
-        ext[:, right, rows_of, :] -= 0.25 * (corner[1] + rc_in[k])
-    ext[:, left, b_rows, :] -= 0.25 * l_in[...]
-    ext[:, right, b_rows, :] -= 0.25 * r_in[...]
-
-    @pl.when(edge[0] == 1)
+    left, right = slice(0, t), slice(last, last + t)
+    ext[:, left, a_rows, :] -= 0.25 * u_in[0]
+    ext[:, left, c_rows, :] -= 0.25 * d_in[0]
+
+    @pl.when(edge[1] == 0)
     def _():
-        ext[:, :, c_rows, :] = jnp.zeros((2, last + t, side, LANES), F32)
-
-    @pl.when(edge[1] == 1)
-    def _():
-        ext[:, right, :, :] = jnp.zeros((2, t, nrows + side, LANES), F32)
+        ext[:, right, a_rows, :] -= 0.25 * u_in[1]
+        ext[:, right, c_rows, :] -= 0.25 * d_in[1]
 
     slot_loop(1, side, batch, live, rows, cols, (forward, backward), now, ext, grad, gprobe,
               measured, (exit_0, exit_1), waves, patches, (back_0, back_1))
     c_rows, own_rows = pl.ds(nrows, side), pl.ds(0, nrows)
     own_cols, right = pl.ds(0, last), pl.ds(last, t)
     pairs = [
-        (grad.at[:, right, c_rows, :], right_c),
+        (grad.at[:, right], right_col),
         (grad.at[:, pl.ds(t, last - t), c_rows, :], down_b),
         (grad.at[:, pl.ds(0, t), c_rows, :], down_a),
-        (grad.at[:, right, own_rows, :], right_ab),
     ]
     copies = run_copies(pairs, moves)
     ext[:, 0:last, 0:nrows, :] = ext[:, 0:last, 0:nrows, :] - 0.25 * grad[:, 0:last, 0:nrows, :]
@@ -282,8 +304,7 @@
         copy.wait()
 
 
-def last_kernel(dims, rate, own, left_ab, above_a, above_b, probe, sum_one, sum_two,
-                object_out, probe_out):
+def object_kernel(dims, own, left_col, above_a, above_b, object_out):
     side, nrows, ncols = dims
     t = side // LANES
     for part in range(2):
@@ -291,14 +312,18 @@
             lanes = slice(j * LANES, (j + 1) * LANES)
             if j < t:
                 top = own[part, j, 0:side, :] - 0.25 * (
-                    left_ab[part, j, 0:side, :] + above_a[part, j])
-                low = own[part, j, side:, :] - 0.25 * left_ab[part, j, side:, :]
+                    left_col[part, j, 0:side, :] + above_a[part, j])
+                low = own[part, j, side:, :] - 0.25 * left_col[part, j, side:nrows, :]
             else:
                 top = own[part, j, 0:side, :] - 0.25 * above_b[part, j - t]
                 low = own[part, j, side:, :]
             object_out[part, 0:side, lanes] = top
             object_out[part, side:, lanes] = low
-        for j in range(t):
+
+
+def probe_kernel(rate, probe, sum_one, sum_two, probe_out):
+    for part in range(2):
+        for j in range(probe.shape[1]):
             probe_out[part, :, j * LANES:(j + 1) * LANES] = (
                 probe[part, j] - rate * (sum_one[part, j] + sum_two[part, j]))
 
@@ -308,7 +333,7 @@
     big = (2, (ncols + side) // LANES, nrows + side, LANES)
     smem = pl.BlockSpec(memory_space=pltpu.SMEM)
     vmem = pl.BlockSpec(memory_space=pltpu.VMEM)
-    anywhere = pl.BlockSpec(memory_space=pl.ANY)
+    anywhere = pl.BlockSpec(memory_space=pltpu.HBM)
     return pl.pallas_call(
         kernel,
         out_shape=[jax.ShapeDtypeStruct(shape, F32) for shape in outs],
@@ -341,19 +366,33 @@
     return swap(given).reshape(shape)
 
 
-def join(left_c, right_c, from_left, from_right):
-    anywhere = pl.BlockSpec(memory_space=pl.ANY)
-    block = (4,) + left_c.shape[1:]
+def join(left_col, right_col, from_left, from_right, side):
+    anywhere = pl.BlockSpec(memory_space=pltpu.HBM)
+    corners = (2,) + left_col.shape[:2] + (side, LANES)
+    block = (4,) + corners[1:]
     return pl.pallas_call(
         join_kernel,
-        out_shape=[jax.ShapeDtypeStruct(left_c.shape, F32)] * 2,
+        out_shape=[jax.ShapeDtypeStruct(corners, F32)] * 2,
         in_specs=[anywhere] * 4,
         out_specs=[anywhere] * 2,
         scratch_shapes=[pltpu.VMEM(block, F32), pltpu.VMEM(block, F32),
                         pltpu.SemaphoreType.DMA((8,)), pltpu.SemaphoreType.DMA((4,))],
         compiler_params=pltpu.CompilerParams(vmem_limit_bytes=16 * 1024 * 1024),
         name="join_corners",
-    )(left_c, right_c, from_left, from_right)
+    )(left_col, right_col, from_left, from_right)
+
+
+def simple(kernel, shape, name, scalars, vectors):
+    smem = pl.BlockSpec(memory_space=pltpu.SMEM)
+    vmem = pl.BlockSpec(memory_space=pltpu.VMEM)
+    return pl.pallas_call(
+        kernel,
+        out_shape=jax.ShapeDtypeStruct(shape, F32),
+        in_specs=[smem] * len(scalars) + [vmem] * len(vectors),
+        out_specs=vmem,
+        compiler_params=pltpu.CompilerParams(vmem_limit_bytes=48 * 1024 * 1024),
+        name=name,
+    )(*scalars, *vectors)
 
 
 def local(object_field, probe, intensity, pool_rows, pool_cols, batch, live):
@@ -369,64 +408,61 @@
     forward, backward = jnp.asarray(forward), jnp.asarray(backward)
     current = probe.reshape(2, side, t, LANES).transpose(0, 2, 1, 3)
 
-    below_a = passed_along(object_field[:, :side, :side], "row", -1)
-    beside = passed_along(object_field[:, :, :side], "tile", -1)
-    below_b = passed_along(object_field[:, :side, side:], "row", -1)
+    first, rest = lax.optimization_barrier((object_field[:, :side, :side], object_field))
+    below_a = passed_along(first, "row", -1)
+    beside = passed_along(rest[:, :, :side], "tile", -1)
+    below_b = passed_along(rest[:, :side, side:], "row", -1)
     corner = passed_along(below_a, "tile", -1)
 
     scalars = (batch, live, pool_rows, pool_cols)
-    corners = (2, 2, t, side, LANES)
-    edge_b = (2, ncols // LANES - t, side, LANES)
-    edge_r = (2, t, nrows - side, LANES)
-    part, gprobe, right_c, left_c, down_b, up_b, right_b, left_b = call(
+    halo = (object_field, below_a, below_b, beside, corner)
+    column = (2, t, nrows + side, LANES)
+    strip = (2, ncols // LANES - t, side, LANES)
+    middle = (2, ncols // LANES - t, nrows - side, LANES)
+    middle, gprobe, right_col, left_col, down_b, up_b = call(
         functools.partial(first_kernel, dims), dims, slots, scalars, (forward, backward, current),
-        (intensity, object_field, below_a, below_b, beside, corner),
-        [(2, total, nrows + side, LANES), current.shape, corners, corners,
-         edge_b, edge_b, edge_r, edge_r], [], "first_iteration")
-
-    from_left_c = passed_along(right_c, "tile", 1)
-    from_right_c = passed_along(left_c, "tile", -1)
+        (intensity,) + halo,
+        [middle, current.shape, column, column, strip, strip], [], "first_iteration")
+
+    from_left = passed_along(right_col, "tile", 1)
+    from_right = passed_along(left_col, "tile", -1)
     from_up_b = passed_along(down_b, "row", 1)
     from_down_b = passed_along(up_b, "row", -1)
     mine = swap(gprobe.reshape(devices, -1, LANES))
-    mine, from_left_c, from_right_c = lax.optimization_barrier((mine, from_left_c, from_right_c))
-    down_c, up_c = join(left_c, right_c, from_left_c, from_right_c)
+    mine, from_left, from_right = lax.optimization_barrier((mine, from_left, from_right))
+    down_c, up_c = join(left_col, right_col, from_left, from_right, side)
     from_up_c = passed_along(down_c, "row", 1)
     from_down_c = passed_along(up_c, "row", -1)
-    mine, right_b, left_b, from_up_b, from_down_b, _ = lax.optimization_barrier(
-        (mine, right_b, left_b, from_up_b, from_down_b, down_c))
-    from_left_b = passed_along(right_b, "tile", 1)
-    from_right_b = passed_along(left_b, "tile", -1)
+    mine, from_up_b, from_down_b, _ = lax.optimization_barrier(
+        (mine, from_up_b, from_down_b, down_c))
     sum_one = hand_out(mine, current.shape)
-
     edge = jnp.stack([
         (lax.axis_index("row") == lax.axis_size("row") - 1).astype(jnp.int32),
         (lax.axis_index("tile") == lax.axis_size("tile") - 1).astype(jnp.int32)])
-    own, gprobe, right_c, right_ab, down_a, down_b = call(
+    part = simple(
+        functools.partial(update_kernel, dims), (2, total, nrows + side, LANES), "update_object",
+        (edge,), halo + (middle, left_col, right_col, down_b, up_b,
+                         from_left, from_right, from_up_b, from_down_b))
+
+    corners = (2, 2, t, side, LANES)
+    own, gprobe, right_col, down_a, down_b = call(
         functools.partial(second_kernel, dims, probe_rate), dims, slots, scalars + (edge,),
-        (forward, backward, current, sum_one),
-        (intensity, part, from_left_c, from_right_c, from_up_c, from_down_c,
-         from_up_b, from_down_b, from_left_b, from_right_b),
-        [(2, ncols // LANES, nrows, LANES), current.shape, (2, t, side, LANES),
-         (2, t, nrows, LANES), (2, t, side, LANES), edge_b],
-        [current.shape, corners, corners, corners, corners, edge_b, edge_b, edge_r, edge_r],
-        "second_iteration")
-
-    from_left_c = passed_along(right_c, "tile", 1)
+        (forward, backward, current, sum_one), (intensity, part, from_up_c, from_down_c),
+        [(2, ncols // LANES, nrows, LANES), current.shape, column, (2, t, side, LANES), strip],
+        [current.shape, corners, corners], "second_iteration")
+
+    from_left = passed_along(right_col, "tile", 1)
     above_b = passed_along(down_b, "row", 1)
     mine = swap(gprobe.reshape(devices, -1, LANES))
-    down_a = down_a + from_left_c
+    down_a = down_a + from_left[:, :, nrows:, :]
     above_a = passed_along(down_a, "row", 1)
-    mine, right_ab, above_b, _ = lax.optimization_barrier((mine, right_ab, above_b, down_a))
-    left_ab = passed_along(right_ab, "tile", 1)
+    mine, above_b, _ = lax.optimization_barrier((mine, above_b, down_a))
     sum_two = hand_out(mine, current.shape)
-    return pl.pallas_call(
-        functools.partial(last_kernel, dims, probe_rate),
-        out_shape=[jax.ShapeDtypeStruct(object_field.shape, F32),
-                   jax.ShapeDtypeStruct(probe.shape, F32)],
-        compiler_params=pltpu.CompilerParams(vmem_limit_bytes=48 * 1024 * 1024),
-        name="last_update",
-    )(own, left_ab, above_a, above_b, current, sum_one, sum_two)
+    object_out = simple(functools.partial(object_kernel, dims), object_field.shape, "last_object",
+                        (), (own, from_left, above_a, above_b))
+    probe_out = simple(functools.partial(probe_kernel, probe_rate), probe.shape, "last_probe",
+                       (), (current, sum_one, sum_two))
+    return (object_out, probe_out)
 
 
 def solution(mesh):

time: 214 us -> 239 us (1.12)
  blocking collectives: 19 us -> 49.4 us
  Pallas kernels: 42.1 us -> 35.2 us
  waiting for transfers between devices: 50.2 us -> 55.5 us
  starting transfers between devices: 82.6 us -> 77.8 us
    ppermute x16 -> x13, waiting for transfers between devices: 14 us -> 47.5 us  [passed_along(): lax.ppermute(value, axis, [(source, source + steps) for source in range(f...]
    all_to_all x1 -> x2, blocking collectives: 19 us -> 49.4 us  [swap(): return lax.all_to_all(shares, ('tile', 'row'), 0, 0, tiled=True)]
    all_to_all x3 -> x2, waiting for transfers between devices: 36.2 us -> 8.01 us  [swap(): return lax.all_to_all(shares, ('tile', 'row'), 0, 0, tiled=True)]
    pallas_call x2, Pallas kernels: 32.8 us -> 18.6 us  [call(): pl.pallas_call(kernel, out_shape=[jax.ShapeDtypeStruct(shape, F32) for sh...]
    all_to_all x3 -> x2, starting transfers between devices: 29.3 us -> 20.6 us  [swap(): return lax.all_to_all(shares, ('tile', 'row'), 0, 0, tiled=True)]
    pallas_call x2 -> x4, Pallas kernels: 5.23 us -> 12.2 us  [the longest x3 10.3 us: simple(): pl.pallas_call(kernel, out_shape=jax.ShapeDtypeStruct(shape, F32), in_spe...]
    ppermute x16 -> x13, starting transfers between devices: 53.3 us -> 57.2 us  [passed_along(): lax.ppermute(value, axis, [(source, source + steps) for source in range(f...]
    slice x2 -> x3, local copies, waits for them, and re-layouts: 3.33 us -> 5.24 us  [the longest x1 2.26 us: local(): beside = passed_along(rest[:, :, :side], 'tile', -1)]
  transfers between devices with their start and end apart: 19 -> 15, of which waited for: 6 -> 7; matrix products, arithmetic and copies ran while one was open for 3% -> 3% of each run, Pallas kernels for 3% -> 5%
where the time goes in v2:
time: 239 us; the launch traced here: 238 us
  starting transfers between devices  77.8 us (33%)
  waiting for transfers between devices  55.5 us (23%)
  blocking collectives  49.4 us (21%)
  Pallas kernels  35.2 us (15%)
  local copies, waits for them, and re-layouts  18.3 us (8%)
    ppermute x13, starting transfers between devices, passed_along(): lax.ppermute(value, axis, [(source, source + steps) for source in range(f...  57.2 us
    all_to_all x2, blocking collectives, swap(): return lax.all_to_all(shares, ('tile', 'row'), 0, 0, tiled=True)  49.4 us
    ppermute x13, waiting for transfers between devices, passed_along(): lax.ppermute(value, axis, [(source, source + steps) for source in range(f...  47.5 us
    all_to_all x2, starting transfers between devices, swap(): return lax.all_to_all(shares, ('tile', 'row'), 0, 0, tiled=True)  20.6 us
    pallas_call x2, Pallas kernels, call(): pl.pallas_call(kernel, out_shape=[jax.ShapeDtypeStruct(shape, F32) for sh...  18.6 us
    unnamed x60, local copies, waits for them, and re-layouts  11.8 us
    pallas_call x3, Pallas kernels, simple(): pl.pallas_call(kernel, out_shape=jax.ShapeDtypeStruct(shape, F32), in_spe...  10.3 us
    all_to_all x2, waiting for transfers between devices, swap(): return lax.all_to_all(shares, ('tile', 'row'), 0, 0, tiled=True)  8.01 us
  transfers between devices with their start and end apart: 15, of which 7 were waited for; matrix products, arithmetic and copies ran while one was open for 3% of the time, Pallas kernels for 5%

profile of v2, /device:TPU:1, one launch (start us, length us, event | category | flops | bytes accessed | tf_op | source)
XLA Modules:
  0.0 238.1 jit_solution(2960505395019171751)
XLA Ops:
  0.6 1.1 slice.12
  1.7 1.4 collective-permute-start
  3.2 2.3 slice.14
  5.5 3.5 %collective-permute-start.2 = (f32[2,512,256]{2,1,0:T(8,128)}, f32[2,512,256]{2,1,0:T(8,128)S(1)}, u32[]{:S(2)}, u32[]{:S(2)}) collective-permute-start(f32[2,512,256]{2,1,0:T(8,128)} %slice.14), channel_id=1, source_target_pairs={{4,0},{8,4},{12,8},{16,12},{20,16},{24,20},{28,24},{32,28},{36,32}... | collective-permute-start | bytes 3145736 | tf_op jit(solution)/shard_map/ppermute | solution.py:21
  8.9 1.9 slice.13
  10.8 1.3 collective-permute-start.1
  12.1 5.0 %collective-permute-done.below_a = f32[2,256,256]{2,1,0:T(8,128)S(1)} collective-permute-done((f32[2,256,256]{2,1,0:T(8,128)S(1)}, f32[2,256,256]{2,1,0:T(8,128)S(1)}, u32[]{:S(2)}, u32[]{:S(2)}) %collective-permute-start) | collective-permute-done | bytes 524320 | tf_op jit(solution)/shard_map/ppermute | solution.py:21
  17.1 4.8 %collective-permute-start.3 = (f32[2,256,256]{2,1,0:T(8,128)S(1)}, f32[2,256,256]{2,1,0:T(8,128)}, u32[]{:S(2)}, u32[]{:S(2)}) collective-permute-start(f32[2,256,256]{2,1,0:T(8,128)S(1)} %collective-permute-done.below_a), channel_id=1, source_target_pairs={{4,0},{8,4},{12,8},{16,12},{20,16},{24,20},{28,24},{32,28},{36,32}... | collective-permute-start | bytes 1572872 | tf_op jit(solution)/shard_map/ppermute | solution.py:21
  21.9 0.1 copy.16.live
  22.0 1.0 copy.13
  23.0 1.2 copy.14
  24.3 4.2 %collective-permute-done.1.below_b = f32[2,256,256]{2,1,0:T(8,128)} collective-permute-done((f32[2,256,256]{2,1,0:T(8,128)}, f32[2,256,256]{2,1,0:T(8,128)}, u32[]{:S(2)}, u32[]{:S(2)}) %collective-permute-start.1) | collective-permute-done | bytes 524320 | tf_op jit(solution)/shard_map/ppermute | solution.py:21
  28.5 1.6 collective-permute-done.3.corner
  30.1 1.0 copy-done.4
  31.1 8.6 %first_iteration.1 = (f32[2,2,256,128]{3,2,1,0:T(8,128)S(1)}, f32[2,2,256,128]{3,2,1,0:T(8,128)S(1)}, f32[2,2,768,128]{3,2,1,0:T(8,128)}, f32[2,2,768,128]{3,2,1...) custom-call(s32[2,12]{1,0:T(2,128)S(1)} %copy-done.24, s32[2,1]{1,0:T(2,128)S(1)} %copy.16.live, ...), custom_call_target="tpu_custom_call" | custom-call | tf_op jit(solution)/shard_map/first_iteration/pallas_call | solution.py:337
  39.7 14.4 %collective-permute-start.4 = (f32[2,2,768,128]{3,2,1,0:T(8,128)}, f32[2,2,768,128]{3,2,1,0:T(8,128)S(1)}, u32[]{:S(2)}, u32[]{:S(2)}) collective-permute-start(f32[2,2,768,128]{3,2,1,0:T(8,128)} %get-tuple-element.28.right_col), channel_id=1, source_target_pairs={{0,4},{4,8},{8,12},{12,16},{16,20},{20,24},{24,28},{28,32},{32,36}... | collective-permute-start | bytes 4718600 | tf_op jit(solution)/shard_map/ppermute | solution.py:21
  54.2 1.9 collective-permute-start.5
  56.1 30.9 %all_to_all.20.received = f32[128,8,128]{2,1,0:T(8,128)} all-to-all(f32[128,8,128]{2,1,0:T(8,128)S(1)} %bitcast.15), channel_id=1, replica_groups=mesh['tile'=32,'row'=4] {'tile','row'}, dimensions={0} | all-to-all | bytes 1048576 | tf_op jit(solution)/shard_map/all_to_all | solution.py:359
  87.0 2.0 copy-done
  89.0 1.4 copy-done.1
  90.4 2.0 join_corners.1
  92.4 1.4 collective-permute-start.9
  93.8 5.0 %collective-permute-start.8 = (f32[2,2,2,256,128]{4,3,2,1,0:T(8,128)}, f32[2,2,2,256,128]{4,3,2,1,0:T(8,128)}, u32[]{:S(2)}, u32[]{:S(2)}) collective-permute-start(f32[2,2,2,256,128]{4,3,2,1,0:T(8,128)} %get-tuple-element.35), channel_id=1, source_target_pairs={{0,1},{1,2},{2,3},{4,5},{5,6},{6,7},{8,9},{9,10},{10,11},{12,13},{... | collective-permute-start | bytes 3145736 | tf_op jit(solution)/shard_map/ppermute | solution.py:21
  98.8 1.3 collective-permute-start.6
  100.1 1.3 collective-permute-start.7
  101.4 28.8 %collective-permute-done.6.from_up = f32[2,2,256,128]{3,2,1,0:T(8,128)S(1)} collective-permute-done((f32[2,2,256,128]{3,2,1,0:T(8,128)S(1)}, f32[2,2,256,128]{3,2,1,0:T(8,128)S(1)}, u32[]{:S(2)}, u32[]{:S(2)}) %collective-permute-start.6) | collective-permute-done | bytes 524320 | tf_op jit(solution)/shard_map/ppermute | solution.py:21
  130.2 2.4 sum_shares.2
  132.6 11.9 %all-to-all-start.1 = ((f32[128,8,128]{2,1,0:T(8,128)}), f32[128,8,128]{2,1,0:T(8,128)S(1)}, u32[]{:S(2)}, u32[]{:S(2)}) async-start(f32[128,8,128]{2,1,0:T(8,128)} %sum_shares.2), calls=%async_computation.1 | async-start | bytes 1048576 | tf_op jit(solution)/shard_map/all_to_all | solution.py:359
  144.6 1.0 copy-done.12
  145.6 1.0 copy-done.15
  146.7 1.0 copy-done.17
  147.7 1.0 copy-done.19
  148.7 1.0 copy-done.21
  149.8 1.0 copy-done.23
  150.8 6.7 %update_object.1.part_in = f32[2,6,768,128]{3,2,1,0:T(8,128)} custom-call(s32[2]{0:T(128)S(1)} %add_convert_fusion.edge, f32[2,512,512]{2,1,0:T(8,128)} %field.3, f32[2,256,256]{2,1,0:T(8,128)S(1)} %copy-done.12, f32[2,256,256]{2,1,0:T(8,128)} %collective-permute-done.1.below_b, f32[2,512,256]{2,1,0:T(8,128)S(1)} %copy-done.5, ...), custom_call_target="tpu_custom_call" | custom-call | tf_op jit(solution)/shard_map/update_object/pallas_call | solution.py:388
  157.5 0.7 all-to-all-done.1
  158.3 10.0 %second_iteration.1 = (f32[2,4,512,128]{3,2,1,0:T(8,128)}, f32[2,2,256,128]{3,2,1,0:T(8,128)S(1)}, f32[2,2,768,128]{3,2,1,0:T(8,128)}, f32[2,2,256,128]{3,2,1,0:T(8,128)S(1)}, f32[2,2,256,128]{3,2,1,0:T(8,128)}) custom-call(s32[2,12]{1,0:T(2,128)S(1)} %copy-done.24, s32[2,1]{1,0:T(2,128)S(1)} %copy.16.live, s32[32]{0:T(128)S(1)} %copy-done.25, ...), custom_call_target="tpu_custom_call" | custom-call | tf_op jit(solution)/shard_map/second_iteration/pallas_call | solution.py:337
  168.3 14.0 %collective-permute-start.10 = (f32[2,2,768,128]{3,2,1,0:T(8,128)}, f32[2,2,768,128]{3,2,1,0:T(8,128)S(1)}, u32[]{:S(2)}, u32[]{:S(2)}) collective-permute-start(f32[2,2,768,128]{3,2,1,0:T(8,128)} %get-tuple-element.42), channel_id=1, source_target_pairs={{0,4},{4,8},{8,12},{12,16},{16,20},{20,24},{24,28},{28,32},{32,36}... | collective-permute-start | bytes 4718600 | tf_op jit(solution)/shard_map/ppermute | solution.py:21
  182.3 3.9 %collective-permute-start.12 = (f32[2,2,256,128]{3,2,1,0:T(8,128)}, f32[2,2,256,128]{3,2,1,0:T(8,128)}, u32[]{:S(2)}, u32[]{:S(2)}) collective-permute-start(f32[2,2,256,128]{3,2,1,0:T(8,128)} %get-tuple-element.45), channel_id=1, source_target_pairs={{0,1},{1,2},{2,3},{4,5},{5,6},{6,7},{8,9},{9,10},{10,11},{12,13},{... | collective-permute-start | bytes 1572872 | tf_op jit(solution)/shard_map/ppermute | solution.py:21
  186.2 8.7 %all-to-all-start.2 = ((f32[128,8,128]{2,1,0:T(8,128)}), f32[128,8,128]{2,1,0:T(8,128)}, u32[]{:S(2)}, u32[]{:S(2)}) async-start(f32[128,8,128]{2,1,0:T(8,128)} %bitcast.14), calls=%async_computation.2 | async-start | bytes 1048576 | tf_op jit(solution)/shard_map/all_to_all | solution.py:359
  194.9 7.9 %collective-permute-done.10.left_col = f32[2,2,768,128]{3,2,1,0:T(8,128)S(1)} collective-permute-done((f32[2,2,768,128]{3,2,1,0:T(8,128)}, f32[2,2,768,128]{3,2,1,0:T(8,128)S(1)}, u32[]{:S(2)}, u32[]{:S(2)}) %collective-permute-start.10) | collective-permute-done | bytes 1572896 | tf_op jit(solution)/shard_map/ppermute | solution.py:21
  202.7 0.9 slice_add_fusion
  203.6 3.1 %collective-permute-start.11 = (f32[2,2,256,128]{3,2,1,0:T(8,128)}, f32[2,2,256,128]{3,2,1,0:T(8,128)S(1)}, u32[]{:S(2)}, u32[]{:S(2)}) collective-permute-start(f32[2,2,256,128]{3,2,1,0:T(8,128)} %slice_add_fusion), channel_id=1, source_target_pairs={{0,1},{1,2},{2,3},{4,5},{5,6},{6,7},{8,9},{9,10},{10,11},{12,13},{... | collective-permute-start | bytes 1572872 | tf_op jit(solution)/shard_map/ppermute | solution.py:21
  206.7 7.3 %all-to-all-done.2.received = f32[128,8,128]{2,1,0:T(8,128)} async-done(((f32[128,8,128]{2,1,0:T(8,128)}), f32[128,8,128]{2,1,0:T(8,128)}, u32[]{:S(2)}, u32[]{:S(2)}) %all-to-all-start.2) | async-done | bytes 524320 | tf_op jit(solution)/shard_map/all_to_all | solution.py:359
  214.0 2.0 sum_shares.3
  216.0 18.5 %all_to_all.21 = f32[128,8,128]{2,1,0:T(8,128)S(1)} all-to-all(f32[128,8,128]{2,1,0:T(8,128)} %sum_shares.3), channel_id=1, replica_groups=mesh['tile'=32,'row'=4] {'tile','row'}, dimensions={0} | all-to-all | bytes 1048576 | tf_op jit(solution)/shard_map/all_to_all | solution.py:359
  234.6 0.9 last_probe.1
  235.4 2.7 %last_object.1 = f32[2,512,512]{2,1,0:T(8,128)} custom-call(f32[2,4,512,128]{3,2,1,0:T(8,128)S(1)} %copy-done.10, f32[2,2,768,128]{3,2,1,0:T(8,128)S(1)} %collective-permute-done.10.left_col, f32[2,2,256,128]{3,2,1,0:T(8,128)S(1)} %collective-permute-done.11.above_a, f32[2,2,256,128]{3,2,1,0:T(8,128)} %collective-permute-done.12.above_b), custom_call_target="tpu_custom_call" | custom-call | tf_op jit(solution)/shard_map/last_object/pallas_call | solution.py:388
  (58 shorter events, 0.2 us)
Async XLA Ops:
  1.7 20.2 %copy-start.28 = (s32[2,1]{0,1:T(1,128)S(1)}, s32[2,1]{0,1:T(1,128)}, u32[]{:S(2)}) copy-start(s32[2,1]{0,1:T(1,128)} %param.15) | copy-start | bytes 28
  1.7 20.3 %copy-start.27 = (f32[2,256,256]{2,1,0:T(8,128)S(1)}, f32[2,256,256]{2,1,0:T(8,128)}, u32[]{:S(2)}) copy-start(f32[2,256,256]{2,1,0:T(8,128)} %param.10) | copy-start | bytes 1572868
  1.7 15.4 %collective-permute-start = (f32[2,256,256]{2,1,0:T(8,128)S(1)}, f32[2,256,256]{2,1,0:T(8,128)S(1)}, u32[]{:S(2)}, u32[]{:S(2)}) collective-permute-start(f32[2,256,256]{2,1,0:T(8,128)S(1)} %slice.12), channel_id=1, source_target_pairs={{1,0},{2,1},{3,2},{5,4},{6,5},{7,6},{9,8},{10,9},{11,10},{13,12},{... | collective-permute-start | bytes 1572872 | tf_op jit(solution)/shard_map/ppermute | solution.py:21
  5.4 25.6 %copy-start.6 = (bf16[512,512]{1,0:T(8,128)(2,1)S(1)}, bf16[512,512]{1,0:T(8,128)(2,1)}, u32[]{:S(2)}) copy-start(bf16[512,512]{1,0:T(8,128)(2,1)} %constant.18.clone.backward) | copy-start | bytes 1572868
  5.4 25.6 %copy-start.8 = (bf16[512,512]{1,0:T(8,128)(2,1)S(1)}, bf16[512,512]{1,0:T(8,128)(2,1)}, u32[]{:S(2)}) copy-start(bf16[512,512]{1,0:T(8,128)(2,1)} %constant.17.clone.forward) | copy-start | bytes 1572868
  5.4 25.6 %copy-start.24 = (s32[2,12]{1,0:T(2,128)S(1)}, s32[2,12]{1,0:T(2,128)}, u32[]{:S(2)}) copy-start(s32[2,12]{1,0:T(2,128)} %batch.3) | copy-start | bytes 292
  5.4 25.6 %copy-start.25 = (s32[32]{0:T(128)S(1)}, s32[32]{0:T(128)}, u32[]{:S(2)}) copy-start(s32[32]{0:T(128)} %rows.3) | copy-start | bytes 388
  5.5 25.6 %copy-start.26 = (s32[32]{0:T(128)S(1)}, s32[32]{0:T(128)}, u32[]{:S(2)}) copy-start(s32[32]{0:T(128)} %cols.3) | copy-start | bytes 388
  5.5 24.6 %collective-permute-start.2 = (f32[2,512,256]{2,1,0:T(8,128)}, f32[2,512,256]{2,1,0:T(8,128)S(1)}, u32[]{:S(2)}, u32[]{:S(2)}) collective-permute-start(f32[2,512,256]{2,1,0:T(8,128)} %slice.14), channel_id=1, source_target_pairs={{4,0},{8,4},{12,8},{16,12},{20,16},{24,20},{28,24},{32,28},{36,32}... | collective-permute-start | bytes 3145736 | tf_op jit(solution)/shard_map/ppermute | solution.py:21
  10.8 17.7 %collective-permute-start.1 = (f32[2,256,256]{2,1,0:T(8,128)}, f32[2,256,256]{2,1,0:T(8,128)}, u32[]{:S(2)}, u32[]{:S(2)}) collective-permute-start(f32[2,256,256]{2,1,0:T(8,128)} %slice.13), channel_id=1, source_target_pairs={{1,0},{2,1},{3,2},{5,4},{6,5},{7,6},{9,8},{10,9},{11,10},{13,12},{... | collective-permute-start | bytes 1572872 | tf_op jit(solution)/shard_map/ppermute | solution.py:21
  17.1 22.6 %copy-start.11 = (f32[2,256,256]{2,1,0:T(8,128)}, f32[2,256,256]{2,1,0:T(8,128)S(1)}, u32[]{:S(2)}) copy-start(f32[2,256,256]{2,1,0:T(8,128)S(1)} %collective-permute-done.below_a) | copy-start | bytes 1572868
  17.1 12.9 %collective-permute-start.3 = (f32[2,256,256]{2,1,0:T(8,128)S(1)}, f32[2,256,256]{2,1,0:T(8,128)}, u32[]{:S(2)}, u32[]{:S(2)}) collective-permute-start(f32[2,256,256]{2,1,0:T(8,128)S(1)} %collective-permute-done.below_a), channel_id=1, source_target_pairs={{4,0},{8,4},{12,8},{16,12},{20,16},{24,20},{28,24},{32,28},{36,32}... | collective-permute-start | bytes 1572872 | tf_op jit(solution)/shard_map/ppermute | solution.py:21
  30.0 1.0 copy-start.4
  39.7 52.7 %copy-start.14 = (f32[2,2,256,128]{3,2,1,0:T(8,128)}, f32[2,2,256,128]{3,2,1,0:T(8,128)S(1)}, u32[]{:S(2)}) copy-start(f32[2,2,256,128]{3,2,1,0:T(8,128)S(1)} %get-tuple-element.37.middle) | copy-start | bytes 1572868
  39.7 59.1 %copy-start.16 = (f32[2,2,256,128]{3,2,1,0:T(8,128)}, f32[2,2,256,128]{3,2,1,0:T(8,128)S(1)}, u32[]{:S(2)}) copy-start(f32[2,2,256,128]{3,2,1,0:T(8,128)S(1)} %get-tuple-element.31.down_b) | copy-start | bytes 1572868
  39.7 60.4 %copy-start.18 = (f32[2,2,256,128]{3,2,1,0:T(8,128)}, f32[2,2,256,128]{3,2,1,0:T(8,128)S(1)}, u32[]{:S(2)}) copy-start(f32[2,2,256,128]{3,2,1,0:T(8,128)S(1)} %get-tuple-element.32.up_b) | copy-start | bytes 1572868
  39.7 47.3 %collective-permute-start.4 = (f32[2,2,768,128]{3,2,1,0:T(8,128)}, f32[2,2,768,128]{3,2,1,0:T(8,128)S(1)}, u32[]{:S(2)}, u32[]{:S(2)}) collective-permute-start(f32[2,2,768,128]{3,2,1,0:T(8,128)} %get-tuple-element.28.right_col), channel_id=1, source_target_pairs={{0,4},{4,8},{8,12},{12,16},{16,20},{20,24},{24,28},{28,32},{32,36}... | collective-permute-start | bytes 4718600 | tf_op jit(solution)/shard_map/ppermute | solution.py:21
  54.2 32.8 %collective-permute-start.5 = (f32[2,2,768,128]{3,2,1,0:T(8,128)}, f32[2,2,768,128]{3,2,1,0:T(8,128)S(1)}, u32[]{:S(2)}, u32[]{:S(2)}) collective-permute-start(f32[2,2,768,128]{3,2,1,0:T(8,128)} %get-tuple-element.29.left_col), channel_id=1, source_target_pairs={{4,0},{8,4},{12,8},{16,12},{20,16},{24,20},{28,24},{32,28},{36,32}... | collective-permute-start | bytes 4718600 | tf_op jit(solution)/shard_map/ppermute | solution.py:21
  87.0 5.4 %copy-start.2 = (f32[2,2,768,128]{3,2,1,0:T(8,128)}, f32[2,2,768,128]{3,2,1,0:T(8,128)S(1)}, u32[]{:S(2)}) copy-start(f32[2,2,768,128]{3,2,1,0:T(8,128)S(1)} %collective-permute-done.4.from_left) | copy-start | bytes 4718596
  87.0 2.0 copy-start
  89.0 1.4 copy-start.1
  90.4 2.0 copy-start.3
  92.4 52.2 %copy-start.5 = (f32[2,512,256]{2,1,0:T(8,128)S(1)}, f32[2,512,256]{2,1,0:T(8,128)}, u32[]{:S(2)}) copy-start(f32[2,512,256]{2,1,0:T(8,128)} %copy-done.4) | copy-start | bytes 3145732
  92.4 65.8 %collective-permute-start.9 = (f32[2,2,2,256,128]{4,3,2,1,0:T(8,128)}, f32[2,2,2,256,128]{4,3,2,1,0:T(8,128)}, u32[]{:S(2)}, u32[]{:S(2)}) collective-permute-start(f32[2,2,2,256,128]{4,3,2,1,0:T(8,128)} %get-tuple-element.40), channel_id=1, source_target_pairs={{1,0},{2,1},{3,2},{5,4},{6,5},{7,6},{9,8},{10,9},{11,10},{13,12},{... | collective-permute-start | bytes 3145736 | tf_op jit(solution)/shard_map/ppermute | solution.py:21
  93.8 64.4 %collective-permute-start.8 = (f32[2,2,2,256,128]{4,3,2,1,0:T(8,128)}, f32[2,2,2,256,128]{4,3,2,1,0:T(8,128)}, u32[]{:S(2)}, u32[]{:S(2)}) collective-permute-start(f32[2,2,2,256,128]{4,3,2,1,0:T(8,128)} %get-tuple-element.35), channel_id=1, source_target_pairs={{0,1},{1,2},{2,3},{4,5},{5,6},{6,7},{8,9},{9,10},{10,11},{12,13},{... | collective-permute-start | bytes 3145736 | tf_op jit(solution)/shard_map/ppermute | solution.py:21
  98.8 31.4 %collective-permute-start.6 = (f32[2,2,256,128]{3,2,1,0:T(8,128)S(1)}, f32[2,2,256,128]{3,2,1,0:T(8,128)S(1)}, u32[]{:S(2)}, u32[]{:S(2)}) collective-permute-start(f32[2,2,256,128]{3,2,1,0:T(8,128)S(1)} %get-tuple-element.31.down_b), channel_id=1, source_target_pairs={{0,1},{1,2},{2,3},{4,5},{5,6},{6,7},{8,9},{9,10},{10,11},{12,13},{... | collective-permute-start | bytes 1572872 | tf_op jit(solution)/shard_map/ppermute | solution.py:21
  100.1 30.1 %collective-permute-start.7 = (f32[2,2,256,128]{3,2,1,0:T(8,128)S(1)}, f32[2,2,256,128]{3,2,1,0:T(8,128)S(1)}, u32[]{:S(2)}, u32[]{:S(2)}) collective-permute-start(f32[2,2,256,128]{3,2,1,0:T(8,128)S(1)} %get-tuple-element.32.up_b), channel_id=1, source_target_pairs={{1,0},{2,1},{3,2},{5,4},{6,5},{7,6},{9,8},{10,9},{11,10},{13,12},{... | collective-permute-start | bytes 1572872 | tf_op jit(solution)/shard_map/ppermute | solution.py:21
  130.2 2.4 %copy-start.20 = (f32[2,2,256,128]{3,2,1,0:T(8,128)}, f32[2,2,256,128]{3,2,1,0:T(8,128)S(1)}, u32[]{:S(2)}) copy-start(f32[2,2,256,128]{3,2,1,0:T(8,128)S(1)} %collective-permute-done.6.from_up) | copy-start | bytes 1572868
  130.2 14.3 %copy-start.22 = (f32[2,2,256,128]{3,2,1,0:T(8,128)}, f32[2,2,256,128]{3,2,1,0:T(8,128)S(1)}, u32[]{:S(2)}) copy-start(f32[2,2,256,128]{3,2,1,0:T(8,128)S(1)} %collective-permute-done.7.from_down) | copy-start | bytes 1572868
  132.6 25.6 %all-to-all-start.1 = ((f32[128,8,128]{2,1,0:T(8,128)}), f32[128,8,128]{2,1,0:T(8,128)S(1)}, u32[]{:S(2)}, u32[]{:S(2)}) async-start(f32[128,8,128]{2,1,0:T(8,128)} %sum_shares.2), calls=%async_computation.1 | async-start | bytes 1048576 | tf_op jit(solution)/shard_map/all_to_all | solution.py:359
  144.6 1.0 copy-start.12
  145.6 1.0 copy-start.15
  146.7 1.0 copy-start.17
  147.7 1.0 copy-start.19
  148.7 1.0 copy-start.21
  149.8 1.0 copy-start.23
  150.8 7.4 %copy-start.7 = (bf16[512,512]{1,0:T(8,128)(2,1)S(1)}, bf16[512,512]{1,0:T(8,128)(2,1)}, u32[]{:S(2)}) copy-start(bf16[512,512]{1,0:T(8,128)(2,1)} %constant.18.clone.backward) | copy-start | bytes 1572868
  150.8 7.4 %copy-start.9 = (bf16[512,512]{1,0:T(8,128)(2,1)S(1)}, bf16[512,512]{1,0:T(8,128)(2,1)}, u32[]{:S(2)}) copy-start(bf16[512,512]{1,0:T(8,128)(2,1)} %constant.17.clone.forward) | copy-start | bytes 1572868
  168.3 17.9 %copy-start.13 = (f32[2,2,256,128]{3,2,1,0:T(8,128)}, f32[2,2,256,128]{3,2,1,0:T(8,128)S(1)}, u32[]{:S(2)}) copy-start(f32[2,2,256,128]{3,2,1,0:T(8,128)S(1)} %get-tuple-element.44) | copy-start | bytes 1572868
  168.3 34.5 %collective-permute-start.10 = (f32[2,2,768,128]{3,2,1,0:T(8,128)}, f32[2,2,768,128]{3,2,1,0:T(8,128)S(1)}, u32[]{:S(2)}, u32[]{:S(2)}) collective-permute-start(f32[2,2,768,128]{3,2,1,0:T(8,128)} %get-tuple-element.42), channel_id=1, source_target_pairs={{0,4},{4,8},{8,12},{12,16},{16,20},{20,24},{24,28},{28,32},{32,36}... | collective-permute-start | bytes 4718600 | tf_op jit(solution)/shard_map/ppermute | solution.py:21
  182.3 31.7 %collective-permute-start.12 = (f32[2,2,256,128]{3,2,1,0:T(8,128)}, f32[2,2,256,128]{3,2,1,0:T(8,128)}, u32[]{:S(2)}, u32[]{:S(2)}) collective-permute-start(f32[2,2,256,128]{3,2,1,0:T(8,128)} %get-tuple-element.45), channel_id=1, source_target_pairs={{0,1},{1,2},{2,3},{4,5},{5,6},{6,7},{8,9},{9,10},{10,11},{12,13},{... | collective-permute-start | bytes 1572872 | tf_op jit(solution)/shard_map/ppermute | solution.py:21
  186.2 27.9 %all-to-all-start.2 = ((f32[128,8,128]{2,1,0:T(8,128)}), f32[128,8,128]{2,1,0:T(8,128)}, u32[]{:S(2)}, u32[]{:S(2)}) async-start(f32[128,8,128]{2,1,0:T(8,128)} %bitcast.14), calls=%async_computation.2 | async-start | bytes 1048576 | tf_op jit(solution)/shard_map/all_to_all | solution.py:359
  203.6 31.8 %collective-permute-start.11 = (f32[2,2,256,128]{3,2,1,0:T(8,128)}, f32[2,2,256,128]{3,2,1,0:T(8,128)S(1)}, u32[]{:S(2)}, u32[]{:S(2)}) collective-permute-start(f32[2,2,256,128]{3,2,1,0:T(8,128)} %slice_add_fusion), channel_id=1, source_target_pairs={{0,1},{1,2},{2,3},{4,5},{5,6},{6,7},{8,9},{9,10},{10,11},{12,13},{... | collective-permute-start | bytes 1572872 | tf_op jit(solution)/shard_map/ppermute | solution.py:21
  216.0 19.4 %copy-start.10 = (f32[2,4,512,128]{3,2,1,0:T(8,128)S(1)}, f32[2,4,512,128]{3,2,1,0:T(8,128)}, u32[]{:S(2)}) copy-start(f32[2,4,512,128]{3,2,1,0:T(8,128)} %get-tuple-element.41.own) | copy-start | bytes 6291460

commit v3 on v1

--- a/solution.py
+++ b/solution.py
@@ -11,6 +11,7 @@
 
 LIVE = 6
 LANES = 128
+MIB = 1024 * 1024
 F32 = jnp.float32
 BF16 = jnp.bfloat16
 
@@ -55,7 +56,7 @@
 
 
 def slot_loop(step, side, batch, live, rows, cols, mats, probe, ext, grad, gprobe,
-              measured, exits, waves, patches, back):
+              measured, exits, waves, patches):
     forward, backward = mats
     lane = lax.broadcasted_iota(jnp.int32, (side, LANES), 1)
     halves = side // LANES
@@ -109,13 +110,13 @@
         row, tile, shift = corner_of(s)
         wave, patch = waves[buffer], patches[buffer]
         mid = mul(backward[...], wave[...]).astype(BF16)
-        back[buffer][...] = mul(jnp.concatenate([mid[:side], mid[side:]], axis=1), forward[...])
+        back = mul(jnp.concatenate([mid[:side], mid[side:]], axis=1), forward[...])
         object_r, object_i = [], []
         for j in range(halves):
             p_r, p_i = probe[0, j], probe[1, j]
             o_r, o_i = patch[0, j], patch[1, j]
-            b_r = back[buffer][:, j * LANES:(j + 1) * LANES]
-            b_i = back[buffer][:, side + j * LANES:side + (j + 1) * LANES]
+            b_r = back[:, j * LANES:(j + 1) * LANES]
+            b_i = back[:, side + j * LANES:side + (j + 1) * LANES]
             object_r.append(p_r * b_r + p_i * b_i)
             object_i.append(p_r * b_i - p_i * b_r)
             gprobe[0, j] += o_r * b_r + o_i * b_i
@@ -158,9 +159,9 @@
 
 def first_kernel(dims, batch, live, rows, cols, forward, backward, probe, intensity,
                  field, below_a, below_b, beside, corner,
-                 part_out, gprobe, right_c, left_c, down_b, up_b, right_b, left_b,
+                 part_out, gprobe_out, right_c, left_c, right_b, left_b, down_b, up_b,
                  ext, grad, measured, exit_0, exit_1, wave_0, wave_1, patch_0, patch_1,
-                 back_0, back_1, sems, moves):
+                 gprobe, sems, moves):
     side, nrows, ncols = dims
     pairs = tiled_copies(field, nrows, ncols, ext, 0, 0)
     pairs += tiled_copies(below_a, side, side, ext, nrows, 0)
@@ -174,21 +175,22 @@
     for copy in copies:
         copy.wait()
     slot_loop(0, side, batch, live, rows, cols, (forward, backward), probe, ext, grad, gprobe,
-              measured, (exit_0, exit_1), waves, patches, (back_0, back_1))
+              measured, (exit_0, exit_1), waves, patches)
     t = side // LANES
     last = ncols // LANES
     a_rows, c_rows = pl.ds(0, side), pl.ds(nrows, side)
     b_rows = pl.ds(side, nrows - side)
     left, mid, right = pl.ds(0, t), pl.ds(t, last - t), pl.ds(last, t)
     pairs = [
+        (gprobe, gprobe_out),
         (grad.at[:, right, a_rows, :], right_c.at[0]),
         (grad.at[:, right, c_rows, :], right_c.at[1]),
         (grad.at[:, left, a_rows, :], left_c.at[0]),
         (grad.at[:, left, c_rows, :], left_c.at[1]),
+        (grad.at[:, right, b_rows, :], right_b),
+        (grad.at[:, left, b_rows, :], left_b),
         (grad.at[:, mid, c_rows, :], down_b),
         (grad.at[:, mid, a_rows, :], up_b),
-        (grad.at[:, right, b_rows, :], right_b),
-        (grad.at[:, left, b_rows, :], left_b),
     ]
     copies = run_copies(pairs, moves)
     ext[...] = ext[...] - 0.25 * grad[...]
@@ -197,23 +199,19 @@
         copy.wait()
 
 
-def join_kernel(left_c, right_c, from_left, from_right, down, up, own, other, moves, stores):
+def join_kernel(left_c, right_c, from_left, from_right, down, up, own, moves, stores):
     places = []
     for band, target in ((1, down), (0, up)):
-        for side, (mine, received) in enumerate(((left_c, from_left), (right_c, from_right))):
-            places.append((mine.at[band], received.at[band], target.at[side]))
-    loads = []
-    for i, (mine, received, target) in enumerate(places):
-        loads.append((pltpu.make_async_copy(mine, own.at[i], moves.at[2 * i]),
-                      pltpu.make_async_copy(received, other.at[i], moves.at[2 * i + 1])))
-    for pair in loads:
-        for copy in pair:
-            copy.start()
+        for which, (mine, received) in enumerate(((left_c, from_left), (right_c, from_right))):
+            places.append((mine.at[band], received, band, target.at[which]))
+    loads = [pltpu.make_async_copy(place[0], own.at[i], moves.at[i])
+             for i, place in enumerate(places)]
+    for copy in loads:
+        copy.start()
     copies = []
-    for i, (mine, received, target) in enumerate(places):
-        for copy in loads[i]:
-            copy.wait()
-        own[i] = own[i] + other[i]
+    for i, (mine, received, band, target) in enumerate(places):
+        loads[i].wait()
+        own[i] = own[i] + received[band]
         copies.append(pltpu.make_async_copy(own.at[i], target, stores.at[i]))
         copies[-1].start()
     for copy in copies:
@@ -228,19 +226,16 @@
         given[i] = summed
 
 
-def second_kernel(dims, rate, batch, live, rows, cols, edge, forward, backward, probe, summed,
-                  intensity, part_in, from_left_c, from_right_c, from_up_c, from_down_c,
-                  from_up, from_down, from_left, from_right,
-                  own_out, gprobe, right_c, right_ab, down_a, down_b,
+def second_kernel(dims, rate, batch, live, rows, cols, edge, forward, backward, probe,
+                  summed, intensity, part_in, from_left_c, from_right_c, from_up_c, from_down_c,
+                  from_left, from_right, from_up, from_down,
+                  own_out, gprobe_out, right_c, right_ab, down_a, down_b,
                   ext, grad, measured, exit_0, exit_1, wave_0, wave_1, patch_0, patch_1,
-                  back_0, back_1, now, lc_in, rc_in, uc_in, dc_in, u_in, d_in, l_in, r_in, sems, moves):
+                  gprobe, now, sems, moves):
     side, nrows, ncols = dims
     t = side // LANES
     last = ncols // LANES
-    pairs = [(part_in, ext), (from_left_c, lc_in), (from_right_c, rc_in), (from_up_c, uc_in),
-             (from_down_c, dc_in), (from_up, u_in), (from_down, d_in),
-             (from_left, l_in), (from_right, r_in)]
-    copies = run_copies(pairs, moves)
+    copies = run_copies([(part_in, ext)], moves)
     copies += start_slots(1, batch, intensity, measured, sems)
     waves, patches = (wave_0, wave_1), (patch_0, patch_1)
     clear(grad, gprobe, waves, patches)
@@ -250,12 +245,13 @@
     a_rows, c_rows = slice(0, side), slice(nrows, nrows + side)
     b_rows = slice(side, nrows)
     left, mid, right = slice(0, t), slice(t, last), slice(last, last + t)
-    for rows_of, corner, strip, k in ((a_rows, uc_in, u_in, 0), (c_rows, dc_in, d_in, 1)):
-        ext[:, left, rows_of, :] -= 0.25 * (corner[0] + lc_in[k])
+    for rows_of, corner, strip, k in ((a_rows, from_up_c, from_up, 0),
+                                      (c_rows, from_down_c, from_down, 1)):
+        ext[:, left, rows_of, :] -= 0.25 * (corner[0] + from_left_c[k])
         ext[:, mid, rows_of, :] -= 0.25 * strip[...]
-        ext[:, right, rows_of, :] -= 0.25 * (corner[1] + rc_in[k])
-    ext[:, left, b_rows, :] -= 0.25 * l_in[...]
-    ext[:, right, b_rows, :] -= 0.25 * r_in[...]
+        ext[:, right, rows_of, :] -= 0.25 * (corner[1] + from_right_c[k])
+    ext[:, left, b_rows, :] -= 0.25 * from_left[...]
+    ext[:, right, b_rows, :] -= 0.25 * from_right[...]
 
     @pl.when(edge[0] == 1)
     def _():
@@ -266,10 +262,11 @@
         ext[:, right, :, :] = jnp.zeros((2, t, nrows + side, LANES), F32)
 
     slot_loop(1, side, batch, live, rows, cols, (forward, backward), now, ext, grad, gprobe,
-              measured, (exit_0, exit_1), waves, patches, (back_0, back_1))
+              measured, (exit_0, exit_1), waves, patches)
     c_rows, own_rows = pl.ds(nrows, side), pl.ds(0, nrows)
     own_cols, right = pl.ds(0, last), pl.ds(last, t)
     pairs = [
+        (gprobe, gprobe_out),
         (grad.at[:, right, c_rows, :], right_c),
         (grad.at[:, pl.ds(t, last - t), c_rows, :], down_b),
         (grad.at[:, pl.ds(0, t), c_rows, :], down_a),
@@ -282,8 +279,7 @@
         copy.wait()
 
 
-def last_kernel(dims, rate, own, left_ab, above_a, above_b, probe, sum_one, sum_two,
-                object_out, probe_out):
+def object_kernel(dims, own, left_ab, above_a, above_b, object_out):
     side, nrows, ncols = dims
     t = side // LANES
     for part in range(2):
@@ -298,62 +294,78 @@
                 low = own[part, j, side:, :]
             object_out[part, 0:side, lanes] = top
             object_out[part, side:, lanes] = low
-        for j in range(t):
+
+
+def probe_kernel(rate, probe, sum_one, sum_two, probe_out):
+    for part in range(2):
+        for j in range(probe.shape[1]):
             probe_out[part, :, j * LANES:(j + 1) * LANES] = (
                 probe[part, j] - rate * (sum_one[part, j] + sum_two[part, j]))
 
 
-def call(kernel, dims, slots, scalars, vectors, plain, outs, extra, name):
+def call(kernel, dims, slots, scalars, vectors, plain, received, outs, extra, limit,
+         name):
     side, nrows, ncols = dims
     big = (2, (ncols + side) // LANES, nrows + side, LANES)
     smem = pl.BlockSpec(memory_space=pltpu.SMEM)
     vmem = pl.BlockSpec(memory_space=pltpu.VMEM)
-    anywhere = pl.BlockSpec(memory_space=pl.ANY)
+    hbm = pl.BlockSpec(memory_space=pltpu.HBM)
     return pl.pallas_call(
         kernel,
         out_shape=[jax.ShapeDtypeStruct(shape, F32) for shape in outs],
-        in_specs=[smem] * len(scalars) + [vmem] * len(vectors) + [anywhere] * len(plain),
-        out_specs=[vmem if i == 1 else anywhere for i in range(len(outs))],
+        in_specs=([smem] * len(scalars) + [vmem] * len(vectors) + [hbm] * len(plain)
+                  + [vmem] * len(received)),
+        out_specs=[hbm] * len(outs),
         scratch_shapes=[
             pltpu.VMEM(big, F32),
             pltpu.VMEM(big, F32),
             pltpu.VMEM((slots, side, side), BF16),
         ] + [pltpu.VMEM((2 * side, side), BF16)] * 4
-        + [pltpu.VMEM((2, side // LANES, side, LANES), F32)] * 2
-        + [pltpu.VMEM((side, 2 * side), F32)] * 2
+        + [pltpu.VMEM((2, side // LANES, side, LANES), F32)] * 3
         + [pltpu.VMEM(shape, F32) for shape in extra] + [
             pltpu.SemaphoreType.DMA((slots,)),
             pltpu.SemaphoreType.DMA((48,)),
         ],
-        compiler_params=pltpu.CompilerParams(vmem_limit_bytes=48 * 1024 * 1024),
+        compiler_params=pltpu.CompilerParams(vmem_limit_bytes=limit * MIB),
         name=name,
-    )(*scalars, *vectors, *plain)
+    )(*scalars, *vectors, *plain, *received)
 
 
 def swap(shares):
     return lax.all_to_all(shares, ("tile", "row"), 0, 0, tiled=True)
 
 
-def hand_out(mine, shape):
-    given = pl.pallas_call(
+def add_up(mine):
+    return pl.pallas_call(
         share_kernel, out_shape=jax.ShapeDtypeStruct(mine.shape, F32), name="sum_shares",
     )(mine)
-    return swap(given).reshape(shape)
 
 
 def join(left_c, right_c, from_left, from_right):
-    anywhere = pl.BlockSpec(memory_space=pl.ANY)
-    block = (4,) + left_c.shape[1:]
+    vmem = pl.BlockSpec(memory_space=pltpu.VMEM)
+    hbm = pl.BlockSpec(memory_space=pltpu.HBM)
     return pl.pallas_call(
         join_kernel,
         out_shape=[jax.ShapeDtypeStruct(left_c.shape, F32)] * 2,
-        in_specs=[anywhere] * 4,
-        out_specs=[anywhere] * 2,
-        scratch_shapes=[pltpu.VMEM(block, F32), pltpu.VMEM(block, F32),
-                        pltpu.SemaphoreType.DMA((8,)), pltpu.SemaphoreType.DMA((4,))],
-        compiler_params=pltpu.CompilerParams(vmem_limit_bytes=16 * 1024 * 1024),
+        in_specs=[hbm] * 2 + [vmem] * 2,
+        out_specs=[hbm] * 2,
+        scratch_shapes=[pltpu.VMEM((4,) + left_c.shape[1:], F32),
+                        pltpu.SemaphoreType.DMA((4,)), pltpu.SemaphoreType.DMA((4,))],
+        compiler_params=pltpu.CompilerParams(vmem_limit_bytes=8 * MIB),
         name="join_corners",
     )(left_c, right_c, from_left, from_right)
+
+
+def simple(kernel, shape, name, limit, vectors):
+    vmem = pl.BlockSpec(memory_space=pltpu.VMEM)
+    return pl.pallas_call(
+        kernel,
+        out_shape=jax.ShapeDtypeStruct(shape, F32),
+        in_specs=[vmem] * len(vectors),
+        out_specs=vmem,
+        compiler_params=pltpu.CompilerParams(vmem_limit_bytes=limit * MIB),
+        name=name,
+    )(*vectors)
 
 
 def local(object_field, probe, intensity, pool_rows, pool_cols, batch, live):
@@ -363,26 +375,31 @@
     slots = batch.shape[1]
     t = side // LANES
     total = (ncols + side) // LANES
-    devices = lax.axis_size("tile") * lax.axis_size("row")
-    probe_rate = 0.125 / math.sqrt(LIVE * devices)
+    probe_rate = 0.125 / math.sqrt(LIVE * lax.axis_size("tile") * lax.axis_size("row"))
     forward, backward = tables(side)
     forward, backward = jnp.asarray(forward), jnp.asarray(backward)
     current = probe.reshape(2, side, t, LANES).transpose(0, 2, 1, 3)
 
-    below_a = passed_along(object_field[:, :side, :side], "row", -1)
-    beside = passed_along(object_field[:, :, :side], "tile", -1)
-    below_b = passed_along(object_field[:, :side, side:], "row", -1)
+    first, rest = lax.optimization_barrier((object_field[:, :side, :side], object_field))
+    below_a = passed_along(first, "row", -1)
+    beside = passed_along(rest[:, :, :side], "tile", -1)
+    below_b = passed_along(rest[:, :side, side:], "row", -1)
     corner = passed_along(below_a, "tile", -1)
 
+    edge = jnp.stack([
+        (lax.axis_index("row") == lax.axis_size("row") - 1).astype(jnp.int32),
+        (lax.axis_index("tile") == lax.axis_size("tile") - 1).astype(jnp.int32)])
     scalars = (batch, live, pool_rows, pool_cols)
+    devices = lax.axis_size("tile") * lax.axis_size("row")
+    big = (2, total, nrows + side, LANES)
     corners = (2, 2, t, side, LANES)
-    edge_b = (2, ncols // LANES - t, side, LANES)
-    edge_r = (2, t, nrows - side, LANES)
-    part, gprobe, right_c, left_c, down_b, up_b, right_b, left_b = call(
+    strip = (2, ncols // LANES - t, side, LANES)
+    side_b = (2, t, nrows - side, LANES)
+    part, gprobe, right_c, left_c, right_b, left_b, down_b, up_b = call(
         functools.partial(first_kernel, dims), dims, slots, scalars, (forward, backward, current),
-        (intensity, object_field, below_a, below_b, beside, corner),
-        [(2, total, nrows + side, LANES), current.shape, corners, corners,
-         edge_b, edge_b, edge_r, edge_r], [], "first_iteration")
+        (intensity, object_field), (below_a, below_b, beside, corner),
+        [big, current.shape, corners, corners, side_b, side_b, strip, strip], [],
+        28, "first_iteration")
 
     from_left_c = passed_along(right_c, "tile", 1)
     from_right_c = passed_along(left_c, "tile", -1)
@@ -393,40 +410,37 @@
     down_c, up_c = join(left_c, right_c, from_left_c, from_right_c)
     from_up_c = passed_along(down_c, "row", 1)
     from_down_c = passed_along(up_c, "row", -1)
-    mine, right_b, left_b, from_up_b, from_down_b, _ = lax.optimization_barrier(
-        (mine, right_b, left_b, from_up_b, from_down_b, down_c))
+    mine, from_up_b, from_down_b, _ = lax.optimization_barrier(
+        (mine, from_up_b, from_down_b, down_c))
+    given, right_b, left_b = lax.optimization_barrier((add_up(mine), right_b, left_b))
     from_left_b = passed_along(right_b, "tile", 1)
     from_right_b = passed_along(left_b, "tile", -1)
-    sum_one = hand_out(mine, current.shape)
-
-    edge = jnp.stack([
-        (lax.axis_index("row") == lax.axis_size("row") - 1).astype(jnp.int32),
-        (lax.axis_index("tile") == lax.axis_size("tile") - 1).astype(jnp.int32)])
+    sum_one = swap(given).reshape(current.shape)
+
     own, gprobe, right_c, right_ab, down_a, down_b = call(
         functools.partial(second_kernel, dims, probe_rate), dims, slots, scalars + (edge,),
-        (forward, backward, current, sum_one),
-        (intensity, part, from_left_c, from_right_c, from_up_c, from_down_c,
-         from_up_b, from_down_b, from_left_b, from_right_b),
+        (forward, backward, current, sum_one), (intensity, part),
+        (from_left_c, from_right_c, from_up_c, from_down_c,
+         from_left_b, from_right_b, from_up_b, from_down_b),
         [(2, ncols // LANES, nrows, LANES), current.shape, (2, t, side, LANES),
-         (2, t, nrows, LANES), (2, t, side, LANES), edge_b],
-        [current.shape, corners, corners, corners, corners, edge_b, edge_b, edge_r, edge_r],
-        "second_iteration")
+         (2, t, nrows, LANES), (2, t, side, LANES), strip],
+        [current.shape], 28, "second_iteration")
 
     from_left_c = passed_along(right_c, "tile", 1)
     above_b = passed_along(down_b, "row", 1)
     mine = swap(gprobe.reshape(devices, -1, LANES))
     down_a = down_a + from_left_c
     above_a = passed_along(down_a, "row", 1)
-    mine, right_ab, above_b, _ = lax.optimization_barrier((mine, right_ab, above_b, down_a))
+    mine, above_b, _ = lax.optimization_barrier((mine, above_b, down_a))
+    given, right_ab = lax.optimization_barrier((add_up(mine), right_ab))
     left_ab = passed_along(right_ab, "tile", 1)
-    sum_two = hand_out(mine, current.shape)
-    return pl.pallas_call(
-        functools.partial(last_kernel, dims, probe_rate),
-        out_shape=[jax.ShapeDtypeStruct(object_field.shape, F32),
-                   jax.ShapeDtypeStruct(probe.shape, F32)],
-        compiler_params=pltpu.CompilerParams(vmem_limit_bytes=48 * 1024 * 1024),
-        name="last_update",
-    )(own, left_ab, above_a, above_b, current, sum_one, sum_two)
+    sum_two = swap(given).reshape(current.shape)
+    object_out = simple(functools.partial(object_kernel, dims), object_field.shape, "last_object",
+                        16, (own, left_ab, above_a, above_b))
+    sum_two, _ = lax.optimization_barrier((sum_two, object_out))
+    probe_out = simple(functools.partial(probe_kernel, probe_rate), probe.shape, "last_probe",
+                       8, (current, sum_one, sum_two))
+    return (object_out, probe_out)
 
 
 def solution(mesh):

time: 214 us -> 221 us (1.033)
  blocking collectives: 19 us -> 0 us
  local copies, waits for them, and re-layouts: 16 us -> 26 us
  waiting for transfers between devices: 50.2 us -> 57.6 us
  starting transfers between devices: 82.6 us -> 86.8 us
  Pallas kernels: 42.1 us -> 45.3 us
    all_to_all x1 -> x0, blocking collectives: 19 us -> none  [swap(): return lax.all_to_all(shares, ('tile', 'row'), 0, 0, tiled=True)]
    unnamed x48 -> x54, local copies, waits for them, and re-layouts: 11.4 us -> 20.5 us
    all_to_all x3 -> x4, starting transfers between devices: 29.3 us -> 37 us  [swap(): return lax.all_to_all(shares, ('tile', 'row'), 0, 0, tiled=True)]
    ppermute x16, waiting for transfers between devices: 14 us -> 18.9 us  [passed_along(): lax.ppermute(value, axis, [(source, source + steps) for source in range(f...]
    ppermute x16, starting transfers between devices: 53.3 us -> 49.9 us  [passed_along(): lax.ppermute(value, axis, [(source, source + steps) for source in range(f...]
    all_to_all x3 -> x4, waiting for transfers between devices: 36.2 us -> 38.7 us  [swap(): return lax.all_to_all(shares, ('tile', 'row'), 0, 0, tiled=True)]
    pallas_call x3 -> x4, Pallas kernels: 7.45 us -> 9.26 us  [the longest x2 5.07 us: simple(): pl.pallas_call(kernel, out_shape=jax.ShapeDtypeStruct(shape, F32), in_spe...]
  transfers between devices with their start and end apart: 19 -> 20, of which waited for: 6 -> 8; matrix products, arithmetic and copies ran while one was open for 3% -> 4% of each run, Pallas kernels for 3% -> 4%
where the time goes in v3:
time: 221 us; the launch traced here: 219 us
  starting transfers between devices  86.8 us (39%)
  waiting for transfers between devices  57.6 us (26%)
  Pallas kernels  45.3 us (20%)
  local copies, waits for them, and re-layouts  26 us (12%)
  other arithmetic  2.27 us (1%)
    ppermute x16, starting transfers between devices, passed_along(): lax.ppermute(value, axis, [(source, source + steps) for source in range(f...  49.9 us
    all_to_all x4, waiting for transfers between devices, swap(): return lax.all_to_all(shares, ('tile', 'row'), 0, 0, tiled=True)  38.7 us
    all_to_all x4, starting transfers between devices, swap(): return lax.all_to_all(shares, ('tile', 'row'), 0, 0, tiled=True)  37 us
    pallas_call x2, Pallas kernels, call(): pl.pallas_call(kernel, out_shape=[jax.ShapeDtypeStruct(shape, F32) for sh...  33.4 us
    unnamed x54, local copies, waits for them, and re-layouts  20.5 us
    ppermute x16, waiting for transfers between devices, passed_along(): lax.ppermute(value, axis, [(source, source + steps) for source in range(f...  18.9 us
    pallas_call x2, Pallas kernels, simple(): pl.pallas_call(kernel, out_shape=jax.ShapeDtypeStruct(shape, F32), in_spe...  5.07 us
  transfers between devices with their start and end apart: 20, of which 8 were waited for; matrix products, arithmetic and copies ran while one was open for 4% of the time, Pallas kernels for 4%

profile of v3, /device:TPU:1, one launch (start us, length us, event | category | flops | bytes accessed | tf_op | source)
XLA Modules:
  0.0 219.0 jit_solution(11475799453533097458)
XLA Ops:
  0.7 1.2 slice.9
  1.9 1.3 collective-permute-start
  3.2 2.3 %slice.11 = f32[2,512,256]{2,1,0:T(8,128)} slice(f32[2,512,512]{2,1,0:T(8,128)} %field.1), slice={[0:2], [0:512], [0:256]} | slice | bytes 2097152 | tf_op jit(solution)/shard_map/slice | solution.py:385
  5.5 3.5 %collective-permute-start.2 = (f32[2,512,256]{2,1,0:T(8,128)}, f32[2,512,256]{2,1,0:T(8,128)}, u32[]{:S(2)}, u32[]{:S(2)}) collective-permute-start(f32[2,512,256]{2,1,0:T(8,128)} %slice.11), channel_id=1, source_target_pairs={{4,0},{8,4},{12,8},{16,12},{20,16},{24,20},{28,24},{32,28},{36,32}... | collective-permute-start | bytes 3145736 | tf_op jit(solution)/shard_map/ppermute | solution.py:22
  9.8 1.3 collective-permute-start.1
  11.1 6.2 %collective-permute-done.below_a = f32[2,256,256]{2,1,0:T(8,128)} collective-permute-done((f32[2,256,256]{2,1,0:T(8,128)S(1)}, f32[2,256,256]{2,1,0:T(8,128)}, u32[]{:S(2)}, u32[]{:S(2)}) %collective-permute-start) | collective-permute-done | bytes 524320 | tf_op jit(solution)/shard_map/ppermute | solution.py:22
  17.3 4.8 %collective-permute-start.3 = (f32[2,256,256]{2,1,0:T(8,128)}, f32[2,256,256]{2,1,0:T(8,128)}, u32[]{:S(2)}, u32[]{:S(2)}) collective-permute-start(f32[2,256,256]{2,1,0:T(8,128)} %collective-permute-done.below_a), channel_id=1, source_target_pairs={{4,0},{8,4},{12,8},{16,12},{20,16},{24,20},{28,24},{32,28},{36,32}... | collective-permute-start | bytes 1572872 | tf_op jit(solution)/shard_map/ppermute | solution.py:22
  23.2 1.2 copy.14
  24.4 4.1 %collective-permute-done.1.below_b = f32[2,256,256]{2,1,0:T(8,128)} collective-permute-done((f32[2,256,256]{2,1,0:T(8,128)}, f32[2,256,256]{2,1,0:T(8,128)}, u32[]{:S(2)}, u32[]{:S(2)}) %collective-permute-start.1) | collective-permute-done | bytes 524320 | tf_op jit(solution)/shard_map/ppermute | solution.py:22
  28.5 1.9 collective-permute-done.3.corner
  30.4 2.2 copy-done
  32.6 1.0 copy-done.9
  33.7 11.9 %first_iteration.1 = (f32[2,6,768,128]{3,2,1,0:T(8,128)S(1)}, f32[2,2,256,128]{3,2,1,0:T(8,128)S(1)}, f32[2,2,2,256,128]{4,3,2,1,0:T(8,128)}, f32[2,2,2,256,128]...) custom-call(s32[2,12]{1,0:T(2,128)S(1)} %copy-done.16, ...), custom_call_target="tpu_custom_call" | custom-call | tf_op jit(solution)/shard_map/first_iteration/pallas_call | solution.py:313
  45.5 2.2 copy-done.3
  50.9 7.2 %collective-permute-start.4 = (f32[2,2,2,256,128]{4,3,2,1,0:T(8,128)}, f32[2,2,2,256,128]{4,3,2,1,0:T(8,128)S(1)}, u32[]{:S(2)}, u32[]{:S(2)}) collective-permute-start(f32[2,2,2,256,128]{4,3,2,1,0:T(8,128)} %get-tuple-element.37.right_c), channel_id=1, source_target_pairs={{0,4},{4,8},{8,12},{12,16},{16,20},{20,24},{24,28},{28,32},{32,36}... | collective-permute-start | bytes 3145736 | tf_op jit(solution)/shard_map/ppermute | solution.py:22
  58.1 2.3 %collective-permute-start.5 = (f32[2,2,2,256,128]{4,3,2,1,0:T(8,128)}, f32[2,2,2,256,128]{4,3,2,1,0:T(8,128)S(1)}, u32[]{:S(2)}, u32[]{:S(2)}) collective-permute-start(f32[2,2,2,256,128]{4,3,2,1,0:T(8,128)} %get-tuple-element.38.left_c), channel_id=1, source_target_pairs={{4,0},{8,4},{12,8},{16,12},{20,16},{24,20},{28,24},{32,28},{36,32}... | collective-permute-start | bytes 3145736 | tf_op jit(solution)/shard_map/ppermute | solution.py:22
  60.5 15.1 %all-to-all-start = ((f32[128,8,128]{2,1,0:T(8,128)}), f32[128,8,128]{2,1,0:T(8,128)}, u32[]{:S(2)}, u32[]{:S(2)}) async-start(f32[128,8,128]{2,1,0:T(8,128)} %bitcast.14), calls=%async_computation | async-start | bytes 1048576 | tf_op jit(solution)/shard_map/all_to_all | solution.py:335
  75.6 3.3 %collective-permute-start.6 = (f32[2,2,256,128]{3,2,1,0:T(8,128)}, f32[2,2,256,128]{3,2,1,0:T(8,128)S(1)}, u32[]{:S(2)}, u32[]{:S(2)}) collective-permute-start(f32[2,2,256,128]{3,2,1,0:T(8,128)} %copy-done.23), channel_id=1, source_target_pairs={{0,1},{1,2},{2,3},{4,5},{5,6},{6,7},{8,9},{9,10},{10,11},{12,13},{... | collective-permute-start | bytes 1572872 | tf_op jit(solution)/shard_map/ppermute | solution.py:22
  78.9 1.3 collective-permute-start.7
  80.2 8.9 %all-to-all-done.received = f32[128,8,128]{2,1,0:T(8,128)} async-done(((f32[128,8,128]{2,1,0:T(8,128)}), f32[128,8,128]{2,1,0:T(8,128)}, u32[]{:S(2)}, u32[]{:S(2)}) %all-to-all-start) | async-done | bytes 524320 | tf_op jit(solution)/shard_map/all_to_all | solution.py:335
  89.1 2.6 %join_corners.1 = (f32[2,2,2,256,128]{4,3,2,1,0:T(8,128)}, f32[2,2,2,256,128]{4,3,2,1,0:T(8,128)}) custom-call(f32[2,2,2,256,128]{4,3,2,1,0:T(8,128)} %get-tuple-element.38.left_c, f32[2,2,2,256,128]{4,3,2,1,0:T(8,128)} %get-tuple-element.37.right_c, f32[2,2,2,256,128]{4,3,2,1,0:T(8,128)S(1)} %collective-permute-done.4.from_left.from_left_c, ...), custom_call_target="tpu_custom_call" | custom-call | tf_op jit(solution)/shard_map/join_corners/pallas_call | solution.py:347
  91.7 1.3 collective-permute-start.9
  93.0 5.0 %collective-permute-start.8 = (f32[2,2,2,256,128]{4,3,2,1,0:T(8,128)}, f32[2,2,2,256,128]{4,3,2,1,0:T(8,128)}, u32[]{:S(2)}, u32[]{:S(2)}) collective-permute-start(f32[2,2,2,256,128]{4,3,2,1,0:T(8,128)} %get-tuple-element.44), channel_id=1, source_target_pairs={{0,1},{1,2},{2,3},{4,5},{5,6},{6,7},{8,9},{9,10},{10,11},{12,13},{... | collective-permute-start | bytes 3145736 | tf_op jit(solution)/shard_map/ppermute | solution.py:22
  98.0 2.2 %sum_shares.2 = f32[128,8,128]{2,1,0:T(8,128)} custom-call(f32[128,8,128]{2,1,0:T(8,128)} %all-to-all-done.received), custom_call_target="tpu_custom_call" | custom-call | tf_op jit(solution)/shard_map/sum_shares/pallas_call | solution.py:339
  100.2 5.2 %collective-permute-start.10 = (f32[2,2,256,128]{3,2,1,0:T(8,128)}, f32[2,2,256,128]{3,2,1,0:T(8,128)}, u32[]{:S(2)}, u32[]{:S(2)}) collective-permute-start(f32[2,2,256,128]{3,2,1,0:T(8,128)} %copy-done.21), channel_id=1, source_target_pairs={{0,4},{4,8},{8,12},{12,16},{16,20},{20,24},{24,28},{28,32},{32,36}... | collective-permute-start | bytes 1572872 | tf_op jit(solution)/shard_map/ppermute | solution.py:22
  105.4 1.9 collective-permute-start.11
  107.4 7.4 %all-to-all-start.1 = ((f32[128,8,128]{2,1,0:T(8,128)}), f32[128,8,128]{2,1,0:T(8,128)S(1)}, u32[]{:S(2)}, u32[]{:S(2)}) async-start(f32[128,8,128]{2,1,0:T(8,128)} %sum_shares.2), calls=%async_computation.1 | async-start | bytes 1048576 | tf_op jit(solution)/shard_map/all_to_all | solution.py:335
  114.9 14.7 %all-to-all-done.1 = f32[128,8,128]{2,1,0:T(8,128)S(1)} async-done(((f32[128,8,128]{2,1,0:T(8,128)}), f32[128,8,128]{2,1,0:T(8,128)S(1)}, u32[]{:S(2)}, u32[]{:S(2)}) %all-to-all-start.1) | async-done | bytes 524320 | tf_op jit(solution)/shard_map/all_to_all | solution.py:335
  129.6 2.2 copy-done.1
  131.8 2.3 %copy-done.4 = f32[2,6,768,128]{3,2,1,0:T(8,128)S(1)} copy-done((f32[2,6,768,128]{3,2,1,0:T(8,128)S(1)}, f32[2,6,768,128]{3,2,1,0:T(8,128)}, u32[]{:S(2)}) %copy-start.4) | copy-done | bytes 4718616
  134.1 1.0 copy-done.8
  135.2 1.0 copy-done.10
  136.2 1.0 copy-done.12
  137.2 21.5 %second_iteration.1 = (f32[2,4,512,128]{3,2,1,0:T(8,128)S(1)}, f32[2,2,256,128]{3,2,1,0:T(8,128)S(1)}, f32[2,2,256,128]{3,2,1,0:T(8,128)}, f32[2,2,512,128]{3,2,...) custom-call(s32[2,12]{1,0:T(2,128)S(1)} %copy-done.16, s32[2,1]{1,0:T(2,128)S(1)} %copy.16.live, ...), custom_call_target="tpu_custom_call" | custom-call | tf_op jit(solution)/shard_map/second_iteration/pallas_call | solution.py:313
  158.8 1.3 copy-done.5
  161.9 1.9 collective-permute-start.13
  163.8 3.8 %collective-permute-start.12 = (f32[2,2,256,128]{3,2,1,0:T(8,128)}, f32[2,2,256,128]{3,2,1,0:T(8,128)}, u32[]{:S(2)}, u32[]{:S(2)}) collective-permute-start(f32[2,2,256,128]{3,2,1,0:T(8,128)} %get-tuple-element.57), channel_id=1, source_target_pairs={{0,1},{1,2},{2,3},{4,5},{5,6},{6,7},{8,9},{9,10},{10,11},{12,13},{... | collective-permute-start | bytes 1572872 | tf_op jit(solution)/shard_map/ppermute | solution.py:22
  167.6 8.7 %all-to-all-start.2 = ((f32[128,8,128]{2,1,0:T(8,128)}), f32[128,8,128]{2,1,0:T(8,128)}, u32[]{:S(2)}, u32[]{:S(2)}) async-start(f32[128,8,128]{2,1,0:T(8,128)} %bitcast.13), calls=%async_computation.2 | async-start | bytes 1048576 | tf_op jit(solution)/shard_map/all_to_all | solution.py:335
  176.4 2.2 %add.3 = f32[2,2,256,128]{3,2,1,0:T(8,128)} add(f32[2,2,256,128]{3,2,1,0:T(8,128)} %copy-done.13, f32[2,2,256,128]{3,2,1,0:T(8,128)} %collective-permute-done.13) | non-fusion elementwise | flops 131072 | bytes 1572864 | tf_op jit(solution)/shard_map/add | solution.py:432
  178.6 11.2 %all-to-all-done.2.received = f32[128,8,128]{2,1,0:T(8,128)} async-done(((f32[128,8,128]{2,1,0:T(8,128)}), f32[128,8,128]{2,1,0:T(8,128)}, u32[]{:S(2)}, u32[]{:S(2)}) %all-to-all-start.2) | async-done | bytes 524320 | tf_op jit(solution)/shard_map/all_to_all | solution.py:335
  189.8 2.0 sum_shares.3
  191.8 2.7 %collective-permute-start.14 = (f32[2,2,512,128]{3,2,1,0:T(8,128)}, f32[2,2,512,128]{3,2,1,0:T(8,128)}, u32[]{:S(2)}, u32[]{:S(2)}) collective-permute-start(f32[2,2,512,128]{3,2,1,0:T(8,128)} %copy-done.19), channel_id=1, source_target_pairs={{0,4},{4,8},{8,12},{12,16},{16,20},{20,24},{24,28},{28,32},{32,36}... | collective-permute-start | bytes 3145736 | tf_op jit(solution)/shard_map/ppermute | solution.py:22
  194.5 3.1 %collective-permute-start.15 = (f32[2,2,256,128]{3,2,1,0:T(8,128)}, f32[2,2,256,128]{3,2,1,0:T(8,128)}, u32[]{:S(2)}, u32[]{:S(2)}) collective-permute-start(f32[2,2,256,128]{3,2,1,0:T(8,128)} %add.3), channel_id=1, source_target_pairs={{0,1},{1,2},{2,3},{4,5},{5,6},{6,7},{8,9},{9,10},{10,11},{12,13},{... | collective-permute-start | bytes 1572872 | tf_op jit(solution)/shard_map/ppermute | solution.py:22
  197.5 5.8 %all-to-all-start.3 = ((f32[128,8,128]{2,1,0:T(8,128)}), f32[128,8,128]{2,1,0:T(8,128)}, u32[]{:S(2)}, u32[]{:S(2)}) async-start(f32[128,8,128]{2,1,0:T(8,128)} %sum_shares.3), calls=%async_computation.3 | async-start | bytes 1048576 | tf_op jit(solution)/shard_map/all_to_all | solution.py:335
  203.3 6.7 %collective-permute-done.15.above_a = f32[2,2,256,128]{3,2,1,0:T(8,128)} collective-permute-done((f32[2,2,256,128]{3,2,1,0:T(8,128)}, f32[2,2,256,128]{3,2,1,0:T(8,128)}, u32[]{:S(2)}, u32[]{:S(2)}) %collective-permute-start.15) | collective-permute-done | bytes 524320 | tf_op jit(solution)/shard_map/ppermute | solution.py:22
  210.0 3.2 %last_object.1 = f32[2,512,512]{2,1,0:T(8,128)} custom-call(f32[2,4,512,128]{3,2,1,0:T(8,128)S(1)} %copy-done.6, f32[2,2,512,128]{3,2,1,0:T(8,128)} %collective-permute-done.14.left_ab, f32[2,2,256,128]{3,2,1,0:T(8,128)} %collective-permute-done.15.above_a, f32[2,2,256,128]{3,2,1,0:T(8,128)} %collective-permute-done.12.above_b), custom_call_target="tpu_custom_call" | custom-call | tf_op jit(solution)/shard_map/last_object/pallas_call | solution.py:361
  213.1 4.0 %all-to-all-done.3 = f32[128,8,128]{2,1,0:T(8,128)} async-done(((f32[128,8,128]{2,1,0:T(8,128)}), f32[128,8,128]{2,1,0:T(8,128)}, u32[]{:S(2)}, u32[]{:S(2)}) %all-to-all-start.3) | async-done | bytes 524320 | tf_op jit(solution)/shard_map/all_to_all | solution.py:335
  217.1 1.9 last_probe.1
  (59 shorter events, 7.1 us)
Async XLA Ops:
  0.6 8.3 %copy-start.2 = (f32[2,512,512]{2,1,0:T(8,128)S(1)}, f32[2,512,512]{2,1,0:T(8,128)}, u32[]{:S(2)}) copy-start(f32[2,512,512]{2,1,0:T(8,128)} %field.1) | copy-start | bytes 6291460
  0.6 21.4 %copy-start.25 = (s32[2,1]{0,1:T(1,128)S(1)}, s32[2,1]{0,1:T(1,128)}, u32[]{:S(2)}) copy-start(s32[2,1]{0,1:T(1,128)} %param.15) | copy-start | bytes 28
  0.7 21.5 %copy-start.24 = (f32[2,256,256]{2,1,0:T(8,128)S(1)}, f32[2,256,256]{2,1,0:T(8,128)}, u32[]{:S(2)}) copy-start(f32[2,256,256]{2,1,0:T(8,128)} %param.10) | copy-start | bytes 1572868
  1.9 15.4 %collective-permute-start = (f32[2,256,256]{2,1,0:T(8,128)S(1)}, f32[2,256,256]{2,1,0:T(8,128)}, u32[]{:S(2)}, u32[]{:S(2)}) collective-permute-start(f32[2,256,256]{2,1,0:T(8,128)S(1)} %slice.9), channel_id=1, source_target_pairs={{1,0},{2,1},{3,2},{5,4},{6,5},{7,6},{9,8},{10,9},{11,10},{13,12},{... | collective-permute-start | bytes 1572872 | tf_op jit(solution)/shard_map/ppermute | solution.py:22
  5.5 24.9 %copy-start.7 = (bf16[512,512]{1,0:T(8,128)(2,1)S(1)}, bf16[512,512]{1,0:T(8,128)(2,1)}, u32[]{:S(2)}) copy-start(bf16[512,512]{1,0:T(8,128)(2,1)} %constant.18.clone.backward) | copy-start | bytes 1572868
  5.5 24.9 %copy-start.16 = (s32[2,12]{1,0:T(2,128)S(1)}, s32[2,12]{1,0:T(2,128)}, u32[]{:S(2)}) copy-start(s32[2,12]{1,0:T(2,128)} %batch.3) | copy-start | bytes 292
  5.5 24.9 %copy-start.17 = (s32[32]{0:T(128)S(1)}, s32[32]{0:T(128)}, u32[]{:S(2)}) copy-start(s32[32]{0:T(128)} %rows.3) | copy-start | bytes 388
  5.5 24.9 %copy-start.18 = (s32[32]{0:T(128)S(1)}, s32[32]{0:T(128)}, u32[]{:S(2)}) copy-start(s32[32]{0:T(128)} %cols.3) | copy-start | bytes 388
  5.5 24.9 %collective-permute-start.2 = (f32[2,512,256]{2,1,0:T(8,128)}, f32[2,512,256]{2,1,0:T(8,128)}, u32[]{:S(2)}, u32[]{:S(2)}) collective-permute-start(f32[2,512,256]{2,1,0:T(8,128)} %slice.11), channel_id=1, source_target_pairs={{4,0},{8,4},{12,8},{16,12},{20,16},{24,20},{28,24},{32,28},{36,32}... | collective-permute-start | bytes 3145736 | tf_op jit(solution)/shard_map/ppermute | solution.py:22
  9.8 18.7 %collective-permute-start.1 = (f32[2,256,256]{2,1,0:T(8,128)}, f32[2,256,256]{2,1,0:T(8,128)}, u32[]{:S(2)}, u32[]{:S(2)}) collective-permute-start(f32[2,256,256]{2,1,0:T(8,128)} %slice.10), channel_id=1, source_target_pairs={{1,0},{2,1},{3,2},{5,4},{6,5},{7,6},{9,8},{10,9},{11,10},{13,12},{... | collective-permute-start | bytes 1572872 | tf_op jit(solution)/shard_map/ppermute | solution.py:22
  17.3 13.1 %collective-permute-start.3 = (f32[2,256,256]{2,1,0:T(8,128)}, f32[2,256,256]{2,1,0:T(8,128)}, u32[]{:S(2)}, u32[]{:S(2)}) collective-permute-start(f32[2,256,256]{2,1,0:T(8,128)} %collective-permute-done.below_a), channel_id=1, source_target_pairs={{4,0},{8,4},{12,8},{16,12},{20,16},{24,20},{28,24},{32,28},{36,32}... | collective-permute-start | bytes 1572872 | tf_op jit(solution)/shard_map/ppermute | solution.py:22
  30.4 2.2 %copy-start = (bf16[32,256,256]{2,1,0:T(8,128)(2,1)S(1)}, bf16[32,256,256]{2,1,0:T(8,128)(2,1)}, u32[]{:S(2)}) copy-start(bf16[32,256,256]{2,1,0:T(8,128)(2,1)} %intensity.3) | copy-start | bytes 12582916
  32.6 1.0 copy-start.9
  45.5 2.2 copy-start.3
  47.7 0.8 copy-start.20
  48.5 0.8 copy-start.21
  49.3 0.8 copy-start.22
  50.1 0.8 copy-start.23
  50.9 9.6 %copy-start.15 = (f32[2,2,256,128]{3,2,1,0:T(8,128)}, f32[2,2,256,128]{3,2,1,0:T(8,128)S(1)}, u32[]{:S(2)}) copy-start(f32[2,2,256,128]{3,2,1,0:T(8,128)S(1)} %get-tuple-element.36) | copy-start | bytes 1572868
  50.9 38.2 %collective-permute-start.4 = (f32[2,2,2,256,128]{4,3,2,1,0:T(8,128)}, f32[2,2,2,256,128]{4,3,2,1,0:T(8,128)S(1)}, u32[]{:S(2)}, u32[]{:S(2)}) collective-permute-start(f32[2,2,2,256,128]{4,3,2,1,0:T(8,128)} %get-tuple-element.37.right_c), channel_id=1, source_target_pairs={{0,4},{4,8},{8,12},{12,16},{16,20},{20,24},{24,28},{28,32},{32,36}... | collective-permute-start | bytes 3145736 | tf_op jit(solution)/shard_map/ppermute | solution.py:22
  58.1 31.0 %collective-permute-start.5 = (f32[2,2,2,256,128]{4,3,2,1,0:T(8,128)}, f32[2,2,2,256,128]{4,3,2,1,0:T(8,128)S(1)}, u32[]{:S(2)}, u32[]{:S(2)}) collective-permute-start(f32[2,2,2,256,128]{4,3,2,1,0:T(8,128)} %get-tuple-element.38.left_c), channel_id=1, source_target_pairs={{4,0},{8,4},{12,8},{16,12},{20,16},{24,20},{28,24},{32,28},{36,32}... | collective-permute-start | bytes 3145736 | tf_op jit(solution)/shard_map/ppermute | solution.py:22
  60.5 28.6 %all-to-all-start = ((f32[128,8,128]{2,1,0:T(8,128)}), f32[128,8,128]{2,1,0:T(8,128)}, u32[]{:S(2)}, u32[]{:S(2)}) async-start(f32[128,8,128]{2,1,0:T(8,128)} %bitcast.14), calls=%async_computation | async-start | bytes 1048576 | tf_op jit(solution)/shard_map/all_to_all | solution.py:335
  75.6 22.4 %collective-permute-start.6 = (f32[2,2,256,128]{3,2,1,0:T(8,128)}, f32[2,2,256,128]{3,2,1,0:T(8,128)S(1)}, u32[]{:S(2)}, u32[]{:S(2)}) collective-permute-start(f32[2,2,256,128]{3,2,1,0:T(8,128)} %copy-done.23), channel_id=1, source_target_pairs={{0,1},{1,2},{2,3},{4,5},{5,6},{6,7},{8,9},{9,10},{10,11},{12,13},{... | collective-permute-start | bytes 1572872 | tf_op jit(solution)/shard_map/ppermute | solution.py:22
  78.9 19.1 %collective-permute-start.7 = (f32[2,2,256,128]{3,2,1,0:T(8,128)}, f32[2,2,256,128]{3,2,1,0:T(8,128)}, u32[]{:S(2)}, u32[]{:S(2)}) collective-permute-start(f32[2,2,256,128]{3,2,1,0:T(8,128)} %copy-done.22), channel_id=1, source_target_pairs={{1,0},{2,1},{3,2},{5,4},{6,5},{7,6},{9,8},{10,9},{11,10},{13,12},{... | collective-permute-start | bytes 1572872 | tf_op jit(solution)/shard_map/ppermute | solution.py:22
  91.7 37.9 %collective-permute-start.9 = (f32[2,2,2,256,128]{4,3,2,1,0:T(8,128)}, f32[2,2,2,256,128]{4,3,2,1,0:T(8,128)}, u32[]{:S(2)}, u32[]{:S(2)}) collective-permute-start(f32[2,2,2,256,128]{4,3,2,1,0:T(8,128)} %get-tuple-element.50), channel_id=1, source_target_pairs={{1,0},{2,1},{3,2},{5,4},{6,5},{7,6},{9,8},{10,9},{11,10},{13,12},{... | collective-permute-start | bytes 3145736 | tf_op jit(solution)/shard_map/ppermute | solution.py:22
  93.0 36.6 %collective-permute-start.8 = (f32[2,2,2,256,128]{4,3,2,1,0:T(8,128)}, f32[2,2,2,256,128]{4,3,2,1,0:T(8,128)}, u32[]{:S(2)}, u32[]{:S(2)}) collective-permute-start(f32[2,2,2,256,128]{4,3,2,1,0:T(8,128)} %get-tuple-element.44), channel_id=1, source_target_pairs={{0,1},{1,2},{2,3},{4,5},{5,6},{6,7},{8,9},{9,10},{10,11},{12,13},{... | collective-permute-start | bytes 3145736 | tf_op jit(solution)/shard_map/ppermute | solution.py:22
  98.0 9.4 %copy-start.11 = (f32[2,2,256,128]{3,2,1,0:T(8,128)}, f32[2,2,256,128]{3,2,1,0:T(8,128)S(1)}, u32[]{:S(2)}) copy-start(f32[2,2,256,128]{3,2,1,0:T(8,128)S(1)} %collective-permute-done.6.from_up) | copy-start | bytes 1572868
  100.2 29.4 %collective-permute-start.10 = (f32[2,2,256,128]{3,2,1,0:T(8,128)}, f32[2,2,256,128]{3,2,1,0:T(8,128)}, u32[]{:S(2)}, u32[]{:S(2)}) collective-permute-start(f32[2,2,256,128]{3,2,1,0:T(8,128)} %copy-done.21), channel_id=1, source_target_pairs={{0,4},{4,8},{8,12},{12,16},{16,20},{20,24},{24,28},{28,32},{32,36}... | collective-permute-start | bytes 1572872 | tf_op jit(solution)/shard_map/ppermute | solution.py:22
  105.4 24.1 %collective-permute-start.11 = (f32[2,2,256,128]{3,2,1,0:T(8,128)}, f32[2,2,256,128]{3,2,1,0:T(8,128)}, u32[]{:S(2)}, u32[]{:S(2)}) collective-permute-start(f32[2,2,256,128]{3,2,1,0:T(8,128)} %copy-done.20), channel_id=1, source_target_pairs={{4,0},{8,4},{12,8},{16,12},{20,16},{24,20},{28,24},{32,28},{36,32}... | collective-permute-start | bytes 1572872 | tf_op jit(solution)/shard_map/ppermute | solution.py:22
  107.4 22.2 %all-to-all-start.1 = ((f32[128,8,128]{2,1,0:T(8,128)}), f32[128,8,128]{2,1,0:T(8,128)S(1)}, u32[]{:S(2)}, u32[]{:S(2)}) async-start(f32[128,8,128]{2,1,0:T(8,128)} %sum_shares.2), calls=%async_computation.1 | async-start | bytes 1048576 | tf_op jit(solution)/shard_map/all_to_all | solution.py:335
  129.6 2.2 %copy-start.1 = (bf16[32,256,256]{2,1,0:T(8,128)(2,1)S(1)}, bf16[32,256,256]{2,1,0:T(8,128)(2,1)}, u32[]{:S(2)}) copy-start(bf16[32,256,256]{2,1,0:T(8,128)(2,1)} %intensity.3) | copy-start | bytes 12582916
  131.8 2.3 %copy-start.4 = (f32[2,6,768,128]{3,2,1,0:T(8,128)S(1)}, f32[2,6,768,128]{3,2,1,0:T(8,128)}, u32[]{:S(2)}) copy-start(f32[2,6,768,128]{3,2,1,0:T(8,128)} %copy-done.3) | copy-start | bytes 14155780
  134.1 1.0 copy-start.8
  135.2 1.0 copy-start.10
  136.2 1.0 copy-start.12
  158.8 1.3 copy-start.5
  160.1 0.8 copy-start.13
  160.9 1.0 copy-start.19
  160.9 6.7 %copy-start.14 = (f32[2,2,256,128]{3,2,1,0:T(8,128)}, f32[2,2,256,128]{3,2,1,0:T(8,128)S(1)}, u32[]{:S(2)}) copy-start(f32[2,2,256,128]{3,2,1,0:T(8,128)S(1)} %get-tuple-element.56) | copy-start | bytes 1572868
  161.9 14.4 %collective-permute-start.13 = (f32[2,2,256,128]{3,2,1,0:T(8,128)}, f32[2,2,256,128]{3,2,1,0:T(8,128)}, u32[]{:S(2)}, u32[]{:S(2)}) collective-permute-start(f32[2,2,256,128]{3,2,1,0:T(8,128)} %get-tuple-element.59), channel_id=1, source_target_pairs={{0,4},{4,8},{8,12},{12,16},{16,20},{20,24},{24,28},{28,32},{32,36}... | collective-permute-start | bytes 1572872 | tf_op jit(solution)/shard_map/ppermute | solution.py:22
  163.8 25.9 %collective-permute-start.12 = (f32[2,2,256,128]{3,2,1,0:T(8,128)}, f32[2,2,256,128]{3,2,1,0:T(8,128)}, u32[]{:S(2)}, u32[]{:S(2)}) collective-permute-start(f32[2,2,256,128]{3,2,1,0:T(8,128)} %get-tuple-element.57), channel_id=1, source_target_pairs={{0,1},{1,2},{2,3},{4,5},{5,6},{6,7},{8,9},{9,10},{10,11},{12,13},{... | collective-permute-start | bytes 1572872 | tf_op jit(solution)/shard_map/ppermute | solution.py:22
  167.6 22.1 %all-to-all-start.2 = ((f32[128,8,128]{2,1,0:T(8,128)}), f32[128,8,128]{2,1,0:T(8,128)}, u32[]{:S(2)}, u32[]{:S(2)}) async-start(f32[128,8,128]{2,1,0:T(8,128)} %bitcast.13), calls=%async_computation.2 | async-start | bytes 1048576 | tf_op jit(solution)/shard_map/all_to_all | solution.py:335
  176.3 33.6 %copy-start.6 = (f32[2,4,512,128]{3,2,1,0:T(8,128)S(1)}, f32[2,4,512,128]{3,2,1,0:T(8,128)}, u32[]{:S(2)}) copy-start(f32[2,4,512,128]{3,2,1,0:T(8,128)} %copy-done.5) | copy-start | bytes 6291460
  191.8 18.2 %collective-permute-start.14 = (f32[2,2,512,128]{3,2,1,0:T(8,128)}, f32[2,2,512,128]{3,2,1,0:T(8,128)}, u32[]{:S(2)}, u32[]{:S(2)}) collective-permute-start(f32[2,2,512,128]{3,2,1,0:T(8,128)} %copy-done.19), channel_id=1, source_target_pairs={{0,4},{4,8},{8,12},{12,16},{16,20},{20,24},{24,28},{28,32},{32,36}... | collective-permute-start | bytes 3145736 | tf_op jit(solution)/shard_map/ppermute | solution.py:22
  194.5 15.5 %collective-permute-start.15 = (f32[2,2,256,128]{3,2,1,0:T(8,128)}, f32[2,2,256,128]{3,2,1,0:T(8,128)}, u32[]{:S(2)}, u32[]{:S(2)}) collective-permute-start(f32[2,2,256,128]{3,2,1,0:T(8,128)} %add.3), channel_id=1, source_target_pairs={{0,1},{1,2},{2,3},{4,5},{5,6},{6,7},{8,9},{9,10},{10,11},{12,13},{... | collective-permute-start | bytes 1572872 | tf_op jit(solution)/shard_map/ppermute | solution.py:22
  197.5 19.5 %all-to-all-start.3 = ((f32[128,8,128]{2,1,0:T(8,128)}), f32[128,8,128]{2,1,0:T(8,128)}, u32[]{:S(2)}, u32[]{:S(2)}) async-start(f32[128,8,128]{2,1,0:T(8,128)} %sum_shares.3), calls=%async_computation.3 | async-start | bytes 1048576 | tf_op jit(solution)/shard_map/all_to_all | solution.py:335

commit v4 on v3

--- a/solution.py
+++ b/solution.py
@@ -57,7 +57,7 @@
 
 def slot_loop(step, side, batch, live, rows, cols, mats, probe, ext, grad, gprobe,
               measured, exits, waves, patches):
-    forward, backward = mats
+    forward, backward = mats.at[0], mats.at[1]
     lane = lax.broadcasted_iota(jnp.int32, (side, LANES), 1)
     halves = side // LANES
     count = live[step, 0]
@@ -157,10 +157,21 @@
     return copies
 
 
-def first_kernel(dims, batch, live, rows, cols, forward, backward, probe, intensity,
+def update_out(ext, grad, target, sems, base):
+    parts, tiles, rows = target.shape[:3]
+    copies = []
+    for part in range(parts):
+        for j in range(tiles):
+            ext[part, j, 0:rows, :] -= 0.25 * grad[part, j, 0:rows, :]
+            copies += run_copies([(ext.at[part, j, pl.ds(0, rows), :], target.at[part, j])],
+                                 sems, base + len(copies))
+    return copies
+
+
+def first_kernel(dims, batch, live, rows, cols, probe, intensity, tables_in,
                  field, below_a, below_b, beside, corner,
                  part_out, gprobe_out, right_c, left_c, right_b, left_b, down_b, up_b,
-                 ext, grad, measured, exit_0, exit_1, wave_0, wave_1, patch_0, patch_1,
+                 ext, grad, mats, measured, exit_0, exit_1, wave_0, wave_1, patch_0, patch_1,
                  gprobe, sems, moves):
     side, nrows, ncols = dims
     pairs = tiled_copies(field, nrows, ncols, ext, 0, 0)
@@ -168,13 +179,13 @@
     pairs += tiled_copies(below_b, side, ncols - side, ext, nrows, side)
     pairs += tiled_copies(beside, nrows, side, ext, 0, ncols)
     pairs += tiled_copies(corner, side, side, ext, nrows, ncols)
-    copies = run_copies(pairs, moves)
+    copies = run_copies(pairs + [(tables_in, mats)], moves)
     copies += start_slots(0, batch, intensity, measured, sems)
     waves, patches = (wave_0, wave_1), (patch_0, patch_1)
     clear(grad, gprobe, waves, patches)
     for copy in copies:
         copy.wait()
-    slot_loop(0, side, batch, live, rows, cols, (forward, backward), probe, ext, grad, gprobe,
+    slot_loop(0, side, batch, live, rows, cols, mats, probe, ext, grad, gprobe,
               measured, (exit_0, exit_1), waves, patches)
     t = side // LANES
     last = ncols // LANES
@@ -193,27 +204,7 @@
         (grad.at[:, mid, a_rows, :], up_b),
     ]
     copies = run_copies(pairs, moves)
-    ext[...] = ext[...] - 0.25 * grad[...]
-    copies += run_copies([(ext, part_out)], moves, len(pairs))
-    for copy in copies:
-        copy.wait()
-
-
-def join_kernel(left_c, right_c, from_left, from_right, down, up, own, moves, stores):
-    places = []
-    for band, target in ((1, down), (0, up)):
-        for which, (mine, received) in enumerate(((left_c, from_left), (right_c, from_right))):
-            places.append((mine.at[band], received, band, target.at[which]))
-    loads = [pltpu.make_async_copy(place[0], own.at[i], moves.at[i])
-             for i, place in enumerate(places)]
-    for copy in loads:
-        copy.start()
-    copies = []
-    for i, (mine, received, band, target) in enumerate(places):
-        loads[i].wait()
-        own[i] = own[i] + received[band]
-        copies.append(pltpu.make_async_copy(own.at[i], target, stores.at[i]))
-        copies[-1].start()
+    copies += update_out(ext, grad, part_out, moves, len(pairs))
     for copy in copies:
         copy.wait()
 
@@ -226,16 +217,16 @@
         given[i] = summed
 
 
-def second_kernel(dims, rate, batch, live, rows, cols, edge, forward, backward, probe,
-                  summed, intensity, part_in, from_left_c, from_right_c, from_up_c, from_down_c,
+def second_kernel(dims, rate, batch, live, rows, cols, edge, probe, summed,
+                  intensity, tables_in, part_in, from_left_c, from_right_c, from_up_c, from_down_c,
                   from_left, from_right, from_up, from_down,
                   own_out, gprobe_out, right_c, right_ab, down_a, down_b,
-                  ext, grad, measured, exit_0, exit_1, wave_0, wave_1, patch_0, patch_1,
+                  ext, grad, mats, measured, exit_0, exit_1, wave_0, wave_1, patch_0, patch_1,
                   gprobe, now, sems, moves):
     side, nrows, ncols = dims
     t = side // LANES
     last = ncols // LANES
-    copies = run_copies([(part_in, ext)], moves)
+    copies = run_copies([(part_in, ext), (tables_in, mats)], moves)
     copies += start_slots(1, batch, intensity, measured, sems)
     waves, patches = (wave_0, wave_1), (patch_0, patch_1)
     clear(grad, gprobe, waves, patches)
@@ -261,10 +252,10 @@
     def _():
         ext[:, right, :, :] = jnp.zeros((2, t, nrows + side, LANES), F32)
 
-    slot_loop(1, side, batch, live, rows, cols, (forward, backward), now, ext, grad, gprobe,
+    slot_loop(1, side, batch, live, rows, cols, mats, now, ext, grad, gprobe,
               measured, (exit_0, exit_1), waves, patches)
     c_rows, own_rows = pl.ds(nrows, side), pl.ds(0, nrows)
-    own_cols, right = pl.ds(0, last), pl.ds(last, t)
+    right = pl.ds(last, t)
     pairs = [
         (gprobe, gprobe_out),
         (grad.at[:, right, c_rows, :], right_c),
@@ -273,8 +264,7 @@
         (grad.at[:, right, own_rows, :], right_ab),
     ]
     copies = run_copies(pairs, moves)
-    ext[:, 0:last, 0:nrows, :] = ext[:, 0:last, 0:nrows, :] - 0.25 * grad[:, 0:last, 0:nrows, :]
-    copies += run_copies([(ext.at[:, own_cols, own_rows, :], own_out)], moves, len(pairs))
+    copies += update_out(ext, grad, own_out, moves, len(pairs))
     for copy in copies:
         copy.wait()
 
@@ -319,6 +309,7 @@
         scratch_shapes=[
             pltpu.VMEM(big, F32),
             pltpu.VMEM(big, F32),
+            pltpu.VMEM((2, 2 * side, 2 * side), BF16),
             pltpu.VMEM((slots, side, side), BF16),
         ] + [pltpu.VMEM((2 * side, side), BF16)] * 4
         + [pltpu.VMEM((2, side // LANES, side, LANES), F32)] * 3
@@ -341,21 +332,6 @@
     )(mine)
 
 
-def join(left_c, right_c, from_left, from_right):
-    vmem = pl.BlockSpec(memory_space=pltpu.VMEM)
-    hbm = pl.BlockSpec(memory_space=pltpu.HBM)
-    return pl.pallas_call(
-        join_kernel,
-        out_shape=[jax.ShapeDtypeStruct(left_c.shape, F32)] * 2,
-        in_specs=[hbm] * 2 + [vmem] * 2,
-        out_specs=[hbm] * 2,
-        scratch_shapes=[pltpu.VMEM((4,) + left_c.shape[1:], F32),
-                        pltpu.SemaphoreType.DMA((4,)), pltpu.SemaphoreType.DMA((4,))],
-        compiler_params=pltpu.CompilerParams(vmem_limit_bytes=8 * MIB),
-        name="join_corners",
-    )(left_c, right_c, from_left, from_right)
-
-
 def simple(kernel, shape, name, limit, vectors):
     vmem = pl.BlockSpec(memory_space=pltpu.VMEM)
     return pl.pallas_call(
@@ -376,8 +352,7 @@
     t = side // LANES
     total = (ncols + side) // LANES
     probe_rate = 0.125 / math.sqrt(LIVE * lax.axis_size("tile") * lax.axis_size("row"))
-    forward, backward = tables(side)
-    forward, backward = jnp.asarray(forward), jnp.asarray(backward)
+    both = jnp.asarray(np.stack(tables(side)))
     current = probe.reshape(2, side, t, LANES).transpose(0, 2, 1, 3)
 
     first, rest = lax.optimization_barrier((object_field[:, :side, :side], object_field))
@@ -396,10 +371,10 @@
     strip = (2, ncols // LANES - t, side, LANES)
     side_b = (2, t, nrows - side, LANES)
     part, gprobe, right_c, left_c, right_b, left_b, down_b, up_b = call(
-        functools.partial(first_kernel, dims), dims, slots, scalars, (forward, backward, current),
-        (intensity, object_field), (below_a, below_b, beside, corner),
+        functools.partial(first_kernel, dims), dims, slots, scalars, (current,),
+        (intensity, both, object_field), (below_a, below_b, beside, corner),
         [big, current.shape, corners, corners, side_b, side_b, strip, strip], [],
-        28, "first_iteration")
+        52, "first_iteration")
 
     from_left_c = passed_along(right_c, "tile", 1)
     from_right_c = passed_along(left_c, "tile", -1)
@@ -407,11 +382,12 @@
     from_down_b = passed_along(up_b, "row", -1)
     mine = swap(gprobe.reshape(devices, -1, LANES))
     mine, from_left_c, from_right_c = lax.optimization_barrier((mine, from_left_c, from_right_c))
-    down_c, up_c = join(left_c, right_c, from_left_c, from_right_c)
+    down_c = jnp.stack([left_c[1] + from_left_c[1], right_c[1] + from_right_c[1]])
+    up_c = jnp.stack([left_c[0] + from_left_c[0], right_c[0] + from_right_c[0]])
     from_up_c = passed_along(down_c, "row", 1)
     from_down_c = passed_along(up_c, "row", -1)
-    mine, from_up_b, from_down_b, _ = lax.optimization_barrier(
-        (mine, from_up_b, from_down_b, down_c))
+    mine, from_up_b, from_down_b, _, _ = lax.optimization_barrier(
+        (mine, from_up_b, from_down_b, down_c, up_c))
     given, right_b, left_b = lax.optimization_barrier((add_up(mine), right_b, left_b))
     from_left_b = passed_along(right_b, "tile", 1)
     from_right_b = passed_along(left_b, "tile", -1)
@@ -419,12 +395,12 @@
 
     own, gprobe, right_c, right_ab, down_a, down_b = call(
         functools.partial(second_kernel, dims, probe_rate), dims, slots, scalars + (edge,),
-        (forward, backward, current, sum_one), (intensity, part),
+        (current, sum_one), (intensity, both, part),
         (from_left_c, from_right_c, from_up_c, from_down_c,
          from_left_b, from_right_b, from_up_b, from_down_b),
         [(2, ncols // LANES, nrows, LANES), current.shape, (2, t, side, LANES),
          (2, t, nrows, LANES), (2, t, side, LANES), strip],
-        [current.shape], 28, "second_iteration")
+        [current.shape], 49, "second_iteration")
 
     from_left_c = passed_along(right_c, "tile", 1)
     above_b = passed_along(down_b, "row", 1)

time: 221 us -> 205 us (0.928)
  local copies, waits for them, and re-layouts: 26 us -> 8.39 us
  Pallas kernels: 45.3 us -> 36.4 us
  starting transfers between devices: 86.8 us -> 94.9 us
  other arithmetic: 2.27 us -> 7.02 us
    unnamed x54 -> x24, local copies, waits for them, and re-layouts: 20.5 us -> 3.13 us
    all_to_all x4, starting transfers between devices: 37 us -> 45.4 us  [swap(): return lax.all_to_all(shares, ('tile', 'row'), 0, 0, tiled=True)]
    pallas_call x2, Pallas kernels: 33.4 us -> 27.3 us  [call(): pl.pallas_call(kernel, out_shape=[jax.ShapeDtypeStruct(shape, F32) for sh...]
    add x0 -> x1, other arithmetic: none -> 2.62 us  [local(): up_c = jnp.stack([left_c[0] + from_left_c[0], right_c[0] + from_right_c[0]])]
    pallas_call x1 -> x0, Pallas kernels: 2.58 us -> none  [join(): pl.pallas_call(join_kernel, out_shape=[jax.ShapeDtypeStruct(left_c.shape,...]
  transfers between devices with their start and end apart: 20 -> 20, of which waited for: 8 -> 8; matrix products, arithmetic and copies ran while one was open for 4% -> 6% of each run, Pallas kernels for 4% -> 3%
where the time goes in v4:
time: 205 us
  starting transfers between devices  94.9 us (46%)
  waiting for transfers between devices  56.9 us (28%)
  Pallas kernels  36.4 us (18%)
  local copies, waits for them, and re-layouts  8.39 us (4%)
  other arithmetic  7.02 us (3%)
    ppermute x16, starting transfers between devices, passed_along(): lax.ppermute(value, axis, [(source, source + steps) for source in range(f...  49.5 us
    all_to_all x4, starting transfers between devices, swap(): return lax.all_to_all(shares, ('tile', 'row'), 0, 0, tiled=True)  45.4 us
    all_to_all x4, waiting for transfers between devices, swap(): return lax.all_to_all(shares, ('tile', 'row'), 0, 0, tiled=True)  38.9 us
    pallas_call x2, Pallas kernels, call(): pl.pallas_call(kernel, out_shape=[jax.ShapeDtypeStruct(shape, F32) for sh...  27.3 us
    ppermute x16, waiting for transfers between devices, passed_along(): lax.ppermute(value, axis, [(source, source + steps) for source in range(f...  18 us
    pallas_call x2, Pallas kernels, simple(): pl.pallas_call(kernel, out_shape=jax.ShapeDtypeStruct(shape, F32), in_spe...  5.07 us
  transfers between devices with their start and end apart: 20, of which 8 were waited for; matrix products, arithmetic and copies ran while one was open for 6% of the time, Pallas kernels for 3%

profile of v4, /device:TPU:1, one launch (start us, length us, event | category | flops | bytes accessed | tf_op | source)
XLA Modules:
  0.0 204.6 jit_solution(6780123977255199425)
XLA Ops:
  0.6 1.1 slice.33
  1.7 1.3 collective-permute-start
  3.0 1.3 slice.35
  4.3 0.0 copy-start.4
  4.4 3.5 %collective-permute-start.2 = (f32[2,512,256]{2,1,0:T(8,128)S(1)}, f32[2,512,256]{2,1,0:T(8,128)S(1)}, u32[]{:S(2)}, u32[]{:S(2)}) collective-permute-start(f32[2,512,256]{2,1,0:T(8,128)S(1)} %slice.35), channel_id=1, source_target_pairs={{4,0},{8,4},{12,8},{16,12},{20,16},{24,20},{28,24},{32,28},{36,32}... | collective-permute-start | bytes 3145736 | tf_op jit(solution)/shard_map/ppermute | solution.py:22
  7.8 1.9 slice.34
  9.7 1.3 collective-permute-start.1
  11.0 6.0 %collective-permute-done.below_a = f32[2,256,256]{2,1,0:T(8,128)S(1)} collective-permute-done((f32[2,256,256]{2,1,0:T(8,128)S(1)}, f32[2,256,256]{2,1,0:T(8,128)S(1)}, u32[]{:S(2)}, u32[]{:S(2)}) %collective-permute-start) | collective-permute-done | bytes 524320 | tf_op jit(solution)/shard_map/ppermute | solution.py:22
  17.0 4.8 %collective-permute-start.3 = (f32[2,256,256]{2,1,0:T(8,128)S(1)}, f32[2,256,256]{2,1,0:T(8,128)}, u32[]{:S(2)}, u32[]{:S(2)}) collective-permute-start(f32[2,256,256]{2,1,0:T(8,128)S(1)} %collective-permute-done.below_a), channel_id=1, source_target_pairs={{4,0},{8,4},{12,8},{16,12},{20,16},{24,20},{28,24},{32,28},{36,32}... | collective-permute-start | bytes 1572872 | tf_op jit(solution)/shard_map/ppermute | solution.py:22
  21.8 0.1 copy.15.live
  21.9 1.2 copy.12
  23.1 1.0 copy.13
  24.1 4.2 %collective-permute-done.1.below_b = f32[2,256,256]{2,1,0:T(8,128)} collective-permute-done((f32[2,256,256]{2,1,0:T(8,128)}, f32[2,256,256]{2,1,0:T(8,128)}, u32[]{:S(2)}, u32[]{:S(2)}) %collective-permute-start.1) | collective-permute-done | bytes 524320 | tf_op jit(solution)/shard_map/ppermute | solution.py:22
  28.3 1.6 collective-permute-done.3.corner
  29.9 1.0 copy-done.8
  30.9 11.1 %first_iteration.1 = (f32[2,6,768,128]{3,2,1,0:T(8,128)}, f32[2,2,256,128]{3,2,1,0:T(8,128)}, f32[2,2,2,256,128]{4,3,2,1,0:T(8,128)}, f32[2,2,2,256,128]{4,3,2,1...) custom-call(s32[2,12]{1,0:T(2,128)S(1)} %copy-done.3, ...), custom_call_target="tpu_custom_call" | custom-call | tf_op jit(solution)/shard_map/first_iteration/pallas_call | solution.py:303
  42.0 3.2 %collective-permute-start.4 = (f32[2,2,2,256,128]{4,3,2,1,0:T(8,128)}, f32[2,2,2,256,128]{4,3,2,1,0:T(8,128)S(1)}, u32[]{:S(2)}, u32[]{:S(2)}) collective-permute-start(f32[2,2,2,256,128]{4,3,2,1,0:T(8,128)} %get-tuple-element.35), channel_id=1, source_target_pairs={{0,4},{4,8},{8,12},{12,16},{16,20},{20,24},{24,28},{28,32},{32,36}... | collective-permute-start | bytes 3145736 | tf_op jit(solution)/shard_map/ppermute | solution.py:22
  45.3 1.9 collective-permute-start.5
  47.2 20.1 %all-to-all-start = ((f32[128,8,128]{2,1,0:T(8,128)}), f32[128,8,128]{2,1,0:T(8,128)S(1)}, u32[]{:S(2)}, u32[]{:S(2)}) async-start(f32[128,8,128]{2,1,0:T(8,128)} %bitcast.4), calls=%async_computation | async-start | bytes 1048576 | tf_op jit(solution)/shard_map/all_to_all | solution.py:326
  67.3 3.3 %collective-permute-start.6 = (f32[2,2,256,128]{3,2,1,0:T(8,128)}, f32[2,2,256,128]{3,2,1,0:T(8,128)S(1)}, u32[]{:S(2)}, u32[]{:S(2)}) collective-permute-start(f32[2,2,256,128]{3,2,1,0:T(8,128)} %get-tuple-element.38), channel_id=1, source_target_pairs={{0,1},{1,2},{2,3},{4,5},{5,6},{6,7},{8,9},{9,10},{10,11},{12,13},{... | collective-permute-start | bytes 1572872 | tf_op jit(solution)/shard_map/ppermute | solution.py:22
  70.7 1.3 collective-permute-start.7
  72.0 9.7 %all-to-all-done.received = f32[128,8,128]{2,1,0:T(8,128)S(1)} async-done(((f32[128,8,128]{2,1,0:T(8,128)}), f32[128,8,128]{2,1,0:T(8,128)S(1)}, u32[]{:S(2)}, u32[]{:S(2)}) %all-to-all-start) | async-done | bytes 524320 | tf_op jit(solution)/shard_map/all_to_all | solution.py:326
  81.7 2.6 %slice_add_fusion = (f32[1,2,2,256,128]{4,3,2,1,0:T(8,128)S(1)}, f32[1,2,2,256,128]{4,3,2,1,0:T(8,128)S(1)}, f32[1,2,2,256,128]{4,3,2,1,0:T(8,128)S(1)}, f32[1,2,2,256,128]{4,3,2,1,0:T(8,128)S(1)}) fusion(f32[2,2,2,256,128]{4,3,2,1,0:T(8,128)} %collective-permute-done.5.from_right_c, f32[2,2,2,256,128]{4,3,2,1,0:T(8,128)} %get-tuple-element.35, ...), kind=kLoop, calls=%fused_computation.2 | loop fusion | flops 524288 | bytes 6291456 | tf_op jit(solution)/shard_map/add | solution.py:386
  84.3 1.0 pad_maximum_fusion
  85.4 4.0 %collective-permute-start.8 = (f32[2,2,2,256,128]{4,3,2,1,0:T(8,128)}, f32[2,2,2,256,128]{4,3,2,1,0:T(8,128)}, u32[]{:S(2)}, u32[]{:S(2)}) collective-permute-start(f32[2,2,2,256,128]{4,3,2,1,0:T(8,128)} %pad_maximum_fusion), channel_id=1, source_target_pairs={{0,1},{1,2},{2,3},{4,5},{5,6},{6,7},{8,9},{9,10},{10,11},{12,13},{... | collective-permute-start | bytes 3145736 | tf_op jit(solution)/shard_map/ppermute | solution.py:22
  89.4 1.1 pad_maximum_fusion.1
  90.5 1.3 collective-permute-start.9
  91.8 2.0 sum_shares.2
  93.8 4.1 %collective-permute-start.10 = (f32[2,2,256,128]{3,2,1,0:T(8,128)}, f32[2,2,256,128]{3,2,1,0:T(8,128)S(1)}, u32[]{:S(2)}, u32[]{:S(2)}) collective-permute-start(f32[2,2,256,128]{3,2,1,0:T(8,128)} %get-tuple-element.47), channel_id=1, source_target_pairs={{0,4},{4,8},{8,12},{12,16},{16,20},{20,24},{24,28},{28,32},{32,36}... | collective-permute-start | bytes 1572872 | tf_op jit(solution)/shard_map/ppermute | solution.py:22
  97.9 1.9 collective-permute-start.11
  99.9 9.7 %all-to-all-start.1 = ((f32[128,8,128]{2,1,0:T(8,128)}), f32[128,8,128]{2,1,0:T(8,128)S(1)}, u32[]{:S(2)}, u32[]{:S(2)}) async-start(f32[128,8,128]{2,1,0:T(8,128)} %sum_shares.2), calls=%async_computation.1 | async-start | bytes 1048576 | tf_op jit(solution)/shard_map/all_to_all | solution.py:326
  109.6 0.1 add_convert_fusion.edge
  109.7 13.7 %all-to-all-done.1 = f32[128,8,128]{2,1,0:T(8,128)S(1)} async-done(((f32[128,8,128]{2,1,0:T(8,128)}), f32[128,8,128]{2,1,0:T(8,128)S(1)}, u32[]{:S(2)}, u32[]{:S(2)}) %all-to-all-start.1) | async-done | bytes 524320 | tf_op jit(solution)/shard_map/all_to_all | solution.py:326
  123.4 16.2 %second_iteration.1 = (f32[2,4,512,128]{3,2,1,0:T(8,128)}, f32[2,2,256,128]{3,2,1,0:T(8,128)}, f32[2,2,256,128]{3,2,1,0:T(8,128)}, f32[2,2,512,128]{3,2,1,0:T(8,...) custom-call(s32[2,12]{1,0:T(2,128)S(1)} %copy-done.3, s32[2,1]{1,0:T(2,128)S(1)} %copy.15.live, ...), custom_call_target="tpu_custom_call" | custom-call | tf_op jit(solution)/shard_map/second_iteration/pallas_call | solution.py:303
  139.7 0.8 copy-done.2
  140.4 9.8 %collective-permute-start.13 = (f32[2,2,256,128]{3,2,1,0:T(8,128)}, f32[2,2,256,128]{3,2,1,0:T(8,128)}, u32[]{:S(2)}, u32[]{:S(2)}) collective-permute-start(f32[2,2,256,128]{3,2,1,0:T(8,128)} %get-tuple-element.55), channel_id=1, source_target_pairs={{0,4},{4,8},{8,12},{12,16},{16,20},{20,24},{24,28},{28,32},{32,36}... | collective-permute-start | bytes 1572872 | tf_op jit(solution)/shard_map/ppermute | solution.py:22
  150.2 2.1 %collective-permute-start.12 = (f32[2,2,256,128]{3,2,1,0:T(8,128)}, f32[2,2,256,128]{3,2,1,0:T(8,128)}, u32[]{:S(2)}, u32[]{:S(2)}) collective-permute-start(f32[2,2,256,128]{3,2,1,0:T(8,128)} %get-tuple-element.53), channel_id=1, source_target_pairs={{0,1},{1,2},{2,3},{4,5},{5,6},{6,7},{8,9},{9,10},{10,11},{12,13},{... | collective-permute-start | bytes 1572872 | tf_op jit(solution)/shard_map/ppermute | solution.py:22
  152.3 9.6 %all-to-all-start.2 = ((f32[128,8,128]{2,1,0:T(8,128)}), f32[128,8,128]{2,1,0:T(8,128)}, u32[]{:S(2)}, u32[]{:S(2)}) async-start(f32[128,8,128]{2,1,0:T(8,128)} %bitcast.6), calls=%async_computation.2 | async-start | bytes 1048576 | tf_op jit(solution)/shard_map/all_to_all | solution.py:326
  161.9 2.2 %add.23 = f32[2,2,256,128]{3,2,1,0:T(8,128)} add(f32[2,2,256,128]{3,2,1,0:T(8,128)} %copy-done.2, f32[2,2,256,128]{3,2,1,0:T(8,128)} %collective-permute-done.13) | non-fusion elementwise | flops 131072 | bytes 1572864 | tf_op jit(solution)/shard_map/add | solution.py:408
  164.1 11.2 %all-to-all-done.2.received = f32[128,8,128]{2,1,0:T(8,128)} async-done(((f32[128,8,128]{2,1,0:T(8,128)}), f32[128,8,128]{2,1,0:T(8,128)}, u32[]{:S(2)}, u32[]{:S(2)}) %all-to-all-start.2) | async-done | bytes 524320 | tf_op jit(solution)/shard_map/all_to_all | solution.py:326
  175.3 2.0 sum_shares.3
  177.3 2.7 %collective-permute-start.14 = (f32[2,2,512,128]{3,2,1,0:T(8,128)}, f32[2,2,512,128]{3,2,1,0:T(8,128)}, u32[]{:S(2)}, u32[]{:S(2)}) collective-permute-start(f32[2,2,512,128]{3,2,1,0:T(8,128)} %get-tuple-element.58), channel_id=1, source_target_pairs={{0,4},{4,8},{8,12},{12,16},{16,20},{20,24},{24,28},{28,32},{32,36}... | collective-permute-start | bytes 3145736 | tf_op jit(solution)/shard_map/ppermute | solution.py:22
  180.0 3.1 %collective-permute-start.15 = (f32[2,2,256,128]{3,2,1,0:T(8,128)}, f32[2,2,256,128]{3,2,1,0:T(8,128)}, u32[]{:S(2)}, u32[]{:S(2)}) collective-permute-start(f32[2,2,256,128]{3,2,1,0:T(8,128)} %add.23), channel_id=1, source_target_pairs={{0,1},{1,2},{2,3},{4,5},{5,6},{6,7},{8,9},{9,10},{10,11},{12,13},{... | collective-permute-start | bytes 1572872 | tf_op jit(solution)/shard_map/ppermute | solution.py:22
  183.0 6.0 %all-to-all-start.3 = ((f32[128,8,128]{2,1,0:T(8,128)}), f32[128,8,128]{2,1,0:T(8,128)}, u32[]{:S(2)}, u32[]{:S(2)}) async-start(f32[128,8,128]{2,1,0:T(8,128)} %sum_shares.3), calls=%async_computation.3 | async-start | bytes 1048576 | tf_op jit(solution)/shard_map/all_to_all | solution.py:326
  189.1 6.2 %collective-permute-done.15.above_a = f32[2,2,256,128]{3,2,1,0:T(8,128)} collective-permute-done((f32[2,2,256,128]{3,2,1,0:T(8,128)}, f32[2,2,256,128]{3,2,1,0:T(8,128)}, u32[]{:S(2)}, u32[]{:S(2)}) %collective-permute-start.15) | collective-permute-done | bytes 524320 | tf_op jit(solution)/shard_map/ppermute | solution.py:22
  195.3 3.2 %last_object.1 = f32[2,512,512]{2,1,0:T(8,128)} custom-call(f32[2,4,512,128]{3,2,1,0:T(8,128)S(1)} %copy-done.1, f32[2,2,512,128]{3,2,1,0:T(8,128)} %collective-permute-done.14.left_ab, f32[2,2,256,128]{3,2,1,0:T(8,128)} %collective-permute-done.15.above_a, f32[2,2,256,128]{3,2,1,0:T(8,128)} %collective-permute-done.12.above_b), custom_call_target="tpu_custom_call" | custom-call | tf_op jit(solution)/shard_map/last_object/pallas_call | solution.py:337
  198.4 4.3 %all-to-all-done.3 = f32[128,8,128]{2,1,0:T(8,128)} async-done(((f32[128,8,128]{2,1,0:T(8,128)}), f32[128,8,128]{2,1,0:T(8,128)}, u32[]{:S(2)}, u32[]{:S(2)}) %all-to-all-start.3) | async-done | bytes 524320 | tf_op jit(solution)/shard_map/all_to_all | solution.py:326
  202.7 1.9 last_probe.1
  (31 shorter events, 0.1 us)
Async XLA Ops:
  0.6 21.2 %copy-start.10 = (s32[2,1]{0,1:T(1,128)S(1)}, s32[2,1]{0,1:T(1,128)}, u32[]{:S(2)}) copy-start(s32[2,1]{0,1:T(1,128)} %param.14) | copy-start | bytes 28
  1.7 15.3 %collective-permute-start = (f32[2,256,256]{2,1,0:T(8,128)S(1)}, f32[2,256,256]{2,1,0:T(8,128)S(1)}, u32[]{:S(2)}, u32[]{:S(2)}) collective-permute-start(f32[2,256,256]{2,1,0:T(8,128)S(1)} %slice.33), channel_id=1, source_target_pairs={{1,0},{2,1},{3,2},{5,4},{6,5},{7,6},{9,8},{10,9},{11,10},{13,12},{... | collective-permute-start | bytes 1572872 | tf_op jit(solution)/shard_map/ppermute | solution.py:22
  4.3 26.6 %copy-start.3 = (s32[2,12]{1,0:T(2,128)S(1)}, s32[2,12]{1,0:T(2,128)}, u32[]{:S(2)}) copy-start(s32[2,12]{1,0:T(2,128)} %batch.3) | copy-start | bytes 292
  4.3 26.5 %copy-start.4 = (s32[32]{0:T(128)S(1)}, s32[32]{0:T(128)}, u32[]{:S(2)}) copy-start(s32[32]{0:T(128)} %rows.3) | copy-start | bytes 388
  4.4 26.5 %copy-start.5 = (s32[32]{0:T(128)S(1)}, s32[32]{0:T(128)}, u32[]{:S(2)}) copy-start(s32[32]{0:T(128)} %cols.3) | copy-start | bytes 388
  4.4 25.5 %collective-permute-start.2 = (f32[2,512,256]{2,1,0:T(8,128)S(1)}, f32[2,512,256]{2,1,0:T(8,128)S(1)}, u32[]{:S(2)}, u32[]{:S(2)}) collective-permute-start(f32[2,512,256]{2,1,0:T(8,128)S(1)} %slice.35), channel_id=1, source_target_pairs={{4,0},{8,4},{12,8},{16,12},{20,16},{24,20},{28,24},{32,28},{36,32}... | collective-permute-start | bytes 3145736 | tf_op jit(solution)/shard_map/ppermute | solution.py:22
  9.7 18.6 %collective-permute-start.1 = (f32[2,256,256]{2,1,0:T(8,128)}, f32[2,256,256]{2,1,0:T(8,128)}, u32[]{:S(2)}, u32[]{:S(2)}) collective-permute-start(f32[2,256,256]{2,1,0:T(8,128)} %slice.34), channel_id=1, source_target_pairs={{1,0},{2,1},{3,2},{5,4},{6,5},{7,6},{9,8},{10,9},{11,10},{13,12},{... | collective-permute-start | bytes 1572872 | tf_op jit(solution)/shard_map/ppermute | solution.py:22
  17.0 12.9 %copy-start.9 = (f32[2,256,256]{2,1,0:T(8,128)}, f32[2,256,256]{2,1,0:T(8,128)S(1)}, u32[]{:S(2)}) copy-start(f32[2,256,256]{2,1,0:T(8,128)S(1)} %collective-permute-done.below_a) | copy-start | bytes 1572868
  17.0 12.9 %collective-permute-start.3 = (f32[2,256,256]{2,1,0:T(8,128)S(1)}, f32[2,256,256]{2,1,0:T(8,128)}, u32[]{:S(2)}, u32[]{:S(2)}) collective-permute-start(f32[2,256,256]{2,1,0:T(8,128)S(1)} %collective-permute-done.below_a), channel_id=1, source_target_pairs={{4,0},{8,4},{12,8},{16,12},{20,16},{24,20},{28,24},{32,28},{36,32}... | collective-permute-start | bytes 1572872 | tf_op jit(solution)/shard_map/ppermute | solution.py:22
  29.9 1.0 copy-start.8
  42.0 39.6 %collective-permute-start.4 = (f32[2,2,2,256,128]{4,3,2,1,0:T(8,128)}, f32[2,2,2,256,128]{4,3,2,1,0:T(8,128)S(1)}, u32[]{:S(2)}, u32[]{:S(2)}) collective-permute-start(f32[2,2,2,256,128]{4,3,2,1,0:T(8,128)} %get-tuple-element.35), channel_id=1, source_target_pairs={{0,4},{4,8},{8,12},{12,16},{16,20},{20,24},{24,28},{28,32},{32,36}... | collective-permute-start | bytes 3145736 | tf_op jit(solution)/shard_map/ppermute | solution.py:22
  45.3 36.4 %collective-permute-start.5 = (f32[2,2,2,256,128]{4,3,2,1,0:T(8,128)}, f32[2,2,2,256,128]{4,3,2,1,0:T(8,128)}, u32[]{:S(2)}, u32[]{:S(2)}) collective-permute-start(f32[2,2,2,256,128]{4,3,2,1,0:T(8,128)} %get-tuple-element.36), channel_id=1, source_target_pairs={{4,0},{8,4},{12,8},{16,12},{20,16},{24,20},{28,24},{32,28},{36,32}... | collective-permute-start | bytes 3145736 | tf_op jit(solution)/shard_map/ppermute | solution.py:22
  47.2 34.5 %all-to-all-start = ((f32[128,8,128]{2,1,0:T(8,128)}), f32[128,8,128]{2,1,0:T(8,128)S(1)}, u32[]{:S(2)}, u32[]{:S(2)}) async-start(f32[128,8,128]{2,1,0:T(8,128)} %bitcast.4), calls=%async_computation | async-start | bytes 1048576 | tf_op jit(solution)/shard_map/all_to_all | solution.py:326
  67.3 24.4 %collective-permute-start.6 = (f32[2,2,256,128]{3,2,1,0:T(8,128)}, f32[2,2,256,128]{3,2,1,0:T(8,128)S(1)}, u32[]{:S(2)}, u32[]{:S(2)}) collective-permute-start(f32[2,2,256,128]{3,2,1,0:T(8,128)} %get-tuple-element.38), channel_id=1, source_target_pairs={{0,1},{1,2},{2,3},{4,5},{5,6},{6,7},{8,9},{9,10},{10,11},{12,13},{... | collective-permute-start | bytes 1572872 | tf_op jit(solution)/shard_map/ppermute | solution.py:22
  70.7 21.1 %collective-permute-start.7 = (f32[2,2,256,128]{3,2,1,0:T(8,128)}, f32[2,2,256,128]{3,2,1,0:T(8,128)}, u32[]{:S(2)}, u32[]{:S(2)}) collective-permute-start(f32[2,2,256,128]{3,2,1,0:T(8,128)} %get-tuple-element.39), channel_id=1, source_target_pairs={{1,0},{2,1},{3,2},{5,4},{6,5},{7,6},{9,8},{10,9},{11,10},{13,12},{... | collective-permute-start | bytes 1572872 | tf_op jit(solution)/shard_map/ppermute | solution.py:22
  81.7 2.6 %copy-start.7 = (f32[128,8,128]{2,1,0:T(8,128)}, f32[128,8,128]{2,1,0:T(8,128)S(1)}, u32[]{:S(2)}) copy-start(f32[128,8,128]{2,1,0:T(8,128)S(1)} %all-to-all-done.received) | copy-start | bytes 1572868
  81.7 2.6 %copy-start.6 = (f32[2,2,2,256,128]{4,3,2,1,0:T(8,128)}, f32[2,2,2,256,128]{4,3,2,1,0:T(8,128)S(1)}, u32[]{:S(2)}) copy-start(f32[2,2,2,256,128]{4,3,2,1,0:T(8,128)S(1)} %collective-permute-done.4.from_left_c) | copy-start | bytes 3145732
  85.4 38.1 %collective-permute-start.8 = (f32[2,2,2,256,128]{4,3,2,1,0:T(8,128)}, f32[2,2,2,256,128]{4,3,2,1,0:T(8,128)}, u32[]{:S(2)}, u32[]{:S(2)}) collective-permute-start(f32[2,2,2,256,128]{4,3,2,1,0:T(8,128)} %pad_maximum_fusion), channel_id=1, source_target_pairs={{0,1},{1,2},{2,3},{4,5},{5,6},{6,7},{8,9},{9,10},{10,11},{12,13},{... | collective-permute-start | bytes 3145736 | tf_op jit(solution)/shard_map/ppermute | solution.py:22
  89.4 34.0 %copy-start = (f32[2,256,2,128]{3,1,2,0:T(8,128)S(1)}, f32[2,256,2,128]{3,1,2,0:T(8,128)}, u32[]{:S(2)}) copy-start(f32[2,256,2,128]{3,1,2,0:T(8,128)} %copy.13) | copy-start | bytes 1572868
  90.5 32.9 %collective-permute-start.9 = (f32[2,2,2,256,128]{4,3,2,1,0:T(8,128)}, f32[2,2,2,256,128]{4,3,2,1,0:T(8,128)}, u32[]{:S(2)}, u32[]{:S(2)}) collective-permute-start(f32[2,2,2,256,128]{4,3,2,1,0:T(8,128)} %pad_maximum_fusion.1), channel_id=1, source_target_pairs={{1,0},{2,1},{3,2},{5,4},{6,5},{7,6},{9,8},{10,9},{11,10},{13,12},{... | collective-permute-start | bytes 3145736 | tf_op jit(solution)/shard_map/ppermute | solution.py:22
  93.8 29.6 %collective-permute-start.10 = (f32[2,2,256,128]{3,2,1,0:T(8,128)}, f32[2,2,256,128]{3,2,1,0:T(8,128)S(1)}, u32[]{:S(2)}, u32[]{:S(2)}) collective-permute-start(f32[2,2,256,128]{3,2,1,0:T(8,128)} %get-tuple-element.47), channel_id=1, source_target_pairs={{0,4},{4,8},{8,12},{12,16},{16,20},{20,24},{24,28},{28,32},{32,36}... | collective-permute-start | bytes 1572872 | tf_op jit(solution)/shard_map/ppermute | solution.py:22
  97.9 25.5 %collective-permute-start.11 = (f32[2,2,256,128]{3,2,1,0:T(8,128)S(1)}, f32[2,2,256,128]{3,2,1,0:T(8,128)S(1)}, u32[]{:S(2)}, u32[]{:S(2)}) collective-permute-start(f32[2,2,256,128]{3,2,1,0:T(8,128)S(1)} %get-tuple-element.48), channel_id=1, source_target_pairs={{4,0},{8,4},{12,8},{16,12},{20,16},{24,20},{28,24},{32,28},{36,32}... | collective-permute-start | bytes 1572872 | tf_op jit(solution)/shard_map/ppermute | solution.py:22
  99.9 23.5 %all-to-all-start.1 = ((f32[128,8,128]{2,1,0:T(8,128)}), f32[128,8,128]{2,1,0:T(8,128)S(1)}, u32[]{:S(2)}, u32[]{:S(2)}) async-start(f32[128,8,128]{2,1,0:T(8,128)} %sum_shares.2), calls=%async_computation.1 | async-start | bytes 1048576 | tf_op jit(solution)/shard_map/all_to_all | solution.py:326
  139.6 0.8 copy-start.2
  140.4 21.4 %collective-permute-start.13 = (f32[2,2,256,128]{3,2,1,0:T(8,128)}, f32[2,2,256,128]{3,2,1,0:T(8,128)}, u32[]{:S(2)}, u32[]{:S(2)}) collective-permute-start(f32[2,2,256,128]{3,2,1,0:T(8,128)} %get-tuple-element.55), channel_id=1, source_target_pairs={{0,4},{4,8},{8,12},{12,16},{16,20},{20,24},{24,28},{28,32},{32,36}... | collective-permute-start | bytes 1572872 | tf_op jit(solution)/shard_map/ppermute | solution.py:22
  150.2 25.1 %collective-permute-start.12 = (f32[2,2,256,128]{3,2,1,0:T(8,128)}, f32[2,2,256,128]{3,2,1,0:T(8,128)}, u32[]{:S(2)}, u32[]{:S(2)}) collective-permute-start(f32[2,2,256,128]{3,2,1,0:T(8,128)} %get-tuple-element.53), channel_id=1, source_target_pairs={{0,1},{1,2},{2,3},{4,5},{5,6},{6,7},{8,9},{9,10},{10,11},{12,13},{... | collective-permute-start | bytes 1572872 | tf_op jit(solution)/shard_map/ppermute | solution.py:22
  152.3 23.0 %all-to-all-start.2 = ((f32[128,8,128]{2,1,0:T(8,128)}), f32[128,8,128]{2,1,0:T(8,128)}, u32[]{:S(2)}, u32[]{:S(2)}) async-start(f32[128,8,128]{2,1,0:T(8,128)} %bitcast.6), calls=%async_computation.2 | async-start | bytes 1048576 | tf_op jit(solution)/shard_map/all_to_all | solution.py:326
  161.9 33.4 %copy-start.1 = (f32[2,4,512,128]{3,2,1,0:T(8,128)S(1)}, f32[2,4,512,128]{3,2,1,0:T(8,128)}, u32[]{:S(2)}) copy-start(f32[2,4,512,128]{3,2,1,0:T(8,128)} %get-tuple-element.51.own) | copy-start | bytes 6291460
  177.3 18.0 %collective-permute-start.14 = (f32[2,2,512,128]{3,2,1,0:T(8,128)}, f32[2,2,512,128]{3,2,1,0:T(8,128)}, u32[]{:S(2)}, u32[]{:S(2)}) collective-permute-start(f32[2,2,512,128]{3,2,1,0:T(8,128)} %get-tuple-element.58), channel_id=1, source_target_pairs={{0,4},{4,8},{8,12},{12,16},{16,20},{20,24},{24,28},{28,32},{32,36}... | collective-permute-start | bytes 3145736 | tf_op jit(solution)/shard_map/ppermute | solution.py:22
  180.0 15.3 %collective-permute-start.15 = (f32[2,2,256,128]{3,2,1,0:T(8,128)}, f32[2,2,256,128]{3,2,1,0:T(8,128)}, u32[]{:S(2)}, u32[]{:S(2)}) collective-permute-start(f32[2,2,256,128]{3,2,1,0:T(8,128)} %add.23), channel_id=1, source_target_pairs={{0,1},{1,2},{2,3},{4,5},{5,6},{6,7},{8,9},{9,10},{10,11},{12,13},{... | collective-permute-start | bytes 1572872 | tf_op jit(solution)/shard_map/ppermute | solution.py:22
  183.0 19.7 %all-to-all-start.3 = ((f32[128,8,128]{2,1,0:T(8,128)}), f32[128,8,128]{2,1,0:T(8,128)}, u32[]{:S(2)}, u32[]{:S(2)}) async-start(f32[128,8,128]{2,1,0:T(8,128)} %sum_shares.3), calls=%async_computation.3 | async-start | bytes 1048576 | tf_op jit(solution)/shard_map/all_to_all | solution.py:326

commit v5 on v4

--- a/solution.py
+++ b/solution.py
@@ -56,7 +56,7 @@
 
 
 def slot_loop(step, side, batch, live, rows, cols, mats, probe, ext, grad, gprobe,
-              measured, exits, waves, patches):
+              measured, exits, waves, patches, apart):
     forward, backward = mats.at[0], mats.at[1]
     lane = lax.broadcasted_iota(jnp.int32, (side, LANES), 1)
     halves = side // LANES
@@ -134,9 +134,33 @@
         first_half(odd, 1, alive)
         return carry
 
+    def two_steps(k, carry):
+        even = 2 * k
+        odd = even + 1
+        second_half(jnp.maximum(even - 1, 0), 1)
+        first_half(even, 0, None)
+
+        @pl.when(odd < count)
+        def _():
+            second_half(even, 0)
+            first_half(odd, 1, None)
+
+        @pl.when(odd == count)
+        def _():
+            second_half(even, 0)
+
+        return carry
+
     pairs = (count + 1) // 2
-    lax.fori_loop(0, pairs, two_slots, 0)
-    second_half(jnp.minimum(2 * pairs - 1, batch.shape[1] - 1), 1)
+    if apart:
+        lax.fori_loop(0, pairs, two_steps, 0)
+
+        @pl.when(count % 2 == 0)
+        def _():
+            second_half(count - 1, 1)
+    else:
+        lax.fori_loop(0, pairs, two_slots, 0)
+        second_half(jnp.minimum(2 * pairs - 1, batch.shape[1] - 1), 1)
 
 
 def tiled_copies(field, part_rows, part_cols, ext, row0, col0):
@@ -186,7 +210,7 @@
     for copy in copies:
         copy.wait()
     slot_loop(0, side, batch, live, rows, cols, mats, probe, ext, grad, gprobe,
-              measured, (exit_0, exit_1), waves, patches)
+              measured, (exit_0, exit_1), waves, patches, False)
     t = side // LANES
     last = ncols // LANES
     a_rows, c_rows = pl.ds(0, side), pl.ds(nrows, side)
@@ -253,7 +277,7 @@
         ext[:, right, :, :] = jnp.zeros((2, t, nrows + side, LANES), F32)
 
     slot_loop(1, side, batch, live, rows, cols, mats, now, ext, grad, gprobe,
-              measured, (exit_0, exit_1), waves, patches)
+              measured, (exit_0, exit_1), waves, patches, True)
     c_rows, own_rows = pl.ds(nrows, side), pl.ds(0, nrows)
     right = pl.ds(last, t)
     pairs = [
@@ -372,7 +396,7 @@
     side_b = (2, t, nrows - side, LANES)
     part, gprobe, right_c, left_c, right_b, left_b, down_b, up_b = call(
         functools.partial(first_kernel, dims), dims, slots, scalars, (current,),
-        (intensity, both, object_field), (below_a, below_b, beside, corner),
+        (intensity, both, object_field, below_a, below_b, beside, corner), (),
         [big, current.shape, corners, corners, side_b, side_b, strip, strip], [],
         52, "first_iteration")
 

time: 205 us -> 207 us (level)
  starting transfers between devices: 94.9 us -> 89.1 us
  Pallas kernels: 36.4 us -> 41.1 us
    pallas_call x2, Pallas kernels: 27.3 us -> 32.1 us  [call(): pl.pallas_call(kernel, out_shape=[jax.ShapeDtypeStruct(shape, F32) for sh...]
    all_to_all x4, starting transfers between devices: 45.4 us -> 41 us  [swap(): return lax.all_to_all(shares, ('tile', 'row'), 0, 0, tiled=True)]
where the time goes in v5:
time: 207 us; the launch traced here: 205 us
  starting transfers between devices  89.1 us (43%)
  waiting for transfers between devices  58.7 us (28%)
  Pallas kernels  41.1 us (20%)
  local copies, waits for them, and re-layouts  8.39 us (4%)
  other arithmetic  7.02 us (3%)
    ppermute x16, starting transfers between devices, passed_along(): lax.ppermute(value, axis, [(source, source + steps) for source in range(f...  48.1 us
    all_to_all x4, starting transfers between devices, swap(): return lax.all_to_all(shares, ('tile', 'row'), 0, 0, tiled=True)  41 us
    all_to_all x4, waiting for transfers between devices, swap(): return lax.all_to_all(shares, ('tile', 'row'), 0, 0, tiled=True)  40.3 us
    pallas_call x2, Pallas kernels, call(): pl.pallas_call(kernel, out_shape=[jax.ShapeDtypeStruct(shape, F32) for sh...  32.1 us
    ppermute x16, waiting for transfers between devices, passed_along(): lax.ppermute(value, axis, [(source, source + steps) for source in range(f...  18.5 us
    pallas_call x2, Pallas kernels, simple(): pl.pallas_call(kernel, out_shape=jax.ShapeDtypeStruct(shape, F32), in_spe...  5.07 us
  transfers between devices with their start and end apart: 20, of which 8 were waited for; matrix products, arithmetic and copies ran while one was open for 6% of the time, Pallas kernels for 3%

profile of v5, /device:TPU:1, one launch (start us, length us, event | category | flops | bytes accessed | tf_op | source)
XLA Modules:
  0.0 205.3 jit_solution(7764141792597641532)
XLA Ops:
  0.6 1.1 slice.33
  1.7 1.3 collective-permute-start
  3.0 1.3 slice.35
  4.3 0.0 copy-start.4
  4.4 3.5 %collective-permute-start.2 = (f32[2,512,256]{2,1,0:T(8,128)S(1)}, f32[2,512,256]{2,1,0:T(8,128)S(1)}, u32[]{:S(2)}, u32[]{:S(2)}) collective-permute-start(f32[2,512,256]{2,1,0:T(8,128)S(1)} %slice.35), channel_id=1, source_target_pairs={{4,0},{8,4},{12,8},{16,12},{20,16},{24,20},{28,24},{32,28},{36,32}... | collective-permute-start | bytes 3145736 | tf_op jit(solution)/shard_map/ppermute | solution.py:22
  7.8 1.9 slice.34
  9.7 1.3 collective-permute-start.1
  11.0 6.0 %collective-permute-done.below_a = f32[2,256,256]{2,1,0:T(8,128)S(1)} collective-permute-done((f32[2,256,256]{2,1,0:T(8,128)S(1)}, f32[2,256,256]{2,1,0:T(8,128)S(1)}, u32[]{:S(2)}, u32[]{:S(2)}) %collective-permute-start) | collective-permute-done | bytes 524320 | tf_op jit(solution)/shard_map/ppermute | solution.py:22
  17.0 4.8 %collective-permute-start.3 = (f32[2,256,256]{2,1,0:T(8,128)S(1)}, f32[2,256,256]{2,1,0:T(8,128)}, u32[]{:S(2)}, u32[]{:S(2)}) collective-permute-start(f32[2,256,256]{2,1,0:T(8,128)S(1)} %collective-permute-done.below_a), channel_id=1, source_target_pairs={{4,0},{8,4},{12,8},{16,12},{20,16},{24,20},{28,24},{32,28},{36,32}... | collective-permute-start | bytes 1572872 | tf_op jit(solution)/shard_map/ppermute | solution.py:22
  21.8 0.1 copy.15.live
  21.9 1.2 copy.12
  23.1 1.0 copy.13
  24.1 4.2 %collective-permute-done.1.below_b = f32[2,256,256]{2,1,0:T(8,128)} collective-permute-done((f32[2,256,256]{2,1,0:T(8,128)}, f32[2,256,256]{2,1,0:T(8,128)}, u32[]{:S(2)}, u32[]{:S(2)}) %collective-permute-start.1) | collective-permute-done | bytes 524320 | tf_op jit(solution)/shard_map/ppermute | solution.py:22
  28.3 1.6 collective-permute-done.3.corner
  29.9 1.0 copy-done.8
  30.9 15.5 %first_iteration.1 = (f32[2,6,768,128]{3,2,1,0:T(8,128)}, f32[2,2,256,128]{3,2,1,0:T(8,128)}, f32[2,2,2,256,128]{4,3,2,1,0:T(8,128)}, f32[2,2,2,256,128]{4,3,2,1...) custom-call(s32[2,12]{1,0:T(2,128)S(1)} %copy-done.3, ...), custom_call_target="tpu_custom_call" | custom-call | tf_op jit(solution)/shard_map/first_iteration/pallas_call | solution.py:327
  46.4 1.9 collective-permute-start.4
  48.3 2.5 %collective-permute-start.5 = (f32[2,2,2,256,128]{4,3,2,1,0:T(8,128)}, f32[2,2,2,256,128]{4,3,2,1,0:T(8,128)}, u32[]{:S(2)}, u32[]{:S(2)}) collective-permute-start(f32[2,2,2,256,128]{4,3,2,1,0:T(8,128)} %get-tuple-element.36), channel_id=1, source_target_pairs={{4,0},{8,4},{12,8},{16,12},{20,16},{24,20},{28,24},{32,28},{36,32}... | collective-permute-start | bytes 3145736 | tf_op jit(solution)/shard_map/ppermute | solution.py:22
  50.8 17.8 %all-to-all-start = ((f32[128,8,128]{2,1,0:T(8,128)}), f32[128,8,128]{2,1,0:T(8,128)S(1)}, u32[]{:S(2)}, u32[]{:S(2)}) async-start(f32[128,8,128]{2,1,0:T(8,128)} %bitcast.4), calls=%async_computation | async-start | bytes 1048576 | tf_op jit(solution)/shard_map/all_to_all | solution.py:350
  68.6 3.3 %collective-permute-start.6 = (f32[2,2,256,128]{3,2,1,0:T(8,128)}, f32[2,2,256,128]{3,2,1,0:T(8,128)S(1)}, u32[]{:S(2)}, u32[]{:S(2)}) collective-permute-start(f32[2,2,256,128]{3,2,1,0:T(8,128)} %get-tuple-element.38), channel_id=1, source_target_pairs={{0,1},{1,2},{2,3},{4,5},{5,6},{6,7},{8,9},{9,10},{10,11},{12,13},{... | collective-permute-start | bytes 1572872 | tf_op jit(solution)/shard_map/ppermute | solution.py:22
  71.9 1.3 collective-permute-start.7
  73.2 10.2 %all-to-all-done.received = f32[128,8,128]{2,1,0:T(8,128)S(1)} async-done(((f32[128,8,128]{2,1,0:T(8,128)}), f32[128,8,128]{2,1,0:T(8,128)S(1)}, u32[]{:S(2)}, u32[]{:S(2)}) %all-to-all-start) | async-done | bytes 524320 | tf_op jit(solution)/shard_map/all_to_all | solution.py:350
  83.4 2.6 %slice_add_fusion = (f32[1,2,2,256,128]{4,3,2,1,0:T(8,128)S(1)}, f32[1,2,2,256,128]{4,3,2,1,0:T(8,128)S(1)}, f32[1,2,2,256,128]{4,3,2,1,0:T(8,128)S(1)}, f32[1,2,2,256,128]{4,3,2,1,0:T(8,128)S(1)}) fusion(f32[2,2,2,256,128]{4,3,2,1,0:T(8,128)} %collective-permute-done.5.from_right_c, f32[2,2,2,256,128]{4,3,2,1,0:T(8,128)} %get-tuple-element.35, ...), kind=kLoop, calls=%fused_computation.2 | loop fusion | flops 524288 | bytes 6291456 | tf_op jit(solution)/shard_map/add | solution.py:410
  86.0 1.0 pad_maximum_fusion
  87.1 2.9 %collective-permute-start.8 = (f32[2,2,2,256,128]{4,3,2,1,0:T(8,128)}, f32[2,2,2,256,128]{4,3,2,1,0:T(8,128)}, u32[]{:S(2)}, u32[]{:S(2)}) collective-permute-start(f32[2,2,2,256,128]{4,3,2,1,0:T(8,128)} %pad_maximum_fusion), channel_id=1, source_target_pairs={{0,1},{1,2},{2,3},{4,5},{5,6},{6,7},{8,9},{9,10},{10,11},{12,13},{... | collective-permute-start | bytes 3145736 | tf_op jit(solution)/shard_map/ppermute | solution.py:22
  90.0 1.1 pad_maximum_fusion.1
  91.1 1.3 collective-permute-start.9
  92.4 2.0 sum_shares.2
  94.4 3.7 %collective-permute-start.10 = (f32[2,2,256,128]{3,2,1,0:T(8,128)}, f32[2,2,256,128]{3,2,1,0:T(8,128)S(1)}, u32[]{:S(2)}, u32[]{:S(2)}) collective-permute-start(f32[2,2,256,128]{3,2,1,0:T(8,128)} %get-tuple-element.47), channel_id=1, source_target_pairs={{0,4},{4,8},{8,12},{12,16},{16,20},{20,24},{24,28},{28,32},{32,36}... | collective-permute-start | bytes 1572872 | tf_op jit(solution)/shard_map/ppermute | solution.py:22
  98.0 1.9 collective-permute-start.11
  100.0 9.6 %all-to-all-start.1 = ((f32[128,8,128]{2,1,0:T(8,128)}), f32[128,8,128]{2,1,0:T(8,128)S(1)}, u32[]{:S(2)}, u32[]{:S(2)}) async-start(f32[128,8,128]{2,1,0:T(8,128)} %sum_shares.2), calls=%async_computation.1 | async-start | bytes 1048576 | tf_op jit(solution)/shard_map/all_to_all | solution.py:350
  109.6 0.1 add_convert_fusion.edge
  109.7 14.9 %all-to-all-done.1 = f32[128,8,128]{2,1,0:T(8,128)S(1)} async-done(((f32[128,8,128]{2,1,0:T(8,128)}), f32[128,8,128]{2,1,0:T(8,128)S(1)}, u32[]{:S(2)}, u32[]{:S(2)}) %all-to-all-start.1) | async-done | bytes 524320 | tf_op jit(solution)/shard_map/all_to_all | solution.py:350
  124.7 16.6 %second_iteration.1 = (f32[2,4,512,128]{3,2,1,0:T(8,128)}, f32[2,2,256,128]{3,2,1,0:T(8,128)}, f32[2,2,256,128]{3,2,1,0:T(8,128)}, f32[2,2,512,128]{3,2,1,0:T(8,...) custom-call(s32[2,12]{1,0:T(2,128)S(1)} %copy-done.3, s32[2,1]{1,0:T(2,128)S(1)} %copy.15.live, ...), custom_call_target="tpu_custom_call" | custom-call | tf_op jit(solution)/shard_map/second_iteration/pallas_call | solution.py:327
  141.3 0.8 copy-done.2
  142.0 1.9 collective-permute-start.13
  144.0 10.9 %collective-permute-start.12 = (f32[2,2,256,128]{3,2,1,0:T(8,128)}, f32[2,2,256,128]{3,2,1,0:T(8,128)}, u32[]{:S(2)}, u32[]{:S(2)}) collective-permute-start(f32[2,2,256,128]{3,2,1,0:T(8,128)} %get-tuple-element.53), channel_id=1, source_target_pairs={{0,1},{1,2},{2,3},{4,5},{5,6},{6,7},{8,9},{9,10},{10,11},{12,13},{... | collective-permute-start | bytes 1572872 | tf_op jit(solution)/shard_map/ppermute | solution.py:22
  154.8 7.8 %all-to-all-start.2 = ((f32[128,8,128]{2,1,0:T(8,128)}), f32[128,8,128]{2,1,0:T(8,128)}, u32[]{:S(2)}, u32[]{:S(2)}) async-start(f32[128,8,128]{2,1,0:T(8,128)} %bitcast.6), calls=%async_computation.2 | async-start | bytes 1048576 | tf_op jit(solution)/shard_map/all_to_all | solution.py:350
  162.7 2.2 %add.23 = f32[2,2,256,128]{3,2,1,0:T(8,128)} add(f32[2,2,256,128]{3,2,1,0:T(8,128)} %copy-done.2, f32[2,2,256,128]{3,2,1,0:T(8,128)} %collective-permute-done.13) | non-fusion elementwise | flops 131072 | bytes 1572864 | tf_op jit(solution)/shard_map/add | solution.py:432
  164.8 11.2 %all-to-all-done.2.received = f32[128,8,128]{2,1,0:T(8,128)} async-done(((f32[128,8,128]{2,1,0:T(8,128)}), f32[128,8,128]{2,1,0:T(8,128)}, u32[]{:S(2)}, u32[]{:S(2)}) %all-to-all-start.2) | async-done | bytes 524320 | tf_op jit(solution)/shard_map/all_to_all | solution.py:350
  176.0 2.0 sum_shares.3
  178.0 3.3 %collective-permute-start.14 = (f32[2,2,512,128]{3,2,1,0:T(8,128)}, f32[2,2,512,128]{3,2,1,0:T(8,128)}, u32[]{:S(2)}, u32[]{:S(2)}) collective-permute-start(f32[2,2,512,128]{3,2,1,0:T(8,128)} %get-tuple-element.58), channel_id=1, source_target_pairs={{0,4},{4,8},{8,12},{12,16},{16,20},{20,24},{24,28},{28,32},{32,36}... | collective-permute-start | bytes 3145736 | tf_op jit(solution)/shard_map/ppermute | solution.py:22
  181.3 2.5 %collective-permute-start.15 = (f32[2,2,256,128]{3,2,1,0:T(8,128)}, f32[2,2,256,128]{3,2,1,0:T(8,128)}, u32[]{:S(2)}, u32[]{:S(2)}) collective-permute-start(f32[2,2,256,128]{3,2,1,0:T(8,128)} %add.23), channel_id=1, source_target_pairs={{0,1},{1,2},{2,3},{4,5},{5,6},{6,7},{8,9},{9,10},{10,11},{12,13},{... | collective-permute-start | bytes 1572872 | tf_op jit(solution)/shard_map/ppermute | solution.py:22
  183.8 5.8 %all-to-all-start.3 = ((f32[128,8,128]{2,1,0:T(8,128)}), f32[128,8,128]{2,1,0:T(8,128)}, u32[]{:S(2)}, u32[]{:S(2)}) async-start(f32[128,8,128]{2,1,0:T(8,128)} %sum_shares.3), calls=%async_computation.3 | async-start | bytes 1048576 | tf_op jit(solution)/shard_map/all_to_all | solution.py:350
  189.6 6.7 %collective-permute-done.15.above_a = f32[2,2,256,128]{3,2,1,0:T(8,128)} collective-permute-done((f32[2,2,256,128]{3,2,1,0:T(8,128)}, f32[2,2,256,128]{3,2,1,0:T(8,128)}, u32[]{:S(2)}, u32[]{:S(2)}) %collective-permute-start.15) | collective-permute-done | bytes 524320 | tf_op jit(solution)/shard_map/ppermute | solution.py:22
  196.3 3.2 %last_object.1 = f32[2,512,512]{2,1,0:T(8,128)} custom-call(f32[2,4,512,128]{3,2,1,0:T(8,128)S(1)} %copy-done.1, f32[2,2,512,128]{3,2,1,0:T(8,128)} %collective-permute-done.14.left_ab, f32[2,2,256,128]{3,2,1,0:T(8,128)} %collective-permute-done.15.above_a, f32[2,2,256,128]{3,2,1,0:T(8,128)} %collective-permute-done.12.above_b), custom_call_target="tpu_custom_call" | custom-call | tf_op jit(solution)/shard_map/last_object/pallas_call | solution.py:361
  199.4 4.0 %all-to-all-done.3 = f32[128,8,128]{2,1,0:T(8,128)} async-done(((f32[128,8,128]{2,1,0:T(8,128)}), f32[128,8,128]{2,1,0:T(8,128)}, u32[]{:S(2)}, u32[]{:S(2)}) %all-to-all-start.3) | async-done | bytes 524320 | tf_op jit(solution)/shard_map/all_to_all | solution.py:350
  203.4 1.9 last_probe.1
  (31 shorter events, 0.1 us)
Async XLA Ops:
  0.6 21.2 %copy-start.10 = (s32[2,1]{0,1:T(1,128)S(1)}, s32[2,1]{0,1:T(1,128)}, u32[]{:S(2)}) copy-start(s32[2,1]{0,1:T(1,128)} %param.14) | copy-start | bytes 28
  1.7 15.3 %collective-permute-start = (f32[2,256,256]{2,1,0:T(8,128)S(1)}, f32[2,256,256]{2,1,0:T(8,128)S(1)}, u32[]{:S(2)}, u32[]{:S(2)}) collective-permute-start(f32[2,256,256]{2,1,0:T(8,128)S(1)} %slice.33), channel_id=1, source_target_pairs={{1,0},{2,1},{3,2},{5,4},{6,5},{7,6},{9,8},{10,9},{11,10},{13,12},{... | collective-permute-start | bytes 1572872 | tf_op jit(solution)/shard_map/ppermute | solution.py:22
  4.3 26.6 %copy-start.3 = (s32[2,12]{1,0:T(2,128)S(1)}, s32[2,12]{1,0:T(2,128)}, u32[]{:S(2)}) copy-start(s32[2,12]{1,0:T(2,128)} %batch.3) | copy-start | bytes 292
  4.3 26.5 %copy-start.4 = (s32[32]{0:T(128)S(1)}, s32[32]{0:T(128)}, u32[]{:S(2)}) copy-start(s32[32]{0:T(128)} %rows.3) | copy-start | bytes 388
  4.4 26.5 %copy-start.5 = (s32[32]{0:T(128)S(1)}, s32[32]{0:T(128)}, u32[]{:S(2)}) copy-start(s32[32]{0:T(128)} %cols.3) | copy-start | bytes 388
  4.4 25.5 %collective-permute-start.2 = (f32[2,512,256]{2,1,0:T(8,128)S(1)}, f32[2,512,256]{2,1,0:T(8,128)S(1)}, u32[]{:S(2)}, u32[]{:S(2)}) collective-permute-start(f32[2,512,256]{2,1,0:T(8,128)S(1)} %slice.35), channel_id=1, source_target_pairs={{4,0},{8,4},{12,8},{16,12},{20,16},{24,20},{28,24},{32,28},{36,32}... | collective-permute-start | bytes 3145736 | tf_op jit(solution)/shard_map/ppermute | solution.py:22
  9.7 18.6 %collective-permute-start.1 = (f32[2,256,256]{2,1,0:T(8,128)}, f32[2,256,256]{2,1,0:T(8,128)}, u32[]{:S(2)}, u32[]{:S(2)}) collective-permute-start(f32[2,256,256]{2,1,0:T(8,128)} %slice.34), channel_id=1, source_target_pairs={{1,0},{2,1},{3,2},{5,4},{6,5},{7,6},{9,8},{10,9},{11,10},{13,12},{... | collective-permute-start | bytes 1572872 | tf_op jit(solution)/shard_map/ppermute | solution.py:22
  17.0 12.9 %copy-start.9 = (f32[2,256,256]{2,1,0:T(8,128)}, f32[2,256,256]{2,1,0:T(8,128)S(1)}, u32[]{:S(2)}) copy-start(f32[2,256,256]{2,1,0:T(8,128)S(1)} %collective-permute-done.below_a) | copy-start | bytes 1572868
  17.0 12.9 %collective-permute-start.3 = (f32[2,256,256]{2,1,0:T(8,128)S(1)}, f32[2,256,256]{2,1,0:T(8,128)}, u32[]{:S(2)}, u32[]{:S(2)}) collective-permute-start(f32[2,256,256]{2,1,0:T(8,128)S(1)} %collective-permute-done.below_a), channel_id=1, source_target_pairs={{4,0},{8,4},{12,8},{16,12},{20,16},{24,20},{28,24},{32,28},{36,32}... | collective-permute-start | bytes 1572872 | tf_op jit(solution)/shard_map/ppermute | solution.py:22
  29.9 1.0 copy-start.8
  46.4 37.0 %collective-permute-start.4 = (f32[2,2,2,256,128]{4,3,2,1,0:T(8,128)}, f32[2,2,2,256,128]{4,3,2,1,0:T(8,128)S(1)}, u32[]{:S(2)}, u32[]{:S(2)}) collective-permute-start(f32[2,2,2,256,128]{4,3,2,1,0:T(8,128)} %get-tuple-element.35), channel_id=1, source_target_pairs={{0,4},{4,8},{8,12},{12,16},{16,20},{20,24},{24,28},{28,32},{32,36}... | collective-permute-start | bytes 3145736 | tf_op jit(solution)/shard_map/ppermute | solution.py:22
  48.3 35.1 %collective-permute-start.5 = (f32[2,2,2,256,128]{4,3,2,1,0:T(8,128)}, f32[2,2,2,256,128]{4,3,2,1,0:T(8,128)}, u32[]{:S(2)}, u32[]{:S(2)}) collective-permute-start(f32[2,2,2,256,128]{4,3,2,1,0:T(8,128)} %get-tuple-element.36), channel_id=1, source_target_pairs={{4,0},{8,4},{12,8},{16,12},{20,16},{24,20},{28,24},{32,28},{36,32}... | collective-permute-start | bytes 3145736 | tf_op jit(solution)/shard_map/ppermute | solution.py:22
  50.8 32.6 %all-to-all-start = ((f32[128,8,128]{2,1,0:T(8,128)}), f32[128,8,128]{2,1,0:T(8,128)S(1)}, u32[]{:S(2)}, u32[]{:S(2)}) async-start(f32[128,8,128]{2,1,0:T(8,128)} %bitcast.4), calls=%async_computation | async-start | bytes 1048576 | tf_op jit(solution)/shard_map/all_to_all | solution.py:350
  68.6 23.8 %collective-permute-start.6 = (f32[2,2,256,128]{3,2,1,0:T(8,128)}, f32[2,2,256,128]{3,2,1,0:T(8,128)S(1)}, u32[]{:S(2)}, u32[]{:S(2)}) collective-permute-start(f32[2,2,256,128]{3,2,1,0:T(8,128)} %get-tuple-element.38), channel_id=1, source_target_pairs={{0,1},{1,2},{2,3},{4,5},{5,6},{6,7},{8,9},{9,10},{10,11},{12,13},{... | collective-permute-start | bytes 1572872 | tf_op jit(solution)/shard_map/ppermute | solution.py:22
  71.9 20.5 %collective-permute-start.7 = (f32[2,2,256,128]{3,2,1,0:T(8,128)}, f32[2,2,256,128]{3,2,1,0:T(8,128)}, u32[]{:S(2)}, u32[]{:S(2)}) collective-permute-start(f32[2,2,256,128]{3,2,1,0:T(8,128)} %get-tuple-element.39), channel_id=1, source_target_pairs={{1,0},{2,1},{3,2},{5,4},{6,5},{7,6},{9,8},{10,9},{11,10},{13,12},{... | collective-permute-start | bytes 1572872 | tf_op jit(solution)/shard_map/ppermute | solution.py:22
  83.4 2.6 %copy-start.7 = (f32[128,8,128]{2,1,0:T(8,128)}, f32[128,8,128]{2,1,0:T(8,128)S(1)}, u32[]{:S(2)}) copy-start(f32[128,8,128]{2,1,0:T(8,128)S(1)} %all-to-all-done.received) | copy-start | bytes 1572868
  83.4 2.6 %copy-start.6 = (f32[2,2,2,256,128]{4,3,2,1,0:T(8,128)}, f32[2,2,2,256,128]{4,3,2,1,0:T(8,128)S(1)}, u32[]{:S(2)}) copy-start(f32[2,2,2,256,128]{4,3,2,1,0:T(8,128)S(1)} %collective-permute-done.4.from_left_c) | copy-start | bytes 3145732
  87.1 37.6 %collective-permute-start.8 = (f32[2,2,2,256,128]{4,3,2,1,0:T(8,128)}, f32[2,2,2,256,128]{4,3,2,1,0:T(8,128)}, u32[]{:S(2)}, u32[]{:S(2)}) collective-permute-start(f32[2,2,2,256,128]{4,3,2,1,0:T(8,128)} %pad_maximum_fusion), channel_id=1, source_target_pairs={{0,1},{1,2},{2,3},{4,5},{5,6},{6,7},{8,9},{9,10},{10,11},{12,13},{... | collective-permute-start | bytes 3145736 | tf_op jit(solution)/shard_map/ppermute | solution.py:22
  90.0 34.7 %copy-start = (f32[2,256,2,128]{3,1,2,0:T(8,128)S(1)}, f32[2,256,2,128]{3,1,2,0:T(8,128)}, u32[]{:S(2)}) copy-start(f32[2,256,2,128]{3,1,2,0:T(8,128)} %copy.13) | copy-start | bytes 1572868
  91.1 33.6 %collective-permute-start.9 = (f32[2,2,2,256,128]{4,3,2,1,0:T(8,128)}, f32[2,2,2,256,128]{4,3,2,1,0:T(8,128)}, u32[]{:S(2)}, u32[]{:S(2)}) collective-permute-start(f32[2,2,2,256,128]{4,3,2,1,0:T(8,128)} %pad_maximum_fusion.1), channel_id=1, source_target_pairs={{1,0},{2,1},{3,2},{5,4},{6,5},{7,6},{9,8},{10,9},{11,10},{13,12},{... | collective-permute-start | bytes 3145736 | tf_op jit(solution)/shard_map/ppermute | solution.py:22
  94.4 30.3 %collective-permute-start.10 = (f32[2,2,256,128]{3,2,1,0:T(8,128)}, f32[2,2,256,128]{3,2,1,0:T(8,128)S(1)}, u32[]{:S(2)}, u32[]{:S(2)}) collective-permute-start(f32[2,2,256,128]{3,2,1,0:T(8,128)} %get-tuple-element.47), channel_id=1, source_target_pairs={{0,4},{4,8},{8,12},{12,16},{16,20},{20,24},{24,28},{28,32},{32,36}... | collective-permute-start | bytes 1572872 | tf_op jit(solution)/shard_map/ppermute | solution.py:22
  98.0 26.6 %collective-permute-start.11 = (f32[2,2,256,128]{3,2,1,0:T(8,128)S(1)}, f32[2,2,256,128]{3,2,1,0:T(8,128)S(1)}, u32[]{:S(2)}, u32[]{:S(2)}) collective-permute-start(f32[2,2,256,128]{3,2,1,0:T(8,128)S(1)} %get-tuple-element.48), channel_id=1, source_target_pairs={{4,0},{8,4},{12,8},{16,12},{20,16},{24,20},{28,24},{32,28},{36,32}... | collective-permute-start | bytes 1572872 | tf_op jit(solution)/shard_map/ppermute | solution.py:22
  100.0 24.6 %all-to-all-start.1 = ((f32[128,8,128]{2,1,0:T(8,128)}), f32[128,8,128]{2,1,0:T(8,128)S(1)}, u32[]{:S(2)}, u32[]{:S(2)}) async-start(f32[128,8,128]{2,1,0:T(8,128)} %sum_shares.2), calls=%async_computation.1 | async-start | bytes 1048576 | tf_op jit(solution)/shard_map/all_to_all | solution.py:350
  141.2 0.8 copy-start.2
  142.0 20.6 %collective-permute-start.13 = (f32[2,2,256,128]{3,2,1,0:T(8,128)}, f32[2,2,256,128]{3,2,1,0:T(8,128)}, u32[]{:S(2)}, u32[]{:S(2)}) collective-permute-start(f32[2,2,256,128]{3,2,1,0:T(8,128)} %get-tuple-element.55), channel_id=1, source_target_pairs={{0,4},{4,8},{8,12},{12,16},{16,20},{20,24},{24,28},{28,32},{32,36}... | collective-permute-start | bytes 1572872 | tf_op jit(solution)/shard_map/ppermute | solution.py:22
  144.0 32.1 %collective-permute-start.12 = (f32[2,2,256,128]{3,2,1,0:T(8,128)}, f32[2,2,256,128]{3,2,1,0:T(8,128)}, u32[]{:S(2)}, u32[]{:S(2)}) collective-permute-start(f32[2,2,256,128]{3,2,1,0:T(8,128)} %get-tuple-element.53), channel_id=1, source_target_pairs={{0,1},{1,2},{2,3},{4,5},{5,6},{6,7},{8,9},{9,10},{10,11},{12,13},{... | collective-permute-start | bytes 1572872 | tf_op jit(solution)/shard_map/ppermute | solution.py:22
  154.8 21.2 %all-to-all-start.2 = ((f32[128,8,128]{2,1,0:T(8,128)}), f32[128,8,128]{2,1,0:T(8,128)}, u32[]{:S(2)}, u32[]{:S(2)}) async-start(f32[128,8,128]{2,1,0:T(8,128)} %bitcast.6), calls=%async_computation.2 | async-start | bytes 1048576 | tf_op jit(solution)/shard_map/all_to_all | solution.py:350
  162.6 33.6 %copy-start.1 = (f32[2,4,512,128]{3,2,1,0:T(8,128)S(1)}, f32[2,4,512,128]{3,2,1,0:T(8,128)}, u32[]{:S(2)}) copy-start(f32[2,4,512,128]{3,2,1,0:T(8,128)} %get-tuple-element.51.own) | copy-start | bytes 6291460
  178.0 18.2 %collective-permute-start.14 = (f32[2,2,512,128]{3,2,1,0:T(8,128)}, f32[2,2,512,128]{3,2,1,0:T(8,128)}, u32[]{:S(2)}, u32[]{:S(2)}) collective-permute-start(f32[2,2,512,128]{3,2,1,0:T(8,128)} %get-tuple-element.58), channel_id=1, source_target_pairs={{0,4},{4,8},{8,12},{12,16},{16,20},{20,24},{24,28},{28,32},{32,36}... | collective-permute-start | bytes 3145736 | tf_op jit(solution)/shard_map/ppermute | solution.py:22
  181.3 14.9 %collective-permute-start.15 = (f32[2,2,256,128]{3,2,1,0:T(8,128)}, f32[2,2,256,128]{3,2,1,0:T(8,128)}, u32[]{:S(2)}, u32[]{:S(2)}) collective-permute-start(f32[2,2,256,128]{3,2,1,0:T(8,128)} %add.23), channel_id=1, source_target_pairs={{0,1},{1,2},{2,3},{4,5},{5,6},{6,7},{8,9},{9,10},{10,11},{12,13},{... | collective-permute-start | bytes 1572872 | tf_op jit(solution)/shard_map/ppermute | solution.py:22
  183.8 19.6 %all-to-all-start.3 = ((f32[128,8,128]{2,1,0:T(8,128)}), f32[128,8,128]{2,1,0:T(8,128)}, u32[]{:S(2)}, u32[]{:S(2)}) async-start(f32[128,8,128]{2,1,0:T(8,128)} %sum_shares.3), calls=%async_computation.3 | async-start | bytes 1048576 | tf_op jit(solution)/shard_map/all_to_all | solution.py:350

commit v6 on v4

--- a/solution.py
+++ b/solution.py
@@ -170,7 +170,7 @@
 
 def first_kernel(dims, batch, live, rows, cols, probe, intensity, tables_in,
                  field, below_a, below_b, beside, corner,
-                 part_out, gprobe_out, right_c, left_c, right_b, left_b, down_b, up_b,
+                 old, middle, gprobe_out, right_c, left_c, right_b, left_b, down_b, up_b,
                  ext, grad, mats, measured, exit_0, exit_1, wave_0, wave_1, patch_0, patch_1,
                  gprobe, sems, moves):
     side, nrows, ncols = dims
@@ -185,6 +185,8 @@
     clear(grad, gprobe, waves, patches)
     for copy in copies:
         copy.wait()
+    keeping = pltpu.make_async_copy(ext, old, moves.at[len(pairs) + 1])
+    keeping.start()
     slot_loop(0, side, batch, live, rows, cols, mats, probe, ext, grad, gprobe,
               measured, (exit_0, exit_1), waves, patches)
     t = side // LANES
@@ -203,9 +205,57 @@
         (grad.at[:, mid, c_rows, :], down_b),
         (grad.at[:, mid, a_rows, :], up_b),
     ]
+    pairs.append((grad.at[:, mid, b_rows, :], middle))
     copies = run_copies(pairs, moves)
-    copies += update_out(ext, grad, part_out, moves, len(pairs))
-    for copy in copies:
+    keeping.wait()
+    for copy in copies:
+        copy.wait()
+
+
+def update_kernel(dims, edge, old, middle, left_c, right_c, left_b, right_b, down_b, up_b,
+                  from_left_c, from_right_c, from_up, from_down,
+                  part, ext, grad, lc_in, rc_in, u_in, d_in, moves):
+    side, nrows, ncols = dims
+    t = side // LANES
+    last = ncols // LANES
+    a_rows, c_rows = pl.ds(0, side), pl.ds(nrows, side)
+    b_rows = pl.ds(side, nrows - side)
+    left, mid, right = pl.ds(0, t), pl.ds(t, last - t), pl.ds(last, t)
+    copies = run_copies([
+        (old, ext), (from_left_c, lc_in), (from_right_c, rc_in), (from_up, u_in),
+        (from_down, d_in),
+        (right_c.at[0], grad.at[:, right, a_rows, :]),
+        (right_c.at[1], grad.at[:, right, c_rows, :]),
+        (left_c.at[0], grad.at[:, left, a_rows, :]),
+        (left_c.at[1], grad.at[:, left, c_rows, :]),
+        (right_b, grad.at[:, right, b_rows, :]),
+        (left_b, grad.at[:, left, b_rows, :]),
+        (down_b, grad.at[:, mid, c_rows, :]),
+        (up_b, grad.at[:, mid, a_rows, :]),
+        (middle, grad.at[:, mid, b_rows, :]),
+    ], moves)
+    for copy in copies:
+        copy.wait()
+    received = {
+        (0, 0): lc_in[0], (0, 2): lc_in[1], (1, 0): u_in[...], (1, 2): d_in[...],
+        (2, 0): rc_in[0], (2, 2): rc_in[1],
+    }
+    for i, tiles in enumerate((slice(0, t), slice(t, last), slice(last, last + t))):
+        for k, band in enumerate((slice(0, side), slice(side, nrows), slice(nrows, nrows + side))):
+            step = grad[:, tiles, band, :]
+            if (i, k) in received:
+                step = step + received[i, k]
+            ext[:, tiles, band, :] = ext[:, tiles, band, :] - 0.25 * step
+
+    @pl.when(edge[0] == 1)
+    def _():
+        ext[:, :, nrows:, :] = jnp.zeros((2, last + t, side, LANES), F32)
+
+    @pl.when(edge[1] == 1)
+    def _():
+        ext[:, last:, :, :] = jnp.zeros((2, t, nrows + side, LANES), F32)
+
+    for copy in run_copies([(ext, part)], moves):
         copy.wait()
 
 
@@ -218,8 +268,7 @@
 
 
 def second_kernel(dims, rate, batch, live, rows, cols, edge, probe, summed,
-                  intensity, tables_in, part_in, from_left_c, from_right_c, from_up_c, from_down_c,
-                  from_left, from_right, from_up, from_down,
+                  intensity, tables_in, part_in, from_up_c, from_down_c, from_left, from_right,
                   own_out, gprobe_out, right_c, right_ab, down_a, down_b,
                   ext, grad, mats, measured, exit_0, exit_1, wave_0, wave_1, patch_0, patch_1,
                   gprobe, now, sems, moves):
@@ -235,22 +284,16 @@
         copy.wait()
     a_rows, c_rows = slice(0, side), slice(nrows, nrows + side)
     b_rows = slice(side, nrows)
-    left, mid, right = slice(0, t), slice(t, last), slice(last, last + t)
-    for rows_of, corner, strip, k in ((a_rows, from_up_c, from_up, 0),
-                                      (c_rows, from_down_c, from_down, 1)):
-        ext[:, left, rows_of, :] -= 0.25 * (corner[0] + from_left_c[k])
-        ext[:, mid, rows_of, :] -= 0.25 * strip[...]
-        ext[:, right, rows_of, :] -= 0.25 * (corner[1] + from_right_c[k])
+    left, right = slice(0, t), slice(last, last + t)
+    for rows_of, corner in ((a_rows, from_up_c), (c_rows, from_down_c)):
+        ext[:, left, rows_of, :] -= 0.25 * corner[0]
     ext[:, left, b_rows, :] -= 0.25 * from_left[...]
-    ext[:, right, b_rows, :] -= 0.25 * from_right[...]
-
-    @pl.when(edge[0] == 1)
+
+    @pl.when(edge[1] == 0)
     def _():
-        ext[:, :, c_rows, :] = jnp.zeros((2, last + t, side, LANES), F32)
-
-    @pl.when(edge[1] == 1)
-    def _():
-        ext[:, right, :, :] = jnp.zeros((2, t, nrows + side, LANES), F32)
+        for rows_of, corner in ((a_rows, from_up_c), (c_rows, from_down_c)):
+            ext[:, right, rows_of, :] -= 0.25 * corner[1]
+        ext[:, right, b_rows, :] -= 0.25 * from_right[...]
 
     slot_loop(1, side, batch, live, rows, cols, mats, now, ext, grad, gprobe,
               measured, (exit_0, exit_1), waves, patches)
@@ -329,7 +372,23 @@
 def add_up(mine):
     return pl.pallas_call(
         share_kernel, out_shape=jax.ShapeDtypeStruct(mine.shape, F32), name="sum_shares",
+        compiler_params=pltpu.CompilerParams(vmem_limit_bytes=4 * MIB),
     )(mine)
+
+
+def update(dims, edge, plain):
+    hbm = pl.BlockSpec(memory_space=pltpu.HBM)
+    scratch = [plain[0], plain[0]] + list(plain[8:])
+    return pl.pallas_call(
+        functools.partial(update_kernel, dims),
+        out_shape=jax.ShapeDtypeStruct(plain[0].shape, F32),
+        in_specs=[pl.BlockSpec(memory_space=pltpu.SMEM)] + [hbm] * len(plain),
+        out_specs=hbm,
+        scratch_shapes=[pltpu.VMEM(array.shape, F32) for array in scratch]
+        + [pltpu.SemaphoreType.DMA((16,))],
+        compiler_params=pltpu.CompilerParams(vmem_limit_bytes=56 * MIB),
+        name="update_object",
+    )(edge, *plain)
 
 
 def simple(kernel, shape, name, limit, vectors):
@@ -370,11 +429,12 @@
     corners = (2, 2, t, side, LANES)
     strip = (2, ncols // LANES - t, side, LANES)
     side_b = (2, t, nrows - side, LANES)
-    part, gprobe, right_c, left_c, right_b, left_b, down_b, up_b = call(
+    middle_b = (2, ncols // LANES - t, nrows - side, LANES)
+    old, middle, gprobe, right_c, left_c, right_b, left_b, down_b, up_b = call(
         functools.partial(first_kernel, dims), dims, slots, scalars, (current,),
-        (intensity, both, object_field), (below_a, below_b, beside, corner),
-        [big, current.shape, corners, corners, side_b, side_b, strip, strip], [],
-        52, "first_iteration")
+        (intensity, both, object_field, below_a, below_b, beside, corner), (),
+        [big, middle_b, current.shape, corners, corners, side_b, side_b, strip, strip], [],
+        54, "first_iteration")
 
     from_left_c = passed_along(right_c, "tile", 1)
     from_right_c = passed_along(left_c, "tile", -1)
@@ -392,15 +452,16 @@
     from_left_b = passed_along(right_b, "tile", 1)
     from_right_b = passed_along(left_b, "tile", -1)
     sum_one = swap(given).reshape(current.shape)
+    part = update(dims, edge, (old, middle, left_c, right_c, left_b, right_b, down_b, up_b,
+                               from_left_c, from_right_c, from_up_b, from_down_b))
 
     own, gprobe, right_c, right_ab, down_a, down_b = call(
         functools.partial(second_kernel, dims, probe_rate), dims, slots, scalars + (edge,),
         (current, sum_one), (intensity, both, part),
-        (from_left_c, from_right_c, from_up_c, from_down_c,
-         from_left_b, from_right_b, from_up_b, from_down_b),
+        (from_up_c, from_down_c, from_left_b, from_right_b),
         [(2, ncols // LANES, nrows, LANES), current.shape, (2, t, side, LANES),
          (2, t, nrows, LANES), (2, t, side, LANES), strip],
-        [current.shape], 49, "second_iteration")
+        [current.shape], 52, "second_iteration")
 
     from_left_c = passed_along(right_c, "tile", 1)
     above_b = passed_along(down_b, "row", 1)

time: 205 us -> 207 us (level)
  waiting for transfers between devices: 56.9 us -> 54 us
  Pallas kernels: 36.4 us -> 39 us
    pallas_call x0 -> x1, Pallas kernels: none -> 8.24 us  [update(): pl.pallas_call(functools.partial(update_kernel, dims), out_shape=jax.Shap...]
    all_to_all x4, waiting for transfers between devices: 38.9 us -> 32.5 us  [swap(): return lax.all_to_all(shares, ('tile', 'row'), 0, 0, tiled=True)]
    ppermute x16, starting transfers between devices: 49.5 us -> 55.8 us  [passed_along(): lax.ppermute(value, axis, [(source, source + steps) for source in range(f...]
    all_to_all x4, starting transfers between devices: 45.4 us -> 40.8 us  [swap(): return lax.all_to_all(shares, ('tile', 'row'), 0, 0, tiled=True)]
    pallas_call x2, Pallas kernels: 27.3 us -> 23.5 us  [call(): pl.pallas_call(kernel, out_shape=[jax.ShapeDtypeStruct(shape, F32) for sh...]
    ppermute x16, waiting for transfers between devices: 18 us -> 21.5 us  [passed_along(): lax.ppermute(value, axis, [(source, source + steps) for source in range(f...]
    unnamed x24 -> x36, local copies, waits for them, and re-layouts: 3.13 us -> 4.77 us
  transfers between devices with their start and end apart: 20 -> 20, of which waited for: 8 -> 7; matrix products, arithmetic and copies ran while one was open for 6% -> 5% of each run, Pallas kernels for 3% -> 6%
where the time goes in v6:
time: 207 us
  starting transfers between devices  96.6 us (47%)
  waiting for transfers between devices  54 us (26%)
  Pallas kernels  39 us (19%)
  local copies, waits for them, and re-layouts  10 us (5%)
  other arithmetic  6.19 us (3%)
    ppermute x16, starting transfers between devices, passed_along(): lax.ppermute(value, axis, [(source, source + steps) for source in range(f...  55.8 us
    all_to_all x4, starting transfers between devices, swap(): return lax.all_to_all(shares, ('tile', 'row'), 0, 0, tiled=True)  40.8 us
    all_to_all x4, waiting for transfers between devices, swap(): return lax.all_to_all(shares, ('tile', 'row'), 0, 0, tiled=True)  32.5 us
    pallas_call x2, Pallas kernels, call(): pl.pallas_call(kernel, out_shape=[jax.ShapeDtypeStruct(shape, F32) for sh...  23.5 us
    ppermute x16, waiting for transfers between devices, passed_along(): lax.ppermute(value, axis, [(source, source + steps) for source in range(f...  21.5 us
    pallas_call x1, Pallas kernels, update(): pl.pallas_call(functools.partial(update_kernel, dims), out_shape=jax.Shap...  8.24 us
    pallas_call x2, Pallas kernels, simple(): pl.pallas_call(kernel, out_shape=jax.ShapeDtypeStruct(shape, F32), in_spe...  5.07 us
    unnamed x36, local copies, waits for them, and re-layouts  4.77 us
  transfers between devices with their start and end apart: 20, of which 7 were waited for; matrix products, arithmetic and copies ran while one was open for 5% of the time, Pallas kernels for 6%

profile of v6, /device:TPU:1, one launch (start us, length us, event | category | flops | bytes accessed | tf_op | source)
XLA Modules:
  0.0 206.9 jit_solution(13122637259622523026)
XLA Ops:
  0.6 1.1 slice.33
  1.7 1.3 slice.35
  3.0 3.3 %collective-permute-start.2 = (f32[2,512,256]{2,1,0:T(8,128)S(1)}, f32[2,512,256]{2,1,0:T(8,128)S(1)}, u32[]{:S(2)}, u32[]{:S(2)}) collective-permute-start(f32[2,512,256]{2,1,0:T(8,128)S(1)} %slice.35), channel_id=1, source_target_pairs={{4,0},{8,4},{12,8},{16,12},{20,16},{24,20},{28,24},{32,28},{36,32}... | collective-permute-start | bytes 3145736 | tf_op jit(solution)/shard_map/ppermute | solution.py:22
  6.4 1.3 collective-permute-start
  7.7 1.9 slice.34
  9.6 1.3 collective-permute-start.1
  10.8 11.5 %collective-permute-done.below_a = f32[2,256,256]{2,1,0:T(8,128)S(1)} collective-permute-done((f32[2,256,256]{2,1,0:T(8,128)S(1)}, f32[2,256,256]{2,1,0:T(8,128)S(1)}, u32[]{:S(2)}, u32[]{:S(2)}) %collective-permute-start) | collective-permute-done | bytes 524320 | tf_op jit(solution)/shard_map/ppermute | solution.py:22
  22.3 1.9 collective-permute-start.3
  24.2 0.6 copy.15.live
  24.8 1.2 copy.12
  26.1 1.0 copy.13
  27.1 6.1 %collective-permute-done.1.below_b = f32[2,256,256]{2,1,0:T(8,128)} collective-permute-done((f32[2,256,256]{2,1,0:T(8,128)}, f32[2,256,256]{2,1,0:T(8,128)}, u32[]{:S(2)}, u32[]{:S(2)}) %collective-permute-start.1) | collective-permute-done | bytes 524320 | tf_op jit(solution)/shard_map/ppermute | solution.py:22
  33.3 1.0 copy-done.13
  34.2 12.2 %first_iteration.1 = (f32[2,6,768,128]{3,2,1,0:T(8,128)}, f32[2,2,256,128]{3,2,1,0:T(8,128)}, f32[2,2,256,128]{3,2,1,0:T(8,128)}, f32[2,2,2,256,128]{4,3,2,1,0:T...) custom-call(s32[2,12]{1,0:T(2,128)} %batch.3, ...), custom_call_target="tpu_custom_call" | custom-call | tf_op jit(solution)/shard_map/first_iteration/pallas_call | solution.py:346
  46.4 1.9 collective-permute-start.4
  48.4 6.1 %collective-permute-start.5 = (f32[2,2,2,256,128]{4,3,2,1,0:T(8,128)}, f32[2,2,2,256,128]{4,3,2,1,0:T(8,128)S(1)}, u32[]{:S(2)}, u32[]{:S(2)}) collective-permute-start(f32[2,2,2,256,128]{4,3,2,1,0:T(8,128)} %get-tuple-element.37.left_c), channel_id=1, source_target_pairs={{4,0},{8,4},{12,8},{16,12},{20,16},{24,20},{28,24},{32,28},{36,32}... | collective-permute-start | bytes 3145736 | tf_op jit(solution)/shard_map/ppermute | solution.py:22
  54.5 17.2 %all-to-all-start = ((f32[128,8,128]{2,1,0:T(8,128)}), f32[128,8,128]{2,1,0:T(8,128)S(1)}, u32[]{:S(2)}, u32[]{:S(2)}) async-start(f32[128,8,128]{2,1,0:T(8,128)} %bitcast.14), calls=%async_computation | async-start | bytes 1048576 | tf_op jit(solution)/shard_map/all_to_all | solution.py:369
  71.7 4.1 %collective-permute-start.6 = (f32[2,2,256,128]{3,2,1,0:T(8,128)}, f32[2,2,256,128]{3,2,1,0:T(8,128)}, u32[]{:S(2)}, u32[]{:S(2)}) collective-permute-start(f32[2,2,256,128]{3,2,1,0:T(8,128)} %get-tuple-element.39.down_b), channel_id=1, source_target_pairs={{0,1},{1,2},{2,3},{4,5},{5,6},{6,7},{8,9},{9,10},{10,11},{12,13},{... | collective-permute-start | bytes 1572872 | tf_op jit(solution)/shard_map/ppermute | solution.py:22
  75.8 1.3 collective-permute-start.7
  77.1 8.4 %all-to-all-done.received = f32[128,8,128]{2,1,0:T(8,128)S(1)} async-done(((f32[128,8,128]{2,1,0:T(8,128)}), f32[128,8,128]{2,1,0:T(8,128)S(1)}, u32[]{:S(2)}, u32[]{:S(2)}) %all-to-all-start) | async-done | bytes 524320 | tf_op jit(solution)/shard_map/all_to_all | solution.py:369
  85.5 2.6 %slice_add_fusion = (f32[1,2,2,256,128]{4,3,2,1,0:T(8,128)S(1)}, f32[1,2,2,256,128]{4,3,2,1,0:T(8,128)S(1)}, f32[1,2,2,256,128]{4,3,2,1,0:T(8,128)S(1)}, f32[1,2,2,256,128]{4,3,2,1,0:T(8,128)S(1)}) fusion(f32[2,2,2,256,128]{4,3,2,1,0:T(8,128)S(1)} %collective-permute-done.5.from_right_c, f32[2,2,2,256,128]{4,3,2,1,0:T(8,128)} %get-tuple-element.36.right_c, ...), kind=kLoop, calls=%fused_computation.2 | loop fusion | flops 524288 | bytes 6291456 | tf_op jit(solution)/shard_map/add | solution.py:446
  88.1 1.0 pad_maximum_fusion
  89.1 3.4 %collective-permute-start.8 = (f32[2,2,2,256,128]{4,3,2,1,0:T(8,128)}, f32[2,2,2,256,128]{4,3,2,1,0:T(8,128)}, u32[]{:S(2)}, u32[]{:S(2)}) collective-permute-start(f32[2,2,2,256,128]{4,3,2,1,0:T(8,128)} %pad_maximum_fusion), channel_id=1, source_target_pairs={{0,1},{1,2},{2,3},{4,5},{5,6},{6,7},{8,9},{9,10},{10,11},{12,13},{... | collective-permute-start | bytes 3145736 | tf_op jit(solution)/shard_map/ppermute | solution.py:22
  92.6 1.3 collective-permute-start.9
  93.9 1.0 sum_shares.2
  94.9 4.2 %collective-permute-start.10 = (f32[2,2,256,128]{3,2,1,0:T(8,128)}, f32[2,2,256,128]{3,2,1,0:T(8,128)}, u32[]{:S(2)}, u32[]{:S(2)}) collective-permute-start(f32[2,2,256,128]{3,2,1,0:T(8,128)} %get-tuple-element.50.right_b), channel_id=1, source_target_pairs={{0,4},{4,8},{8,12},{12,16},{16,20},{20,24},{24,28},{28,32},{32,36}... | collective-permute-start | bytes 1572872 | tf_op jit(solution)/shard_map/ppermute | solution.py:22
  99.1 1.9 collective-permute-start.11
  101.1 8.9 %all-to-all-start.1 = ((f32[128,8,128]{2,1,0:T(8,128)}), f32[128,8,128]{2,1,0:T(8,128)S(1)}, u32[]{:S(2)}, u32[]{:S(2)}) async-start(f32[128,8,128]{2,1,0:T(8,128)} %sum_shares.2), calls=%async_computation.1 | async-start | bytes 1048576 | tf_op jit(solution)/shard_map/all_to_all | solution.py:369
  109.9 0.6 add_convert_fusion.edge
  110.6 8.2 %update_object.1.part_in = f32[2,6,768,128]{3,2,1,0:T(8,128)} custom-call(s32[2]{0:T(128)} %add_convert_fusion.edge, f32[2,6,768,128]{3,2,1,0:T(8,128)} %get-tuple-element.47.old, f32[2,2,256,128]{3,2,1,0:T(8,128)} %get-tuple-element.48.middle, f32[2,2,2,256,128]{4,3,2,1,0:T(8,128)} %get-tuple-element.37.left_c, ...), custom_call_target="tpu_custom_call" | custom-call | tf_op jit(solution)/shard_map/update_object/pallas_call | solution.py:382
  118.8 6.3 %all-to-all-done.1 = f32[128,8,128]{2,1,0:T(8,128)S(1)} async-done(((f32[128,8,128]{2,1,0:T(8,128)}), f32[128,8,128]{2,1,0:T(8,128)S(1)}, u32[]{:S(2)}, u32[]{:S(2)}) %all-to-all-start.1) | async-done | bytes 524320 | tf_op jit(solution)/shard_map/all_to_all | solution.py:369
  125.1 0.7 copy-done.1
  125.8 0.4 copy-done.12
  126.2 11.3 %second_iteration.1 = (f32[2,4,512,128]{3,2,1,0:T(8,128)}, f32[2,2,256,128]{3,2,1,0:T(8,128)}, f32[2,2,256,128]{3,2,1,0:T(8,128)S(1)}, f32[2,2,512,128]{3,2,1,0:...) custom-call(s32[2,12]{1,0:T(2,128)S(1)} %copy-done.5, s32[2,1]{1,0:T(2,128)S(1)} %copy-done.6, ...), custom_call_target="tpu_custom_call" | custom-call | tf_op jit(solution)/shard_map/second_iteration/pallas_call | solution.py:346
  137.6 16.0 %collective-permute-start.13 = (f32[2,2,256,128]{3,2,1,0:T(8,128)S(1)}, f32[2,2,256,128]{3,2,1,0:T(8,128)}, u32[]{:S(2)}, u32[]{:S(2)}) collective-permute-start(f32[2,2,256,128]{3,2,1,0:T(8,128)S(1)} %get-tuple-element.57), channel_id=1, source_target_pairs={{0,4},{4,8},{8,12},{12,16},{16,20},{20,24},{24,28},{28,32},{32,36}... | collective-permute-start | bytes 1572872 | tf_op jit(solution)/shard_map/ppermute | solution.py:22
  153.6 2.1 %collective-permute-start.12 = (f32[2,2,256,128]{3,2,1,0:T(8,128)}, f32[2,2,256,128]{3,2,1,0:T(8,128)}, u32[]{:S(2)}, u32[]{:S(2)}) collective-permute-start(f32[2,2,256,128]{3,2,1,0:T(8,128)} %get-tuple-element.55), channel_id=1, source_target_pairs={{0,1},{1,2},{2,3},{4,5},{5,6},{6,7},{8,9},{9,10},{10,11},{12,13},{... | collective-permute-start | bytes 1572872 | tf_op jit(solution)/shard_map/ppermute | solution.py:22
  155.7 7.7 %all-to-all-start.2 = ((f32[128,8,128]{2,1,0:T(8,128)}), f32[128,8,128]{2,1,0:T(8,128)}, u32[]{:S(2)}, u32[]{:S(2)}) async-start(f32[128,8,128]{2,1,0:T(8,128)} %bitcast.6), calls=%async_computation.2 | async-start | bytes 1048576 | tf_op jit(solution)/shard_map/all_to_all | solution.py:369
  163.4 1.9 add.23
  165.3 11.5 %all-to-all-done.2.received = f32[128,8,128]{2,1,0:T(8,128)} async-done(((f32[128,8,128]{2,1,0:T(8,128)}), f32[128,8,128]{2,1,0:T(8,128)}, u32[]{:S(2)}, u32[]{:S(2)}) %all-to-all-start.2) | async-done | bytes 524320 | tf_op jit(solution)/shard_map/all_to_all | solution.py:369
  176.8 1.2 sum_shares.3
  178.0 0.8 copy-done.4
  178.8 3.0 %collective-permute-start.14 = (f32[2,2,512,128]{3,2,1,0:T(8,128)}, f32[2,2,512,128]{3,2,1,0:T(8,128)}, u32[]{:S(2)}, u32[]{:S(2)}) collective-permute-start(f32[2,2,512,128]{3,2,1,0:T(8,128)} %get-tuple-element.60), channel_id=1, source_target_pairs={{0,4},{4,8},{8,12},{12,16},{16,20},{20,24},{24,28},{28,32},{32,36}... | collective-permute-start | bytes 3145736 | tf_op jit(solution)/shard_map/ppermute | solution.py:22
  181.8 2.8 %collective-permute-start.15 = (f32[2,2,256,128]{3,2,1,0:T(8,128)}, f32[2,2,256,128]{3,2,1,0:T(8,128)}, u32[]{:S(2)}, u32[]{:S(2)}) collective-permute-start(f32[2,2,256,128]{3,2,1,0:T(8,128)} %add.23), channel_id=1, source_target_pairs={{0,1},{1,2},{2,3},{4,5},{5,6},{6,7},{8,9},{9,10},{10,11},{12,13},{... | collective-permute-start | bytes 1572872 | tf_op jit(solution)/shard_map/ppermute | solution.py:22
  184.6 7.0 %all-to-all-start.3 = ((f32[128,8,128]{2,1,0:T(8,128)}), f32[128,8,128]{2,1,0:T(8,128)}, u32[]{:S(2)}, u32[]{:S(2)}) async-start(f32[128,8,128]{2,1,0:T(8,128)} %copy-done.4), calls=%async_computation.3 | async-start | bytes 1048576 | tf_op jit(solution)/shard_map/all_to_all | solution.py:369
  191.6 3.9 %collective-permute-done.15.above_a = f32[2,2,256,128]{3,2,1,0:T(8,128)} collective-permute-done((f32[2,2,256,128]{3,2,1,0:T(8,128)}, f32[2,2,256,128]{3,2,1,0:T(8,128)}, u32[]{:S(2)}, u32[]{:S(2)}) %collective-permute-start.15) | collective-permute-done | bytes 524320 | tf_op jit(solution)/shard_map/ppermute | solution.py:22
  195.4 3.2 %last_object.1 = f32[2,512,512]{2,1,0:T(8,128)} custom-call(f32[2,4,512,128]{3,2,1,0:T(8,128)S(1)} %copy-done.3, f32[2,2,512,128]{3,2,1,0:T(8,128)} %collective-permute-done.14.left_ab, f32[2,2,256,128]{3,2,1,0:T(8,128)} %collective-permute-done.15.above_a, f32[2,2,256,128]{3,2,1,0:T(8,128)} %collective-permute-done.12.above_b), custom_call_target="tpu_custom_call" | custom-call | tf_op jit(solution)/shard_map/last_object/pallas_call | solution.py:396
  198.6 6.4 %all-to-all-done.3 = f32[128,8,128]{2,1,0:T(8,128)} async-done(((f32[128,8,128]{2,1,0:T(8,128)}), f32[128,8,128]{2,1,0:T(8,128)}, u32[]{:S(2)}, u32[]{:S(2)}) %all-to-all-start.3) | async-done | bytes 524320 | tf_op jit(solution)/shard_map/all_to_all | solution.py:369
  205.0 1.9 last_probe.1
  (44 shorter events, 0.2 us)
Async XLA Ops:
  0.6 23.6 %copy-start.16 = (s32[2,1]{0,1:T(1,128)S(1)}, s32[2,1]{0,1:T(1,128)}, u32[]{:S(2)}) copy-start(s32[2,1]{0,1:T(1,128)} %param.14) | copy-start | bytes 28
  3.0 30.2 %collective-permute-start.2 = (f32[2,512,256]{2,1,0:T(8,128)S(1)}, f32[2,512,256]{2,1,0:T(8,128)S(1)}, u32[]{:S(2)}, u32[]{:S(2)}) collective-permute-start(f32[2,512,256]{2,1,0:T(8,128)S(1)} %slice.35), channel_id=1, source_target_pairs={{4,0},{8,4},{12,8},{16,12},{20,16},{24,20},{28,24},{32,28},{36,32}... | collective-permute-start | bytes 3145736 | tf_op jit(solution)/shard_map/ppermute | solution.py:22
  6.4 15.9 %collective-permute-start = (f32[2,256,256]{2,1,0:T(8,128)S(1)}, f32[2,256,256]{2,1,0:T(8,128)S(1)}, u32[]{:S(2)}, u32[]{:S(2)}) collective-permute-start(f32[2,256,256]{2,1,0:T(8,128)S(1)} %slice.33), channel_id=1, source_target_pairs={{1,0},{2,1},{3,2},{5,4},{6,5},{7,6},{9,8},{10,9},{11,10},{13,12},{... | collective-permute-start | bytes 1572872 | tf_op jit(solution)/shard_map/ppermute | solution.py:22
  9.6 23.7 %collective-permute-start.1 = (f32[2,256,256]{2,1,0:T(8,128)}, f32[2,256,256]{2,1,0:T(8,128)}, u32[]{:S(2)}, u32[]{:S(2)}) collective-permute-start(f32[2,256,256]{2,1,0:T(8,128)} %slice.34), channel_id=1, source_target_pairs={{1,0},{2,1},{3,2},{5,4},{6,5},{7,6},{9,8},{10,9},{11,10},{13,12},{... | collective-permute-start | bytes 1572872 | tf_op jit(solution)/shard_map/ppermute | solution.py:22
  22.3 10.9 %copy-start.15 = (f32[2,256,256]{2,1,0:T(8,128)}, f32[2,256,256]{2,1,0:T(8,128)S(1)}, u32[]{:S(2)}) copy-start(f32[2,256,256]{2,1,0:T(8,128)S(1)} %collective-permute-done.below_a) | copy-start | bytes 1572868
  22.3 10.9 %collective-permute-start.3 = (f32[2,256,256]{2,1,0:T(8,128)S(1)}, f32[2,256,256]{2,1,0:T(8,128)}, u32[]{:S(2)}, u32[]{:S(2)}) collective-permute-start(f32[2,256,256]{2,1,0:T(8,128)S(1)} %collective-permute-done.below_a), channel_id=1, source_target_pairs={{4,0},{8,4},{12,8},{16,12},{20,16},{24,20},{28,24},{32,28},{36,32}... | collective-permute-start | bytes 1572872 | tf_op jit(solution)/shard_map/ppermute | solution.py:22
  33.2 1.0 copy-start.13
  46.4 39.0 %collective-permute-start.4 = (f32[2,2,2,256,128]{4,3,2,1,0:T(8,128)}, f32[2,2,2,256,128]{4,3,2,1,0:T(8,128)S(1)}, u32[]{:S(2)}, u32[]{:S(2)}) collective-permute-start(f32[2,2,2,256,128]{4,3,2,1,0:T(8,128)} %get-tuple-element.36.right_c), channel_id=1, source_target_pairs={{0,4},{4,8},{8,12},{12,16},{16,20},{20,24},{24,28},{28,32},{32,36}... | collective-permute-start | bytes 3145736 | tf_op jit(solution)/shard_map/ppermute | solution.py:22
  48.4 37.1 %collective-permute-start.5 = (f32[2,2,2,256,128]{4,3,2,1,0:T(8,128)}, f32[2,2,2,256,128]{4,3,2,1,0:T(8,128)S(1)}, u32[]{:S(2)}, u32[]{:S(2)}) collective-permute-start(f32[2,2,2,256,128]{4,3,2,1,0:T(8,128)} %get-tuple-element.37.left_c), channel_id=1, source_target_pairs={{4,0},{8,4},{12,8},{16,12},{20,16},{24,20},{28,24},{32,28},{36,32}... | collective-permute-start | bytes 3145736 | tf_op jit(solution)/shard_map/ppermute | solution.py:22
  54.5 31.0 %all-to-all-start = ((f32[128,8,128]{2,1,0:T(8,128)}), f32[128,8,128]{2,1,0:T(8,128)S(1)}, u32[]{:S(2)}, u32[]{:S(2)}) async-start(f32[128,8,128]{2,1,0:T(8,128)} %bitcast.14), calls=%async_computation | async-start | bytes 1048576 | tf_op jit(solution)/shard_map/all_to_all | solution.py:369
  71.7 22.2 %collective-permute-start.6 = (f32[2,2,256,128]{3,2,1,0:T(8,128)}, f32[2,2,256,128]{3,2,1,0:T(8,128)}, u32[]{:S(2)}, u32[]{:S(2)}) collective-permute-start(f32[2,2,256,128]{3,2,1,0:T(8,128)} %get-tuple-element.39.down_b), channel_id=1, source_target_pairs={{0,1},{1,2},{2,3},{4,5},{5,6},{6,7},{8,9},{9,10},{10,11},{12,13},{... | collective-permute-start | bytes 1572872 | tf_op jit(solution)/shard_map/ppermute | solution.py:22
  75.8 18.1 %collective-permute-start.7 = (f32[2,2,256,128]{3,2,1,0:T(8,128)}, f32[2,2,256,128]{3,2,1,0:T(8,128)}, u32[]{:S(2)}, u32[]{:S(2)}) collective-permute-start(f32[2,2,256,128]{3,2,1,0:T(8,128)} %get-tuple-element.40.up_b), channel_id=1, source_target_pairs={{1,0},{2,1},{3,2},{5,4},{6,5},{7,6},{9,8},{10,9},{11,10},{13,12},{... | collective-permute-start | bytes 1572872 | tf_op jit(solution)/shard_map/ppermute | solution.py:22
  85.5 3.7 %copy-start.10 = (f32[2,2,2,256,128]{4,3,2,1,0:T(8,128)}, f32[2,2,2,256,128]{4,3,2,1,0:T(8,128)S(1)}, u32[]{:S(2)}) copy-start(f32[2,2,2,256,128]{4,3,2,1,0:T(8,128)S(1)} %collective-permute-done.4.from_left_c) | copy-start | bytes 3145732
  85.5 3.7 %copy-start.11 = (f32[2,2,2,256,128]{4,3,2,1,0:T(8,128)}, f32[2,2,2,256,128]{4,3,2,1,0:T(8,128)S(1)}, u32[]{:S(2)}) copy-start(f32[2,2,2,256,128]{4,3,2,1,0:T(8,128)S(1)} %collective-permute-done.5.from_right_c) | copy-start | bytes 3145732
  88.1 11.0 %copy-start.14 = (f32[2,2,256,128]{3,2,1,0:T(8,128)S(1)}, f32[2,2,256,128]{3,2,1,0:T(8,128)}, u32[]{:S(2)}) copy-start(f32[2,2,256,128]{3,2,1,0:T(8,128)} %get-tuple-element.49.left_b) | copy-start | bytes 1572868
  89.1 35.9 %collective-permute-start.8 = (f32[2,2,2,256,128]{4,3,2,1,0:T(8,128)}, f32[2,2,2,256,128]{4,3,2,1,0:T(8,128)}, u32[]{:S(2)}, u32[]{:S(2)}) collective-permute-start(f32[2,2,2,256,128]{4,3,2,1,0:T(8,128)} %pad_maximum_fusion), channel_id=1, source_target_pairs={{0,1},{1,2},{2,3},{4,5},{5,6},{6,7},{8,9},{9,10},{10,11},{12,13},{... | collective-permute-start | bytes 3145736 | tf_op jit(solution)/shard_map/ppermute | solution.py:22
  92.6 32.5 %collective-permute-start.9 = (f32[2,2,2,256,128]{4,3,2,1,0:T(8,128)S(1)}, f32[2,2,2,256,128]{4,3,2,1,0:T(8,128)S(1)}, u32[]{:S(2)}, u32[]{:S(2)}) collective-permute-start(f32[2,2,2,256,128]{4,3,2,1,0:T(8,128)S(1)} %pad_maximum_fusion.1), channel_id=1, source_target_pairs={{1,0},{2,1},{3,2},{5,4},{6,5},{7,6},{9,8},{10,9},{11,10},{13,12},{... | collective-permute-start | bytes 3145736 | tf_op jit(solution)/shard_map/ppermute | solution.py:22
  94.9 30.2 %collective-permute-start.10 = (f32[2,2,256,128]{3,2,1,0:T(8,128)}, f32[2,2,256,128]{3,2,1,0:T(8,128)}, u32[]{:S(2)}, u32[]{:S(2)}) collective-permute-start(f32[2,2,256,128]{3,2,1,0:T(8,128)} %get-tuple-element.50.right_b), channel_id=1, source_target_pairs={{0,4},{4,8},{8,12},{12,16},{16,20},{20,24},{24,28},{28,32},{32,36}... | collective-permute-start | bytes 1572872 | tf_op jit(solution)/shard_map/ppermute | solution.py:22
  99.1 25.9 %collective-permute-start.11 = (f32[2,2,256,128]{3,2,1,0:T(8,128)S(1)}, f32[2,2,256,128]{3,2,1,0:T(8,128)}, u32[]{:S(2)}, u32[]{:S(2)}) collective-permute-start(f32[2,2,256,128]{3,2,1,0:T(8,128)S(1)} %copy-done.14), channel_id=1, source_target_pairs={{4,0},{8,4},{12,8},{16,12},{20,16},{24,20},{28,24},{32,28},{36,32}... | collective-permute-start | bytes 1572872 | tf_op jit(solution)/shard_map/ppermute | solution.py:22
  101.1 24.0 %all-to-all-start.1 = ((f32[128,8,128]{2,1,0:T(8,128)}), f32[128,8,128]{2,1,0:T(8,128)S(1)}, u32[]{:S(2)}, u32[]{:S(2)}) async-start(f32[128,8,128]{2,1,0:T(8,128)} %sum_shares.2), calls=%async_computation.1 | async-start | bytes 1048576 | tf_op jit(solution)/shard_map/all_to_all | solution.py:369
  110.5 15.7 %copy-start.5 = (s32[2,12]{1,0:T(2,128)S(1)}, s32[2,12]{1,0:T(2,128)}, u32[]{:S(2)}) copy-start(s32[2,12]{1,0:T(2,128)} %batch.3) | copy-start | bytes 292
  110.5 15.7 %copy-start.6 = (s32[2,1]{1,0:T(2,128)S(1)}, s32[2,1]{1,0:T(2,128)}, u32[]{:S(2)}) copy-start(s32[2,1]{1,0:T(2,128)} %copy.15.live) | copy-start | bytes 28
  110.5 15.7 %copy-start.7 = (s32[2]{0:T(128)S(1)}, s32[2]{0:T(128)}, u32[]{:S(2)}) copy-start(s32[2]{0:T(128)} %add_convert_fusion.edge) | copy-start | bytes 28
  110.5 15.7 %copy-start.8 = (s32[32]{0:T(128)S(1)}, s32[32]{0:T(128)}, u32[]{:S(2)}) copy-start(s32[32]{0:T(128)} %rows.3) | copy-start | bytes 388
  110.5 15.7 %copy-start.9 = (s32[32]{0:T(128)S(1)}, s32[32]{0:T(128)}, u32[]{:S(2)}) copy-start(s32[32]{0:T(128)} %cols.3) | copy-start | bytes 388
  125.1 0.8 copy-start.1
  125.1 1.1 copy-start.12
  137.6 57.9 %copy-start.3 = (f32[2,4,512,128]{3,2,1,0:T(8,128)S(1)}, f32[2,4,512,128]{3,2,1,0:T(8,128)}, u32[]{:S(2)}) copy-start(f32[2,4,512,128]{3,2,1,0:T(8,128)} %get-tuple-element.53.own) | copy-start | bytes 6291460
  137.6 25.8 %collective-permute-start.13 = (f32[2,2,256,128]{3,2,1,0:T(8,128)S(1)}, f32[2,2,256,128]{3,2,1,0:T(8,128)}, u32[]{:S(2)}, u32[]{:S(2)}) collective-permute-start(f32[2,2,256,128]{3,2,1,0:T(8,128)S(1)} %get-tuple-element.57), channel_id=1, source_target_pairs={{0,4},{4,8},{8,12},{12,16},{16,20},{20,24},{24,28},{28,32},{32,36}... | collective-permute-start | bytes 1572872 | tf_op jit(solution)/shard_map/ppermute | solution.py:22
  153.6 23.2 %collective-permute-start.12 = (f32[2,2,256,128]{3,2,1,0:T(8,128)}, f32[2,2,256,128]{3,2,1,0:T(8,128)}, u32[]{:S(2)}, u32[]{:S(2)}) collective-permute-start(f32[2,2,256,128]{3,2,1,0:T(8,128)} %get-tuple-element.55), channel_id=1, source_target_pairs={{0,1},{1,2},{2,3},{4,5},{5,6},{6,7},{8,9},{9,10},{10,11},{12,13},{... | collective-permute-start | bytes 1572872 | tf_op jit(solution)/shard_map/ppermute | solution.py:22
  155.7 21.1 %all-to-all-start.2 = ((f32[128,8,128]{2,1,0:T(8,128)}), f32[128,8,128]{2,1,0:T(8,128)}, u32[]{:S(2)}, u32[]{:S(2)}) async-start(f32[128,8,128]{2,1,0:T(8,128)} %bitcast.6), calls=%async_computation.2 | async-start | bytes 1048576 | tf_op jit(solution)/shard_map/all_to_all | solution.py:369
  165.3 39.7 %copy-start = (f32[2,256,2,128]{3,1,2,0:T(8,128)S(1)}, f32[2,256,2,128]{3,1,2,0:T(8,128)}, u32[]{:S(2)}) copy-start(f32[2,256,2,128]{3,1,2,0:T(8,128)} %copy.13) | copy-start | bytes 1572868
  165.3 39.7 %copy-start.2 = (f32[128,8,128]{2,1,0:T(8,128)S(1)}, f32[128,8,128]{2,1,0:T(8,128)}, u32[]{:S(2)}) copy-start(f32[128,8,128]{2,1,0:T(8,128)} %copy-done.1) | copy-start | bytes 1572868
  178.0 0.8 copy-start.4
  178.8 16.6 %collective-permute-start.14 = (f32[2,2,512,128]{3,2,1,0:T(8,128)}, f32[2,2,512,128]{3,2,1,0:T(8,128)}, u32[]{:S(2)}, u32[]{:S(2)}) collective-permute-start(f32[2,2,512,128]{3,2,1,0:T(8,128)} %get-tuple-element.60), channel_id=1, source_target_pairs={{0,4},{4,8},{8,12},{12,16},{16,20},{20,24},{24,28},{28,32},{32,36}... | collective-permute-start | bytes 3145736 | tf_op jit(solution)/shard_map/ppermute | solution.py:22
  181.8 13.6 %collective-permute-start.15 = (f32[2,2,256,128]{3,2,1,0:T(8,128)}, f32[2,2,256,128]{3,2,1,0:T(8,128)}, u32[]{:S(2)}, u32[]{:S(2)}) collective-permute-start(f32[2,2,256,128]{3,2,1,0:T(8,128)} %add.23), channel_id=1, source_target_pairs={{0,1},{1,2},{2,3},{4,5},{5,6},{6,7},{8,9},{9,10},{10,11},{12,13},{... | collective-permute-start | bytes 1572872 | tf_op jit(solution)/shard_map/ppermute | solution.py:22
  184.6 20.4 %all-to-all-start.3 = ((f32[128,8,128]{2,1,0:T(8,128)}), f32[128,8,128]{2,1,0:T(8,128)}, u32[]{:S(2)}, u32[]{:S(2)}) async-start(f32[128,8,128]{2,1,0:T(8,128)} %copy-done.4), calls=%async_computation.3 | async-start | bytes 1048576 | tf_op jit(solution)/shard_map/all_to_all | solution.py:369

commit v7 on v6

--- a/solution.py
+++ b/solution.py
@@ -169,7 +169,7 @@
 
 
 def first_kernel(dims, batch, live, rows, cols, probe, intensity, tables_in,
-                 field, below_a, below_b, beside, corner,
+                 field, below_a, below_b, beside_a, beside_b, corner,
                  old, middle, gprobe_out, right_c, left_c, right_b, left_b, down_b, up_b,
                  ext, grad, mats, measured, exit_0, exit_1, wave_0, wave_1, patch_0, patch_1,
                  gprobe, sems, moves):
@@ -177,7 +177,8 @@
     pairs = tiled_copies(field, nrows, ncols, ext, 0, 0)
     pairs += tiled_copies(below_a, side, side, ext, nrows, 0)
     pairs += tiled_copies(below_b, side, ncols - side, ext, nrows, side)
-    pairs += tiled_copies(beside, nrows, side, ext, 0, ncols)
+    pairs += tiled_copies(beside_a, side, side, ext, 0, ncols)
+    pairs += tiled_copies(beside_b, nrows - side, side, ext, side, ncols)
     pairs += tiled_copies(corner, side, side, ext, nrows, ncols)
     copies = run_copies(pairs + [(tables_in, mats)], moves)
     copies += start_slots(0, batch, intensity, measured, sems)
@@ -416,7 +417,8 @@
 
     first, rest = lax.optimization_barrier((object_field[:, :side, :side], object_field))
     below_a = passed_along(first, "row", -1)
-    beside = passed_along(rest[:, :, :side], "tile", -1)
+    beside_a = passed_along(first, "tile", -1)
+    beside_b = passed_along(rest[:, side:, :side], "tile", -1)
     below_b = passed_along(rest[:, :side, side:], "row", -1)
     corner = passed_along(below_a, "tile", -1)
 
@@ -432,7 +434,7 @@
     middle_b = (2, ncols // LANES - t, nrows - side, LANES)
     old, middle, gprobe, right_c, left_c, right_b, left_b, down_b, up_b = call(
         functools.partial(first_kernel, dims), dims, slots, scalars, (current,),
-        (intensity, both, object_field, below_a, below_b, beside, corner), (),
+        (intensity, both, object_field, below_a, below_b, beside_a, beside_b, corner), (),
         [big, middle_b, current.shape, corners, corners, side_b, side_b, strip, strip], [],
         54, "first_iteration")
 
@@ -463,14 +465,12 @@
          (2, t, nrows, LANES), (2, t, side, LANES), strip],
         [current.shape], 52, "second_iteration")
 
+    given = add_up(swap(gprobe.reshape(devices, -1, LANES)))
+    given, right_c, right_ab, down_b = lax.optimization_barrier((given, right_c, right_ab, down_b))
     from_left_c = passed_along(right_c, "tile", 1)
     above_b = passed_along(down_b, "row", 1)
-    mine = swap(gprobe.reshape(devices, -1, LANES))
-    down_a = down_a + from_left_c
-    above_a = passed_along(down_a, "row", 1)
-    mine, above_b, _ = lax.optimization_barrier((mine, above_b, down_a))
-    given, right_ab = lax.optimization_barrier((add_up(mine), right_ab))
     left_ab = passed_along(right_ab, "tile", 1)
+    above_a = passed_along(down_a + from_left_c, "row", 1)
     sum_two = swap(given).reshape(current.shape)
     object_out = simple(functools.partial(object_kernel, dims), object_field.shape, "last_object",
                         16, (own, left_ab, above_a, above_b))

time: 207 us -> 214 us (1.034); the launches traced: 207 us -> 211 us
  blocking collectives: 0 us -> 32.3 us
  starting transfers between devices: 96.6 us -> 72.3 us
  waiting for transfers between devices: 54 us -> 38.3 us
  Pallas kernels: 39 us -> 49.6 us
    all_to_all x0 -> x1, blocking collectives: none -> 32.3 us  [swap(): return lax.all_to_all(shares, ('tile', 'row'), 0, 0, tiled=True)]
    all_to_all x4 -> x3, waiting for transfers between devices: 32.5 us -> 13.9 us  [swap(): return lax.all_to_all(shares, ('tile', 'row'), 0, 0, tiled=True)]
    all_to_all x4 -> x3, starting transfers between devices: 40.8 us -> 28 us  [swap(): return lax.all_to_all(shares, ('tile', 'row'), 0, 0, tiled=True)]
    ppermute x16 -> x17, starting transfers between devices: 55.8 us -> 44.3 us  [passed_along(): lax.ppermute(value, axis, [(source, source + steps) for source in range(f...]
    pallas_call x2, Pallas kernels: 23.5 us -> 34.5 us  [call(): pl.pallas_call(kernel, out_shape=[jax.ShapeDtypeStruct(shape, F32) for sh...]
    ppermute x16 -> x17, waiting for transfers between devices: 21.5 us -> 24.5 us  [passed_along(): lax.ppermute(value, axis, [(source, source + steps) for source in range(f...]
    unnamed x36 -> x44, local copies, waits for them, and re-layouts: 4.77 us -> 6.41 us
where the time goes in v7:
time: 214 us; the launch traced here: 211 us
  starting transfers between devices  72.3 us (34%)
  Pallas kernels  49.6 us (23%)
  waiting for transfers between devices  38.3 us (18%)
  blocking collectives  32.3 us (15%)
  local copies, waits for them, and re-layouts  11.6 us (5%)
  other arithmetic  6.09 us (3%)
    ppermute x17, starting transfers between devices, passed_along(): lax.ppermute(value, axis, [(source, source + steps) for source in range(f...  44.3 us
    pallas_call x2, Pallas kernels, call(): pl.pallas_call(kernel, out_shape=[jax.ShapeDtypeStruct(shape, F32) for sh...  34.5 us
    all_to_all x1, blocking collectives, swap(): return lax.all_to_all(shares, ('tile', 'row'), 0, 0, tiled=True)  32.3 us
    all_to_all x3, starting transfers between devices, swap(): return lax.all_to_all(shares, ('tile', 'row'), 0, 0, tiled=True)  28 us
    ppermute x17, waiting for transfers between devices, passed_along(): lax.ppermute(value, axis, [(source, source + steps) for source in range(f...  24.5 us
    all_to_all x3, waiting for transfers between devices, swap(): return lax.all_to_all(shares, ('tile', 'row'), 0, 0, tiled=True)  13.9 us
    pallas_call x1, Pallas kernels, update(): pl.pallas_call(functools.partial(update_kernel, dims), out_shape=jax.Shap...  8.28 us
    unnamed x44, local copies, waits for them, and re-layouts  6.41 us
  transfers between devices with their start and end apart: 20, of which 7 were waited for; matrix products, arithmetic and copies ran while one was open for 5% of the time, Pallas kernels for 6%

profile of v7, /device:TPU:1, one launch (start us, length us, event | category | flops | bytes accessed | tf_op | source)
XLA Modules:
  0.0 211.2 jit_solution(15565247402856633234)
XLA Ops:
  0.6 1.9 slice.33
  2.5 1.3 collective-permute-start
  3.8 3.3 %collective-permute-start.2 = (f32[2,256,256]{2,1,0:T(8,128)}, f32[2,256,256]{2,1,0:T(8,128)S(1)}, u32[]{:S(2)}, u32[]{:S(2)}) collective-permute-start(f32[2,256,256]{2,1,0:T(8,128)} %slice.33), channel_id=1, source_target_pairs={{4,0},{8,4},{12,8},{16,12},{20,16},{24,20},{28,24},{32,28},{36,32}... | collective-permute-start | bytes 1572872 | tf_op jit(solution)/shard_map/ppermute | solution.py:22
  7.1 2.3 %fusion = (f32[2,256,256]{2,1,0:T(8,128)}, f32[2,256,256]{2,1,0:T(8,128)}) fusion(f32[2,512,512]{2,1,0:T(8,128)} %field.1), kind=kLoop, calls=%fused_computation.7 | loop fusion | bytes 2097152 | tf_op jit(solution)/shard_map/slice | solution.py:421
  9.5 1.3 collective-permute-start.1
  10.8 1.9 collective-permute-start.3
  12.7 5.3 %collective-permute-done.below_a = f32[2,256,256]{2,1,0:T(8,128)S(1)} collective-permute-done((f32[2,256,256]{2,1,0:T(8,128)}, f32[2,256,256]{2,1,0:T(8,128)S(1)}, u32[]{:S(2)}, u32[]{:S(2)}) %collective-permute-start) | collective-permute-done | bytes 524320 | tf_op jit(solution)/shard_map/ppermute | solution.py:22
  18.0 4.8 %collective-permute-start.4 = (f32[2,256,256]{2,1,0:T(8,128)S(1)}, f32[2,256,256]{2,1,0:T(8,128)S(1)}, u32[]{:S(2)}, u32[]{:S(2)}) collective-permute-start(f32[2,256,256]{2,1,0:T(8,128)S(1)} %collective-permute-done.below_a), channel_id=1, source_target_pairs={{4,0},{8,4},{12,8},{16,12},{20,16},{24,20},{28,24},{32,28},{36,32}... | collective-permute-start | bytes 1572872 | tf_op jit(solution)/shard_map/ppermute | solution.py:22
  22.8 0.6 copy.15.live
  23.4 1.2 copy.12
  24.6 1.0 copy.13
  25.6 3.6 %collective-permute-done.1.below_b = f32[2,256,256]{2,1,0:T(8,128)S(1)} collective-permute-done((f32[2,256,256]{2,1,0:T(8,128)}, f32[2,256,256]{2,1,0:T(8,128)S(1)}, u32[]{:S(2)}, u32[]{:S(2)}) %collective-permute-start.1) | collective-permute-done | bytes 524320 | tf_op jit(solution)/shard_map/ppermute | solution.py:22
  29.2 1.5 collective-permute-done.4.corner
  30.8 0.8 copy-done.19
  31.6 21.0 %first_iteration.1 = (f32[2,6,768,128]{3,2,1,0:T(8,128)}, f32[2,2,256,128]{3,2,1,0:T(8,128)}, f32[2,2,256,128]{3,2,1,0:T(8,128)}, f32[2,2,2,256,128]{4,3,2,1,0:T...) custom-call(s32[2,12]{1,0:T(2,128)} %batch.3, ...), custom_call_target="tpu_custom_call" | custom-call | tf_op jit(solution)/shard_map/first_iteration/pallas_call | solution.py:347
  52.6 3.8 %collective-permute-start.5 = (f32[2,2,2,256,128]{4,3,2,1,0:T(8,128)}, f32[2,2,2,256,128]{4,3,2,1,0:T(8,128)S(1)}, u32[]{:S(2)}, u32[]{:S(2)}) collective-permute-start(f32[2,2,2,256,128]{4,3,2,1,0:T(8,128)} %get-tuple-element.36.right_c), channel_id=1, source_target_pairs={{0,4},{4,8},{8,12},{12,16},{16,20},{20,24},{24,28},{28,32},{32,36}... | collective-permute-start | bytes 3145736 | tf_op jit(solution)/shard_map/ppermute | solution.py:22
  56.4 1.9 collective-permute-start.6
  58.3 10.6 %all-to-all-start = ((f32[128,8,128]{2,1,0:T(8,128)}), f32[128,8,128]{2,1,0:T(8,128)S(1)}, u32[]{:S(2)}, u32[]{:S(2)}) async-start(f32[128,8,128]{2,1,0:T(8,128)} %bitcast.15), calls=%async_computation | async-start | bytes 1048576 | tf_op jit(solution)/shard_map/all_to_all | solution.py:370
  68.9 4.1 %collective-permute-start.7 = (f32[2,2,256,128]{3,2,1,0:T(8,128)}, f32[2,2,256,128]{3,2,1,0:T(8,128)}, u32[]{:S(2)}, u32[]{:S(2)}) collective-permute-start(f32[2,2,256,128]{3,2,1,0:T(8,128)} %get-tuple-element.39.down_b), channel_id=1, source_target_pairs={{0,1},{1,2},{2,3},{4,5},{5,6},{6,7},{8,9},{9,10},{10,11},{12,13},{... | collective-permute-start | bytes 1572872 | tf_op jit(solution)/shard_map/ppermute | solution.py:22
  73.0 1.3 collective-permute-start.8
  74.3 8.4 %all-to-all-done.received = f32[128,8,128]{2,1,0:T(8,128)S(1)} async-done(((f32[128,8,128]{2,1,0:T(8,128)}), f32[128,8,128]{2,1,0:T(8,128)S(1)}, u32[]{:S(2)}, u32[]{:S(2)}) %all-to-all-start) | async-done | bytes 524320 | tf_op jit(solution)/shard_map/all_to_all | solution.py:370
  82.7 2.5 %slice_add_fusion = (f32[1,2,2,256,128]{4,3,2,1,0:T(8,128)S(1)}, f32[1,2,2,256,128]{4,3,2,1,0:T(8,128)S(1)}, f32[1,2,2,256,128]{4,3,2,1,0:T(8,128)S(1)}, f32[1,2,2,256,128]{4,3,2,1,0:T(8,128)S(1)}) fusion(f32[2,2,2,256,128]{4,3,2,1,0:T(8,128)S(1)} %collective-permute-done.6.from_right_c, f32[2,2,2,256,128]{4,3,2,1,0:T(8,128)} %get-tuple-element.36.right_c, ...), kind=kLoop, calls=%fused_computation.2 | loop fusion | flops 524288 | bytes 6291456 | tf_op jit(solution)/shard_map/add | solution.py:448
  85.2 1.1 pad_maximum_fusion
  86.3 2.4 %collective-permute-start.9 = (f32[2,2,2,256,128]{4,3,2,1,0:T(8,128)}, f32[2,2,2,256,128]{4,3,2,1,0:T(8,128)S(1)}, u32[]{:S(2)}, u32[]{:S(2)}) collective-permute-start(f32[2,2,2,256,128]{4,3,2,1,0:T(8,128)} %pad_maximum_fusion), channel_id=1, source_target_pairs={{0,1},{1,2},{2,3},{4,5},{5,6},{6,7},{8,9},{9,10},{10,11},{12,13},{... | collective-permute-start | bytes 3145736 | tf_op jit(solution)/shard_map/ppermute | solution.py:22
  88.8 1.0 pad_maximum_fusion.1
  89.8 1.3 collective-permute-start.10
  91.1 1.0 sum_shares.2
  92.1 4.2 %collective-permute-start.11 = (f32[2,2,256,128]{3,2,1,0:T(8,128)}, f32[2,2,256,128]{3,2,1,0:T(8,128)}, u32[]{:S(2)}, u32[]{:S(2)}) collective-permute-start(f32[2,2,256,128]{3,2,1,0:T(8,128)} %get-tuple-element.50.right_b), channel_id=1, source_target_pairs={{0,4},{4,8},{8,12},{12,16},{16,20},{20,24},{24,28},{28,32},{32,36}... | collective-permute-start | bytes 1572872 | tf_op jit(solution)/shard_map/ppermute | solution.py:22
  96.3 1.9 collective-permute-start.12
  98.2 9.8 %all-to-all-start.1 = ((f32[128,8,128]{2,1,0:T(8,128)}), f32[128,8,128]{2,1,0:T(8,128)S(1)}, u32[]{:S(2)}, u32[]{:S(2)}) async-start(f32[128,8,128]{2,1,0:T(8,128)} %sum_shares.2), calls=%async_computation.1 | async-start | bytes 1048576 | tf_op jit(solution)/shard_map/all_to_all | solution.py:370
  108.7 8.3 %update_object.1.part_in = f32[2,6,768,128]{3,2,1,0:T(8,128)} custom-call(s32[2]{0:T(128)} %add_convert_fusion.edge, f32[2,6,768,128]{3,2,1,0:T(8,128)} %get-tuple-element.47.old, f32[2,2,256,128]{3,2,1,0:T(8,128)} %get-tuple-element.48.middle, f32[2,2,2,256,128]{4,3,2,1,0:T(8,128)} %get-tuple-element.37.left_c, ...), custom_call_target="tpu_custom_call" | custom-call | tf_op jit(solution)/shard_map/update_object/pallas_call | solution.py:383
  117.0 5.5 %all-to-all-done.1 = f32[128,8,128]{2,1,0:T(8,128)S(1)} async-done(((f32[128,8,128]{2,1,0:T(8,128)}), f32[128,8,128]{2,1,0:T(8,128)S(1)}, u32[]{:S(2)}, u32[]{:S(2)}) %all-to-all-start.1) | async-done | bytes 524320 | tf_op jit(solution)/shard_map/all_to_all | solution.py:370
  122.5 0.8 copy-done.1
  124.0 13.5 %second_iteration.1 = (f32[2,4,512,128]{3,2,1,0:T(8,128)}, f32[2,2,256,128]{3,2,1,0:T(8,128)S(1)}, f32[2,2,256,128]{3,2,1,0:T(8,128)S(1)}, f32[2,2,512,128]{3,2,...) custom-call(s32[2,12]{1,0:T(2,128)S(1)} %copy-done.6, s32[2,1]{1,0:T(2,128)S(1)} %copy-done.7, ...), custom_call_target="tpu_custom_call" | custom-call | tf_op jit(solution)/shard_map/second_iteration/pallas_call | solution.py:347
  137.5 32.3 %all_to_all.20.received = f32[128,8,128]{2,1,0:T(8,128)S(1)} all-to-all(f32[128,8,128]{2,1,0:T(8,128)S(1)} %bitcast.13), channel_id=1, replica_groups=mesh['tile'=32,'row'=4] {'tile','row'}, dimensions={0} | all-to-all | bytes 1048576 | tf_op jit(solution)/shard_map/all_to_all | solution.py:370
  169.8 1.0 sum_shares.3
  170.8 2.7 %collective-permute-start.14 = (f32[2,2,256,128]{3,2,1,0:T(8,128)S(1)}, f32[2,2,256,128]{3,2,1,0:T(8,128)S(1)}, u32[]{:S(2)}, u32[]{:S(2)}) collective-permute-start(f32[2,2,256,128]{3,2,1,0:T(8,128)S(1)} %get-tuple-element.60), channel_id=1, source_target_pairs={{0,4},{4,8},{8,12},{12,16},{16,20},{20,24},{24,28},{28,32},{32,36}... | collective-permute-start | bytes 1572872 | tf_op jit(solution)/shard_map/ppermute | solution.py:22
  173.5 1.9 collective-permute-start.13
  175.4 3.1 %collective-permute-start.16 = (f32[2,2,256,128]{3,2,1,0:T(8,128)}, f32[2,2,256,128]{3,2,1,0:T(8,128)}, u32[]{:S(2)}, u32[]{:S(2)}) collective-permute-start(f32[2,2,256,128]{3,2,1,0:T(8,128)} %get-tuple-element.61), channel_id=1, source_target_pairs={{0,1},{1,2},{2,3},{4,5},{5,6},{6,7},{8,9},{9,10},{10,11},{12,13},{... | collective-permute-start | bytes 1572872 | tf_op jit(solution)/shard_map/ppermute | solution.py:22
  178.5 1.1 collective-permute-done.14
  179.6 0.9 add.23
  180.4 3.1 %collective-permute-start.15 = (f32[2,2,256,128]{3,2,1,0:T(8,128)}, f32[2,2,256,128]{3,2,1,0:T(8,128)}, u32[]{:S(2)}, u32[]{:S(2)}) collective-permute-start(f32[2,2,256,128]{3,2,1,0:T(8,128)} %add.23), channel_id=1, source_target_pairs={{0,1},{1,2},{2,3},{4,5},{5,6},{6,7},{8,9},{9,10},{10,11},{12,13},{... | collective-permute-start | bytes 1572872 | tf_op jit(solution)/shard_map/ppermute | solution.py:22
  183.5 7.7 %all-to-all-start.3 = ((f32[128,8,128]{2,1,0:T(8,128)}), f32[128,8,128]{2,1,0:T(8,128)}, u32[]{:S(2)}, u32[]{:S(2)}) async-start(f32[128,8,128]{2,1,0:T(8,128)} %sum_shares.3), calls=%async_computation.3 | async-start | bytes 1048576 | tf_op jit(solution)/shard_map/all_to_all | solution.py:370
  191.2 12.9 %collective-permute-done.15.above_a = f32[2,2,256,128]{3,2,1,0:T(8,128)} collective-permute-done((f32[2,2,256,128]{3,2,1,0:T(8,128)}, f32[2,2,256,128]{3,2,1,0:T(8,128)}, u32[]{:S(2)}, u32[]{:S(2)}) %collective-permute-start.15) | collective-permute-done | bytes 524320 | tf_op jit(solution)/shard_map/ppermute | solution.py:22
  204.1 1.0 copy-done.4
  205.1 1.2 copy-done.5
  206.4 2.9 %last_object.1 = f32[2,512,512]{2,1,0:T(8,128)} custom-call(f32[2,4,512,128]{3,2,1,0:T(8,128)S(1)} %copy-done.3, f32[2,2,512,128]{3,2,1,0:T(8,128)S(1)} %copy-done.5, f32[2,2,256,128]{3,2,1,0:T(8,128)} %collective-permute-done.15.above_a, f32[2,2,256,128]{3,2,1,0:T(8,128)} %collective-permute-done.16.above_b), custom_call_target="tpu_custom_call" | custom-call | tf_op jit(solution)/shard_map/last_object/pallas_call | solution.py:397
  209.3 1.9 last_probe.1
  (52 shorter events, 1.4 us)
Async XLA Ops:
  0.6 22.1 %copy-start.20 = (s32[2,1]{0,1:T(1,128)S(1)}, s32[2,1]{0,1:T(1,128)}, u32[]{:S(2)}) copy-start(s32[2,1]{0,1:T(1,128)} %param.14) | copy-start | bytes 28
  2.5 15.5 %collective-permute-start = (f32[2,256,256]{2,1,0:T(8,128)}, f32[2,256,256]{2,1,0:T(8,128)S(1)}, u32[]{:S(2)}, u32[]{:S(2)}) collective-permute-start(f32[2,256,256]{2,1,0:T(8,128)} %slice.33), channel_id=1, source_target_pairs={{1,0},{2,1},{3,2},{5,4},{6,5},{7,6},{9,8},{10,9},{11,10},{13,12},{... | collective-permute-start | bytes 1572872 | tf_op jit(solution)/shard_map/ppermute | solution.py:22
  3.8 25.4 %collective-permute-start.2 = (f32[2,256,256]{2,1,0:T(8,128)}, f32[2,256,256]{2,1,0:T(8,128)S(1)}, u32[]{:S(2)}, u32[]{:S(2)}) collective-permute-start(f32[2,256,256]{2,1,0:T(8,128)} %slice.33), channel_id=1, source_target_pairs={{4,0},{8,4},{12,8},{16,12},{20,16},{24,20},{28,24},{32,28},{36,32}... | collective-permute-start | bytes 1572872 | tf_op jit(solution)/shard_map/ppermute | solution.py:22
  9.5 19.7 %collective-permute-start.1 = (f32[2,256,256]{2,1,0:T(8,128)}, f32[2,256,256]{2,1,0:T(8,128)S(1)}, u32[]{:S(2)}, u32[]{:S(2)}) collective-permute-start(f32[2,256,256]{2,1,0:T(8,128)} %get-tuple-element.69), channel_id=1, source_target_pairs={{1,0},{2,1},{3,2},{5,4},{6,5},{7,6},{9,8},{10,9},{11,10},{13,12},{... | collective-permute-start | bytes 1572872 | tf_op jit(solution)/shard_map/ppermute | solution.py:22
  10.8 18.5 %collective-permute-start.3 = (f32[2,256,256]{2,1,0:T(8,128)}, f32[2,256,256]{2,1,0:T(8,128)S(1)}, u32[]{:S(2)}, u32[]{:S(2)}) collective-permute-start(f32[2,256,256]{2,1,0:T(8,128)} %get-tuple-element.68), channel_id=1, source_target_pairs={{4,0},{8,4},{12,8},{16,12},{20,16},{24,20},{28,24},{32,28},{36,32}... | collective-permute-start | bytes 1572872 | tf_op jit(solution)/shard_map/ppermute | solution.py:22
  18.0 12.8 %copy-start.15 = (f32[2,256,256]{2,1,0:T(8,128)}, f32[2,256,256]{2,1,0:T(8,128)S(1)}, u32[]{:S(2)}) copy-start(f32[2,256,256]{2,1,0:T(8,128)S(1)} %collective-permute-done.below_a) | copy-start | bytes 1572868
  18.0 12.8 %collective-permute-start.4 = (f32[2,256,256]{2,1,0:T(8,128)S(1)}, f32[2,256,256]{2,1,0:T(8,128)S(1)}, u32[]{:S(2)}, u32[]{:S(2)}) collective-permute-start(f32[2,256,256]{2,1,0:T(8,128)S(1)} %collective-permute-done.below_a), channel_id=1, source_target_pairs={{4,0},{8,4},{12,8},{16,12},{20,16},{24,20},{28,24},{32,28},{36,32}... | collective-permute-start | bytes 1572872 | tf_op jit(solution)/shard_map/ppermute | solution.py:22
  29.2 1.6 copy-start.17
  29.2 1.6 copy-start.16
  29.2 1.6 copy-start.18
  30.8 0.8 copy-start.19
  52.6 30.1 %collective-permute-start.5 = (f32[2,2,2,256,128]{4,3,2,1,0:T(8,128)}, f32[2,2,2,256,128]{4,3,2,1,0:T(8,128)S(1)}, u32[]{:S(2)}, u32[]{:S(2)}) collective-permute-start(f32[2,2,2,256,128]{4,3,2,1,0:T(8,128)} %get-tuple-element.36.right_c), channel_id=1, source_target_pairs={{0,4},{4,8},{8,12},{12,16},{16,20},{20,24},{24,28},{28,32},{32,36}... | collective-permute-start | bytes 3145736 | tf_op jit(solution)/shard_map/ppermute | solution.py:22
  56.4 26.3 %collective-permute-start.6 = (f32[2,2,2,256,128]{4,3,2,1,0:T(8,128)}, f32[2,2,2,256,128]{4,3,2,1,0:T(8,128)S(1)}, u32[]{:S(2)}, u32[]{:S(2)}) collective-permute-start(f32[2,2,2,256,128]{4,3,2,1,0:T(8,128)} %get-tuple-element.37.left_c), channel_id=1, source_target_pairs={{4,0},{8,4},{12,8},{16,12},{20,16},{24,20},{28,24},{32,28},{36,32}... | collective-permute-start | bytes 3145736 | tf_op jit(solution)/shard_map/ppermute | solution.py:22
  58.3 24.3 %all-to-all-start = ((f32[128,8,128]{2,1,0:T(8,128)}), f32[128,8,128]{2,1,0:T(8,128)S(1)}, u32[]{:S(2)}, u32[]{:S(2)}) async-start(f32[128,8,128]{2,1,0:T(8,128)} %bitcast.15), calls=%async_computation | async-start | bytes 1048576 | tf_op jit(solution)/shard_map/all_to_all | solution.py:370
  68.9 22.2 %collective-permute-start.7 = (f32[2,2,256,128]{3,2,1,0:T(8,128)}, f32[2,2,256,128]{3,2,1,0:T(8,128)}, u32[]{:S(2)}, u32[]{:S(2)}) collective-permute-start(f32[2,2,256,128]{3,2,1,0:T(8,128)} %get-tuple-element.39.down_b), channel_id=1, source_target_pairs={{0,1},{1,2},{2,3},{4,5},{5,6},{6,7},{8,9},{9,10},{10,11},{12,13},{... | collective-permute-start | bytes 1572872 | tf_op jit(solution)/shard_map/ppermute | solution.py:22
  73.0 18.1 %collective-permute-start.8 = (f32[2,2,256,128]{3,2,1,0:T(8,128)}, f32[2,2,256,128]{3,2,1,0:T(8,128)}, u32[]{:S(2)}, u32[]{:S(2)}) collective-permute-start(f32[2,2,256,128]{3,2,1,0:T(8,128)} %get-tuple-element.40.up_b), channel_id=1, source_target_pairs={{1,0},{2,1},{3,2},{5,4},{6,5},{7,6},{9,8},{10,9},{11,10},{13,12},{... | collective-permute-start | bytes 1572872 | tf_op jit(solution)/shard_map/ppermute | solution.py:22
  82.7 2.5 %copy-start.11 = (f32[2,2,2,256,128]{4,3,2,1,0:T(8,128)}, f32[2,2,2,256,128]{4,3,2,1,0:T(8,128)S(1)}, u32[]{:S(2)}) copy-start(f32[2,2,2,256,128]{4,3,2,1,0:T(8,128)S(1)} %collective-permute-done.5.from_left_c) | copy-start | bytes 3145732
  82.7 2.5 %copy-start.12 = (f32[2,2,2,256,128]{4,3,2,1,0:T(8,128)}, f32[2,2,2,256,128]{4,3,2,1,0:T(8,128)S(1)}, u32[]{:S(2)}) copy-start(f32[2,2,2,256,128]{4,3,2,1,0:T(8,128)S(1)} %collective-permute-done.6.from_right_c) | copy-start | bytes 3145732
  86.3 36.2 %collective-permute-start.9 = (f32[2,2,2,256,128]{4,3,2,1,0:T(8,128)}, f32[2,2,2,256,128]{4,3,2,1,0:T(8,128)S(1)}, u32[]{:S(2)}, u32[]{:S(2)}) collective-permute-start(f32[2,2,2,256,128]{4,3,2,1,0:T(8,128)} %pad_maximum_fusion), channel_id=1, source_target_pairs={{0,1},{1,2},{2,3},{4,5},{5,6},{6,7},{8,9},{9,10},{10,11},{12,13},{... | collective-permute-start | bytes 3145736 | tf_op jit(solution)/shard_map/ppermute | solution.py:22
  89.8 32.7 %collective-permute-start.10 = (f32[2,2,2,256,128]{4,3,2,1,0:T(8,128)}, f32[2,2,2,256,128]{4,3,2,1,0:T(8,128)S(1)}, u32[]{:S(2)}, u32[]{:S(2)}) collective-permute-start(f32[2,2,2,256,128]{4,3,2,1,0:T(8,128)} %pad_maximum_fusion.1), channel_id=1, source_target_pairs={{1,0},{2,1},{3,2},{5,4},{6,5},{7,6},{9,8},{10,9},{11,10},{13,12},{... | collective-permute-start | bytes 3145736 | tf_op jit(solution)/shard_map/ppermute | solution.py:22
  92.1 30.4 %collective-permute-start.11 = (f32[2,2,256,128]{3,2,1,0:T(8,128)}, f32[2,2,256,128]{3,2,1,0:T(8,128)}, u32[]{:S(2)}, u32[]{:S(2)}) collective-permute-start(f32[2,2,256,128]{3,2,1,0:T(8,128)} %get-tuple-element.50.right_b), channel_id=1, source_target_pairs={{0,4},{4,8},{8,12},{12,16},{16,20},{20,24},{24,28},{28,32},{32,36}... | collective-permute-start | bytes 1572872 | tf_op jit(solution)/shard_map/ppermute | solution.py:22
  96.3 26.2 %collective-permute-start.12 = (f32[2,2,256,128]{3,2,1,0:T(8,128)}, f32[2,2,256,128]{3,2,1,0:T(8,128)}, u32[]{:S(2)}, u32[]{:S(2)}) collective-permute-start(f32[2,2,256,128]{3,2,1,0:T(8,128)} %get-tuple-element.49.left_b), channel_id=1, source_target_pairs={{4,0},{8,4},{12,8},{16,12},{20,16},{24,20},{28,24},{32,28},{36,32}... | collective-permute-start | bytes 1572872 | tf_op jit(solution)/shard_map/ppermute | solution.py:22
  98.2 24.2 %all-to-all-start.1 = ((f32[128,8,128]{2,1,0:T(8,128)}), f32[128,8,128]{2,1,0:T(8,128)S(1)}, u32[]{:S(2)}, u32[]{:S(2)}) async-start(f32[128,8,128]{2,1,0:T(8,128)} %sum_shares.2), calls=%async_computation.1 | async-start | bytes 1048576 | tf_op jit(solution)/shard_map/all_to_all | solution.py:370
  108.7 15.3 %copy-start.6 = (s32[2,12]{1,0:T(2,128)S(1)}, s32[2,12]{1,0:T(2,128)}, u32[]{:S(2)}) copy-start(s32[2,12]{1,0:T(2,128)} %batch.3) | copy-start | bytes 292
  108.7 15.3 %copy-start.7 = (s32[2,1]{1,0:T(2,128)S(1)}, s32[2,1]{1,0:T(2,128)}, u32[]{:S(2)}) copy-start(s32[2,1]{1,0:T(2,128)} %copy.15.live) | copy-start | bytes 28
  108.7 15.3 %copy-start.8 = (s32[2]{0:T(128)S(1)}, s32[2]{0:T(128)}, u32[]{:S(2)}) copy-start(s32[2]{0:T(128)} %add_convert_fusion.edge) | copy-start | bytes 28
  108.7 15.3 %copy-start.9 = (s32[32]{0:T(128)S(1)}, s32[32]{0:T(128)}, u32[]{:S(2)}) copy-start(s32[32]{0:T(128)} %rows.3) | copy-start | bytes 388
  108.7 15.3 %copy-start.10 = (s32[32]{0:T(128)S(1)}, s32[32]{0:T(128)}, u32[]{:S(2)}) copy-start(s32[32]{0:T(128)} %cols.3) | copy-start | bytes 388
  122.5 0.8 copy-start.1
  122.5 1.1 copy-start.13
  122.5 1.5 copy-start.14
  169.8 35.4 %copy-start.3 = (f32[2,4,512,128]{3,2,1,0:T(8,128)S(1)}, f32[2,4,512,128]{3,2,1,0:T(8,128)}, u32[]{:S(2)}) copy-start(f32[2,4,512,128]{3,2,1,0:T(8,128)} %get-tuple-element.53.own) | copy-start | bytes 6291460
  170.8 8.8 %collective-permute-start.14 = (f32[2,2,256,128]{3,2,1,0:T(8,128)S(1)}, f32[2,2,256,128]{3,2,1,0:T(8,128)S(1)}, u32[]{:S(2)}, u32[]{:S(2)}) collective-permute-start(f32[2,2,256,128]{3,2,1,0:T(8,128)S(1)} %get-tuple-element.60), channel_id=1, source_target_pairs={{0,4},{4,8},{8,12},{12,16},{16,20},{20,24},{24,28},{28,32},{32,36}... | collective-permute-start | bytes 1572872 | tf_op jit(solution)/shard_map/ppermute | solution.py:22
  173.5 30.7 %collective-permute-start.13 = (f32[2,2,512,128]{3,2,1,0:T(8,128)}, f32[2,2,512,128]{3,2,1,0:T(8,128)S(1)}, u32[]{:S(2)}, u32[]{:S(2)}) collective-permute-start(f32[2,2,512,128]{3,2,1,0:T(8,128)} %get-tuple-element.58), channel_id=1, source_target_pairs={{0,4},{4,8},{8,12},{12,16},{16,20},{20,24},{24,28},{28,32},{32,36}... | collective-permute-start | bytes 3145736 | tf_op jit(solution)/shard_map/ppermute | solution.py:22
  175.4 15.8 %collective-permute-start.16 = (f32[2,2,256,128]{3,2,1,0:T(8,128)}, f32[2,2,256,128]{3,2,1,0:T(8,128)}, u32[]{:S(2)}, u32[]{:S(2)}) collective-permute-start(f32[2,2,256,128]{3,2,1,0:T(8,128)} %get-tuple-element.61), channel_id=1, source_target_pairs={{0,1},{1,2},{2,3},{4,5},{5,6},{6,7},{8,9},{9,10},{10,11},{12,13},{... | collective-permute-start | bytes 1572872 | tf_op jit(solution)/shard_map/ppermute | solution.py:22
  180.4 23.7 %collective-permute-start.15 = (f32[2,2,256,128]{3,2,1,0:T(8,128)}, f32[2,2,256,128]{3,2,1,0:T(8,128)}, u32[]{:S(2)}, u32[]{:S(2)}) collective-permute-start(f32[2,2,256,128]{3,2,1,0:T(8,128)} %add.23), channel_id=1, source_target_pairs={{0,1},{1,2},{2,3},{4,5},{5,6},{6,7},{8,9},{9,10},{10,11},{12,13},{... | collective-permute-start | bytes 1572872 | tf_op jit(solution)/shard_map/ppermute | solution.py:22
  183.5 25.8 %all-to-all-start.3 = ((f32[128,8,128]{2,1,0:T(8,128)}), f32[128,8,128]{2,1,0:T(8,128)}, u32[]{:S(2)}, u32[]{:S(2)}) async-start(f32[128,8,128]{2,1,0:T(8,128)} %sum_shares.3), calls=%async_computation.3 | async-start | bytes 1048576 | tf_op jit(solution)/shard_map/all_to_all | solution.py:370
  204.1 1.0 copy-start.4
  205.1 1.2 copy-start.5
  206.4 2.9 %copy-start = (f32[2,256,2,128]{3,1,2,0:T(8,128)S(1)}, f32[2,256,2,128]{3,1,2,0:T(8,128)}, u32[]{:S(2)}) copy-start(f32[2,256,2,128]{3,1,2,0:T(8,128)} %copy.13) | copy-start | bytes 1572868
  206.4 2.9 %copy-start.2 = (f32[128,8,128]{2,1,0:T(8,128)S(1)}, f32[128,8,128]{2,1,0:T(8,128)}, u32[]{:S(2)}) copy-start(f32[128,8,128]{2,1,0:T(8,128)} %copy-done.1) | copy-start | bytes 1572868

commit v8 on v7

--- a/solution.py
+++ b/solution.py
@@ -446,13 +446,15 @@
     mine, from_left_c, from_right_c = lax.optimization_barrier((mine, from_left_c, from_right_c))
     down_c = jnp.stack([left_c[1] + from_left_c[1], right_c[1] + from_right_c[1]])
     up_c = jnp.stack([left_c[0] + from_left_c[0], right_c[0] + from_right_c[0]])
+    from_left_b = passed_along(right_b, "tile", 1)
+    from_right_b = passed_along(left_b, "tile", -1)
+    down_c, up_c, from_up_b, from_down_b, from_left_b, from_right_b = lax.optimization_barrier(
+        (down_c, up_c, from_up_b, from_down_b, from_left_b, from_right_b))
     from_up_c = passed_along(down_c, "row", 1)
     from_down_c = passed_along(up_c, "row", -1)
     mine, from_up_b, from_down_b, _, _ = lax.optimization_barrier(
         (mine, from_up_b, from_down_b, down_c, up_c))
-    given, right_b, left_b = lax.optimization_barrier((add_up(mine), right_b, left_b))
-    from_left_b = passed_along(right_b, "tile", 1)
-    from_right_b = passed_along(left_b, "tile", -1)
+    given = add_up(mine)
     sum_one = swap(given).reshape(current.shape)
     part = update(dims, edge, (old, middle, left_c, right_c, left_b, right_b, down_b, up_b,
                                from_left_c, from_right_c, from_up_b, from_down_b))
@@ -463,14 +465,16 @@
         (from_up_c, from_down_c, from_left_b, from_right_b),
         [(2, ncols // LANES, nrows, LANES), current.shape, (2, t, side, LANES),
          (2, t, nrows, LANES), (2, t, side, LANES), strip],
-        [current.shape], 52, "second_iteration")
-
-    given = add_up(swap(gprobe.reshape(devices, -1, LANES)))
-    given, right_c, right_ab, down_b = lax.optimization_barrier((given, right_c, right_ab, down_b))
+        [current.shape], 50, "second_iteration")
+
     from_left_c = passed_along(right_c, "tile", 1)
     above_b = passed_along(down_b, "row", 1)
+    mine = swap(gprobe.reshape(devices, -1, LANES))
+    down_a = down_a + from_left_c
+    above_a = passed_along(down_a, "row", 1)
+    mine, above_b, _ = lax.optimization_barrier((mine, above_b, down_a))
+    given, right_ab = lax.optimization_barrier((add_up(mine), right_ab))
     left_ab = passed_along(right_ab, "tile", 1)
-    above_a = passed_along(down_a + from_left_c, "row", 1)
     sum_two = swap(given).reshape(current.shape)
     object_out = simple(functools.partial(object_kernel, dims), object_field.shape, "last_object",
                         16, (own, left_ab, above_a, above_b))

time: 214 us -> 209 us (0.977)
  blocking collectives: 32.3 us -> 0 us
  starting transfers between devices: 72.3 us -> 84.5 us
  waiting for transfers between devices: 38.3 us -> 48.9 us
  Pallas kernels: 49.6 us -> 56.1 us
    all_to_all x1 -> x0, blocking collectives: 32.3 us -> none  [swap(): return lax.all_to_all(shares, ('tile', 'row'), 0, 0, tiled=True)]
    all_to_all x3 -> x4, waiting for transfers between devices: 13.9 us -> 31.3 us  [swap(): return lax.all_to_all(shares, ('tile', 'row'), 0, 0, tiled=True)]
    all_to_all x3 -> x4, starting transfers between devices: 28 us -> 41.6 us  [swap(): return lax.all_to_all(shares, ('tile', 'row'), 0, 0, tiled=True)]
    ppermute x17, waiting for transfers between devices: 24.5 us -> 17.6 us  [passed_along(): lax.ppermute(value, axis, [(source, source + steps) for source in range(f...]
    pallas_call x2, Pallas kernels: 34.5 us -> 40.6 us  [call(): pl.pallas_call(kernel, out_shape=[jax.ShapeDtypeStruct(shape, F32) for sh...]
    unnamed x44 -> x38, local copies, waits for them, and re-layouts: 6.41 us -> 5.28 us
  transfers between devices with their start and end apart: 20 -> 21, of which waited for: 7 -> 10; matrix products, arithmetic and copies ran while one was open for 5% -> 6% of each run, Pallas kernels for 6% -> 6%
where the time goes in v8:
time: 209 us; the launch traced here: 208 us
  starting transfers between devices  84.5 us (40%)
  Pallas kernels  56.1 us (27%)
  waiting for transfers between devices  48.9 us (23%)
  local copies, waits for them, and re-layouts  10.5 us (5%)
  other arithmetic  7.16 us (3%)
    ppermute x17, starting transfers between devices, passed_along(): lax.ppermute(value, axis, [(source, source + steps) for source in range(f...  42.9 us
    all_to_all x4, starting transfers between devices, swap(): return lax.all_to_all(shares, ('tile', 'row'), 0, 0, tiled=True)  41.6 us
    pallas_call x2, Pallas kernels, call(): pl.pallas_call(kernel, out_shape=[jax.ShapeDtypeStruct(shape, F32) for sh...  40.6 us
    all_to_all x4, waiting for transfers between devices, swap(): return lax.all_to_all(shares, ('tile', 'row'), 0, 0, tiled=True)  31.3 us
    ppermute x17, waiting for transfers between devices, passed_along(): lax.ppermute(value, axis, [(source, source + steps) for source in range(f...  17.6 us
    pallas_call x1, Pallas kernels, update(): pl.pallas_call(functools.partial(update_kernel, dims), out_shape=jax.Shap...  8.27 us
    unnamed x38, local copies, waits for them, and re-layouts  5.28 us
    pallas_call x2, Pallas kernels, simple(): pl.pallas_call(kernel, out_shape=jax.ShapeDtypeStruct(shape, F32), in_spe...  5.07 us
  transfers between devices with their start and end apart: 21, of which 10 were waited for; matrix products, arithmetic and copies ran while one was open for 6% of the time, Pallas kernels for 6%

profile of v8, /device:TPU:1, one launch (start us, length us, event | category | flops | bytes accessed | tf_op | source)
XLA Modules:
  0.0 208.0 jit_solution(15510559796485487320)
XLA Ops:
  0.6 1.9 slice.33
  2.5 1.3 collective-permute-start
  3.8 3.3 %collective-permute-start.2 = (f32[2,256,256]{2,1,0:T(8,128)}, f32[2,256,256]{2,1,0:T(8,128)S(1)}, u32[]{:S(2)}, u32[]{:S(2)}) collective-permute-start(f32[2,256,256]{2,1,0:T(8,128)} %slice.33), channel_id=1, source_target_pairs={{4,0},{8,4},{12,8},{16,12},{20,16},{24,20},{28,24},{32,28},{36,32}... | collective-permute-start | bytes 1572872 | tf_op jit(solution)/shard_map/ppermute | solution.py:22
  7.1 2.3 %fusion = (f32[2,256,256]{2,1,0:T(8,128)}, f32[2,256,256]{2,1,0:T(8,128)}) fusion(f32[2,512,512]{2,1,0:T(8,128)} %field.1), kind=kLoop, calls=%fused_computation.7 | loop fusion | bytes 2097152 | tf_op jit(solution)/shard_map/slice | solution.py:421
  9.4 1.9 collective-permute-start.3
  11.4 1.3 collective-permute-start.1
  12.7 5.3 %collective-permute-done.below_a = f32[2,256,256]{2,1,0:T(8,128)S(1)} collective-permute-done((f32[2,256,256]{2,1,0:T(8,128)}, f32[2,256,256]{2,1,0:T(8,128)S(1)}, u32[]{:S(2)}, u32[]{:S(2)}) %collective-permute-start) | collective-permute-done | bytes 524320 | tf_op jit(solution)/shard_map/ppermute | solution.py:22
  18.0 4.8 %collective-permute-start.4 = (f32[2,256,256]{2,1,0:T(8,128)S(1)}, f32[2,256,256]{2,1,0:T(8,128)S(1)}, u32[]{:S(2)}, u32[]{:S(2)}) collective-permute-start(f32[2,256,256]{2,1,0:T(8,128)S(1)} %collective-permute-done.below_a), channel_id=1, source_target_pairs={{4,0},{8,4},{12,8},{16,12},{20,16},{24,20},{28,24},{32,28},{36,32}... | collective-permute-start | bytes 1572872 | tf_op jit(solution)/shard_map/ppermute | solution.py:22
  23.4 1.2 copy.12
  24.7 1.0 copy.13
  25.7 3.5 %collective-permute-done.1.below_b = f32[2,256,256]{2,1,0:T(8,128)S(1)} collective-permute-done((f32[2,256,256]{2,1,0:T(8,128)}, f32[2,256,256]{2,1,0:T(8,128)S(1)}, u32[]{:S(2)}, u32[]{:S(2)}) %collective-permute-start.1) | collective-permute-done | bytes 524320 | tf_op jit(solution)/shard_map/ppermute | solution.py:22
  29.2 1.6 collective-permute-done.4.corner
  30.8 0.8 copy-done.16
  31.6 21.0 %first_iteration.1 = (f32[2,6,768,128]{3,2,1,0:T(8,128)}, f32[2,2,256,128]{3,2,1,0:T(8,128)}, f32[2,2,256,128]{3,2,1,0:T(8,128)}, f32[2,2,2,256,128]{4,3,2,1,0:T...) custom-call(s32[2,12]{1,0:T(2,128)} %batch.3, ...), custom_call_target="tpu_custom_call" | custom-call | tf_op jit(solution)/shard_map/first_iteration/pallas_call | solution.py:347
  52.6 1.9 collective-permute-start.5
  54.5 2.5 %collective-permute-start.6 = (f32[2,2,2,256,128]{4,3,2,1,0:T(8,128)}, f32[2,2,2,256,128]{4,3,2,1,0:T(8,128)}, u32[]{:S(2)}, u32[]{:S(2)}) collective-permute-start(f32[2,2,2,256,128]{4,3,2,1,0:T(8,128)} %get-tuple-element.40.left_c), channel_id=1, source_target_pairs={{4,0},{8,4},{12,8},{16,12},{20,16},{24,20},{28,24},{32,28},{36,32}... | collective-permute-start | bytes 3145736 | tf_op jit(solution)/shard_map/ppermute | solution.py:22
  57.0 11.5 %all-to-all-start = ((f32[128,8,128]{2,1,0:T(8,128)}), f32[128,8,128]{2,1,0:T(8,128)S(1)}, u32[]{:S(2)}, u32[]{:S(2)}) async-start(f32[128,8,128]{2,1,0:T(8,128)} %bitcast.14), calls=%async_computation | async-start | bytes 1048576 | tf_op jit(solution)/shard_map/all_to_all | solution.py:370
  68.5 4.1 %collective-permute-start.7 = (f32[2,2,256,128]{3,2,1,0:T(8,128)}, f32[2,2,256,128]{3,2,1,0:T(8,128)}, u32[]{:S(2)}, u32[]{:S(2)}) collective-permute-start(f32[2,2,256,128]{3,2,1,0:T(8,128)} %get-tuple-element.44.down_b), channel_id=1, source_target_pairs={{0,1},{1,2},{2,3},{4,5},{5,6},{6,7},{8,9},{9,10},{10,11},{12,13},{... | collective-permute-start | bytes 1572872 | tf_op jit(solution)/shard_map/ppermute | solution.py:22
  72.6 1.3 collective-permute-start.8
  73.9 3.6 %collective-permute-start.9 = (f32[2,2,256,128]{3,2,1,0:T(8,128)}, f32[2,2,256,128]{3,2,1,0:T(8,128)S(1)}, u32[]{:S(2)}, u32[]{:S(2)}) collective-permute-start(f32[2,2,256,128]{3,2,1,0:T(8,128)} %get-tuple-element.46.right_b), channel_id=1, source_target_pairs={{0,4},{4,8},{8,12},{12,16},{16,20},{20,24},{24,28},{28,32},{32,36}... | collective-permute-start | bytes 1572872 | tf_op jit(solution)/shard_map/ppermute | solution.py:22
  77.5 1.9 collective-permute-start.10
  79.4 3.7 %all-to-all-done.received = f32[128,8,128]{2,1,0:T(8,128)S(1)} async-done(((f32[128,8,128]{2,1,0:T(8,128)}), f32[128,8,128]{2,1,0:T(8,128)S(1)}, u32[]{:S(2)}, u32[]{:S(2)}) %all-to-all-start) | async-done | bytes 524320 | tf_op jit(solution)/shard_map/all_to_all | solution.py:370
  83.1 2.1 %slice_add_fusion = (f32[1,2,2,256,128]{4,3,2,1,0:T(8,128)S(1)}, f32[1,2,2,256,128]{4,3,2,1,0:T(8,128)S(1)}, f32[1,2,2,256,128]{4,3,2,1,0:T(8,128)S(1)}, f32[1,2,2,256,128]{4,3,2,1,0:T(8,128)S(1)}) fusion(f32[2,2,2,256,128]{4,3,2,1,0:T(8,128)} %collective-permute-done.6.from_right_c, f32[2,2,2,256,128]{4,3,2,1,0:T(8,128)} %get-tuple-element.39.right_c, ...), kind=kLoop, calls=%fused_computation.2 | loop fusion | flops 524288 | bytes 6291456 | tf_op jit(solution)/shard_map/add | solution.py:448
  85.3 1.1 pad_maximum_fusion.1
  86.4 1.1 pad_maximum_fusion
  88.6 3.9 %collective-permute-start.11 = (f32[2,2,2,256,128]{4,3,2,1,0:T(8,128)}, f32[2,2,2,256,128]{4,3,2,1,0:T(8,128)S(1)}, u32[]{:S(2)}, u32[]{:S(2)}) collective-permute-start(f32[2,2,2,256,128]{4,3,2,1,0:T(8,128)} %pad_maximum_fusion), channel_id=1, source_target_pairs={{0,1},{1,2},{2,3},{4,5},{5,6},{6,7},{8,9},{9,10},{10,11},{12,13},{... | collective-permute-start | bytes 3145736 | tf_op jit(solution)/shard_map/ppermute | solution.py:22
  92.5 1.3 collective-permute-start.12
  93.8 1.0 sum_shares.2
  94.8 12.6 %all-to-all-start.1 = ((f32[128,8,128]{2,1,0:T(8,128)}), f32[128,8,128]{2,1,0:T(8,128)S(1)}, u32[]{:S(2)}, u32[]{:S(2)}) async-start(f32[128,8,128]{2,1,0:T(8,128)} %sum_shares.2), calls=%async_computation.1 | async-start | bytes 1048576 | tf_op jit(solution)/shard_map/all_to_all | solution.py:370
  108.2 8.3 %update_object.1.part_in = f32[2,6,768,128]{3,2,1,0:T(8,128)} custom-call(s32[2]{0:T(128)} %add_convert_fusion.edge, f32[2,6,768,128]{3,2,1,0:T(8,128)} %get-tuple-element.53.old, f32[2,2,256,128]{3,2,1,0:T(8,128)} %get-tuple-element.54.middle, f32[2,2,2,256,128]{4,3,2,1,0:T(8,128)} %get-tuple-element.40.left_c, ...), custom_call_target="tpu_custom_call" | custom-call | tf_op jit(solution)/shard_map/update_object/pallas_call | solution.py:383
  116.5 11.6 %all-to-all-done.1 = f32[128,8,128]{2,1,0:T(8,128)S(1)} async-done(((f32[128,8,128]{2,1,0:T(8,128)}), f32[128,8,128]{2,1,0:T(8,128)S(1)}, u32[]{:S(2)}, u32[]{:S(2)}) %all-to-all-start.1) | async-done | bytes 524320 | tf_op jit(solution)/shard_map/all_to_all | solution.py:370
  128.0 1.0 copy-done.10
  129.0 19.6 %second_iteration.1 = (f32[2,4,512,128]{3,2,1,0:T(8,128)}, f32[2,2,256,128]{3,2,1,0:T(8,128)}, f32[2,2,256,128]{3,2,1,0:T(8,128)}, f32[2,2,512,128]{3,2,1,0:T(8,...) custom-call(s32[2,12]{1,0:T(2,128)S(1)} %copy-done.4, s32[2,1]{1,0:T(2,128)S(1)} %copy-done.5, ...), custom_call_target="tpu_custom_call" | custom-call | tf_op jit(solution)/shard_map/second_iteration/pallas_call | solution.py:347
  148.7 0.8 copy-done.3
  149.5 1.9 collective-permute-start.14
  151.4 2.1 %collective-permute-start.13 = (f32[2,2,256,128]{3,2,1,0:T(8,128)}, f32[2,2,256,128]{3,2,1,0:T(8,128)}, u32[]{:S(2)}, u32[]{:S(2)}) collective-permute-start(f32[2,2,256,128]{3,2,1,0:T(8,128)} %get-tuple-element.61), channel_id=1, source_target_pairs={{0,1},{1,2},{2,3},{4,5},{5,6},{6,7},{8,9},{9,10},{10,11},{12,13},{... | collective-permute-start | bytes 1572872 | tf_op jit(solution)/shard_map/ppermute | solution.py:22
  153.5 11.4 %all-to-all-start.2 = ((f32[128,8,128]{2,1,0:T(8,128)}), f32[128,8,128]{2,1,0:T(8,128)}, u32[]{:S(2)}, u32[]{:S(2)}) async-start(f32[128,8,128]{2,1,0:T(8,128)} %bitcast.6), calls=%async_computation.2 | async-start | bytes 1048576 | tf_op jit(solution)/shard_map/all_to_all | solution.py:370
  164.9 2.2 %add.23 = f32[2,2,256,128]{3,2,1,0:T(8,128)} add(f32[2,2,256,128]{3,2,1,0:T(8,128)} %copy-done.3, f32[2,2,256,128]{3,2,1,0:T(8,128)} %collective-permute-done.14) | non-fusion elementwise | flops 131072 | bytes 1572864 | tf_op jit(solution)/shard_map/add | solution.py:473
  167.1 11.2 %all-to-all-done.2.received = f32[128,8,128]{2,1,0:T(8,128)} async-done(((f32[128,8,128]{2,1,0:T(8,128)}), f32[128,8,128]{2,1,0:T(8,128)}, u32[]{:S(2)}, u32[]{:S(2)}) %all-to-all-start.2) | async-done | bytes 524320 | tf_op jit(solution)/shard_map/all_to_all | solution.py:370
  178.2 1.2 sum_shares.3
  179.5 0.8 copy-done.2
  180.3 2.7 %collective-permute-start.15 = (f32[2,2,512,128]{3,2,1,0:T(8,128)}, f32[2,2,512,128]{3,2,1,0:T(8,128)}, u32[]{:S(2)}, u32[]{:S(2)}) collective-permute-start(f32[2,2,512,128]{3,2,1,0:T(8,128)} %get-tuple-element.66), channel_id=1, source_target_pairs={{0,4},{4,8},{8,12},{12,16},{16,20},{20,24},{24,28},{28,32},{32,36}... | collective-permute-start | bytes 3145736 | tf_op jit(solution)/shard_map/ppermute | solution.py:22
  183.0 3.1 %collective-permute-start.16 = (f32[2,2,256,128]{3,2,1,0:T(8,128)}, f32[2,2,256,128]{3,2,1,0:T(8,128)}, u32[]{:S(2)}, u32[]{:S(2)}) collective-permute-start(f32[2,2,256,128]{3,2,1,0:T(8,128)} %add.23), channel_id=1, source_target_pairs={{0,1},{1,2},{2,3},{4,5},{5,6},{6,7},{8,9},{9,10},{10,11},{12,13},{... | collective-permute-start | bytes 1572872 | tf_op jit(solution)/shard_map/ppermute | solution.py:22
  186.0 6.1 %all-to-all-start.3 = ((f32[128,8,128]{2,1,0:T(8,128)}), f32[128,8,128]{2,1,0:T(8,128)}, u32[]{:S(2)}, u32[]{:S(2)}) async-start(f32[128,8,128]{2,1,0:T(8,128)} %copy-done.2), calls=%async_computation.3 | async-start | bytes 1048576 | tf_op jit(solution)/shard_map/all_to_all | solution.py:370
  192.1 6.0 %collective-permute-done.16.above_a = f32[2,2,256,128]{3,2,1,0:T(8,128)} collective-permute-done((f32[2,2,256,128]{3,2,1,0:T(8,128)}, f32[2,2,256,128]{3,2,1,0:T(8,128)}, u32[]{:S(2)}, u32[]{:S(2)}) %collective-permute-start.16) | collective-permute-done | bytes 524320 | tf_op jit(solution)/shard_map/ppermute | solution.py:22
  198.1 3.2 %last_object.1 = f32[2,512,512]{2,1,0:T(8,128)} custom-call(f32[2,4,512,128]{3,2,1,0:T(8,128)S(1)} %copy-done.1, f32[2,2,512,128]{3,2,1,0:T(8,128)} %collective-permute-done.15.left_ab, f32[2,2,256,128]{3,2,1,0:T(8,128)} %collective-permute-done.16.above_a, f32[2,2,256,128]{3,2,1,0:T(8,128)} %collective-permute-done.13.above_b), custom_call_target="tpu_custom_call" | custom-call | tf_op jit(solution)/shard_map/last_object/pallas_call | solution.py:397
  201.3 4.8 %all-to-all-done.3 = f32[128,8,128]{2,1,0:T(8,128)} async-done(((f32[128,8,128]{2,1,0:T(8,128)}), f32[128,8,128]{2,1,0:T(8,128)}, u32[]{:S(2)}, u32[]{:S(2)}) %all-to-all-start.3) | async-done | bytes 524320 | tf_op jit(solution)/shard_map/all_to_all | solution.py:370
  206.1 1.9 last_probe.1
  (47 shorter events, 2.6 us)
Async XLA Ops:
  0.6 22.1 %copy-start.17 = (s32[2,1]{0,1:T(1,128)S(1)}, s32[2,1]{0,1:T(1,128)}, u32[]{:S(2)}) copy-start(s32[2,1]{0,1:T(1,128)} %param.14) | copy-start | bytes 28
  2.5 15.5 %collective-permute-start = (f32[2,256,256]{2,1,0:T(8,128)}, f32[2,256,256]{2,1,0:T(8,128)S(1)}, u32[]{:S(2)}, u32[]{:S(2)}) collective-permute-start(f32[2,256,256]{2,1,0:T(8,128)} %slice.33), channel_id=1, source_target_pairs={{1,0},{2,1},{3,2},{5,4},{6,5},{7,6},{9,8},{10,9},{11,10},{13,12},{... | collective-permute-start | bytes 1572872 | tf_op jit(solution)/shard_map/ppermute | solution.py:22
  3.8 21.9 %collective-permute-start.2 = (f32[2,256,256]{2,1,0:T(8,128)}, f32[2,256,256]{2,1,0:T(8,128)S(1)}, u32[]{:S(2)}, u32[]{:S(2)}) collective-permute-start(f32[2,256,256]{2,1,0:T(8,128)} %slice.33), channel_id=1, source_target_pairs={{4,0},{8,4},{12,8},{16,12},{20,16},{24,20},{28,24},{32,28},{36,32}... | collective-permute-start | bytes 1572872 | tf_op jit(solution)/shard_map/ppermute | solution.py:22
  9.4 16.2 %collective-permute-start.3 = (f32[2,256,256]{2,1,0:T(8,128)}, f32[2,256,256]{2,1,0:T(8,128)S(1)}, u32[]{:S(2)}, u32[]{:S(2)}) collective-permute-start(f32[2,256,256]{2,1,0:T(8,128)} %get-tuple-element.74), channel_id=1, source_target_pairs={{4,0},{8,4},{12,8},{16,12},{20,16},{24,20},{28,24},{32,28},{36,32}... | collective-permute-start | bytes 1572872 | tf_op jit(solution)/shard_map/ppermute | solution.py:22
  11.4 17.9 %collective-permute-start.1 = (f32[2,256,256]{2,1,0:T(8,128)}, f32[2,256,256]{2,1,0:T(8,128)S(1)}, u32[]{:S(2)}, u32[]{:S(2)}) collective-permute-start(f32[2,256,256]{2,1,0:T(8,128)} %get-tuple-element.75), channel_id=1, source_target_pairs={{1,0},{2,1},{3,2},{5,4},{6,5},{7,6},{9,8},{10,9},{11,10},{13,12},{... | collective-permute-start | bytes 1572872 | tf_op jit(solution)/shard_map/ppermute | solution.py:22
  18.0 12.8 %copy-start.12 = (f32[2,256,256]{2,1,0:T(8,128)}, f32[2,256,256]{2,1,0:T(8,128)S(1)}, u32[]{:S(2)}) copy-start(f32[2,256,256]{2,1,0:T(8,128)S(1)} %collective-permute-done.below_a) | copy-start | bytes 1572868
  18.0 12.8 %collective-permute-start.4 = (f32[2,256,256]{2,1,0:T(8,128)S(1)}, f32[2,256,256]{2,1,0:T(8,128)S(1)}, u32[]{:S(2)}, u32[]{:S(2)}) collective-permute-start(f32[2,256,256]{2,1,0:T(8,128)S(1)} %collective-permute-done.below_a), channel_id=1, source_target_pairs={{4,0},{8,4},{12,8},{16,12},{20,16},{24,20},{28,24},{32,28},{36,32}... | collective-permute-start | bytes 1572872 | tf_op jit(solution)/shard_map/ppermute | solution.py:22
  25.7 5.1 %copy-start.13 = (f32[2,256,256]{2,1,0:T(8,128)}, f32[2,256,256]{2,1,0:T(8,128)S(1)}, u32[]{:S(2)}) copy-start(f32[2,256,256]{2,1,0:T(8,128)S(1)} %collective-permute-done.2.beside_a) | copy-start | bytes 1572868
  25.7 5.1 %copy-start.14 = (f32[2,256,256]{2,1,0:T(8,128)}, f32[2,256,256]{2,1,0:T(8,128)S(1)}, u32[]{:S(2)}) copy-start(f32[2,256,256]{2,1,0:T(8,128)S(1)} %collective-permute-done.3.beside_b) | copy-start | bytes 1572868
  29.2 1.6 copy-start.15
  30.8 0.8 copy-start.16
  52.6 24.9 %collective-permute-start.5 = (f32[2,2,2,256,128]{4,3,2,1,0:T(8,128)}, f32[2,2,2,256,128]{4,3,2,1,0:T(8,128)S(1)}, u32[]{:S(2)}, u32[]{:S(2)}) collective-permute-start(f32[2,2,2,256,128]{4,3,2,1,0:T(8,128)} %get-tuple-element.39.right_c), channel_id=1, source_target_pairs={{0,4},{4,8},{8,12},{12,16},{16,20},{20,24},{24,28},{28,32},{32,36}... | collective-permute-start | bytes 3145736 | tf_op jit(solution)/shard_map/ppermute | solution.py:22
  54.5 28.6 %collective-permute-start.6 = (f32[2,2,2,256,128]{4,3,2,1,0:T(8,128)}, f32[2,2,2,256,128]{4,3,2,1,0:T(8,128)}, u32[]{:S(2)}, u32[]{:S(2)}) collective-permute-start(f32[2,2,2,256,128]{4,3,2,1,0:T(8,128)} %get-tuple-element.40.left_c), channel_id=1, source_target_pairs={{4,0},{8,4},{12,8},{16,12},{20,16},{24,20},{28,24},{32,28},{36,32}... | collective-permute-start | bytes 3145736 | tf_op jit(solution)/shard_map/ppermute | solution.py:22
  57.0 26.2 %all-to-all-start = ((f32[128,8,128]{2,1,0:T(8,128)}), f32[128,8,128]{2,1,0:T(8,128)S(1)}, u32[]{:S(2)}, u32[]{:S(2)}) async-start(f32[128,8,128]{2,1,0:T(8,128)} %bitcast.14), calls=%async_computation | async-start | bytes 1048576 | tf_op jit(solution)/shard_map/all_to_all | solution.py:370
  68.5 19.0 %collective-permute-start.7 = (f32[2,2,256,128]{3,2,1,0:T(8,128)}, f32[2,2,256,128]{3,2,1,0:T(8,128)}, u32[]{:S(2)}, u32[]{:S(2)}) collective-permute-start(f32[2,2,256,128]{3,2,1,0:T(8,128)} %get-tuple-element.44.down_b), channel_id=1, source_target_pairs={{0,1},{1,2},{2,3},{4,5},{5,6},{6,7},{8,9},{9,10},{10,11},{12,13},{... | collective-permute-start | bytes 1572872 | tf_op jit(solution)/shard_map/ppermute | solution.py:22
  72.6 15.6 %collective-permute-start.8 = (f32[2,2,256,128]{3,2,1,0:T(8,128)}, f32[2,2,256,128]{3,2,1,0:T(8,128)}, u32[]{:S(2)}, u32[]{:S(2)}) collective-permute-start(f32[2,2,256,128]{3,2,1,0:T(8,128)} %get-tuple-element.45.up_b), channel_id=1, source_target_pairs={{1,0},{2,1},{3,2},{5,4},{6,5},{7,6},{9,8},{10,9},{11,10},{13,12},{... | collective-permute-start | bytes 1572872 | tf_op jit(solution)/shard_map/ppermute | solution.py:22
  73.9 14.3 %collective-permute-start.9 = (f32[2,2,256,128]{3,2,1,0:T(8,128)}, f32[2,2,256,128]{3,2,1,0:T(8,128)S(1)}, u32[]{:S(2)}, u32[]{:S(2)}) collective-permute-start(f32[2,2,256,128]{3,2,1,0:T(8,128)} %get-tuple-element.46.right_b), channel_id=1, source_target_pairs={{0,4},{4,8},{8,12},{12,16},{16,20},{20,24},{24,28},{28,32},{32,36}... | collective-permute-start | bytes 1572872 | tf_op jit(solution)/shard_map/ppermute | solution.py:22
  77.5 7.8 %copy-start.9 = (f32[2,2,2,256,128]{4,3,2,1,0:T(8,128)}, f32[2,2,2,256,128]{4,3,2,1,0:T(8,128)S(1)}, u32[]{:S(2)}) copy-start(f32[2,2,2,256,128]{4,3,2,1,0:T(8,128)S(1)} %collective-permute-done.5.from_left_c) | copy-start | bytes 3145732
  77.5 11.1 %collective-permute-start.10 = (f32[2,2,256,128]{3,2,1,0:T(8,128)}, f32[2,2,256,128]{3,2,1,0:T(8,128)S(1)}, u32[]{:S(2)}, u32[]{:S(2)}) collective-permute-start(f32[2,2,256,128]{3,2,1,0:T(8,128)} %get-tuple-element.47.left_b), channel_id=1, source_target_pairs={{4,0},{8,4},{12,8},{16,12},{20,16},{24,20},{28,24},{32,28},{36,32}... | collective-permute-start | bytes 1572872 | tf_op jit(solution)/shard_map/ppermute | solution.py:22
  88.6 27.8 %copy-start.11 = (f32[2,2,256,128]{3,2,1,0:T(8,128)}, f32[2,2,256,128]{3,2,1,0:T(8,128)S(1)}, u32[]{:S(2)}) copy-start(f32[2,2,256,128]{3,2,1,0:T(8,128)S(1)} %collective-permute-done.10.from_right) | copy-start | bytes 1572868
  88.6 39.4 %collective-permute-start.11 = (f32[2,2,2,256,128]{4,3,2,1,0:T(8,128)}, f32[2,2,2,256,128]{4,3,2,1,0:T(8,128)S(1)}, u32[]{:S(2)}, u32[]{:S(2)}) collective-permute-start(f32[2,2,2,256,128]{4,3,2,1,0:T(8,128)} %pad_maximum_fusion), channel_id=1, source_target_pairs={{0,1},{1,2},{2,3},{4,5},{5,6},{6,7},{8,9},{9,10},{10,11},{12,13},{... | collective-permute-start | bytes 3145736 | tf_op jit(solution)/shard_map/ppermute | solution.py:22
  92.5 35.5 %collective-permute-start.12 = (f32[2,2,2,256,128]{4,3,2,1,0:T(8,128)}, f32[2,2,2,256,128]{4,3,2,1,0:T(8,128)}, u32[]{:S(2)}, u32[]{:S(2)}) collective-permute-start(f32[2,2,2,256,128]{4,3,2,1,0:T(8,128)} %pad_maximum_fusion.1), channel_id=1, source_target_pairs={{1,0},{2,1},{3,2},{5,4},{6,5},{7,6},{9,8},{10,9},{11,10},{13,12},{... | collective-permute-start | bytes 3145736 | tf_op jit(solution)/shard_map/ppermute | solution.py:22
  94.8 33.2 %all-to-all-start.1 = ((f32[128,8,128]{2,1,0:T(8,128)}), f32[128,8,128]{2,1,0:T(8,128)S(1)}, u32[]{:S(2)}, u32[]{:S(2)}) async-start(f32[128,8,128]{2,1,0:T(8,128)} %sum_shares.2), calls=%async_computation.1 | async-start | bytes 1048576 | tf_op jit(solution)/shard_map/all_to_all | solution.py:370
  108.1 20.9 %copy-start = (f32[2,256,2,128]{3,1,2,0:T(8,128)S(1)}, f32[2,256,2,128]{3,1,2,0:T(8,128)}, u32[]{:S(2)}) copy-start(f32[2,256,2,128]{3,1,2,0:T(8,128)} %copy.13) | copy-start | bytes 1572868
  108.1 20.9 %copy-start.4 = (s32[2,12]{1,0:T(2,128)S(1)}, s32[2,12]{1,0:T(2,128)}, u32[]{:S(2)}) copy-start(s32[2,12]{1,0:T(2,128)} %batch.3) | copy-start | bytes 292
  108.1 20.9 %copy-start.5 = (s32[2,1]{1,0:T(2,128)S(1)}, s32[2,1]{1,0:T(2,128)}, u32[]{:S(2)}) copy-start(s32[2,1]{1,0:T(2,128)} %copy.15.live) | copy-start | bytes 28
  108.1 20.9 %copy-start.6 = (s32[2]{0:T(128)S(1)}, s32[2]{0:T(128)}, u32[]{:S(2)}) copy-start(s32[2]{0:T(128)} %add_convert_fusion.edge) | copy-start | bytes 28
  108.1 20.9 %copy-start.7 = (s32[32]{0:T(128)S(1)}, s32[32]{0:T(128)}, u32[]{:S(2)}) copy-start(s32[32]{0:T(128)} %rows.3) | copy-start | bytes 388
  108.2 20.9 %copy-start.8 = (s32[32]{0:T(128)S(1)}, s32[32]{0:T(128)}, u32[]{:S(2)}) copy-start(s32[32]{0:T(128)} %cols.3) | copy-start | bytes 388
  128.0 1.0 copy-start.10
  148.7 0.8 copy-start.3
  149.5 15.4 %collective-permute-start.14 = (f32[2,2,256,128]{3,2,1,0:T(8,128)}, f32[2,2,256,128]{3,2,1,0:T(8,128)}, u32[]{:S(2)}, u32[]{:S(2)}) collective-permute-start(f32[2,2,256,128]{3,2,1,0:T(8,128)} %get-tuple-element.63), channel_id=1, source_target_pairs={{0,4},{4,8},{8,12},{12,16},{16,20},{20,24},{24,28},{28,32},{32,36}... | collective-permute-start | bytes 1572872 | tf_op jit(solution)/shard_map/ppermute | solution.py:22
  151.4 26.9 %collective-permute-start.13 = (f32[2,2,256,128]{3,2,1,0:T(8,128)}, f32[2,2,256,128]{3,2,1,0:T(8,128)}, u32[]{:S(2)}, u32[]{:S(2)}) collective-permute-start(f32[2,2,256,128]{3,2,1,0:T(8,128)} %get-tuple-element.61), channel_id=1, source_target_pairs={{0,1},{1,2},{2,3},{4,5},{5,6},{6,7},{8,9},{9,10},{10,11},{12,13},{... | collective-permute-start | bytes 1572872 | tf_op jit(solution)/shard_map/ppermute | solution.py:22
  153.5 24.8 %all-to-all-start.2 = ((f32[128,8,128]{2,1,0:T(8,128)}), f32[128,8,128]{2,1,0:T(8,128)}, u32[]{:S(2)}, u32[]{:S(2)}) async-start(f32[128,8,128]{2,1,0:T(8,128)} %bitcast.6), calls=%async_computation.2 | async-start | bytes 1048576 | tf_op jit(solution)/shard_map/all_to_all | solution.py:370
  164.8 33.3 %copy-start.1 = (f32[2,4,512,128]{3,2,1,0:T(8,128)S(1)}, f32[2,4,512,128]{3,2,1,0:T(8,128)}, u32[]{:S(2)}) copy-start(f32[2,4,512,128]{3,2,1,0:T(8,128)} %get-tuple-element.59.own) | copy-start | bytes 6291460
  179.5 0.8 copy-start.2
  180.3 17.9 %collective-permute-start.15 = (f32[2,2,512,128]{3,2,1,0:T(8,128)}, f32[2,2,512,128]{3,2,1,0:T(8,128)}, u32[]{:S(2)}, u32[]{:S(2)}) collective-permute-start(f32[2,2,512,128]{3,2,1,0:T(8,128)} %get-tuple-element.66), channel_id=1, source_target_pairs={{0,4},{4,8},{8,12},{12,16},{16,20},{20,24},{24,28},{28,32},{32,36}... | collective-permute-start | bytes 3145736 | tf_op jit(solution)/shard_map/ppermute | solution.py:22
  183.0 15.2 %collective-permute-start.16 = (f32[2,2,256,128]{3,2,1,0:T(8,128)}, f32[2,2,256,128]{3,2,1,0:T(8,128)}, u32[]{:S(2)}, u32[]{:S(2)}) collective-permute-start(f32[2,2,256,128]{3,2,1,0:T(8,128)} %add.23), channel_id=1, source_target_pairs={{0,1},{1,2},{2,3},{4,5},{5,6},{6,7},{8,9},{9,10},{10,11},{12,13},{... | collective-permute-start | bytes 1572872 | tf_op jit(solution)/shard_map/ppermute | solution.py:22
  186.0 20.1 %all-to-all-start.3 = ((f32[128,8,128]{2,1,0:T(8,128)}), f32[128,8,128]{2,1,0:T(8,128)}, u32[]{:S(2)}, u32[]{:S(2)}) async-start(f32[128,8,128]{2,1,0:T(8,128)} %copy-done.2), calls=%async_computation.3 | async-start | bytes 1048576 | tf_op jit(solution)/shard_map/all_to_all | solution.py:370

commit v9 on v8

--- a/solution.py
+++ b/solution.py
@@ -446,15 +446,13 @@
     mine, from_left_c, from_right_c = lax.optimization_barrier((mine, from_left_c, from_right_c))
     down_c = jnp.stack([left_c[1] + from_left_c[1], right_c[1] + from_right_c[1]])
     up_c = jnp.stack([left_c[0] + from_left_c[0], right_c[0] + from_right_c[0]])
-    from_left_b = passed_along(right_b, "tile", 1)
-    from_right_b = passed_along(left_b, "tile", -1)
-    down_c, up_c, from_up_b, from_down_b, from_left_b, from_right_b = lax.optimization_barrier(
-        (down_c, up_c, from_up_b, from_down_b, from_left_b, from_right_b))
     from_up_c = passed_along(down_c, "row", 1)
     from_down_c = passed_along(up_c, "row", -1)
     mine, from_up_b, from_down_b, _, _ = lax.optimization_barrier(
         (mine, from_up_b, from_down_b, down_c, up_c))
-    given = add_up(mine)
+    given, right_b, left_b = lax.optimization_barrier((add_up(mine), right_b, left_b))
+    from_left_b = passed_along(right_b, "tile", 1)
+    from_right_b = passed_along(left_b, "tile", -1)
     sum_one = swap(given).reshape(current.shape)
     part = update(dims, edge, (old, middle, left_c, right_c, left_b, right_b, down_b, up_b,
                                from_left_c, from_right_c, from_up_b, from_down_b))

time: 209 us -> 206 us (0.986)
  starting transfers between devices: 84.5 us -> 96.2 us
  Pallas kernels: 56.1 us -> 45.2 us
  waiting for transfers between devices: 48.9 us -> 45.3 us
    ppermute x17, starting transfers between devices: 42.9 us -> 56.2 us  [passed_along(): lax.ppermute(value, axis, [(source, source + steps) for source in range(f...]
    pallas_call x2, Pallas kernels: 40.6 us -> 29.7 us  [call(): pl.pallas_call(kernel, out_shape=[jax.ShapeDtypeStruct(shape, F32) for sh...]
    all_to_all x4, waiting for transfers between devices: 31.3 us -> 28.2 us  [swap(): return lax.all_to_all(shares, ('tile', 'row'), 0, 0, tiled=True)]
    unnamed x38 -> x40, local copies, waits for them, and re-layouts: 5.28 us -> 5.27 us
  transfers between devices with their start and end apart: 21 -> 21, of which waited for: 10 -> 8; matrix products, arithmetic and copies ran while one was open for 6% -> 6% of each run, Pallas kernels for 6% -> 6%
where the time goes in v9:
time: 206 us
  starting transfers between devices  96.2 us (47%)
  waiting for transfers between devices  45.3 us (22%)
  Pallas kernels  45.2 us (22%)
  local copies, waits for them, and re-layouts  10.5 us (5%)
  other arithmetic  7.48 us (4%)
    ppermute x17, starting transfers between devices, passed_along(): lax.ppermute(value, axis, [(source, source + steps) for source in range(f...  56.2 us
    all_to_all x4, starting transfers between devices, swap(): return lax.all_to_all(shares, ('tile', 'row'), 0, 0, tiled=True)  40 us
    pallas_call x2, Pallas kernels, call(): pl.pallas_call(kernel, out_shape=[jax.ShapeDtypeStruct(shape, F32) for sh...  29.7 us
    all_to_all x4, waiting for transfers between devices, swap(): return lax.all_to_all(shares, ('tile', 'row'), 0, 0, tiled=True)  28.2 us
    ppermute x17, waiting for transfers between devices, passed_along(): lax.ppermute(value, axis, [(source, source + steps) for source in range(f...  17.1 us
    pallas_call x1, Pallas kernels, update(): pl.pallas_call(functools.partial(update_kernel, dims), out_shape=jax.Shap...  8.25 us
    unnamed x40, local copies, waits for them, and re-layouts  5.27 us
    pallas_call x2, Pallas kernels, simple(): pl.pallas_call(kernel, out_shape=jax.ShapeDtypeStruct(shape, F32), in_spe...  5.07 us
  transfers between devices with their start and end apart: 21, of which 8 were waited for; matrix products, arithmetic and copies ran while one was open for 6% of the time, Pallas kernels for 6%

profile of v9, /device:TPU:1, one launch (start us, length us, event | category | flops | bytes accessed | tf_op | source)
XLA Modules:
  0.0 205.7 jit_solution(8541696116020903507)
XLA Ops:
  0.6 1.9 slice.33
  2.5 1.3 collective-permute-start
  3.8 3.3 %collective-permute-start.2 = (f32[2,256,256]{2,1,0:T(8,128)}, f32[2,256,256]{2,1,0:T(8,128)S(1)}, u32[]{:S(2)}, u32[]{:S(2)}) collective-permute-start(f32[2,256,256]{2,1,0:T(8,128)} %slice.33), channel_id=1, source_target_pairs={{4,0},{8,4},{12,8},{16,12},{20,16},{24,20},{28,24},{32,28},{36,32}... | collective-permute-start | bytes 1572872 | tf_op jit(solution)/shard_map/ppermute | solution.py:22
  7.1 2.3 %fusion = (f32[2,256,256]{2,1,0:T(8,128)}, f32[2,256,256]{2,1,0:T(8,128)}) fusion(f32[2,512,512]{2,1,0:T(8,128)} %field.1), kind=kLoop, calls=%fused_computation.7 | loop fusion | bytes 2097152 | tf_op jit(solution)/shard_map/slice | solution.py:421
  9.5 1.3 collective-permute-start.1
  10.8 1.9 collective-permute-start.3
  12.7 5.3 %collective-permute-done.below_a = f32[2,256,256]{2,1,0:T(8,128)S(1)} collective-permute-done((f32[2,256,256]{2,1,0:T(8,128)}, f32[2,256,256]{2,1,0:T(8,128)S(1)}, u32[]{:S(2)}, u32[]{:S(2)}) %collective-permute-start) | collective-permute-done | bytes 524320 | tf_op jit(solution)/shard_map/ppermute | solution.py:22
  18.0 4.8 %collective-permute-start.4 = (f32[2,256,256]{2,1,0:T(8,128)S(1)}, f32[2,256,256]{2,1,0:T(8,128)S(1)}, u32[]{:S(2)}, u32[]{:S(2)}) collective-permute-start(f32[2,256,256]{2,1,0:T(8,128)S(1)} %collective-permute-done.below_a), channel_id=1, source_target_pairs={{4,0},{8,4},{12,8},{16,12},{20,16},{24,20},{28,24},{32,28},{36,32}... | collective-permute-start | bytes 1572872 | tf_op jit(solution)/shard_map/ppermute | solution.py:22
  23.5 1.2 copy.12
  24.7 1.0 copy.13
  25.7 3.5 %collective-permute-done.1.below_b = f32[2,256,256]{2,1,0:T(8,128)S(1)} collective-permute-done((f32[2,256,256]{2,1,0:T(8,128)}, f32[2,256,256]{2,1,0:T(8,128)S(1)}, u32[]{:S(2)}, u32[]{:S(2)}) %collective-permute-start.1) | collective-permute-done | bytes 524320 | tf_op jit(solution)/shard_map/ppermute | solution.py:22
  29.2 1.5 collective-permute-done.4.corner
  30.8 0.8 copy-done.17
  31.6 12.1 %first_iteration.1 = (f32[2,6,768,128]{3,2,1,0:T(8,128)}, f32[2,2,256,128]{3,2,1,0:T(8,128)}, f32[2,2,256,128]{3,2,1,0:T(8,128)}, f32[2,2,2,256,128]{4,3,2,1,0:T...) custom-call(s32[2,12]{1,0:T(2,128)} %batch.3, ...), custom_call_target="tpu_custom_call" | custom-call | tf_op jit(solution)/shard_map/first_iteration/pallas_call | solution.py:347
  43.7 12.5 %collective-permute-start.5 = (f32[2,2,2,256,128]{4,3,2,1,0:T(8,128)}, f32[2,2,2,256,128]{4,3,2,1,0:T(8,128)S(1)}, u32[]{:S(2)}, u32[]{:S(2)}) collective-permute-start(f32[2,2,2,256,128]{4,3,2,1,0:T(8,128)} %get-tuple-element.36.right_c), channel_id=1, source_target_pairs={{0,4},{4,8},{8,12},{12,16},{16,20},{20,24},{24,28},{28,32},{32,36}... | collective-permute-start | bytes 3145736 | tf_op jit(solution)/shard_map/ppermute | solution.py:22
  56.3 1.9 collective-permute-start.6
  58.2 10.3 %all-to-all-start = ((f32[128,8,128]{2,1,0:T(8,128)}), f32[128,8,128]{2,1,0:T(8,128)S(1)}, u32[]{:S(2)}, u32[]{:S(2)}) async-start(f32[128,8,128]{2,1,0:T(8,128)} %bitcast.14), calls=%async_computation | async-start | bytes 1048576 | tf_op jit(solution)/shard_map/all_to_all | solution.py:370
  68.5 4.1 %collective-permute-start.7 = (f32[2,2,256,128]{3,2,1,0:T(8,128)}, f32[2,2,256,128]{3,2,1,0:T(8,128)}, u32[]{:S(2)}, u32[]{:S(2)}) collective-permute-start(f32[2,2,256,128]{3,2,1,0:T(8,128)} %get-tuple-element.39.down_b), channel_id=1, source_target_pairs={{0,1},{1,2},{2,3},{4,5},{5,6},{6,7},{8,9},{9,10},{10,11},{12,13},{... | collective-permute-start | bytes 1572872 | tf_op jit(solution)/shard_map/ppermute | solution.py:22
  72.6 1.3 collective-permute-start.8
  73.9 8.2 %all-to-all-done.received = f32[128,8,128]{2,1,0:T(8,128)S(1)} async-done(((f32[128,8,128]{2,1,0:T(8,128)}), f32[128,8,128]{2,1,0:T(8,128)S(1)}, u32[]{:S(2)}, u32[]{:S(2)}) %all-to-all-start) | async-done | bytes 524320 | tf_op jit(solution)/shard_map/all_to_all | solution.py:370
  82.2 2.6 %slice_add_fusion = (f32[1,2,2,256,128]{4,3,2,1,0:T(8,128)S(1)}, f32[1,2,2,256,128]{4,3,2,1,0:T(8,128)S(1)}, f32[1,2,2,256,128]{4,3,2,1,0:T(8,128)S(1)}, f32[1,2,2,256,128]{4,3,2,1,0:T(8,128)S(1)}) fusion(f32[2,2,2,256,128]{4,3,2,1,0:T(8,128)S(1)} %collective-permute-done.6.from_right_c, f32[2,2,2,256,128]{4,3,2,1,0:T(8,128)} %get-tuple-element.36.right_c, ...), kind=kLoop, calls=%fused_computation.2 | loop fusion | flops 524288 | bytes 6291456 | tf_op jit(solution)/shard_map/add | solution.py:448
  84.7 1.0 pad_maximum_fusion
  85.8 2.7 %collective-permute-start.9 = (f32[2,2,2,256,128]{4,3,2,1,0:T(8,128)}, f32[2,2,2,256,128]{4,3,2,1,0:T(8,128)S(1)}, u32[]{:S(2)}, u32[]{:S(2)}) collective-permute-start(f32[2,2,2,256,128]{4,3,2,1,0:T(8,128)} %pad_maximum_fusion), channel_id=1, source_target_pairs={{0,1},{1,2},{2,3},{4,5},{5,6},{6,7},{8,9},{9,10},{10,11},{12,13},{... | collective-permute-start | bytes 3145736 | tf_op jit(solution)/shard_map/ppermute | solution.py:22
  88.5 1.1 pad_maximum_fusion.1
  89.6 1.3 collective-permute-start.10
  90.9 1.0 sum_shares.2
  91.8 4.3 %collective-permute-start.11 = (f32[2,2,256,128]{3,2,1,0:T(8,128)}, f32[2,2,256,128]{3,2,1,0:T(8,128)S(1)}, u32[]{:S(2)}, u32[]{:S(2)}) collective-permute-start(f32[2,2,256,128]{3,2,1,0:T(8,128)} %get-tuple-element.50.right_b), channel_id=1, source_target_pairs={{0,4},{4,8},{8,12},{12,16},{16,20},{20,24},{24,28},{28,32},{32,36}... | collective-permute-start | bytes 1572872 | tf_op jit(solution)/shard_map/ppermute | solution.py:22
  96.2 1.9 collective-permute-start.12
  98.1 11.3 %all-to-all-start.1 = ((f32[128,8,128]{2,1,0:T(8,128)}), f32[128,8,128]{2,1,0:T(8,128)S(1)}, u32[]{:S(2)}, u32[]{:S(2)}) async-start(f32[128,8,128]{2,1,0:T(8,128)} %sum_shares.2), calls=%async_computation.1 | async-start | bytes 1048576 | tf_op jit(solution)/shard_map/all_to_all | solution.py:370
  110.1 8.3 %update_object.1.part_in = f32[2,6,768,128]{3,2,1,0:T(8,128)} custom-call(s32[2]{0:T(128)} %add_convert_fusion.edge, f32[2,6,768,128]{3,2,1,0:T(8,128)} %get-tuple-element.47.old, f32[2,2,256,128]{3,2,1,0:T(8,128)} %get-tuple-element.48.middle, f32[2,2,2,256,128]{4,3,2,1,0:T(8,128)} %get-tuple-element.37.left_c, ...), custom_call_target="tpu_custom_call" | custom-call | tf_op jit(solution)/shard_map/update_object/pallas_call | solution.py:383
  118.4 4.9 %all-to-all-done.1 = f32[128,8,128]{2,1,0:T(8,128)S(1)} async-done(((f32[128,8,128]{2,1,0:T(8,128)}), f32[128,8,128]{2,1,0:T(8,128)S(1)}, u32[]{:S(2)}, u32[]{:S(2)}) %all-to-all-start.1) | async-done | bytes 524320 | tf_op jit(solution)/shard_map/all_to_all | solution.py:370
  123.3 0.9 copy-done.11
  124.2 17.6 %second_iteration.1 = (f32[2,4,512,128]{3,2,1,0:T(8,128)}, f32[2,2,256,128]{3,2,1,0:T(8,128)}, f32[2,2,256,128]{3,2,1,0:T(8,128)}, f32[2,2,512,128]{3,2,1,0:T(8,...) custom-call(s32[2,12]{1,0:T(2,128)S(1)} %copy-done.4, s32[2,1]{1,0:T(2,128)S(1)} %copy-done.5, ...), custom_call_target="tpu_custom_call" | custom-call | tf_op jit(solution)/shard_map/second_iteration/pallas_call | solution.py:347
  141.8 0.8 copy-done.3
  142.6 5.7 %collective-permute-start.14 = (f32[2,2,256,128]{3,2,1,0:T(8,128)}, f32[2,2,256,128]{3,2,1,0:T(8,128)}, u32[]{:S(2)}, u32[]{:S(2)}) collective-permute-start(f32[2,2,256,128]{3,2,1,0:T(8,128)} %get-tuple-element.57), channel_id=1, source_target_pairs={{0,4},{4,8},{8,12},{12,16},{16,20},{20,24},{24,28},{28,32},{32,36}... | collective-permute-start | bytes 1572872 | tf_op jit(solution)/shard_map/ppermute | solution.py:22
  148.3 2.1 %collective-permute-start.13 = (f32[2,2,256,128]{3,2,1,0:T(8,128)}, f32[2,2,256,128]{3,2,1,0:T(8,128)}, u32[]{:S(2)}, u32[]{:S(2)}) collective-permute-start(f32[2,2,256,128]{3,2,1,0:T(8,128)} %get-tuple-element.55), channel_id=1, source_target_pairs={{0,1},{1,2},{2,3},{4,5},{5,6},{6,7},{8,9},{9,10},{10,11},{12,13},{... | collective-permute-start | bytes 1572872 | tf_op jit(solution)/shard_map/ppermute | solution.py:22
  150.4 12.6 %all-to-all-start.2 = ((f32[128,8,128]{2,1,0:T(8,128)}), f32[128,8,128]{2,1,0:T(8,128)}, u32[]{:S(2)}, u32[]{:S(2)}) async-start(f32[128,8,128]{2,1,0:T(8,128)} %bitcast.6), calls=%async_computation.2 | async-start | bytes 1048576 | tf_op jit(solution)/shard_map/all_to_all | solution.py:370
  163.0 2.2 %add.23 = f32[2,2,256,128]{3,2,1,0:T(8,128)} add(f32[2,2,256,128]{3,2,1,0:T(8,128)} %copy-done.3, f32[2,2,256,128]{3,2,1,0:T(8,128)} %collective-permute-done.14) | non-fusion elementwise | flops 131072 | bytes 1572864 | tf_op jit(solution)/shard_map/add | solution.py:471
  165.2 11.2 %all-to-all-done.2.received = f32[128,8,128]{2,1,0:T(8,128)} async-done(((f32[128,8,128]{2,1,0:T(8,128)}), f32[128,8,128]{2,1,0:T(8,128)}, u32[]{:S(2)}, u32[]{:S(2)}) %all-to-all-start.2) | async-done | bytes 524320 | tf_op jit(solution)/shard_map/all_to_all | solution.py:370
  176.4 1.2 sum_shares.3
  177.7 0.8 copy-done.2
  178.4 2.7 %collective-permute-start.15 = (f32[2,2,512,128]{3,2,1,0:T(8,128)}, f32[2,2,512,128]{3,2,1,0:T(8,128)}, u32[]{:S(2)}, u32[]{:S(2)}) collective-permute-start(f32[2,2,512,128]{3,2,1,0:T(8,128)} %get-tuple-element.60), channel_id=1, source_target_pairs={{0,4},{4,8},{8,12},{12,16},{16,20},{20,24},{24,28},{28,32},{32,36}... | collective-permute-start | bytes 3145736 | tf_op jit(solution)/shard_map/ppermute | solution.py:22
  181.1 3.1 %collective-permute-start.16 = (f32[2,2,256,128]{3,2,1,0:T(8,128)}, f32[2,2,256,128]{3,2,1,0:T(8,128)}, u32[]{:S(2)}, u32[]{:S(2)}) collective-permute-start(f32[2,2,256,128]{3,2,1,0:T(8,128)} %add.23), channel_id=1, source_target_pairs={{0,1},{1,2},{2,3},{4,5},{5,6},{6,7},{8,9},{9,10},{10,11},{12,13},{... | collective-permute-start | bytes 1572872 | tf_op jit(solution)/shard_map/ppermute | solution.py:22
  184.2 5.8 %all-to-all-start.3 = ((f32[128,8,128]{2,1,0:T(8,128)}), f32[128,8,128]{2,1,0:T(8,128)}, u32[]{:S(2)}, u32[]{:S(2)}) async-start(f32[128,8,128]{2,1,0:T(8,128)} %copy-done.2), calls=%async_computation.3 | async-start | bytes 1048576 | tf_op jit(solution)/shard_map/all_to_all | solution.py:370
  190.0 6.6 %collective-permute-done.16.above_a = f32[2,2,256,128]{3,2,1,0:T(8,128)} collective-permute-done((f32[2,2,256,128]{3,2,1,0:T(8,128)}, f32[2,2,256,128]{3,2,1,0:T(8,128)}, u32[]{:S(2)}, u32[]{:S(2)}) %collective-permute-start.16) | collective-permute-done | bytes 524320 | tf_op jit(solution)/shard_map/ppermute | solution.py:22
  196.6 3.2 %last_object.1 = f32[2,512,512]{2,1,0:T(8,128)} custom-call(f32[2,4,512,128]{3,2,1,0:T(8,128)S(1)} %copy-done.1, f32[2,2,512,128]{3,2,1,0:T(8,128)} %collective-permute-done.15.left_ab, f32[2,2,256,128]{3,2,1,0:T(8,128)} %collective-permute-done.16.above_a, f32[2,2,256,128]{3,2,1,0:T(8,128)} %collective-permute-done.13.above_b), custom_call_target="tpu_custom_call" | custom-call | tf_op jit(solution)/shard_map/last_object/pallas_call | solution.py:397
  199.8 4.0 %all-to-all-done.3 = f32[128,8,128]{2,1,0:T(8,128)} async-done(((f32[128,8,128]{2,1,0:T(8,128)}), f32[128,8,128]{2,1,0:T(8,128)}, u32[]{:S(2)}, u32[]{:S(2)}) %all-to-all-start.3) | async-done | bytes 524320 | tf_op jit(solution)/shard_map/all_to_all | solution.py:370
  203.7 1.9 last_probe.1
  (49 shorter events, 1.4 us)
Async XLA Ops:
  0.6 22.1 %copy-start.18 = (s32[2,1]{0,1:T(1,128)S(1)}, s32[2,1]{0,1:T(1,128)}, u32[]{:S(2)}) copy-start(s32[2,1]{0,1:T(1,128)} %param.14) | copy-start | bytes 28
  2.5 15.5 %collective-permute-start = (f32[2,256,256]{2,1,0:T(8,128)}, f32[2,256,256]{2,1,0:T(8,128)S(1)}, u32[]{:S(2)}, u32[]{:S(2)}) collective-permute-start(f32[2,256,256]{2,1,0:T(8,128)} %slice.33), channel_id=1, source_target_pairs={{1,0},{2,1},{3,2},{5,4},{6,5},{7,6},{9,8},{10,9},{11,10},{13,12},{... | collective-permute-start | bytes 1572872 | tf_op jit(solution)/shard_map/ppermute | solution.py:22
  3.8 25.4 %collective-permute-start.2 = (f32[2,256,256]{2,1,0:T(8,128)}, f32[2,256,256]{2,1,0:T(8,128)S(1)}, u32[]{:S(2)}, u32[]{:S(2)}) collective-permute-start(f32[2,256,256]{2,1,0:T(8,128)} %slice.33), channel_id=1, source_target_pairs={{4,0},{8,4},{12,8},{16,12},{20,16},{24,20},{28,24},{32,28},{36,32}... | collective-permute-start | bytes 1572872 | tf_op jit(solution)/shard_map/ppermute | solution.py:22
  9.5 19.8 %collective-permute-start.1 = (f32[2,256,256]{2,1,0:T(8,128)}, f32[2,256,256]{2,1,0:T(8,128)S(1)}, u32[]{:S(2)}, u32[]{:S(2)}) collective-permute-start(f32[2,256,256]{2,1,0:T(8,128)} %get-tuple-element.69), channel_id=1, source_target_pairs={{1,0},{2,1},{3,2},{5,4},{6,5},{7,6},{9,8},{10,9},{11,10},{13,12},{... | collective-permute-start | bytes 1572872 | tf_op jit(solution)/shard_map/ppermute | solution.py:22
  10.8 18.5 %collective-permute-start.3 = (f32[2,256,256]{2,1,0:T(8,128)}, f32[2,256,256]{2,1,0:T(8,128)S(1)}, u32[]{:S(2)}, u32[]{:S(2)}) collective-permute-start(f32[2,256,256]{2,1,0:T(8,128)} %get-tuple-element.68), channel_id=1, source_target_pairs={{4,0},{8,4},{12,8},{16,12},{20,16},{24,20},{28,24},{32,28},{36,32}... | collective-permute-start | bytes 1572872 | tf_op jit(solution)/shard_map/ppermute | solution.py:22
  18.0 12.8 %copy-start.13 = (f32[2,256,256]{2,1,0:T(8,128)}, f32[2,256,256]{2,1,0:T(8,128)S(1)}, u32[]{:S(2)}) copy-start(f32[2,256,256]{2,1,0:T(8,128)S(1)} %collective-permute-done.below_a) | copy-start | bytes 1572868
  18.0 12.8 %collective-permute-start.4 = (f32[2,256,256]{2,1,0:T(8,128)S(1)}, f32[2,256,256]{2,1,0:T(8,128)S(1)}, u32[]{:S(2)}, u32[]{:S(2)}) collective-permute-start(f32[2,256,256]{2,1,0:T(8,128)S(1)} %collective-permute-done.below_a), channel_id=1, source_target_pairs={{4,0},{8,4},{12,8},{16,12},{20,16},{24,20},{28,24},{32,28},{36,32}... | collective-permute-start | bytes 1572872 | tf_op jit(solution)/shard_map/ppermute | solution.py:22
  29.2 1.6 copy-start.15
  29.2 1.6 copy-start.14
  29.2 1.6 copy-start.16
  30.8 0.8 copy-start.17
  43.7 38.4 %collective-permute-start.5 = (f32[2,2,2,256,128]{4,3,2,1,0:T(8,128)}, f32[2,2,2,256,128]{4,3,2,1,0:T(8,128)S(1)}, u32[]{:S(2)}, u32[]{:S(2)}) collective-permute-start(f32[2,2,2,256,128]{4,3,2,1,0:T(8,128)} %get-tuple-element.36.right_c), channel_id=1, source_target_pairs={{0,4},{4,8},{8,12},{12,16},{16,20},{20,24},{24,28},{28,32},{32,36}... | collective-permute-start | bytes 3145736 | tf_op jit(solution)/shard_map/ppermute | solution.py:22
  56.3 25.9 %collective-permute-start.6 = (f32[2,2,2,256,128]{4,3,2,1,0:T(8,128)}, f32[2,2,2,256,128]{4,3,2,1,0:T(8,128)S(1)}, u32[]{:S(2)}, u32[]{:S(2)}) collective-permute-start(f32[2,2,2,256,128]{4,3,2,1,0:T(8,128)} %get-tuple-element.37.left_c), channel_id=1, source_target_pairs={{4,0},{8,4},{12,8},{16,12},{20,16},{24,20},{28,24},{32,28},{36,32}... | collective-permute-start | bytes 3145736 | tf_op jit(solution)/shard_map/ppermute | solution.py:22
  58.2 23.9 %all-to-all-start = ((f32[128,8,128]{2,1,0:T(8,128)}), f32[128,8,128]{2,1,0:T(8,128)S(1)}, u32[]{:S(2)}, u32[]{:S(2)}) async-start(f32[128,8,128]{2,1,0:T(8,128)} %bitcast.14), calls=%async_computation | async-start | bytes 1048576 | tf_op jit(solution)/shard_map/all_to_all | solution.py:370
  68.5 22.4 %collective-permute-start.7 = (f32[2,2,256,128]{3,2,1,0:T(8,128)}, f32[2,2,256,128]{3,2,1,0:T(8,128)}, u32[]{:S(2)}, u32[]{:S(2)}) collective-permute-start(f32[2,2,256,128]{3,2,1,0:T(8,128)} %get-tuple-element.39.down_b), channel_id=1, source_target_pairs={{0,1},{1,2},{2,3},{4,5},{5,6},{6,7},{8,9},{9,10},{10,11},{12,13},{... | collective-permute-start | bytes 1572872 | tf_op jit(solution)/shard_map/ppermute | solution.py:22
  72.6 18.3 %collective-permute-start.8 = (f32[2,2,256,128]{3,2,1,0:T(8,128)}, f32[2,2,256,128]{3,2,1,0:T(8,128)}, u32[]{:S(2)}, u32[]{:S(2)}) collective-permute-start(f32[2,2,256,128]{3,2,1,0:T(8,128)} %get-tuple-element.40.up_b), channel_id=1, source_target_pairs={{1,0},{2,1},{3,2},{5,4},{6,5},{7,6},{9,8},{10,9},{11,10},{13,12},{... | collective-permute-start | bytes 1572872 | tf_op jit(solution)/shard_map/ppermute | solution.py:22
  82.1 2.6 %copy-start.9 = (f32[2,2,2,256,128]{4,3,2,1,0:T(8,128)}, f32[2,2,2,256,128]{4,3,2,1,0:T(8,128)S(1)}, u32[]{:S(2)}) copy-start(f32[2,2,2,256,128]{4,3,2,1,0:T(8,128)S(1)} %collective-permute-done.5.from_left_c) | copy-start | bytes 3145732
  82.1 2.6 %copy-start.10 = (f32[2,2,2,256,128]{4,3,2,1,0:T(8,128)}, f32[2,2,2,256,128]{4,3,2,1,0:T(8,128)S(1)}, u32[]{:S(2)}) copy-start(f32[2,2,2,256,128]{4,3,2,1,0:T(8,128)S(1)} %collective-permute-done.6.from_right_c) | copy-start | bytes 3145732
  85.8 10.4 %copy-start.12 = (f32[2,2,256,128]{3,2,1,0:T(8,128)S(1)}, f32[2,2,256,128]{3,2,1,0:T(8,128)}, u32[]{:S(2)}) copy-start(f32[2,2,256,128]{3,2,1,0:T(8,128)} %get-tuple-element.49.left_b) | copy-start | bytes 1572868
  85.8 37.5 %collective-permute-start.9 = (f32[2,2,2,256,128]{4,3,2,1,0:T(8,128)}, f32[2,2,2,256,128]{4,3,2,1,0:T(8,128)S(1)}, u32[]{:S(2)}, u32[]{:S(2)}) collective-permute-start(f32[2,2,2,256,128]{4,3,2,1,0:T(8,128)} %pad_maximum_fusion), channel_id=1, source_target_pairs={{0,1},{1,2},{2,3},{4,5},{5,6},{6,7},{8,9},{9,10},{10,11},{12,13},{... | collective-permute-start | bytes 3145736 | tf_op jit(solution)/shard_map/ppermute | solution.py:22
  89.6 33.7 %collective-permute-start.10 = (f32[2,2,2,256,128]{4,3,2,1,0:T(8,128)}, f32[2,2,2,256,128]{4,3,2,1,0:T(8,128)}, u32[]{:S(2)}, u32[]{:S(2)}) collective-permute-start(f32[2,2,2,256,128]{4,3,2,1,0:T(8,128)} %pad_maximum_fusion.1), channel_id=1, source_target_pairs={{1,0},{2,1},{3,2},{5,4},{6,5},{7,6},{9,8},{10,9},{11,10},{13,12},{... | collective-permute-start | bytes 3145736 | tf_op jit(solution)/shard_map/ppermute | solution.py:22
  91.8 31.4 %collective-permute-start.11 = (f32[2,2,256,128]{3,2,1,0:T(8,128)}, f32[2,2,256,128]{3,2,1,0:T(8,128)S(1)}, u32[]{:S(2)}, u32[]{:S(2)}) collective-permute-start(f32[2,2,256,128]{3,2,1,0:T(8,128)} %get-tuple-element.50.right_b), channel_id=1, source_target_pairs={{0,4},{4,8},{8,12},{12,16},{16,20},{20,24},{24,28},{28,32},{32,36}... | collective-permute-start | bytes 1572872 | tf_op jit(solution)/shard_map/ppermute | solution.py:22
  96.2 27.0 %collective-permute-start.12 = (f32[2,2,256,128]{3,2,1,0:T(8,128)S(1)}, f32[2,2,256,128]{3,2,1,0:T(8,128)}, u32[]{:S(2)}, u32[]{:S(2)}) collective-permute-start(f32[2,2,256,128]{3,2,1,0:T(8,128)S(1)} %copy-done.12), channel_id=1, source_target_pairs={{4,0},{8,4},{12,8},{16,12},{20,16},{24,20},{28,24},{32,28},{36,32}... | collective-permute-start | bytes 1572872 | tf_op jit(solution)/shard_map/ppermute | solution.py:22
  98.1 25.1 %all-to-all-start.1 = ((f32[128,8,128]{2,1,0:T(8,128)}), f32[128,8,128]{2,1,0:T(8,128)S(1)}, u32[]{:S(2)}, u32[]{:S(2)}) async-start(f32[128,8,128]{2,1,0:T(8,128)} %sum_shares.2), calls=%async_computation.1 | async-start | bytes 1048576 | tf_op jit(solution)/shard_map/all_to_all | solution.py:370
  110.1 14.1 %copy-start = (f32[2,256,2,128]{3,1,2,0:T(8,128)S(1)}, f32[2,256,2,128]{3,1,2,0:T(8,128)}, u32[]{:S(2)}) copy-start(f32[2,256,2,128]{3,1,2,0:T(8,128)} %copy.13) | copy-start | bytes 1572868
  110.1 14.1 %copy-start.4 = (s32[2,12]{1,0:T(2,128)S(1)}, s32[2,12]{1,0:T(2,128)}, u32[]{:S(2)}) copy-start(s32[2,12]{1,0:T(2,128)} %batch.3) | copy-start | bytes 292
  110.1 14.1 %copy-start.5 = (s32[2,1]{1,0:T(2,128)S(1)}, s32[2,1]{1,0:T(2,128)}, u32[]{:S(2)}) copy-start(s32[2,1]{1,0:T(2,128)} %copy.15.live) | copy-start | bytes 28
  110.1 14.1 %copy-start.6 = (s32[2]{0:T(128)S(1)}, s32[2]{0:T(128)}, u32[]{:S(2)}) copy-start(s32[2]{0:T(128)} %add_convert_fusion.edge) | copy-start | bytes 28
  110.1 14.1 %copy-start.7 = (s32[32]{0:T(128)S(1)}, s32[32]{0:T(128)}, u32[]{:S(2)}) copy-start(s32[32]{0:T(128)} %rows.3) | copy-start | bytes 388
  110.1 14.1 %copy-start.8 = (s32[32]{0:T(128)S(1)}, s32[32]{0:T(128)}, u32[]{:S(2)}) copy-start(s32[32]{0:T(128)} %cols.3) | copy-start | bytes 388
  123.2 1.0 copy-start.11
  141.8 0.8 copy-start.3
  142.6 20.4 %collective-permute-start.14 = (f32[2,2,256,128]{3,2,1,0:T(8,128)}, f32[2,2,256,128]{3,2,1,0:T(8,128)}, u32[]{:S(2)}, u32[]{:S(2)}) collective-permute-start(f32[2,2,256,128]{3,2,1,0:T(8,128)} %get-tuple-element.57), channel_id=1, source_target_pairs={{0,4},{4,8},{8,12},{12,16},{16,20},{20,24},{24,28},{28,32},{32,36}... | collective-permute-start | bytes 1572872 | tf_op jit(solution)/shard_map/ppermute | solution.py:22
  148.3 28.1 %collective-permute-start.13 = (f32[2,2,256,128]{3,2,1,0:T(8,128)}, f32[2,2,256,128]{3,2,1,0:T(8,128)}, u32[]{:S(2)}, u32[]{:S(2)}) collective-permute-start(f32[2,2,256,128]{3,2,1,0:T(8,128)} %get-tuple-element.55), channel_id=1, source_target_pairs={{0,1},{1,2},{2,3},{4,5},{5,6},{6,7},{8,9},{9,10},{10,11},{12,13},{... | collective-permute-start | bytes 1572872 | tf_op jit(solution)/shard_map/ppermute | solution.py:22
  150.4 26.0 %all-to-all-start.2 = ((f32[128,8,128]{2,1,0:T(8,128)}), f32[128,8,128]{2,1,0:T(8,128)}, u32[]{:S(2)}, u32[]{:S(2)}) async-start(f32[128,8,128]{2,1,0:T(8,128)} %bitcast.6), calls=%async_computation.2 | async-start | bytes 1048576 | tf_op jit(solution)/shard_map/all_to_all | solution.py:370
  163.0 33.6 %copy-start.1 = (f32[2,4,512,128]{3,2,1,0:T(8,128)S(1)}, f32[2,4,512,128]{3,2,1,0:T(8,128)}, u32[]{:S(2)}) copy-start(f32[2,4,512,128]{3,2,1,0:T(8,128)} %get-tuple-element.53.own) | copy-start | bytes 6291460
  177.6 0.8 copy-start.2
  178.4 18.2 %collective-permute-start.15 = (f32[2,2,512,128]{3,2,1,0:T(8,128)}, f32[2,2,512,128]{3,2,1,0:T(8,128)}, u32[]{:S(2)}, u32[]{:S(2)}) collective-permute-start(f32[2,2,512,128]{3,2,1,0:T(8,128)} %get-tuple-element.60), channel_id=1, source_target_pairs={{0,4},{4,8},{8,12},{12,16},{16,20},{20,24},{24,28},{28,32},{32,36}... | collective-permute-start | bytes 3145736 | tf_op jit(solution)/shard_map/ppermute | solution.py:22
  181.1 15.5 %collective-permute-start.16 = (f32[2,2,256,128]{3,2,1,0:T(8,128)}, f32[2,2,256,128]{3,2,1,0:T(8,128)}, u32[]{:S(2)}, u32[]{:S(2)}) collective-permute-start(f32[2,2,256,128]{3,2,1,0:T(8,128)} %add.23), channel_id=1, source_target_pairs={{0,1},{1,2},{2,3},{4,5},{5,6},{6,7},{8,9},{9,10},{10,11},{12,13},{... | collective-permute-start | bytes 1572872 | tf_op jit(solution)/shard_map/ppermute | solution.py:22
  184.2 19.5 %all-to-all-start.3 = ((f32[128,8,128]{2,1,0:T(8,128)}), f32[128,8,128]{2,1,0:T(8,128)}, u32[]{:S(2)}, u32[]{:S(2)}) async-start(f32[128,8,128]{2,1,0:T(8,128)} %copy-done.2), calls=%async_computation.3 | async-start | bytes 1048576 | tf_op jit(solution)/shard_map/all_to_all | solution.py:370

commit v10 on v9

--- a/solution.py
+++ b/solution.py
@@ -466,12 +466,12 @@
         [current.shape], 50, "second_iteration")
 
     from_left_c = passed_along(right_c, "tile", 1)
-    above_b = passed_along(down_b, "row", 1)
     mine = swap(gprobe.reshape(devices, -1, LANES))
     down_a = down_a + from_left_c
+    mine, down_a = lax.optimization_barrier((mine, down_a))
+    given, right_ab, down_b = lax.optimization_barrier((add_up(mine), right_ab, down_b))
     above_a = passed_along(down_a, "row", 1)
-    mine, above_b, _ = lax.optimization_barrier((mine, above_b, down_a))
-    given, right_ab = lax.optimization_barrier((add_up(mine), right_ab))
+    above_b = passed_along(down_b, "row", 1)
     left_ab = passed_along(right_ab, "tile", 1)
     sum_two = swap(given).reshape(current.shape)
     object_out = simple(functools.partial(object_kernel, dims), object_field.shape, "last_object",

time: 206 us -> 215 us (1.044)
  waiting for transfers between devices: 45.3 us -> 55.3 us
  starting transfers between devices: 96.2 us -> 87.3 us
  Pallas kernels: 45.2 us -> 51.6 us
    ppermute x17, starting transfers between devices: 56.2 us -> 44.9 us  [passed_along(): lax.ppermute(value, axis, [(source, source + steps) for source in range(f...]
    ppermute x17, waiting for transfers between devices: 17.1 us -> 28.1 us  [passed_along(): lax.ppermute(value, axis, [(source, source + steps) for source in range(f...]
    pallas_call x2, Pallas kernels: 29.7 us -> 36.1 us  [call(): pl.pallas_call(kernel, out_shape=[jax.ShapeDtypeStruct(shape, F32) for sh...]
    all_to_all x4, starting transfers between devices: 40 us -> 42.4 us  [swap(): return lax.all_to_all(shares, ('tile', 'row'), 0, 0, tiled=True)]
    unnamed x40 -> x42, local copies, waits for them, and re-layouts: 5.27 us -> 6.15 us
  transfers between devices with their start and end apart: 21 -> 21, of which waited for: 8 -> 9; matrix products, arithmetic and copies ran while one was open for 6% -> 6% of each run, Pallas kernels for 6% -> 6%
where the time goes in v10:
time: 215 us; the launch traced here: 214 us
  starting transfers between devices  87.3 us (41%)
  waiting for transfers between devices  55.3 us (26%)
  Pallas kernels  51.6 us (24%)
  local copies, waits for them, and re-layouts  11.3 us (5%)
  other arithmetic  7.51 us (3%)
    ppermute x17, starting transfers between devices, passed_along(): lax.ppermute(value, axis, [(source, source + steps) for source in range(f...  44.9 us
    all_to_all x4, starting transfers between devices, swap(): return lax.all_to_all(shares, ('tile', 'row'), 0, 0, tiled=True)  42.4 us
    pallas_call x2, Pallas kernels, call(): pl.pallas_call(kernel, out_shape=[jax.ShapeDtypeStruct(shape, F32) for sh...  36.1 us
    ppermute x17, waiting for transfers between devices, passed_along(): lax.ppermute(value, axis, [(source, source + steps) for source in range(f...  28.1 us
    all_to_all x4, waiting for transfers between devices, swap(): return lax.all_to_all(shares, ('tile', 'row'), 0, 0, tiled=True)  27.2 us
    pallas_call x1, Pallas kernels, update(): pl.pallas_call(functools.partial(update_kernel, dims), out_shape=jax.Shap...  8.25 us
    unnamed x42, local copies, waits for them, and re-layouts  6.15 us
    pallas_call x2, Pallas kernels, simple(): pl.pallas_call(kernel, out_shape=jax.ShapeDtypeStruct(shape, F32), in_spe...  5.07 us
  transfers between devices with their start and end apart: 21, of which 9 were waited for; matrix products, arithmetic and copies ran while one was open for 6% of the time, Pallas kernels for 6%

profile of v10, /device:TPU:1, one launch (start us, length us, event | category | flops | bytes accessed | tf_op | source)
XLA Modules:
  0.0 214.0 jit_solution(16146508330783431498)
XLA Ops:
  0.6 1.9 slice.33
  2.5 1.3 collective-permute-start
  3.8 3.3 %collective-permute-start.2 = (f32[2,256,256]{2,1,0:T(8,128)}, f32[2,256,256]{2,1,0:T(8,128)S(1)}, u32[]{:S(2)}, u32[]{:S(2)}) collective-permute-start(f32[2,256,256]{2,1,0:T(8,128)} %slice.33), channel_id=1, source_target_pairs={{4,0},{8,4},{12,8},{16,12},{20,16},{24,20},{28,24},{32,28},{36,32}... | collective-permute-start | bytes 1572872 | tf_op jit(solution)/shard_map/ppermute | solution.py:22
  7.1 2.3 %fusion = (f32[2,256,256]{2,1,0:T(8,128)}, f32[2,256,256]{2,1,0:T(8,128)}) fusion(f32[2,512,512]{2,1,0:T(8,128)} %field.1), kind=kLoop, calls=%fused_computation.7 | loop fusion | bytes 2097152 | tf_op jit(solution)/shard_map/slice | solution.py:421
  9.5 1.3 collective-permute-start.1
  10.7 1.9 collective-permute-start.3
  12.7 5.3 %collective-permute-done.below_a = f32[2,256,256]{2,1,0:T(8,128)S(1)} collective-permute-done((f32[2,256,256]{2,1,0:T(8,128)}, f32[2,256,256]{2,1,0:T(8,128)S(1)}, u32[]{:S(2)}, u32[]{:S(2)}) %collective-permute-start) | collective-permute-done | bytes 524320 | tf_op jit(solution)/shard_map/ppermute | solution.py:22
  18.0 4.8 %collective-permute-start.4 = (f32[2,256,256]{2,1,0:T(8,128)S(1)}, f32[2,256,256]{2,1,0:T(8,128)S(1)}, u32[]{:S(2)}, u32[]{:S(2)}) collective-permute-start(f32[2,256,256]{2,1,0:T(8,128)S(1)} %collective-permute-done.below_a), channel_id=1, source_target_pairs={{4,0},{8,4},{12,8},{16,12},{20,16},{24,20},{28,24},{32,28},{36,32}... | collective-permute-start | bytes 1572872 | tf_op jit(solution)/shard_map/ppermute | solution.py:22
  23.5 1.2 copy.12
  24.7 1.0 copy.13
  25.7 3.5 %collective-permute-done.1.below_b = f32[2,256,256]{2,1,0:T(8,128)S(1)} collective-permute-done((f32[2,256,256]{2,1,0:T(8,128)}, f32[2,256,256]{2,1,0:T(8,128)S(1)}, u32[]{:S(2)}, u32[]{:S(2)}) %collective-permute-start.1) | collective-permute-done | bytes 524320 | tf_op jit(solution)/shard_map/ppermute | solution.py:22
  29.2 1.5 collective-permute-done.4.corner
  31.6 14.4 %first_iteration.1 = (f32[2,6,768,128]{3,2,1,0:T(8,128)}, f32[2,2,256,128]{3,2,1,0:T(8,128)}, f32[2,2,256,128]{3,2,1,0:T(8,128)}, f32[2,2,2,256,128]{4,3,2,1,0:T...) custom-call(s32[2,12]{1,0:T(2,128)} %batch.3, ...), custom_call_target="tpu_custom_call" | custom-call | tf_op jit(solution)/shard_map/first_iteration/pallas_call | solution.py:347
  46.0 3.8 %collective-permute-start.5 = (f32[2,2,2,256,128]{4,3,2,1,0:T(8,128)}, f32[2,2,2,256,128]{4,3,2,1,0:T(8,128)S(1)}, u32[]{:S(2)}, u32[]{:S(2)}) collective-permute-start(f32[2,2,2,256,128]{4,3,2,1,0:T(8,128)} %get-tuple-element.37.right_c), channel_id=1, source_target_pairs={{0,4},{4,8},{8,12},{12,16},{16,20},{20,24},{24,28},{28,32},{32,36}... | collective-permute-start | bytes 3145736 | tf_op jit(solution)/shard_map/ppermute | solution.py:22
  49.7 2.2 %collective-permute-start.6 = (f32[2,2,2,256,128]{4,3,2,1,0:T(8,128)}, f32[2,2,2,256,128]{4,3,2,1,0:T(8,128)S(1)}, u32[]{:S(2)}, u32[]{:S(2)}) collective-permute-start(f32[2,2,2,256,128]{4,3,2,1,0:T(8,128)} %get-tuple-element.38.left_c), channel_id=1, source_target_pairs={{4,0},{8,4},{12,8},{16,12},{20,16},{24,20},{28,24},{32,28},{36,32}... | collective-permute-start | bytes 3145736 | tf_op jit(solution)/shard_map/ppermute | solution.py:22
  52.0 16.6 %all-to-all-start = ((f32[128,8,128]{2,1,0:T(8,128)}), f32[128,8,128]{2,1,0:T(8,128)S(1)}, u32[]{:S(2)}, u32[]{:S(2)}) async-start(f32[128,8,128]{2,1,0:T(8,128)} %bitcast.14), calls=%async_computation | async-start | bytes 1048576 | tf_op jit(solution)/shard_map/all_to_all | solution.py:370
  68.5 4.1 %collective-permute-start.7 = (f32[2,2,256,128]{3,2,1,0:T(8,128)}, f32[2,2,256,128]{3,2,1,0:T(8,128)}, u32[]{:S(2)}, u32[]{:S(2)}) collective-permute-start(f32[2,2,256,128]{3,2,1,0:T(8,128)} %get-tuple-element.40.down_b), channel_id=1, source_target_pairs={{0,1},{1,2},{2,3},{4,5},{5,6},{6,7},{8,9},{9,10},{10,11},{12,13},{... | collective-permute-start | bytes 1572872 | tf_op jit(solution)/shard_map/ppermute | solution.py:22
  72.7 1.3 collective-permute-start.8
  73.9 8.9 %all-to-all-done.received = f32[128,8,128]{2,1,0:T(8,128)S(1)} async-done(((f32[128,8,128]{2,1,0:T(8,128)}), f32[128,8,128]{2,1,0:T(8,128)S(1)}, u32[]{:S(2)}, u32[]{:S(2)}) %all-to-all-start) | async-done | bytes 524320 | tf_op jit(solution)/shard_map/all_to_all | solution.py:370
  82.9 2.6 %slice_add_fusion = (f32[1,2,2,256,128]{4,3,2,1,0:T(8,128)S(1)}, f32[1,2,2,256,128]{4,3,2,1,0:T(8,128)S(1)}, f32[1,2,2,256,128]{4,3,2,1,0:T(8,128)S(1)}, f32[1,2,2,256,128]{4,3,2,1,0:T(8,128)S(1)}) fusion(f32[2,2,2,256,128]{4,3,2,1,0:T(8,128)S(1)} %collective-permute-done.6.from_right_c, f32[2,2,2,256,128]{4,3,2,1,0:T(8,128)} %get-tuple-element.37.right_c, ...), kind=kLoop, calls=%fused_computation.2 | loop fusion | flops 524288 | bytes 6291456 | tf_op jit(solution)/shard_map/add | solution.py:448
  85.5 1.0 pad_maximum_fusion
  86.5 2.0 collective-permute-start.9
  88.5 1.1 pad_maximum_fusion.1
  89.6 1.3 collective-permute-start.10
  90.9 1.0 sum_shares.2
  91.9 4.6 %collective-permute-start.11 = (f32[2,2,256,128]{3,2,1,0:T(8,128)}, f32[2,2,256,128]{3,2,1,0:T(8,128)S(1)}, u32[]{:S(2)}, u32[]{:S(2)}) collective-permute-start(f32[2,2,256,128]{3,2,1,0:T(8,128)} %get-tuple-element.51.right_b), channel_id=1, source_target_pairs={{0,4},{4,8},{8,12},{12,16},{16,20},{20,24},{24,28},{28,32},{32,36}... | collective-permute-start | bytes 1572872 | tf_op jit(solution)/shard_map/ppermute | solution.py:22
  96.5 1.9 collective-permute-start.12
  98.5 10.5 %all-to-all-start.1 = ((f32[128,8,128]{2,1,0:T(8,128)}), f32[128,8,128]{2,1,0:T(8,128)S(1)}, u32[]{:S(2)}, u32[]{:S(2)}) async-start(f32[128,8,128]{2,1,0:T(8,128)} %sum_shares.2), calls=%async_computation.1 | async-start | bytes 1048576 | tf_op jit(solution)/shard_map/all_to_all | solution.py:370
  109.6 8.2 %update_object.1.part_in = f32[2,6,768,128]{3,2,1,0:T(8,128)} custom-call(s32[2]{0:T(128)} %add_convert_fusion.edge, f32[2,6,768,128]{3,2,1,0:T(8,128)} %get-tuple-element.48.old, f32[2,2,256,128]{3,2,1,0:T(8,128)} %get-tuple-element.49.middle, f32[2,2,2,256,128]{4,3,2,1,0:T(8,128)} %get-tuple-element.38.left_c, ...), custom_call_target="tpu_custom_call" | custom-call | tf_op jit(solution)/shard_map/update_object/pallas_call | solution.py:383
  117.8 4.9 %all-to-all-done.1 = f32[128,8,128]{2,1,0:T(8,128)S(1)} async-done(((f32[128,8,128]{2,1,0:T(8,128)}), f32[128,8,128]{2,1,0:T(8,128)S(1)}, u32[]{:S(2)}, u32[]{:S(2)}) %all-to-all-start.1) | async-done | bytes 524320 | tf_op jit(solution)/shard_map/all_to_all | solution.py:370
  122.7 1.0 copy-done.12
  123.7 21.7 %second_iteration.1 = (f32[2,4,512,128]{3,2,1,0:T(8,128)}, f32[2,2,256,128]{3,2,1,0:T(8,128)}, f32[2,2,256,128]{3,2,1,0:T(8,128)}, f32[2,2,512,128]{3,2,1,0:T(8,...) custom-call(s32[2,12]{1,0:T(2,128)S(1)} %copy-done.4, s32[2,1]{1,0:T(2,128)S(1)} %copy-done.5, ...), custom_call_target="tpu_custom_call" | custom-call | tf_op jit(solution)/shard_map/second_iteration/pallas_call | solution.py:347
  145.5 0.8 copy-done.3
  146.3 0.8 copy-done.9
  147.1 3.1 %collective-permute-start.13 = (f32[2,2,256,128]{3,2,1,0:T(8,128)}, f32[2,2,256,128]{3,2,1,0:T(8,128)}, u32[]{:S(2)}, u32[]{:S(2)}) collective-permute-start(f32[2,2,256,128]{3,2,1,0:T(8,128)} %get-tuple-element.57), channel_id=1, source_target_pairs={{0,4},{4,8},{8,12},{12,16},{16,20},{20,24},{24,28},{28,32},{32,36}... | collective-permute-start | bytes 1572872 | tf_op jit(solution)/shard_map/ppermute | solution.py:22
  150.2 10.0 %all-to-all-start.2 = ((f32[128,8,128]{2,1,0:T(8,128)}), f32[128,8,128]{2,1,0:T(8,128)}, u32[]{:S(2)}, u32[]{:S(2)}) async-start(f32[128,8,128]{2,1,0:T(8,128)} %bitcast.6), calls=%async_computation.2 | async-start | bytes 1048576 | tf_op jit(solution)/shard_map/all_to_all | solution.py:370
  160.2 2.2 %add.23 = f32[2,2,256,128]{3,2,1,0:T(8,128)} add(f32[2,2,256,128]{3,2,1,0:T(8,128)} %copy-done.3, f32[2,2,256,128]{3,2,1,0:T(8,128)} %collective-permute-done.13) | non-fusion elementwise | flops 131072 | bytes 1572864 | tf_op jit(solution)/shard_map/add | solution.py:470
  162.4 11.2 %all-to-all-done.2.received = f32[128,8,128]{2,1,0:T(8,128)} async-done(((f32[128,8,128]{2,1,0:T(8,128)}), f32[128,8,128]{2,1,0:T(8,128)}, u32[]{:S(2)}, u32[]{:S(2)}) %all-to-all-start.2) | async-done | bytes 524320 | tf_op jit(solution)/shard_map/all_to_all | solution.py:370
  173.6 1.2 sum_shares.3
  175.6 2.7 %collective-permute-start.14 = (f32[2,2,512,128]{3,2,1,0:T(8,128)}, f32[2,2,512,128]{3,2,1,0:T(8,128)}, u32[]{:S(2)}, u32[]{:S(2)}) collective-permute-start(f32[2,2,512,128]{3,2,1,0:T(8,128)} %get-tuple-element.61), channel_id=1, source_target_pairs={{0,4},{4,8},{8,12},{12,16},{16,20},{20,24},{24,28},{28,32},{32,36}... | collective-permute-start | bytes 3145736 | tf_op jit(solution)/shard_map/ppermute | solution.py:22
  178.3 3.1 %collective-permute-start.15 = (f32[2,2,256,128]{3,2,1,0:T(8,128)}, f32[2,2,256,128]{3,2,1,0:T(8,128)}, u32[]{:S(2)}, u32[]{:S(2)}) collective-permute-start(f32[2,2,256,128]{3,2,1,0:T(8,128)} %add.23), channel_id=1, source_target_pairs={{0,1},{1,2},{2,3},{4,5},{5,6},{6,7},{8,9},{9,10},{10,11},{12,13},{... | collective-permute-start | bytes 1572872 | tf_op jit(solution)/shard_map/ppermute | solution.py:22
  181.3 2.3 %collective-permute-start.16 = (f32[2,2,256,128]{3,2,1,0:T(8,128)}, f32[2,2,256,128]{3,2,1,0:T(8,128)}, u32[]{:S(2)}, u32[]{:S(2)}) collective-permute-start(f32[2,2,256,128]{3,2,1,0:T(8,128)} %copy-done.9), channel_id=1, source_target_pairs={{0,1},{1,2},{2,3},{4,5},{5,6},{6,7},{8,9},{9,10},{10,11},{12,13},{... | collective-permute-start | bytes 1572872 | tf_op jit(solution)/shard_map/ppermute | solution.py:22
  183.7 5.4 %all-to-all-start.3 = ((f32[128,8,128]{2,1,0:T(8,128)}), f32[128,8,128]{2,1,0:T(8,128)}, u32[]{:S(2)}, u32[]{:S(2)}) async-start(f32[128,8,128]{2,1,0:T(8,128)} %copy-done.2), calls=%async_computation.3 | async-start | bytes 1048576 | tf_op jit(solution)/shard_map/all_to_all | solution.py:370
  189.0 2.4 %collective-permute-done.15.above_a = f32[2,2,256,128]{3,2,1,0:T(8,128)} collective-permute-done((f32[2,2,256,128]{3,2,1,0:T(8,128)}, f32[2,2,256,128]{3,2,1,0:T(8,128)}, u32[]{:S(2)}, u32[]{:S(2)}) %collective-permute-start.15) | collective-permute-done | bytes 524320 | tf_op jit(solution)/shard_map/ppermute | solution.py:22
  191.5 15.2 %collective-permute-done.16.above_b = f32[2,2,256,128]{3,2,1,0:T(8,128)} collective-permute-done((f32[2,2,256,128]{3,2,1,0:T(8,128)}, f32[2,2,256,128]{3,2,1,0:T(8,128)}, u32[]{:S(2)}, u32[]{:S(2)}) %collective-permute-start.16) | collective-permute-done | bytes 524320 | tf_op jit(solution)/shard_map/ppermute | solution.py:22
  206.7 3.2 %last_object.1 = f32[2,512,512]{2,1,0:T(8,128)} custom-call(f32[2,4,512,128]{3,2,1,0:T(8,128)S(1)} %copy-done.1, f32[2,2,512,128]{3,2,1,0:T(8,128)} %collective-permute-done.14.left_ab, f32[2,2,256,128]{3,2,1,0:T(8,128)} %collective-permute-done.15.above_a, f32[2,2,256,128]{3,2,1,0:T(8,128)} %collective-permute-done.16.above_b), custom_call_target="tpu_custom_call" | custom-call | tf_op jit(solution)/shard_map/last_object/pallas_call | solution.py:397
  209.9 2.3 %all-to-all-done.3 = f32[128,8,128]{2,1,0:T(8,128)} async-done(((f32[128,8,128]{2,1,0:T(8,128)}), f32[128,8,128]{2,1,0:T(8,128)}, u32[]{:S(2)}, u32[]{:S(2)}) %all-to-all-start.3) | async-done | bytes 524320 | tf_op jit(solution)/shard_map/all_to_all | solution.py:370
  212.1 1.9 last_probe.1
  (51 shorter events, 2.9 us)
Async XLA Ops:
  0.6 22.1 %copy-start.19 = (s32[2,1]{0,1:T(1,128)S(1)}, s32[2,1]{0,1:T(1,128)}, u32[]{:S(2)}) copy-start(s32[2,1]{0,1:T(1,128)} %param.14) | copy-start | bytes 28
  2.5 15.5 %collective-permute-start = (f32[2,256,256]{2,1,0:T(8,128)}, f32[2,256,256]{2,1,0:T(8,128)S(1)}, u32[]{:S(2)}, u32[]{:S(2)}) collective-permute-start(f32[2,256,256]{2,1,0:T(8,128)} %slice.33), channel_id=1, source_target_pairs={{1,0},{2,1},{3,2},{5,4},{6,5},{7,6},{9,8},{10,9},{11,10},{13,12},{... | collective-permute-start | bytes 1572872 | tf_op jit(solution)/shard_map/ppermute | solution.py:22
  3.8 25.4 %collective-permute-start.2 = (f32[2,256,256]{2,1,0:T(8,128)}, f32[2,256,256]{2,1,0:T(8,128)S(1)}, u32[]{:S(2)}, u32[]{:S(2)}) collective-permute-start(f32[2,256,256]{2,1,0:T(8,128)} %slice.33), channel_id=1, source_target_pairs={{4,0},{8,4},{12,8},{16,12},{20,16},{24,20},{28,24},{32,28},{36,32}... | collective-permute-start | bytes 1572872 | tf_op jit(solution)/shard_map/ppermute | solution.py:22
  9.5 19.8 %collective-permute-start.1 = (f32[2,256,256]{2,1,0:T(8,128)}, f32[2,256,256]{2,1,0:T(8,128)S(1)}, u32[]{:S(2)}, u32[]{:S(2)}) collective-permute-start(f32[2,256,256]{2,1,0:T(8,128)} %get-tuple-element.71), channel_id=1, source_target_pairs={{1,0},{2,1},{3,2},{5,4},{6,5},{7,6},{9,8},{10,9},{11,10},{13,12},{... | collective-permute-start | bytes 1572872 | tf_op jit(solution)/shard_map/ppermute | solution.py:22
  10.7 18.5 %collective-permute-start.3 = (f32[2,256,256]{2,1,0:T(8,128)}, f32[2,256,256]{2,1,0:T(8,128)S(1)}, u32[]{:S(2)}, u32[]{:S(2)}) collective-permute-start(f32[2,256,256]{2,1,0:T(8,128)} %get-tuple-element.70), channel_id=1, source_target_pairs={{4,0},{8,4},{12,8},{16,12},{20,16},{24,20},{28,24},{32,28},{36,32}... | collective-permute-start | bytes 1572872 | tf_op jit(solution)/shard_map/ppermute | solution.py:22
  18.0 12.8 %copy-start.14 = (f32[2,256,256]{2,1,0:T(8,128)}, f32[2,256,256]{2,1,0:T(8,128)S(1)}, u32[]{:S(2)}) copy-start(f32[2,256,256]{2,1,0:T(8,128)S(1)} %collective-permute-done.below_a) | copy-start | bytes 1572868
  18.0 12.8 %collective-permute-start.4 = (f32[2,256,256]{2,1,0:T(8,128)S(1)}, f32[2,256,256]{2,1,0:T(8,128)S(1)}, u32[]{:S(2)}, u32[]{:S(2)}) collective-permute-start(f32[2,256,256]{2,1,0:T(8,128)S(1)} %collective-permute-done.below_a), channel_id=1, source_target_pairs={{4,0},{8,4},{12,8},{16,12},{20,16},{24,20},{28,24},{32,28},{36,32}... | collective-permute-start | bytes 1572872 | tf_op jit(solution)/shard_map/ppermute | solution.py:22
  29.2 1.6 copy-start.16
  29.2 1.6 copy-start.15
  29.2 1.6 copy-start.17
  30.8 0.8 copy-start.18
  46.0 36.9 %collective-permute-start.5 = (f32[2,2,2,256,128]{4,3,2,1,0:T(8,128)}, f32[2,2,2,256,128]{4,3,2,1,0:T(8,128)S(1)}, u32[]{:S(2)}, u32[]{:S(2)}) collective-permute-start(f32[2,2,2,256,128]{4,3,2,1,0:T(8,128)} %get-tuple-element.37.right_c), channel_id=1, source_target_pairs={{0,4},{4,8},{8,12},{12,16},{16,20},{20,24},{24,28},{28,32},{32,36}... | collective-permute-start | bytes 3145736 | tf_op jit(solution)/shard_map/ppermute | solution.py:22
  49.7 33.1 %collective-permute-start.6 = (f32[2,2,2,256,128]{4,3,2,1,0:T(8,128)}, f32[2,2,2,256,128]{4,3,2,1,0:T(8,128)S(1)}, u32[]{:S(2)}, u32[]{:S(2)}) collective-permute-start(f32[2,2,2,256,128]{4,3,2,1,0:T(8,128)} %get-tuple-element.38.left_c), channel_id=1, source_target_pairs={{4,0},{8,4},{12,8},{16,12},{20,16},{24,20},{28,24},{32,28},{36,32}... | collective-permute-start | bytes 3145736 | tf_op jit(solution)/shard_map/ppermute | solution.py:22
  52.0 30.9 %all-to-all-start = ((f32[128,8,128]{2,1,0:T(8,128)}), f32[128,8,128]{2,1,0:T(8,128)S(1)}, u32[]{:S(2)}, u32[]{:S(2)}) async-start(f32[128,8,128]{2,1,0:T(8,128)} %bitcast.14), calls=%async_computation | async-start | bytes 1048576 | tf_op jit(solution)/shard_map/all_to_all | solution.py:370
  68.5 22.4 %collective-permute-start.7 = (f32[2,2,256,128]{3,2,1,0:T(8,128)}, f32[2,2,256,128]{3,2,1,0:T(8,128)}, u32[]{:S(2)}, u32[]{:S(2)}) collective-permute-start(f32[2,2,256,128]{3,2,1,0:T(8,128)} %get-tuple-element.40.down_b), channel_id=1, source_target_pairs={{0,1},{1,2},{2,3},{4,5},{5,6},{6,7},{8,9},{9,10},{10,11},{12,13},{... | collective-permute-start | bytes 1572872 | tf_op jit(solution)/shard_map/ppermute | solution.py:22
  72.7 18.3 %collective-permute-start.8 = (f32[2,2,256,128]{3,2,1,0:T(8,128)}, f32[2,2,256,128]{3,2,1,0:T(8,128)}, u32[]{:S(2)}, u32[]{:S(2)}) collective-permute-start(f32[2,2,256,128]{3,2,1,0:T(8,128)} %get-tuple-element.41.up_b), channel_id=1, source_target_pairs={{1,0},{2,1},{3,2},{5,4},{6,5},{7,6},{9,8},{10,9},{11,10},{13,12},{... | collective-permute-start | bytes 1572872 | tf_op jit(solution)/shard_map/ppermute | solution.py:22
  82.9 2.6 %copy-start.10 = (f32[2,2,2,256,128]{4,3,2,1,0:T(8,128)}, f32[2,2,2,256,128]{4,3,2,1,0:T(8,128)S(1)}, u32[]{:S(2)}) copy-start(f32[2,2,2,256,128]{4,3,2,1,0:T(8,128)S(1)} %collective-permute-done.5.from_left_c) | copy-start | bytes 3145732
  82.9 2.6 %copy-start.11 = (f32[2,2,2,256,128]{4,3,2,1,0:T(8,128)}, f32[2,2,2,256,128]{4,3,2,1,0:T(8,128)S(1)}, u32[]{:S(2)}) copy-start(f32[2,2,2,256,128]{4,3,2,1,0:T(8,128)S(1)} %collective-permute-done.6.from_right_c) | copy-start | bytes 3145732
  86.5 10.0 %copy-start.13 = (f32[2,2,256,128]{3,2,1,0:T(8,128)S(1)}, f32[2,2,256,128]{3,2,1,0:T(8,128)}, u32[]{:S(2)}) copy-start(f32[2,2,256,128]{3,2,1,0:T(8,128)} %get-tuple-element.50.left_b) | copy-start | bytes 1572868
  86.5 36.2 %collective-permute-start.9 = (f32[2,2,2,256,128]{4,3,2,1,0:T(8,128)}, f32[2,2,2,256,128]{4,3,2,1,0:T(8,128)S(1)}, u32[]{:S(2)}, u32[]{:S(2)}) collective-permute-start(f32[2,2,2,256,128]{4,3,2,1,0:T(8,128)} %pad_maximum_fusion), channel_id=1, source_target_pairs={{0,1},{1,2},{2,3},{4,5},{5,6},{6,7},{8,9},{9,10},{10,11},{12,13},{... | collective-permute-start | bytes 3145736 | tf_op jit(solution)/shard_map/ppermute | solution.py:22
  89.6 33.1 %collective-permute-start.10 = (f32[2,2,2,256,128]{4,3,2,1,0:T(8,128)}, f32[2,2,2,256,128]{4,3,2,1,0:T(8,128)}, u32[]{:S(2)}, u32[]{:S(2)}) collective-permute-start(f32[2,2,2,256,128]{4,3,2,1,0:T(8,128)} %pad_maximum_fusion.1), channel_id=1, source_target_pairs={{1,0},{2,1},{3,2},{5,4},{6,5},{7,6},{9,8},{10,9},{11,10},{13,12},{... | collective-permute-start | bytes 3145736 | tf_op jit(solution)/shard_map/ppermute | solution.py:22
  91.9 30.8 %collective-permute-start.11 = (f32[2,2,256,128]{3,2,1,0:T(8,128)}, f32[2,2,256,128]{3,2,1,0:T(8,128)S(1)}, u32[]{:S(2)}, u32[]{:S(2)}) collective-permute-start(f32[2,2,256,128]{3,2,1,0:T(8,128)} %get-tuple-element.51.right_b), channel_id=1, source_target_pairs={{0,4},{4,8},{8,12},{12,16},{16,20},{20,24},{24,28},{28,32},{32,36}... | collective-permute-start | bytes 1572872 | tf_op jit(solution)/shard_map/ppermute | solution.py:22
  96.5 26.2 %collective-permute-start.12 = (f32[2,2,256,128]{3,2,1,0:T(8,128)S(1)}, f32[2,2,256,128]{3,2,1,0:T(8,128)}, u32[]{:S(2)}, u32[]{:S(2)}) collective-permute-start(f32[2,2,256,128]{3,2,1,0:T(8,128)S(1)} %copy-done.13), channel_id=1, source_target_pairs={{4,0},{8,4},{12,8},{16,12},{20,16},{24,20},{28,24},{32,28},{36,32}... | collective-permute-start | bytes 1572872 | tf_op jit(solution)/shard_map/ppermute | solution.py:22
  98.5 24.2 %all-to-all-start.1 = ((f32[128,8,128]{2,1,0:T(8,128)}), f32[128,8,128]{2,1,0:T(8,128)S(1)}, u32[]{:S(2)}, u32[]{:S(2)}) async-start(f32[128,8,128]{2,1,0:T(8,128)} %sum_shares.2), calls=%async_computation.1 | async-start | bytes 1048576 | tf_op jit(solution)/shard_map/all_to_all | solution.py:370
  109.5 14.2 %copy-start = (f32[2,256,2,128]{3,1,2,0:T(8,128)S(1)}, f32[2,256,2,128]{3,1,2,0:T(8,128)}, u32[]{:S(2)}) copy-start(f32[2,256,2,128]{3,1,2,0:T(8,128)} %copy.13) | copy-start | bytes 1572868
  109.5 14.2 %copy-start.4 = (s32[2,12]{1,0:T(2,128)S(1)}, s32[2,12]{1,0:T(2,128)}, u32[]{:S(2)}) copy-start(s32[2,12]{1,0:T(2,128)} %batch.3) | copy-start | bytes 292
  109.5 14.2 %copy-start.5 = (s32[2,1]{1,0:T(2,128)S(1)}, s32[2,1]{1,0:T(2,128)}, u32[]{:S(2)}) copy-start(s32[2,1]{1,0:T(2,128)} %copy.15.live) | copy-start | bytes 28
  109.5 14.2 %copy-start.6 = (s32[2]{0:T(128)S(1)}, s32[2]{0:T(128)}, u32[]{:S(2)}) copy-start(s32[2]{0:T(128)} %add_convert_fusion.edge) | copy-start | bytes 28
  109.5 14.2 %copy-start.7 = (s32[32]{0:T(128)S(1)}, s32[32]{0:T(128)}, u32[]{:S(2)}) copy-start(s32[32]{0:T(128)} %rows.3) | copy-start | bytes 388
  109.6 14.2 %copy-start.8 = (s32[32]{0:T(128)S(1)}, s32[32]{0:T(128)}, u32[]{:S(2)}) copy-start(s32[32]{0:T(128)} %cols.3) | copy-start | bytes 388
  122.7 1.0 copy-start.12
  145.5 0.8 copy-start.3
  146.3 0.8 copy-start.9
  147.1 13.1 %collective-permute-start.13 = (f32[2,2,256,128]{3,2,1,0:T(8,128)}, f32[2,2,256,128]{3,2,1,0:T(8,128)}, u32[]{:S(2)}, u32[]{:S(2)}) collective-permute-start(f32[2,2,256,128]{3,2,1,0:T(8,128)} %get-tuple-element.57), channel_id=1, source_target_pairs={{0,4},{4,8},{8,12},{12,16},{16,20},{20,24},{24,28},{28,32},{32,36}... | collective-permute-start | bytes 1572872 | tf_op jit(solution)/shard_map/ppermute | solution.py:22
  150.2 23.4 %all-to-all-start.2 = ((f32[128,8,128]{2,1,0:T(8,128)}), f32[128,8,128]{2,1,0:T(8,128)}, u32[]{:S(2)}, u32[]{:S(2)}) async-start(f32[128,8,128]{2,1,0:T(8,128)} %bitcast.6), calls=%async_computation.2 | async-start | bytes 1048576 | tf_op jit(solution)/shard_map/all_to_all | solution.py:370
  160.2 46.5 %copy-start.1 = (f32[2,4,512,128]{3,2,1,0:T(8,128)S(1)}, f32[2,4,512,128]{3,2,1,0:T(8,128)}, u32[]{:S(2)}) copy-start(f32[2,4,512,128]{3,2,1,0:T(8,128)} %get-tuple-element.54.own) | copy-start | bytes 6291460
  174.8 0.8 copy-start.2
  175.6 31.1 %collective-permute-start.14 = (f32[2,2,512,128]{3,2,1,0:T(8,128)}, f32[2,2,512,128]{3,2,1,0:T(8,128)}, u32[]{:S(2)}, u32[]{:S(2)}) collective-permute-start(f32[2,2,512,128]{3,2,1,0:T(8,128)} %get-tuple-element.61), channel_id=1, source_target_pairs={{0,4},{4,8},{8,12},{12,16},{16,20},{20,24},{24,28},{28,32},{32,36}... | collective-permute-start | bytes 3145736 | tf_op jit(solution)/shard_map/ppermute | solution.py:22
  178.3 13.2 %collective-permute-start.15 = (f32[2,2,256,128]{3,2,1,0:T(8,128)}, f32[2,2,256,128]{3,2,1,0:T(8,128)}, u32[]{:S(2)}, u32[]{:S(2)}) collective-permute-start(f32[2,2,256,128]{3,2,1,0:T(8,128)} %add.23), channel_id=1, source_target_pairs={{0,1},{1,2},{2,3},{4,5},{5,6},{6,7},{8,9},{9,10},{10,11},{12,13},{... | collective-permute-start | bytes 1572872 | tf_op jit(solution)/shard_map/ppermute | solution.py:22
  181.3 25.4 %collective-permute-start.16 = (f32[2,2,256,128]{3,2,1,0:T(8,128)}, f32[2,2,256,128]{3,2,1,0:T(8,128)}, u32[]{:S(2)}, u32[]{:S(2)}) collective-permute-start(f32[2,2,256,128]{3,2,1,0:T(8,128)} %copy-done.9), channel_id=1, source_target_pairs={{0,1},{1,2},{2,3},{4,5},{5,6},{6,7},{8,9},{9,10},{10,11},{12,13},{... | collective-permute-start | bytes 1572872 | tf_op jit(solution)/shard_map/ppermute | solution.py:22
  183.7 28.5 %all-to-all-start.3 = ((f32[128,8,128]{2,1,0:T(8,128)}), f32[128,8,128]{2,1,0:T(8,128)}, u32[]{:S(2)}, u32[]{:S(2)}) async-start(f32[128,8,128]{2,1,0:T(8,128)} %copy-done.2), calls=%async_computation.3 | async-start | bytes 1048576 | tf_op jit(solution)/shard_map/all_to_all | solution.py:370
